TPU v7x, 32 devices: a whole 2x2x4 slice. The times are simulated.
32 devices in a mesh: dp: 8 (over y, x, core), tensor: 4 (over z).
Axes of the slice: x: 2, y: 2, z: 4, core: 2. Of those that a mesh axis runs over, the one named last changes fastest.
Arguments:
- tokens: bfloat16 [8192, 2048], P('dp'), may hold values from -6 to 6
- project_weight: float32 [2048, 6144], P('dp', 'tensor'), may hold values from -0.125 to 0.125
- project_bias: float32 [8, 768], P('tensor', 'dp'), may hold values from -1.2 to 1.2
- dense_weight: float32 [2048, 2048], P('tensor', 'dp'), may hold values from -2 to 2
- dense_bias: float32 [2048], P('dp'), may hold values from -1.2 to 1.2
- expand_weight: float32 [2048, 8192], P('dp', 'tensor'), may hold values from -0.125 to 0.125
- expand_bias: float32 [8, 1024], P('tensor', 'dp'), may hold values from -1.2 to 1.2
- shrink_weight: float32 [8192, 2048], P('tensor', 'dp'), may hold values from -0.0625 to 0.0625
- shrink_bias: float32 [2048], P('dp'), may hold values from -1.2 to 1.2
- first_gain: float32 [2048], P('dp'), may hold values from 0.5 to 1.5
- first_shift: float32 [2048], P('dp'), may hold values from -1.2 to 1.2
- second_gain: float32 [2048], P('dp'), may hold values from 0.5 to 1.5
- second_shift: float32 [2048], P('dp'), may hold values from -1.2 to 1.2
- lengths: int32 [24], replicated, may hold values from 0 to 1024, as said below
- prefix: int32 [24], replicated, may hold values from 102 to 512
- upstream: bfloat16 [8192, 2048], P('dp'), may hold values from -6 to 6
Outputs:
- output: bfloat16 [8192, 2048], P('dp')
- tokens_grad: bfloat16 [8192, 2048], P('dp')
- project_weight_grad: float32 [2048, 6144], P('dp', 'tensor')
- project_bias_grad: float32 [8, 768], P('tensor', 'dp')
- dense_weight_grad: float32 [2048, 2048], P('tensor', 'dp')
- dense_bias_grad: float32 [2048], P('dp')
- expand_weight_grad: float32 [2048, 8192], P('dp', 'tensor')
- expand_bias_grad: float32 [8, 1024], P('tensor', 'dp')
- shrink_weight_grad: float32 [8192, 2048], P('tensor', 'dp')
- shrink_bias_grad: float32 [2048], P('dp')
- first_gain_grad: float32 [2048], P('dp')
- first_shift_grad: float32 [2048], P('dp')
- second_gain_grad: float32 [2048], P('dp')
- second_shift_grad: float32 [2048], P('dp')
Inputs may be any that keep to these rules, and one draw needn't show every extreme that they name: `lengths`: sequences lie end to end in order and fill all 8192 rows; some slots are empty (length 0); the longest has exactly 1024 tokens; every boundary between blocks of 1024 rows lies inside a sequence.
All inputs are finite; a program needn't handle non-finite values.
Results may differ from a plain program's by a relative error of at most 0.025.
Values may be sent and summed in bfloat16 or wider, within the bound.
No kernel may reach another device: no remote copies, remote signals or barrier semaphores. Data moves between devices by JAX's collectives and lax.ppermute only.
A program may use at most 256 MiB of HBM per device.

v0:
```python
import functools
import math

import jax
import jax.numpy as jnp
from jax import lax
from jax.sharding import PartitionSpec as P

HD = 256
ROT = 64
SEQ_MAX = 1024


EPSILON = 1e-05
MASKED = -1e30


def with_halo(cells, sides, width):
    for axis, dim in sides:
        count = lax.axis_size(axis)
        ends = count - 1
        head = lax.slice_in_dim(cells, 0, width, axis=dim)
        tail = lax.slice_in_dim(cells, cells.shape[dim] - width, cells.shape[dim], axis=dim)
        cells = jnp.concatenate(
            [
                lax.ppermute(tail, axis, [(i, (i + 1) % count) for i in range(ends)]),
                cells,
                lax.ppermute(head, axis, [((i + 1) % count, i) for i in range(ends)]),
            ],
            axis=dim,
        )
    return cells


def rotary(values, places):
    half_rot = ROT // 2
    exponents = jnp.arange(half_rot).astype(jnp.float32) * (2.0 / ROT)
    frequency = jnp.exp(exponents * -math.log(10000.0))
    angles = places[:, None] * frequency[None, :]
    cosine = jnp.cos(angles)[:, None, :]
    sines = jnp.sin(angles)[:, None, :]
    leading = values[:, :, :half_rot]
    trailing = values[:, :, half_rot:ROT]
    return jnp.concatenate(
        [
            leading * cosine - trailing * sines,
            trailing * cosine + leading * sines,
            values[:, :, ROT:],
        ],
        axis=2,
    )


def locate(token_index, lengths, prefix, total_rows):
    seq_count = lengths.shape[0]
    starts = jnp.cumsum(lengths) - lengths
    inside = (token_index >= 0) & (token_index < total_rows)
    member = jnp.sum((starts[None, :] <= token_index[:, None]).astype(jnp.int32), axis=1) - 1
    member = jnp.where(inside, member, -1)
    onehot = jnp.arange(seq_count, dtype=jnp.int32)[None, :] == member[:, None]
    seq_begin = jnp.sum(jnp.where(onehot, starts[None, :], 0), axis=1)
    limits = jnp.sum(jnp.where(onehot, jnp.minimum(prefix, lengths)[None, :], 0), axis=1)
    return (member, token_index - seq_begin, limits)


def visible(query_index, key_index, lengths, prefix, total_rows):
    query_member, unused_place, query_limit = locate(query_index, lengths, prefix, total_rows)
    key_member, key_place, unused_limit = locate(key_index, lengths, prefix, total_rows)
    same_seq = (query_member[:, None] == key_member[None, :]) & (key_member[None, :] >= 0)
    earlier = key_index[None, :] <= query_index[:, None]
    opened = key_place[None, :] < query_limit[:, None]
    return same_seq & (earlier | opened)


def on_device(
    tokens,
    project_weight,
    project_bias,
    dense_weight,
    dense_bias,
    expand_weight,
    expand_bias,
    shrink_weight,
    shrink_bias,
    first_gain,
    first_shift,
    second_gain,
    second_shift,
    lengths,
    prefix,
    upstream,
):
    row_count = tokens.shape[0]
    total_rows = row_count * lax.axis_size("dp")
    shard_index = lax.axis_index("dp")
    halo_width = SEQ_MAX
    scale = HD ** (-0.5)
    block_rows = 512
    block_count = row_count // block_rows
    window = block_rows + 2 * halo_width
    bf16 = jnp.bfloat16
    f32 = jnp.float32
    gathered = (
        lax.all_gather(project_weight.astype(bf16), "dp", axis=0, tiled=True),
        lax.all_gather(project_bias.astype(bf16), "dp", axis=1, tiled=True),
        lax.all_gather(dense_weight.astype(bf16), "dp", axis=1, tiled=True),
        lax.all_gather(dense_bias.astype(bf16), "dp", axis=0, tiled=True),
        lax.all_gather(expand_weight.astype(bf16), "dp", axis=0, tiled=True),
        lax.all_gather(expand_bias.astype(bf16), "dp", axis=1, tiled=True),
        lax.all_gather(shrink_weight.astype(bf16), "dp", axis=1, tiled=True),
        lax.all_gather(shrink_bias.astype(bf16), "dp", axis=0, tiled=True),
        lax.all_gather(first_gain.astype(bf16), "dp", axis=0, tiled=True),
        lax.all_gather(first_shift.astype(bf16), "dp", axis=0, tiled=True),
        lax.all_gather(second_gain.astype(bf16), "dp", axis=0, tiled=True),
        lax.all_gather(second_shift.astype(bf16), "dp", axis=0, tiled=True),
    )
    (
        full_project,
        full_project_bias,
        full_dense,
        full_dense_bias,
        full_expand,
        full_expand_bias,
        full_shrink,
        full_shrink_bias,
        gain_one,
        shift_one,
        gain_two,
        shift_two,
    ) = gathered
    head_local = full_project_bias.shape[0]
    token_values = tokens.astype(f32)
    center = token_values - jnp.mean(token_values, axis=1, keepdims=True)
    inverse = lax.rsqrt(jnp.mean(center * center, axis=1, keepdims=True) + EPSILON)
    normed = center * inverse
    first_normed = (normed * gain_one.astype(f32) + shift_one.astype(f32)).astype(bf16)
    second_normed = (normed * gain_two.astype(f32) + shift_two.astype(f32)).astype(bf16)
    mixed_rows = jnp.dot(
        first_normed, full_project, preferred_element_type=f32
    ) + full_project_bias.astype(f32).reshape(-1)
    mixed_rows = mixed_rows.reshape(row_count, head_local, 3, HD)
    token_index = shard_index * row_count + jnp.arange(row_count, dtype=jnp.int32)
    unused_member, places, unused_limit = locate(token_index, lengths, prefix, total_rows)
    places = places.astype(f32)
    queries = rotary(mixed_rows[:, :, 0], places).astype(bf16)
    key_rows = rotary(mixed_rows[:, :, 1], places).astype(bf16)
    value_rows = mixed_rows[:, :, 2].astype(bf16)
    extended = with_halo(jnp.stack([key_rows, value_rows]), (("dp", 1),), halo_width)
    key_ext = extended[0]
    value_ext = extended[1]

    def block_scores(block_index):
        query_start = block_index * block_rows
        query_block = lax.dynamic_slice_in_dim(queries, query_start, block_rows, 0)
        key_block = lax.dynamic_slice_in_dim(key_ext, query_start, window, 0)
        value_block = lax.dynamic_slice_in_dim(value_ext, query_start, window, 0)
        query_index = (
            shard_index * row_count + query_start + jnp.arange(block_rows, dtype=jnp.int32)
        )
        key_index = query_index[0] - halo_width + jnp.arange(window, dtype=jnp.int32)
        allowed = visible(query_index, key_index, lengths, prefix, total_rows)
        raw_scores = (
            jnp.einsum("qhd,khd->hqk", query_block, key_block, preferred_element_type=f32) * scale
        )
        return (query_block, key_block, value_block, jnp.where(allowed[None], raw_scores, MASKED))

    def forward_block(block_index):
        query_block, key_block, value_block, scores = block_scores(block_index)
        largest = jnp.max(scores, axis=2, keepdims=True)
        weights = jnp.exp(scores - largest)
        totals = jnp.sum(weights, axis=2, keepdims=True)
        probs = weights / totals
        result = jnp.einsum(
            "hqk,khd->qhd", probs.astype(bf16), value_block, preferred_element_type=f32
        )
        return (result, largest[:, :, 0] + jnp.log(totals[:, :, 0]))

    attended_blocks, log_totals = lax.map(forward_block, jnp.arange(block_count, dtype=jnp.int32))
    attended = attended_blocks.reshape(row_count, head_local * HD).astype(bf16)
    hidden = jnp.dot(
        second_normed, full_expand, preferred_element_type=f32
    ) + full_expand_bias.astype(f32).reshape(-1)
    active = jax.nn.gelu(hidden, approximate=False).astype(bf16)
    partial_sum = jnp.dot(attended, full_dense, preferred_element_type=f32) + jnp.dot(
        active, full_shrink, preferred_element_type=f32
    )
    bias_total = full_dense_bias.astype(f32) + full_shrink_bias.astype(f32)
    branch = lax.psum(partial_sum.astype(jnp.bfloat16), "tensor").astype(jnp.float32)
    output = (token_values + branch + bias_total).astype(bf16)
    again = (
        lax.all_gather(project_weight.astype(bf16), "dp", axis=0, tiled=True),
        lax.all_gather(dense_weight.astype(bf16), "dp", axis=1, tiled=True),
        lax.all_gather(expand_weight.astype(bf16), "dp", axis=0, tiled=True),
        lax.all_gather(shrink_weight.astype(bf16), "dp", axis=1, tiled=True),
        lax.all_gather(first_gain.astype(bf16), "dp", axis=0, tiled=True),
        lax.all_gather(second_gain.astype(bf16), "dp", axis=0, tiled=True),
    )
    full_project, full_dense, full_expand, full_shrink, gain_one, gain_two = again
    grad_out = upstream.astype(f32)
    grad_bias = jnp.sum(grad_out, axis=0)
    grad_attended = jnp.einsum(
        "td,ad->ta", upstream, full_dense, preferred_element_type=f32
    ).astype(bf16)
    grad_active = jnp.einsum("td,fd->tf", upstream, full_shrink, preferred_element_type=f32)
    unused_value, gelu_back = jax.vjp(functools.partial(jax.nn.gelu, approximate=False), hidden)
    grad_hidden = gelu_back(grad_active)[0].astype(bf16)
    grad_shrink = jnp.einsum("tf,td->fd", active, upstream, preferred_element_type=f32)
    grad_dense = jnp.einsum("ta,td->ad", attended, upstream, preferred_element_type=f32)
    grad_expand = jnp.einsum("td,tf->df", second_normed, grad_hidden, preferred_element_type=f32)
    grad_expand_bias = jnp.sum(grad_hidden.astype(f32), axis=0).reshape(head_local, -1)
    grad_second = jnp.einsum("tf,df->td", grad_hidden, full_expand, preferred_element_type=f32)
    grad_heads = grad_attended.reshape(row_count, head_local, HD)
    zeros_ext = jnp.zeros((2, row_count + 2 * halo_width, head_local, HD), f32)

    def backward_block(carry, block_index):
        query_block, key_block, value_block, scores = block_scores(block_index)
        query_start = block_index * block_rows
        probs = jnp.exp(scores - log_totals[block_index][:, :, None])
        grad_block = lax.dynamic_slice_in_dim(grad_heads, query_start, block_rows, 0)
        grad_probs = jnp.einsum("qhd,khd->hqk", grad_block, value_block, preferred_element_type=f32)
        delta = jnp.sum(probs * grad_probs, axis=2, keepdims=True)
        grad_scores = (probs * (grad_probs - delta)).astype(bf16)
        grad_query = (
            jnp.einsum("hqk,khd->qhd", grad_scores, key_block, preferred_element_type=f32) * scale
        )
        grad_key = (
            jnp.einsum("hqk,qhd->khd", grad_scores, query_block, preferred_element_type=f32) * scale
        )
        grad_value = jnp.einsum(
            "hqk,qhd->khd", probs.astype(bf16), grad_block, preferred_element_type=f32
        )
        window_now = lax.dynamic_slice_in_dim(carry, query_start, window, 1)
        carry = lax.dynamic_update_slice_in_dim(
            carry, window_now + jnp.stack([grad_key, grad_value]), query_start, 1
        )
        return (carry, grad_query)

    grad_ext, grad_queries = lax.scan(
        backward_block, zeros_ext, jnp.arange(block_count, dtype=jnp.int32)
    )
    outgoing = jnp.concatenate(
        [grad_ext[:, :halo_width], grad_ext[:, row_count + halo_width :]], axis=1
    )
    incoming = with_halo(outgoing.astype(jnp.bfloat16), (("dp", 1),), halo_width).astype(
        outgoing.dtype
    )
    own_grads = grad_ext[:, halo_width : halo_width + row_count]
    own_grads = own_grads.at[:, :halo_width].add(incoming[:, :halo_width])
    own_grads = own_grads.at[:, row_count - halo_width :].add(incoming[:, 3 * halo_width :])
    grad_queries = grad_queries.reshape(row_count, head_local, HD)
    grad_mixed = jnp.stack(
        [rotary(grad_queries, -places), rotary(own_grads[0], -places), own_grads[1]], axis=2
    )
    grad_mixed = grad_mixed.reshape(row_count, head_local * 3 * HD).astype(bf16)
    grad_project = jnp.einsum("td,tc->dc", first_normed, grad_mixed, preferred_element_type=f32)
    grad_project_bias = jnp.sum(grad_mixed.astype(f32), axis=0).reshape(head_local, -1)
    grad_first = jnp.einsum("tc,dc->td", grad_mixed, full_project, preferred_element_type=f32)
    grad_normed = grad_first * gain_one.astype(f32) + grad_second * gain_two.astype(f32)
    part_gain_one = jnp.sum(grad_first * normed, axis=0)
    part_shift_one = jnp.sum(grad_first, axis=0)
    part_gain_two = jnp.sum(grad_second * normed, axis=0)
    part_shift_two = jnp.sum(grad_second, axis=0)
    part_tokens = inverse * (
        grad_normed
        - jnp.mean(grad_normed, axis=1, keepdims=True)
        - normed * jnp.mean(grad_normed * normed, axis=1, keepdims=True)
    )
    summed = (
        lax.psum(part_tokens.astype(jnp.bfloat16), "tensor").astype(jnp.float32),
        lax.psum(part_gain_one.astype(jnp.bfloat16), "tensor").astype(jnp.float32),
        lax.psum(part_shift_one.astype(jnp.bfloat16), "tensor").astype(jnp.float32),
        lax.psum(part_gain_two.astype(jnp.bfloat16), "tensor").astype(jnp.float32),
        lax.psum(part_shift_two.astype(jnp.bfloat16), "tensor").astype(jnp.float32),
    )
    tokens_grad = (grad_out + summed[0]).astype(bf16)
    grads = (
        lax.psum_scatter(
            grad_project.astype(jnp.bfloat16), "dp", scatter_dimension=0, tiled=True
        ).astype(jnp.float32),
        lax.psum_scatter(
            grad_project_bias.astype(jnp.bfloat16), "dp", scatter_dimension=1, tiled=True
        ).astype(jnp.float32),
        lax.psum_scatter(
            grad_dense.astype(jnp.bfloat16), "dp", scatter_dimension=1, tiled=True
        ).astype(jnp.float32),
        lax.psum_scatter(
            grad_bias.astype(jnp.bfloat16), "dp", scatter_dimension=0, tiled=True
        ).astype(jnp.float32),
        lax.psum_scatter(
            grad_expand.astype(jnp.bfloat16), "dp", scatter_dimension=0, tiled=True
        ).astype(jnp.float32),
        lax.psum_scatter(
            grad_expand_bias.astype(jnp.bfloat16), "dp", scatter_dimension=1, tiled=True
        ).astype(jnp.float32),
        lax.psum_scatter(
            grad_shrink.astype(jnp.bfloat16), "dp", scatter_dimension=1, tiled=True
        ).astype(jnp.float32),
        lax.psum_scatter(
            summed[1].astype(jnp.bfloat16), "dp", scatter_dimension=0, tiled=True
        ).astype(jnp.float32),
        lax.psum_scatter(
            summed[2].astype(jnp.bfloat16), "dp", scatter_dimension=0, tiled=True
        ).astype(jnp.float32),
        lax.psum_scatter(
            summed[3].astype(jnp.bfloat16), "dp", scatter_dimension=0, tiled=True
        ).astype(jnp.float32),
        lax.psum_scatter(
            summed[4].astype(jnp.bfloat16), "dp", scatter_dimension=0, tiled=True
        ).astype(jnp.float32),
    )
    return (
        output,
        tokens_grad,
        grads[0],
        grads[1],
        grads[2],
        grads[3],
        grads[4],
        grads[5],
        grads[6],
        grads[3],
        grads[7],
        grads[8],
        grads[9],
        grads[10],
    )


def solution(mesh):
    placed = (
        P("dp", None),
        P("dp", "tensor"),
        P("tensor", "dp"),
        P("tensor", "dp"),
        P("dp"),
        P("dp", "tensor"),
        P("tensor", "dp"),
        P("tensor", "dp"),
        P("dp"),
        P("dp"),
        P("dp"),
        P("dp"),
        P("dp"),
        P(),
        P(),
        P("dp", None),
    )
    return jax.shard_map(
        on_device,
        mesh=mesh,
        in_specs=placed,
        out_specs=(
            P("dp", None),
            P("dp", None),
            P("dp", "tensor"),
            P("tensor", "dp"),
            P("tensor", "dp"),
            P("dp"),
            P("dp", "tensor"),
            P("tensor", "dp"),
            P("tensor", "dp"),
            P("dp"),
            P("dp"),
            P("dp"),
            P("dp"),
            P("dp"),
        ),
        check_vma=False,
    )
```

profile of v0, /device:TPU:0, one launch (start us, length us, event | category | flops | bytes accessed | tf_op | source)
XLA Modules:
  0.0 1154.5 jit_solution(17408892827401054506)
XLA Ops:
  14.6 10.4 all-gather
  25.1 8.9 all-gather.1
  34.0 7.8 all-gather.2
  47.6 11.2 all-gather.12.cloned.1.call-done
  58.8 12.3 %convolution_add_fusion = f32[1024,1536]{1,0:T(8,128)} fusion(bf16[2048,1536]{1,0:T(8,128)(2,1)} %all-gather.12.cloned.1.call-done, f32[1536]{0:T(1024)S(1)} %reshape.750, bf16[1024,2048]{1,0:T(8,128)(2,1)} %param.28, f32[2048]{0:T(1024)S(1)} %bitcast.182, f32[2048]{0:T(1024)S(1)} %bitcast.179, f32[1024]{0:T(1024)S(1)} %add_rsqrt_fusion, ...), kind=kOutput, calls=%fused_computation.126 | convolution fusion | flops 6456606720 | bytes 16807936 | tf_op jit(solution)/shard_map/dot_general | solution.py:138
  71.1 6.6 copy.108
  93.5 69.6 %all-gather.3 = bf16[8,1,256]{2,1,0:T(2,128)(2,1)S(1)} all-gather(bf16[1,1,256]{2,1,0:T(2,128)(2,1)S(1)} %reshape.758), channel_id=1, replica_groups=mesh['dp'=8,'tensor'=4] {'dp'}, dimensions={0}, use_global_device_ids=true | all-gather | bytes 4608 | tf_op jit(solution)/shard_map/all_gather | solution.py:114
  163.7 9.7 all-gather.4
  174.1 7.7 all_gather.50
  204.6 36.7 %while.34 = (s32[]{:T(128)}, bf16[2,512,2,256]{1,3,2,0:T(8,128)(2,1)}, f32[2,2,512]{2,1,0:T(2,128)S(1)}, s32[2]{0:T(128)S(1)}, bf16[3072,2,256]{0,2,1:T(8,128)(2...) while((s32[]{:T(128)}, ...), condition=%wide.region_12.13_spmd, body=%wide.region_5.12_spmd.sunk | while | flops 2724140544 | bytes 43698348 | solution.py:178
  216.8 6.2 fusion.144
  246.9 205.1 %while.35 = (s32[]{:T(128)}, f32[2,3072,2,256]{3,1,2,0:T(8,128)}, f32[2,512,2,256]{3,1,0,2:T(8,128)}, s32[2]{0:T(128)S(1)}, bf16[1024,2,256]{2,0,1:T(8,128)(2,1)...) while((s32[]{:T(128)}, f32[2,3072,2,256]{3,1,2,0:T(8,128)}, ...), condition=%wide.region_20.21_spmd, body=%wide.region_14.20_spmd.sunk | while | flops 6749623808 | bytes 378706560 | solution.py:238
  248.7 7.2 fusion.153
  261.6 10.4 multiply_reduce_fusion.2
  272.5 8.8 multiply_convert_fusion.3
  281.3 7.0 multiply_bitcast_fusion.2
  298.8 11.5 copy.162
  310.3 13.2 %maximum_add_fusion.2 = f32[2,2560,2,256]{1,3,2,0:T(8,128)} fusion(f32[2,2560,2,256]{1,3,2,0:T(8,128)} %copy.162, f32[1,2560,2,256]{1,3,2,0:T(8,128)} %fusion.155, f32[1,2560,2,256]{1,3,2,0:T(8,128)} %multiply_bitcast_fusion.2), kind=kLoop, calls=%fused_computation.33.clone.1 | loop fusion | flops 5242880 | bytes 31457280 | tf_op jit(solution)/shard_map/while/body/eval_jaxpr/add | solution.py:234
  323.5 11.6 %copy.163 = f32[2,2560,2,256]{3,1,2,0:T(8,128)} copy(f32[2,2560,2,256]{1,3,2,0:T(8,128)} %maximum_add_fusion.2) | data formatting | bytes 20971520 | tf_op jit(solution)/shard_map/while/body/eval_jaxpr/dynamic_update_slice | solution.py:233
  335.1 9.0 constant_dynamic-update-slice_fusion.4
  351.0 7.2 fusion.153
  363.9 10.4 multiply_reduce_fusion.2
  374.8 8.8 multiply_convert_fusion.3
  383.6 7.0 multiply_bitcast_fusion.2
  401.1 11.5 copy.162
  412.6 13.2 %maximum_add_fusion.2 = f32[2,2560,2,256]{1,3,2,0:T(8,128)} fusion(f32[2,2560,2,256]{1,3,2,0:T(8,128)} %copy.162, f32[1,2560,2,256]{1,3,2,0:T(8,128)} %fusion.155, f32[1,2560,2,256]{1,3,2,0:T(8,128)} %multiply_bitcast_fusion.2), kind=kLoop, calls=%fused_computation.33.clone.1 | loop fusion | flops 5242880 | bytes 31457280 | tf_op jit(solution)/shard_map/while/body/eval_jaxpr/add | solution.py:234
  425.8 11.6 %copy.163 = f32[2,2560,2,256]{3,1,2,0:T(8,128)} copy(f32[2,2560,2,256]{1,3,2,0:T(8,128)} %maximum_add_fusion.2) | data formatting | bytes 20971520 | tf_op jit(solution)/shard_map/while/body/eval_jaxpr/dynamic_update_slice | solution.py:233
  437.3 9.0 constant_dynamic-update-slice_fusion.4
  468.5 14.6 %fusion.86 = f32[1024,2048]{1,0:T(8,128)} fusion(bf16[2048,2048]{1,0:T(8,128)(2,1)} %all-gather.16.cloned.1.call-done, bf16[1024,2048]{1,0:T(8,128)(2,1)} %param.28, f32[2048]{0:T(1024)S(1)} %bitcast.187, f32[2048]{0:T(1024)S(1)} %bitcast.184, f32[1024]{0:T(1024)S(1)} %copy-done.24, f32[1024]{0:T(1024)S(1)} %copy-done.20), kind=kOutput, calls=%fused_computation.184 | convolution fusion | flops 8602517504 | bytes 20996096 | tf_op jit(solution)/shard_map/dot_general | solution.py:180
  483.1 33.2 %fusion.93 = (bf16[2048]{0:T(1024)(128)(2,1)S(1)}, bf16[1024,2048]{1,0:T(8,128)(2,1)}, f32[1024,2048]{1,0:T(8,128)}) fusion(f32[1024,2048]{1,0:T(8,128)} %fusion.86, f32[2048]{0:T(1024)S(1)} %bitcast.172, bf16[1024,2048]{1,0:T(8,128)(2,1)} %param.43, bf16[2048,2048]{1,0:T(8,128)(2,1)} %all-gather.18.cloned.1.call-done), kind=kOutput, calls=%fused_computation.188 | convolution fusion | flops 8745121792 | bytes 33566720 | tf_op jit(solution)/shard_map/td,fd->tf/dot_general | solution.py:204
  527.8 6.2 convolution_convert_fusion.3
  534.1 10.0 multiply_convert_fusion.1
  544.2 13.0 %fusion.98 = f32[1024,2048]{1,0:T(8,128)S(1)} fusion(bf16[1024,2048]{1,0:T(8,128)(2,1)} %multiply_convert_fusion.1, bf16[2048,2048]{1,0:T(8,128)(2,1)} %all-gather.18.cloned.1.call-done), kind=kOutput, calls=%fused_computation.192 | convolution fusion | flops 8589934592 | bytes 20971520 | tf_op jit(solution)/shard_map/dot_general | solution.py:184
  564.6 11.8 %fusion.99 = f32[1024,2048]{1,0:T(8,128)} fusion(bf16[1024,1536]{0,1:T(8,128)(2,1)} %bitcast.157, bf16[2048,1536]{1,0:T(8,128)(2,1)} %all-gather.12.cloned.1.call-done), kind=kOutput, calls=%fused_computation.193 | convolution fusion | flops 6442450944 | bytes 17825792 | tf_op jit(solution)/shard_map/tc,dc->td/dot_general | solution.py:257
  576.5 20.5 %fusion.90 = (bf16[2048]{0:T(1024)(128)(2,1)S(1)}, bf16[2048]{0:T(1024)(128)(2,1)S(1)}, f32[1024]{0:T(1024)S(1)}, f32[1024]{0:T(1024)S(1)}, f32[1024,2048]{1,0:T...) fusion(f32[1024]{0:T(1024)S(1)} %copy-done.25, f32[1024]{0:T(1024)S(1)} %copy-done.21, ...), kind=kOutput, calls=%fused_computation.185 | convolution fusion | flops 8621381632 | bytes 33603584 | tf_op jit(solution)/shard_map/tf,df->td/dot_general | solution.py:211
  597.0 7.6 fusion.65
  606.6 13.1 %convolution_convert_fusion.2 = bf16[2048,1536]{1,0:T(8,128)(2,1)} fusion(bf16[1024,1536]{0,1:T(8,128)(2,1)S(1)} %bitcast.158, bf16[1024,2048]{1,0:T(8,128)(2,1)} %param.28, f32[2048]{0:T(1024)S(1)} %bitcast.183, f32[2048]{0:T(1024)S(1)} %bitcast.181, f32[1024]{0:T(1024)S(1)} %copy-done.25, f32[1024]{0:T(1024)S(1)} %copy-done.21), kind=kOutput, calls=%fused_computation.123 | convolution fusion | flops 6458179584 | bytes 13656064 | tf_op jit(solution)/shard_map/td,tc->dc/dot_general | solution.py:255
  619.8 14.4 %convolution_convert_fusion = bf16[2048,2048]{1,0:T(8,128)(2,1)} fusion(bf16[1024,2048]{1,0:T(8,128)(2,1)} %multiply_convert_fusion.1, bf16[1024,2048]{1,0:T(8,128)(2,1)} %param.43), kind=kOutput, calls=%fused_computation.121 | convolution fusion | flops 8594128896 | bytes 16777216 | tf_op jit(solution)/shard_map/tf,td->fd/dot_general | solution.py:207
  634.9 14.5 %convolution_convert_fusion.1 = bf16[2048,2048]{1,0:T(8,128)(2,1)} fusion(bf16[1024,2048]{1,0:T(8,128)(2,1)} %get-tuple-element.602, bf16[1024,2048]{1,0:T(8,128)(2,1)} %param.28, f32[2048]{0:T(1024)S(1)} %bitcast.188, f32[2048]{0:T(1024)S(1)} %bitcast.186, f32[1024]{0:T(1024)S(1)} %copy-done.25, f32[1024]{0:T(1024)S(1)} %copy-done.21), kind=kOutput, calls=%fused_computation.122 | convolution fusion | flops 8606711808 | bytes 16801792 | tf_op jit(solution)/shard_map/td,tf->df/dot_general | solution.py:209
  653.6 10.9 all-gather.5
  664.5 7.7 all-gather.6
  673.6 25.2 %all-reduce.5 = (bf16[2048]{0:T(1024)(128)(2,1)S(1)}, bf16[2048]{0:T(1024)(128)(2,1)S(1)}, bf16[2048]{0:T(1024)(128)(2,1)S(1)}, bf16[2048]{0:T(1024)(128)(2,1)S(1)}, bf16[2048]{0:T(1024)(128)(2,1)S(1)}) all-reduce(bf16[2048]{0:T(1024)(128)(2,1)S(1)} %reduce_sum.263, ...), channel_id=5, replica_groups=mesh['dp'=8,'tensor'=4] {'dp'}, use_global_device_ids=true, to_apply=%region_29.30.clone | all-reduce | flops 10240 | bytes 40960
  699.1 13.4 %all-reduce.6 = (bf16[256]{0:T(256)(128)(2,1)S(1)}, bf16[256]{0:T(256)(128)(2,1)S(1)}, bf16[256]{0:T(256)(128)(2,1)S(1)}, bf16[256]{0:T(256)(128)(2,1)S(1)}) all-reduce(bf16[256]{0:T(256)(128)(2,1)S(1)} %dynamic-slice.13, bf16[256]{0:T(256)(128)(2,1)S(1)} %dynamic-slice.15, ...), channel_id=1, replica_groups=mesh['dp'=8,'tensor'=4] {'tensor'}, use_global_device_ids=true, to_apply=%region_35.36 | all-reduce | flops 1024 | bytes 4096 | tf_op jit(solution)/shard_map/psum | solution.py:270
  718.0 211.9 %all-reduce.10.cloned.1.call-done = (bf16[1024,2048]{1,0:T(8,128)(2,1)}, bf16[1024,2048]{1,0:T(8,128)(2,1)}) async-done(((bf16[1024,2048]{1,0:T(8,128)(2,1)}, bf16[1024,2048]{1,0:T(8,128)(2,1)}), (bf16[1024,2048]{1,0:T(8,128)(2,1)}, bf16[1024,2048]{1,0:T(8,128)(2,1)})) %all-reduce.10.cloned.1.call-update) | async-done | bytes 8388624 | tf_op jit(solution)/shard_map/psum | solution.py:188
  929.9 7.9 add_convert_fusion
  942.1 52.4 %reduce-scatter.11.cloned.1.call-done = bf16[256,1536]{1,0:T(8,128)(2,1)} async-done(((bf16[2048,1536]{1,0:T(8,128)(2,1)}), bf16[256,1536]{1,0:T(8,128)(2,1)}) %reduce-scatter.11.cloned.1.call-update) | async-done | bytes 786448 | tf_op jit(solution)/shard_map/reduce_scatter | solution.py:277
  996.9 72.1 %reduce-scatter.17.cloned.1.call-done = bf16[2048,256]{1,0:T(8,128)(2,1)} async-done(((bf16[2048,2048]{1,0:T(8,128)(2,1)}), bf16[2048,256]{1,0:T(8,128)(2,1)}) %reduce-scatter.17.cloned.1.call-update) | async-done | bytes 1048592 | tf_op jit(solution)/shard_map/reduce_scatter | solution.py:295
  1071.8 72.5 %reduce-scatter.15.cloned.1.call-done = bf16[256,2048]{1,0:T(8,128)(2,1)} async-done(((bf16[2048,2048]{1,0:T(8,128)(2,1)}), bf16[256,2048]{1,0:T(8,128)(2,1)}) %reduce-scatter.15.cloned.1.call-update) | async-done | bytes 1048592 | tf_op jit(solution)/shard_map/reduce_scatter | solution.py:289
  (351 shorter events, 188.0 us)
Async XLA Ops:
  7.2 17.8 %copy-start.39 = (f32[256]{0:T(256)S(1)}, f32[256]{0:T(256)}, u32[]{:S(2)}) copy-start(f32[256]{0:T(256)} %param.38) | copy-start | bytes 3076
  7.2 26.7 %copy-start.40 = (f32[2,96]{1,0:T(2,128)S(1)}, f32[2,96]{1,0:T(2,128)}, u32[]{:S(2)}) copy-start(f32[2,96]{1,0:T(2,128)} %param.30) | copy-start | bytes 2308
  7.2 34.7 %copy-start.36 = (s32[24]{0:T(128)S(1)}, s32[24]{0:T(128)}, u32[]{:S(2)}) copy-start(s32[24]{0:T(128)} %param.42) | copy-start | bytes 292
  7.2 51.6 %all-gather.12.cloned.1.call-start = ((), (), s32[]{:S(2)}) async-start(), calls=%async_computation.6 | async-start | bytes 7077888 | tf_op jit(solution)/shard_map/all_gather | solution.py:104
  9.7 172.8 %all-gather.14.cloned.1.call-start = ((), (), s32[]{:S(2)}) async-start(), calls=%async_computation.7 | async-start | bytes 2359296 | tf_op jit(solution)/shard_map/all_gather | solution.py:106
  11.5 456.9 %all-gather.16.cloned.1.call-start = ((), (), s32[]{:S(2)}) async-start(), calls=%async_computation.8 | async-start | bytes 9437184 | tf_op jit(solution)/shard_map/all_gather | solution.py:108
  14.3 468.8 %all-gather.18.cloned.1.call-start = ((), (), s32[]{:S(2)}) async-start(), calls=%async_computation.9 | async-start | bytes 9437184 | tf_op jit(solution)/shard_map/all_gather | solution.py:110
  25.0 46.1 %copy-start.26 = (f32[8,1,256]{2,1,0:T(1,128)}, f32[8,1,256]{2,1,0:T(1,128)S(1)}, u32[]{:S(2)}) copy-start(f32[8,1,256]{2,1,0:T(1,128)S(1)} %convert_element_type.352) | copy-start | bytes 24580
  34.0 37.1 %copy-start.28 = (f32[8,1,256]{2,1,0:T(1,128)}, f32[8,1,256]{2,1,0:T(1,128)S(1)}, u32[]{:S(2)}) copy-start(f32[8,1,256]{2,1,0:T(1,128)S(1)} %convert_element_type.353) | copy-start | bytes 24580
  45.3 25.8 %copy-start.19 = (f32[1024]{0:T(1024)}, f32[1024]{0:T(1024)S(1)}, u32[]{:S(2)}) copy-start(f32[1024]{0:T(1024)S(1)} %broadcast_multiply_fusion.2) | copy-start | bytes 12292
  46.6 24.5 %copy-start.23 = (f32[1024]{0:T(1024)}, f32[1024]{0:T(1024)S(1)}, u32[]{:S(2)}) copy-start(f32[1024]{0:T(1024)S(1)} %add_rsqrt_fusion) | copy-start | bytes 12292
  80.7 11.8 %copy-start.17 = (bf16[1,1024,2,32]{1,3,2,0:T(8,128)(2,1)}, bf16[1,1024,2,32]{1,3,2,0:T(8,128)(2,1)S(1)}, u32[]{:S(2)}) copy-start(bf16[1,1024,2,32]{1,3,2,0:T(8,128)(2,1)S(1)} %get-tuple-element.635) | copy-start | bytes 393220
  80.9 12.6 %copy-start.41 = (f32[256]{0:T(256)S(1)}, f32[256]{0:T(256)}, u32[]{:S(2)}) copy-start(f32[256]{0:T(256)} %param.39) | copy-start | bytes 3076
  80.9 82.9 %copy-start.42 = (f32[256]{0:T(256)S(1)}, f32[256]{0:T(256)}, u32[]{:S(2)}) copy-start(f32[256]{0:T(256)} %param.40) | copy-start | bytes 3076
  80.9 93.2 %copy-start.43 = (f32[2,128]{1,0:T(2,128)S(1)}, f32[2,128]{1,0:T(2,128)}, u32[]{:S(2)}) copy-start(f32[2,128]{1,0:T(2,128)} %param.34) | copy-start | bytes 3076
  85.4 106.5 %collective-permute-start = (bf16[2,1024,2,256]{1,3,2,0:T(8,128)(2,1)}, bf16[2,1024,2,256]{1,3,2,0:T(8,128)(2,1)}, u32[]{:S(2)}, u32[]{:S(2)}) collective-permute-start(bf16[2,1024,2,256]{1,3,2,0:T(8,128)(2,1)} %pad_maximum_fusion.4), channel_id=1, source_target_pairs={{0,4},{4,8},{8,12},{12,16},{16,20},{20,24},{24,28},{1,5},{5,9},{9,... | collective-permute-start | bytes 6291464 | tf_op jit(solution)/shard_map/ppermute | solution.py:26
  88.9 102.9 %collective-permute-start.1 = (bf16[2,1024,2,256]{1,3,2,0:T(8,128)(2,1)}, bf16[2,1024,2,256]{1,3,2,0:T(8,128)(2,1)}, u32[]{:S(2)}, u32[]{:S(2)}) collective-permute-start(bf16[2,1024,2,256]{1,3,2,0:T(8,128)(2,1)} %pad_maximum_fusion.4), channel_id=1, source_target_pairs={{4,0},{8,4},{12,8},{16,12},{20,16},{24,20},{28,24},{5,1},{9,5},{13... | collective-permute-start | bytes 6291464 | tf_op jit(solution)/shard_map/ppermute | solution.py:28
  91.4 580.8 %reduce-scatter.21.cloned.1.call-start = ((), (), s32[]{:S(2)}) async-start(), calls=%async_computation.15 | async-start | bytes 294912
  247.4 14.2 %copy-start.4 = (bf16[1024,2,256]{2,0,1:T(8,128)(2,1)}, bf16[1024,2,256]{2,0,1:T(8,128)(2,1)S(1)}, u32[]{:S(2)}) copy-start(bf16[1024,2,256]{2,0,1:T(8,128)(2,1)S(1)} %get-tuple-element.886) | copy-start | bytes 3145732 | tf_op jit(solution)/shard_map/while
  272.5 21.5 %slice-start.3 = ((s8[12582912]{0:T(1024)(128)(4,1)}), s8[4194304]{0:T(1024)(128)(4,1)S(1)}, s32[]{:S(2)}) async-start(s8[12582912]{0:T(1024)(128)(4,1)} %bitcast.145), calls=%async_computation.20 | async-start | bytes 8388608 | tf_op jit(solution)/shard_map/while
  272.5 21.5 %slice-start.4 = ((s8[12582912]{0:T(1024)(128)(4,1)}), s8[4194304]{0:T(1024)(128)(4,1)S(1)}, s32[]{:S(2)}) async-start(s8[12582912]{0:T(1024)(128)(4,1)} %bitcast.145), calls=%async_computation.21 | async-start | bytes 8388608 | tf_op jit(solution)/shard_map/while
  281.3 12.7 %slice-start.5 = ((s8[12582912]{0:T(1024)(128)(4,1)}), s8[4194304]{0:T(1024)(128)(4,1)S(1)}, s32[]{:S(2)}) async-start(s8[12582912]{0:T(1024)(128)(4,1)} %bitcast.145), calls=%async_computation.22 | async-start | bytes 8388608 | tf_op jit(solution)/shard_map/while
  323.5 20.6 %slice-start.6 = ((s8[5242880]{0:T(1024)(128)(4,1)}), s8[1048576]{0:T(1024)(128)(4,1)S(1)}, s32[]{:S(2)}) async-start(s8[5242880]{0:T(1024)(128)(4,1)} %bitcast.147), calls=%async_computation.23 | async-start | bytes 2097152 | tf_op jit(solution)/shard_map/while
  349.6 14.2 %copy-start.4 = (bf16[1024,2,256]{2,0,1:T(8,128)(2,1)}, bf16[1024,2,256]{2,0,1:T(8,128)(2,1)S(1)}, u32[]{:S(2)}) copy-start(bf16[1024,2,256]{2,0,1:T(8,128)(2,1)S(1)} %get-tuple-element.886) | copy-start | bytes 3145732 | tf_op jit(solution)/shard_map/while
  374.8 21.5 %slice-start.3 = ((s8[12582912]{0:T(1024)(128)(4,1)}), s8[4194304]{0:T(1024)(128)(4,1)S(1)}, s32[]{:S(2)}) async-start(s8[12582912]{0:T(1024)(128)(4,1)} %bitcast.145), calls=%async_computation.20 | async-start | bytes 8388608 | tf_op jit(solution)/shard_map/while
  374.8 21.5 %slice-start.4 = ((s8[12582912]{0:T(1024)(128)(4,1)}), s8[4194304]{0:T(1024)(128)(4,1)S(1)}, s32[]{:S(2)}) async-start(s8[12582912]{0:T(1024)(128)(4,1)} %bitcast.145), calls=%async_computation.21 | async-start | bytes 8388608 | tf_op jit(solution)/shard_map/while
  383.6 12.7 %slice-start.5 = ((s8[12582912]{0:T(1024)(128)(4,1)}), s8[4194304]{0:T(1024)(128)(4,1)S(1)}, s32[]{:S(2)}) async-start(s8[12582912]{0:T(1024)(128)(4,1)} %bitcast.145), calls=%async_computation.22 | async-start | bytes 8388608 | tf_op jit(solution)/shard_map/while
  425.8 20.6 %slice-start.6 = ((s8[5242880]{0:T(1024)(128)(4,1)}), s8[1048576]{0:T(1024)(128)(4,1)S(1)}, s32[]{:S(2)}) async-start(s8[5242880]{0:T(1024)(128)(4,1)} %bitcast.147), calls=%async_computation.23 | async-start | bytes 2097152 | tf_op jit(solution)/shard_map/while
  457.2 11.3 copy-start.20
  457.2 11.3 copy-start.24
  457.2 11.3 copy-start.30
  457.2 11.3 copy-start.32
  459.5 57.8 %collective-permute-start.2 = (bf16[2,1024,2,256]{3,1,2,0:T(8,128)(2,1)}, bf16[2,1024,2,256]{3,1,2,0:T(8,128)(2,1)}, u32[]{:S(2)}, u32[]{:S(2)}) collective-permute-start(bf16[2,1024,2,256]{3,1,2,0:T(8,128)(2,1)} %get-tuple-element.618), channel_id=1, source_target_pairs={{0,4},{4,8},{8,12},{12,16},{16,20},{20,24},{24,28},{1,5},{5,9},{9,... | collective-permute-start | bytes 6291464 | tf_op jit(solution)/shard_map/ppermute | solution.py:26
  463.0 54.3 %collective-permute-start.3 = (bf16[2,1024,2,256]{3,1,2,0:T(8,128)(2,1)}, bf16[2,1024,2,256]{3,1,2,0:T(8,128)(2,1)}, u32[]{:S(2)}, u32[]{:S(2)}) collective-permute-start(bf16[2,1024,2,256]{3,1,2,0:T(8,128)(2,1)} %get-tuple-element.619), channel_id=1, source_target_pairs={{4,0},{8,4},{12,8},{16,12},{20,16},{24,20},{28,24},{5,1},{9,5},{13... | collective-permute-start | bytes 6291464 | tf_op jit(solution)/shard_map/ppermute | solution.py:28
  468.5 14.6 %copy-start.22 = (f32[1,8,2,128]{3,1,2,0:T(8,128)S(1)}, f32[1,8,2,128]{3,1,2,0:T(8,128)}, u32[]{:S(2)}) copy-start(f32[1,8,2,128]{3,1,2,0:T(8,128)} %copy.158) | copy-start | bytes 24580
  517.2 197.6 %reduce-scatter.19.cloned.1.call-start = ((), (), s32[]{:S(2)}) async-start(), calls=%async_computation.14 | async-start | bytes 221184
  527.7 188.5 %reduce-scatter.13.cloned.1.call-start = ((), (), s32[]{:S(2)}) async-start(), calls=%async_computation.11 | async-start | bytes 2359296 | tf_op jit(solution)/shard_map/reduce_scatter | solution.py:283
  534.1 395.8 %all-reduce.10.cloned.1.call-start = ((), (), s32[]{:S(2)}) async-start(), calls=%async_computation.16 | async-start | bytes 16777216 | tf_op jit(solution)/shard_map/psum | solution.py:188
  544.2 13.0 %copy-start.18 = (bf16[128,8,2,256]{3,1,2,0:T(8,128)(2,1)S(1)}, bf16[128,8,2,256]{3,1,2,0:T(8,128)(2,1)}, u32[]{:S(2)}) copy-start(bf16[128,8,2,256]{3,1,2,0:T(8,128)(2,1)} %copy.149) | copy-start | bytes 3145732
  544.2 13.1 %copy-start.37 = (bf16[512,2048]{1,0:T(8,128)(2,1)S(1)}, bf16[512,2048]{1,0:T(8,128)(2,1)}, u32[]{:S(2)}) copy-start(bf16[512,2048]{1,0:T(8,128)(2,1)} %all-gather.14.cloned.1.call-done) | copy-start | bytes 6291460
  564.6 11.9 %copy-start.21 = (f32[1024]{0:T(1024)S(1)}, f32[1024]{0:T(1024)}, u32[]{:S(2)}) copy-start(f32[1024]{0:T(1024)} %copy-done.19) | copy-start | bytes 12292
  564.6 11.9 %copy-start.25 = (f32[1024]{0:T(1024)S(1)}, f32[1024]{0:T(1024)}, u32[]{:S(2)}) copy-start(f32[1024]{0:T(1024)} %copy-done.23) | copy-start | bytes 12292
  564.6 11.9 %copy-start.27 = (f32[8,1,256]{2,1,0:T(1,128)S(1)}, f32[8,1,256]{2,1,0:T(1,128)}, u32[]{:S(2)}) copy-start(f32[8,1,256]{2,1,0:T(1,128)} %copy-done.26) | copy-start | bytes 24580
  564.6 11.9 %copy-start.31 = (f32[8,1,256]{2,1,0:T(1,128)S(1)}, f32[8,1,256]{2,1,0:T(1,128)}, u32[]{:S(2)}) copy-start(f32[8,1,256]{2,1,0:T(1,128)} %convert_element_type.354) | copy-start | bytes 24580
  604.6 389.9 %reduce-scatter.11.cloned.1.call-start = ((), (), s32[]{:S(2)}) async-start(), calls=%async_computation.10 | async-start | bytes 7077888 | tf_op jit(solution)/shard_map/reduce_scatter | solution.py:277
  619.7 449.3 %reduce-scatter.17.cloned.1.call-start = ((), (), s32[]{:S(2)}) async-start(), calls=%async_computation.13 | async-start | bytes 9437184 | tf_op jit(solution)/shard_map/reduce_scatter | solution.py:295
  634.2 510.0 %reduce-scatter.15.cloned.1.call-start = ((), (), s32[]{:S(2)}) async-start(), calls=%async_computation.12 | async-start | bytes 9437184 | tf_op jit(solution)/shard_map/reduce_scatter | solution.py:289
  714.8 432.2 %copy-start.34 = (f32[256]{0:T(256)}, f32[256]{0:T(256)S(1)}, u32[]{:S(2)}) copy-start(f32[256]{0:T(256)S(1)} %dynamic-slice_convert_fusion) | copy-start | bytes 3076
  (36 other events, 230.3 us)
Sparse Core Ops, SparseCore 0:
  10.5 48.2 all-gather.11
  61.2 30.8 all-gather.13
  94.6 76.8 all-gather.15
  173.2 55.2 all-gather.17
  517.3 35.4 reduce-scatter.20
  556.6 33.5 reduce-scatter.18
  594.0 41.1 reduce-scatter.12
  638.0 291.8 all-reduce.9
  933.6 60.7 reduce-scatter.10
  997.8 71.2 reduce-scatter.16
  1072.9 71.2 reduce-scatter.14
where the time goes:
time: 1160 us; the launch traced here: 1150 us
  waiting for transfers between devices  420 us (36%)
  matrix products  250 us (22%)
  blocking collectives  171 us (15%)
  other arithmetic  141 us (12%)
  local copies, waits for them, and re-layouts  136 us (12%)
  between operations  15.8 us (1%)
    psum x1, waiting for transfers between devices, on_device(): lax.psum(partial_sum.astype(jnp.bfloat16), 'tensor').astype(jnp.float32)  212 us
    reduce_scatter x1, waiting for transfers between devices, on_device(): lax.psum_scatter(grad_expand.astype(jnp.bfloat16), 'dp', scatter_dimensio...  72.5 us
    reduce_scatter x1, waiting for transfers between devices, on_device(): lax.psum_scatter(grad_shrink.astype(jnp.bfloat16), 'dp', scatter_dimensio...  72.1 us
    all_gather x1, blocking collectives, on_device(): lax.all_gather(second_gain.astype(bf16), 'dp', axis=0, tiled=True)  69.6 us
    reduce_scatter x1, waiting for transfers between devices, on_device(): lax.psum_scatter(grad_project.astype(jnp.bfloat16), 'dp', scatter_dimensi...  52.4 us
    dynamic_update_slice x4, local copies, waits for them, and re-layouts, backward_block(): lax.dynamic_update_slice_in_dim(carry, window_now + jnp.stack([grad_key,...  41.1 us
    dot_general x1, matrix products, on_device(): jnp.einsum('td,fd->tf', upstream, full_shrink, preferred_element_type=f32)  33.2 us
    dynamic_slice x4, local copies, waits for them, and re-layouts, backward_block(): window_now = lax.dynamic_slice_in_dim(carry, query_start, window, 1)  32.5 us
  transfers between devices with their start and end apart: 15, of which 5 were waited for; matrix products, arithmetic and copies ran while one was open for 45% of the time, Pallas kernels for 0%

commit v1 on v0

v1 whole, which is shorter than its diff:
```python
import functools
import math

import jax
import jax.numpy as jnp
from jax import lax
from jax.experimental import pallas as pl
from jax.experimental.pallas import tpu as pltpu
from jax.sharding import PartitionSpec as P

HD = 256
ROT = 64
SEQ_MAX = 1024
PREFIX_MAX = 512
BLOCK = 256
BLOCKS = 8
HALF = 4
EPSILON = 1e-05
MASKED = -1e30
bf16 = jnp.bfloat16
f32 = jnp.float32
NN = (((1,), (0,)), ((), ()))
NT = (((1,), (1,)), ((), ()))
TN = (((0,), (0,)), ((), ()))
VMEM_BYTES = 56 * 2**20


def mul(a, b, dims=NN):
    return lax.dot_general(a, b, dims, preferred_element_type=f32)


def params(**more):
    return pltpu.CompilerParams(vmem_limit_bytes=VMEM_BYTES, **more)


def cost(flops, moved, transcendentals=0):
    return pl.CostEstimate(flops=flops, bytes_accessed=moved, transcendentals=transcendentals)


def whole_spec(array):
    zeros = (0,) * array.ndim
    return pl.BlockSpec(array.shape, lambda *_: zeros)


def swap(value, bit):
    count = lax.axis_size("dp")
    return lax.ppermute(value, "dp", [(i, i ^ bit) for i in range(count)])


CORE, ALONG_X, ALONG_Y = 1, 2, 4


def is_cube():
    return lax.axis_size("dp") == BLOCKS


def natural_places():
    place = jnp.arange(BLOCKS, dtype=jnp.int32)
    if not is_cube():
        return place
    owner = ((place >> 2) & 1) * CORE + ((place >> 1) & 1) * ALONG_Y + (place & 1) * ALONG_X
    return owner ^ lax.axis_index("dp")


class Spread:
    def __init__(self, weight):
        self.weight = weight

    def first(self):
        if is_cube():
            self.from_x = swap(self.weight, ALONG_X)
            self.from_y = swap(self.weight, ALONG_Y)
            return self.from_x, self.from_y
        self.full = lax.all_gather(self.weight, "dp", axis=0, tiled=True)
        return (self.full,)

    def second(self, *seen):
        if is_cube():
            half = self.weight.shape[0] // 2
            self.over_x = swap(after(self.from_x[:half], seen), ALONG_Y)
            self.over_y = swap(after(self.from_y[half:], seen), ALONG_X)
            return self.over_x, self.over_y
        return (self.full,)

    def join(self, *seen):
        if is_cube():
            parts = [self.weight, self.from_x, self.from_y, self.over_x, self.over_y]
            mine = jnp.concatenate(after(parts, seen), axis=0)
            return mine, swap(mine, CORE)
        half = self.full.shape[0] // 2
        return self.full[:half], self.full[half:]


def gather_columns(weight):
    if is_cube():
        return lax.all_gather(weight, "dp", axis=0)
    full = lax.all_gather(weight, "dp", axis=1, tiled=True)
    return full.reshape(full.shape[0], BLOCKS, -1).transpose(1, 0, 2)


def after(value, seen):
    return lax.optimization_barrier((value, seen))[0]


def norm_kernel(places, tokens, upstream, gains, tok, one_a, one_b, two_a, two_b, up_a, up_b, mean, inverse, grad_bias):
    values = tokens[...].astype(f32)
    average = jnp.mean(values, axis=1, keepdims=True)
    center = values - average
    scale = lax.rsqrt(jnp.mean(center * center, axis=1, keepdims=True) + EPSILON)
    mean[...] = average
    inverse[...] = scale

    @pl.when(pl.program_id(0) == 0)
    def _():
        grad_bias[...] = jnp.zeros_like(grad_bias)

    for place in range(BLOCKS):
        from_ = pl.ds(pl.multiple_of(places[place] * BLOCK, BLOCK), BLOCK)
        to = pl.ds(place * BLOCK, BLOCK)
        inner = pl.ds(place % HALF * BLOCK, BLOCK)
        first, second, up = (one_a, two_a, up_a) if place < HALF else (one_b, two_b, up_b)
        low = tokens[:, from_]
        tok[:, to] = low
        normed = (low.astype(f32) - average) * scale
        first[:, inner] = (normed * gains[0:1, to] + gains[1:2, to]).astype(bf16)
        second[:, inner] = (normed * gains[2:3, to] + gains[3:4, to]).astype(bf16)
        grad = upstream[:, from_]
        up[:, inner] = grad
        grad_bias[0:1, to] += jnp.sum(grad.astype(f32), axis=0, keepdims=True)


def norm(places, tokens, upstream, gains, tile=256):
    rows, width = tokens.shape
    row = lambda w: pl.BlockSpec((tile, w), lambda i, *_: (i, 0))
    shape = lambda w, kind: jax.ShapeDtypeStruct((rows, w), kind)
    half = width // 2
    return pl.pallas_call(
        norm_kernel,
        grid_spec=pltpu.PrefetchScalarGridSpec(
            num_scalar_prefetch=1,
            grid=(rows // tile,),
            in_specs=[row(width), row(width), whole_spec(gains)],
            out_specs=[row(width)] + [row(half)] * 6 + [row(1), row(1), pl.BlockSpec((8, width), lambda *_: (0, 0))],
        ),
        out_shape=[shape(width, bf16)]
        + [shape(half, bf16)] * 6
        + [shape(1, f32), shape(1, f32), jax.ShapeDtypeStruct((8, width), f32)],
        compiler_params=params(),
        cost_estimate=cost(20 * rows * width, 20 * rows * width),
        name="norm",
    )(places, tokens, upstream, gains)


def turn(part, cos, sin, sign):
    lane = lax.broadcasted_iota(jnp.int32, part.shape, 1)
    partner = jnp.where(lane < ROT // 2, pltpu.roll(part, 128 - ROT // 2, 1), pltpu.roll(part, ROT // 2, 1))
    if sign > 0:
        return part * cos + partner * sin
    return part * cos - partner * sin


def project_kernel(one_a, one_b, w_a, w_b, bias, cos, sin, queries, pairs):
    for part in range(3):
        at = slice(part * HD, (part + 1) * HD)
        mixed = mul(one_a[...], w_a[:, at]) + mul(one_b[...], w_b[:, at]) + bias[:, at]
        if part < 2:
            ref, to = (queries, 0) if part == 0 else (pairs, 0)
            ref[:, to : to + 128] = turn(mixed[:, :128], cos[...], sin[...], 1).astype(bf16)
            ref[:, to + 128 : to + HD] = mixed[:, 128:].astype(bf16)
        else:
            pairs[:, HD:] = mixed.astype(bf16)


def project(one_a, one_b, w_a, w_b, bias, cos, sin):
    rows, half = one_a.shape
    heads = w_a.shape[1] // (3 * HD)
    weight = pl.BlockSpec((half, 3 * HD), lambda h: (0, h))
    return pl.pallas_call(
        project_kernel,
        grid=(heads,),
        in_specs=[
            whole_spec(one_a),
            whole_spec(one_b),
            weight,
            weight,
            pl.BlockSpec((1, 3 * HD), lambda h: (0, h)),
            whole_spec(cos),
            whole_spec(sin),
        ],
        out_specs=[pl.BlockSpec((rows, HD), lambda h: (0, h)), pl.BlockSpec((rows, 2 * HD), lambda h: (0, h))],
        out_shape=[
            jax.ShapeDtypeStruct((rows, heads * HD), bf16),
            jax.ShapeDtypeStruct((rows, heads * 2 * HD), bf16),
        ],
        compiler_params=params(),
        cost_estimate=cost(4 * rows * half * w_a.shape[1], 14_000_000),
        name="project",
    )(one_a, one_b, w_a, w_b, bias, cos, sin)


def expand_kernel(two_a, two_b, w_a, w_b, bias, active, slope):
    rows = two_a.shape[0]
    for start in range(0, rows, 512):
        at = slice(start, start + 512)
        hidden = mul(two_a[at], w_a[...]) + mul(two_b[at], w_b[...]) + bias[...]
        below = 0.5 + 0.5 * lax.erf(hidden * (0.5**0.5))
        density = jnp.exp(hidden * hidden * -0.5) * (1.0 / math.sqrt(2.0 * math.pi))
        active[at] = (hidden * below).astype(bf16)
        slope[at] = (below + hidden * density).astype(bf16)


def expand(two_a, two_b, w_a, w_b, bias, tile=512):
    rows, half = two_a.shape
    width = w_a.shape[1]
    column = lambda r: pl.BlockSpec((r, tile), lambda n: (0, n))
    return pl.pallas_call(
        expand_kernel,
        grid=(width // tile,),
        in_specs=[whole_spec(two_a), whole_spec(two_b), column(half), column(half), column(1)],
        out_specs=[column(rows), column(rows)],
        out_shape=[jax.ShapeDtypeStruct((rows, width), bf16)] * 2,
        compiler_params=params(),
        cost_estimate=cost(4 * rows * half * width, 22_000_000, 2 * rows * width),
        name="expand",
    )(two_a, two_b, w_a, w_b, bias)


def branch_kernel(attended, active, mine, theirs, out):
    depth = attended.shape[1]
    slabs = BLOCK // 128
    for number, weight in enumerate((mine, theirs)):
        full = (mul(attended[...], weight[:depth]) + mul(active[...], weight[depth:])).astype(bf16)
        for slab in range(slabs):
            out[number * slabs + slab] = full[:, slab * 128 : (slab + 1) * 128]


def branch_piece(attended, active, mine, theirs, tile=512):
    rows = attended.shape[0]
    depth = mine.shape[0]
    slabs = 2 * BLOCK // 128
    row = lambda a: pl.BlockSpec((tile, a.shape[1]), lambda i: (i, 0))
    return pl.pallas_call(
        branch_kernel,
        grid=(rows // tile,),
        in_specs=[row(attended), row(active), whole_spec(mine), whole_spec(theirs)],
        out_specs=pl.BlockSpec((slabs, tile, 128), lambda i: (0, i, 0)),
        out_shape=jax.ShapeDtypeStruct((slabs, rows, 128), bf16),
        compiler_params=params(),
        cost_estimate=cost(4 * rows * depth * BLOCK, 2 * (rows * depth + 2 * (rows + depth) * BLOCK)),
        name="branch",
    )(attended, active, mine, theirs)


def branch_place(places, attended, active, weight, place, tile=512):
    rows = attended.shape[0]
    depth = weight.shape[1]
    slabs = 2 * BLOCK // 128
    row = lambda a: pl.BlockSpec((tile, a.shape[1]), lambda i, *_: (i, 0))
    block = lambda p: pl.BlockSpec((None, depth, BLOCK), lambda i, w: (w[p], 0, 0))
    return pl.pallas_call(
        lambda _, *refs: branch_kernel(*refs),
        grid_spec=pltpu.PrefetchScalarGridSpec(
            num_scalar_prefetch=1,
            grid=(rows // tile,),
            in_specs=[row(attended), row(active), block(place), block(place + HALF)],
            out_specs=pl.BlockSpec((slabs, tile, 128), lambda i, *_: (0, i, 0)),
        ),
        out_shape=jax.ShapeDtypeStruct((slabs, rows, 128), bf16),
        compiler_params=params(),
        cost_estimate=cost(4 * rows * depth * BLOCK, 2 * (rows * depth + 2 * (rows + depth) * BLOCK)),
        name="branch",
    )(places, attended, active, weight, weight)


def back_kernel(places, up_a, up_b, blocks, slope, out, sums, joined):
    for place in range(BLOCKS):
        joined[:, place * BLOCK : (place + 1) * BLOCK] = blocks[places[place]]
    half = HALF * BLOCK
    total = jnp.zeros((1, out.shape[1]), f32)
    for start in range(0, out.shape[0], 512):
        at = slice(start, start + 512)
        grad = mul(up_a[at], joined[:, :half], NT) + mul(up_b[at], joined[:, half:], NT)
        if slope is not None:
            grad = grad * slope[at].astype(f32)
        grad = grad.astype(bf16)
        out[at] = grad
        if sums is not None:
            total = total + jnp.sum(grad.astype(f32), axis=0, keepdims=True)
    if sums is not None:
        sums[...] = total


def back(places, up_a, up_b, blocks, start, width, slope=None, tile=512):
    rows, half = up_a.shape
    weight = pl.BlockSpec((BLOCKS, tile, BLOCK), lambda n, *_: (0, n + start // tile, 0))
    column = lambda r: pl.BlockSpec((r, tile), lambda n, *_: (0, n))
    scaled = slope is not None

    def body(w, a, b, c, *rest):
        if scaled:
            s, out, sums, joined = rest
        else:
            (out, joined), s, sums = rest, None, None
        back_kernel(w, a, b, c, s, out, sums, joined)

    out = jax.ShapeDtypeStruct((rows, width), bf16)
    return pl.pallas_call(
        body,
        grid_spec=pltpu.PrefetchScalarGridSpec(
            num_scalar_prefetch=1,
            grid=(width // tile,),
            in_specs=[whole_spec(up_a), whole_spec(up_b), weight] + [column(rows)] * scaled,
            out_specs=[column(rows), column(1)] if scaled else column(rows),
            scratch_shapes=[pltpu.VMEM((tile, 2 * half), bf16)],
        ),
        out_shape=[out, jax.ShapeDtypeStruct((1, width), f32)] if scaled else out,
        compiler_params=params(),
        cost_estimate=cost(4 * rows * half * width, 4 * rows * half + 4 * half * width + 4 * rows * width),
        name="back",
    )(places, up_a, up_b, blocks, *([slope] if scaled else []))


def second_kernel(grad, w_a, w_b, out):
    step = pl.program_id(0)

    @pl.when(step < 2)
    def _():
        out[...] = mul(grad[...], w_a[...], NT).astype(bf16)

    @pl.when(step >= 2)
    def _():
        out[...] = mul(grad[...], w_b[...], NT).astype(bf16)


def second_back(grad, w_a, w_b):
    rows, width = grad.shape
    half = w_a.shape[0]
    tile = half // 2
    return pl.pallas_call(
        second_kernel,
        grid=(4,),
        in_specs=[
            whole_spec(grad),
            pl.BlockSpec((tile, width), lambda n: (jnp.minimum(n, 1), 0)),
            pl.BlockSpec((tile, width), lambda n: (jnp.maximum(n - 2, 0), 0)),
        ],
        out_specs=pl.BlockSpec((rows, tile), lambda n: (0, n)),
        out_shape=jax.ShapeDtypeStruct((rows, 2 * half), bf16),
        compiler_params=params(),
        cost_estimate=cost(4 * rows * half * width, 2 * rows * width + 4 * half * width + 4 * rows * half),
        name="second_back",
    )(grad, w_a, w_b)


def row_grad_kernel(where, left_a, left_b, right, *rest):
    out = rest[-1]
    for number, left in enumerate((left_a, left_b)):
        full = mul(left[...], right[...], TN)
        for place in range(HALF):
            out[where[number * HALF + place]] = full[place * BLOCK : (place + 1) * BLOCK].astype(bf16)


def row_grad(where, left_a, left_b, right, total, start=0, into=None, tile=512):
    rows, width = right.shape
    blocks = 2 * HALF
    extra = [] if into is None else [into]
    return pl.pallas_call(
        row_grad_kernel,
        grid_spec=pltpu.PrefetchScalarGridSpec(
            num_scalar_prefetch=1,
            grid=(width // tile,),
            in_specs=[whole_spec(left_a), whole_spec(left_b), pl.BlockSpec((rows, tile), lambda n, *_: (0, n))]
            + [pl.BlockSpec(memory_space=pl.ANY)] * len(extra),
            out_specs=pl.BlockSpec((blocks, BLOCK, tile), lambda n, *_: (0, 0, n + start // tile)),
        ),
        out_shape=jax.ShapeDtypeStruct((blocks, BLOCK, total), bf16),
        input_output_aliases={4: 0} if extra else {},
        compiler_params=params(),
        cost_estimate=cost(2 * rows * blocks * BLOCK * width, 2 * blocks * BLOCK * (rows + width) + 2 * rows * width),
        name="row_grad",
    )(where, left_a, left_b, right, *extra)


def column_grad_kernel(where, first, second, right_a, right_b, out):
    def store(left):
        for number, right in enumerate((right_a, right_b)):
            full = mul(left[...], right[...], TN)
            for place in range(HALF):
                out[where[number * HALF + place]] = full[:, place * BLOCK : (place + 1) * BLOCK].astype(bf16)

    ahead = first.shape[1] // out.shape[1]
    assert ahead == 1
    pl.when(pl.program_id(0) == 0)(lambda: store(first))
    pl.when(pl.program_id(0) > 0)(lambda: store(second))


def column_grad(where, first, second, right_a, right_b, tile=512):
    rows = first.shape[0]
    width = first.shape[1] + second.shape[1]
    blocks = 2 * HALF
    return pl.pallas_call(
        column_grad_kernel,
        grid_spec=pltpu.PrefetchScalarGridSpec(
            num_scalar_prefetch=1,
            grid=(width // tile,),
            in_specs=[
                pl.BlockSpec((rows, tile), lambda n, *_: (0, 0)),
                pl.BlockSpec((rows, tile), lambda n, *_: (0, jnp.maximum(n - 1, 0))),
                whole_spec(right_a),
                whole_spec(right_b),
            ],
            out_specs=pl.BlockSpec((blocks, tile, BLOCK), lambda n, *_: (0, n, 0)),
        ),
        out_shape=jax.ShapeDtypeStruct((blocks, width, BLOCK), bf16),
        compiler_params=params(),
        cost_estimate=cost(2 * rows * blocks * BLOCK * width, 2 * blocks * BLOCK * (rows + width) + 2 * rows * width),
        name="column_grad",
    )(where, first, second, right_a, right_b)


def attend_kernel(first, last, q, left, own, right, low, high, out, lse, keys, values_turned, *, wide):
    step = pl.program_id(1)
    tall = q.shape[0]

    @pl.when(step == 0)
    def _():
        at = 0
        for ref in (left, own, right):
            count = ref.shape[0]
            keys[at : at + count, :] = ref[:, :HD]
            for r in range(0, count, 512):
                values_turned[:, at + r : at + r + 512] = jnp.transpose(ref[r : r + 512, HD:])
            at += count

    scaled = q[...] * jnp.asarray(HD**-0.5, bf16)
    low_row = low[...]
    high_row = high[...]

    def block(j, carry):
        top, total, acc = carry
        rows = pl.ds(pl.multiple_of(j * wide, wide), wide)
        scores = mul(keys[rows, :], scaled, NT)
        key = j * wide + lax.broadcasted_iota(jnp.int32, (wide, tall), 0)
        scores = jnp.where((key >= low_row) & (key <= high_row), scores, MASKED)
        new = jnp.maximum(top, jnp.max(scores, axis=0, keepdims=True))
        weights = jnp.exp(scores - new)
        fade = jnp.exp(top - new)
        total = total * fade + jnp.sum(weights, axis=0, keepdims=True)
        acc = acc * fade + mul(values_turned[:, rows], weights.astype(bf16))
        return new, total, acc

    start = (jnp.full((1, tall), MASKED, f32), jnp.zeros((1, tall), f32), jnp.zeros((HD, tall), f32))
    top, total, acc = lax.fori_loop(first[step], last[step] + 1, block, start)
    out[...] = jnp.transpose(acc / total).astype(bf16)
    lse[0] = top + jnp.log(total)


def key_blocks(low, high, tall, wide):
    return jnp.min(low.reshape(-1, tall), axis=1) // wide, jnp.max(high.reshape(-1, tall), axis=1) // wide


def attend(q, left, own, right, low, high, tall=512, wide=512):
    rows, width = q.shape
    heads = width // HD
    extent = left.shape[0] + rows + right.shape[0]
    pair = lambda a: pl.BlockSpec((a.shape[0], 2 * HD), lambda h, i, *_: (0, h))
    row = pl.BlockSpec((1, tall), lambda h, i, *_: (0, i))
    mine = pl.BlockSpec((tall, HD), lambda h, i, *_: (i, h))
    return pl.pallas_call(
        functools.partial(attend_kernel, wide=wide),
        grid_spec=pltpu.PrefetchScalarGridSpec(
            num_scalar_prefetch=2,
            grid=(heads, rows // tall),
            in_specs=[mine, pair(left), pair(own), pair(right), row, row],
            out_specs=[mine, pl.BlockSpec((1, 1, tall), lambda h, i, *_: (h, 0, i))],
            scratch_shapes=[pltpu.VMEM((extent, HD), bf16), pltpu.VMEM((HD, extent), bf16)],
        ),
        out_shape=[jax.ShapeDtypeStruct((rows, width), bf16), jax.ShapeDtypeStruct((heads, 1, rows), f32)],
        compiler_params=params(),
        cost_estimate=cost(8_000_000_000, 10_000_000, 3_000_000),
        name="attend",
    )(*key_blocks(low, high, tall, wide), q, left, own, right, low.reshape(1, rows), high.reshape(1, rows))


def attend_back_kernel(
    first, last, q, left, own, right, low, high, lse, attended, grad, cos, sin,
    dq, dleft, down, dright, keys, values, keys_turned, dk, dv, *, wide,
):
    step = pl.program_id(1)
    tall = q.shape[0]

    @pl.when(step == 0)
    def _():
        at = 0
        for ref in (left, own, right):
            count = ref.shape[0]
            keys[at : at + count, :] = ref[:, :HD]
            values[at : at + count, :] = ref[:, HD:]
            for r in range(0, count, 512):
                keys_turned[:, at + r : at + r + 512] = jnp.transpose(ref[r : r + 512, :HD])
            at += count
        dk[...] = jnp.zeros_like(dk)
        dv[...] = jnp.zeros_like(dv)

    scaled = q[...] * jnp.asarray(HD**-0.5, bf16)
    low_row = low[...]
    high_row = high[...]
    log_total = lse[0]
    given = grad[...]
    delta = jnp.sum(jnp.transpose(given.astype(f32) * attended[...].astype(f32)), axis=0, keepdims=True)

    def block(j, acc):
        rows = pl.ds(pl.multiple_of(j * wide, wide), wide)
        scores = mul(keys[rows, :], scaled, NT)
        grad_probs = mul(values[rows, :], given, NT)
        key = j * wide + lax.broadcasted_iota(jnp.int32, (wide, tall), 0)
        probs = jnp.exp(jnp.where((key >= low_row) & (key <= high_row), scores - log_total, MASKED))
        grad_scores = (probs * (grad_probs - delta)).astype(bf16)
        dv[rows, :] += mul(probs.astype(bf16), given)
        dk[rows, :] += mul(grad_scores, scaled)
        return acc + mul(keys_turned[:, rows], grad_scores)

    acc = lax.fori_loop(first[step], last[step] + 1, block, jnp.zeros((HD, tall), f32))
    full = jnp.transpose(acc) * (HD**-0.5)
    dq[:, :128] = turn(full[:, :128], cos[...], sin[...], -1).astype(bf16)
    dq[:, 128:] = full[:, 128:].astype(bf16)

    @pl.when(step == pl.num_programs(1) - 1)
    def _():
        at = 0
        for ref in (dleft, down, dright):
            count = ref.shape[0]
            ref[:, :HD] = dk[at : at + count, :].astype(ref.dtype)
            ref[:, HD:] = dv[at : at + count, :].astype(ref.dtype)
            at += count


def attend_back(q, left, own, right, low, high, lse, attended, grad, cos, sin, tall=512, wide=512):
    rows, width = q.shape
    heads = width // HD
    extent = left.shape[0] + rows + right.shape[0]
    pair = lambda a: pl.BlockSpec((a.shape[0], 2 * HD), lambda h, i, *_: (0, h))
    row = pl.BlockSpec((1, tall), lambda h, i, *_: (0, i))
    mine = pl.BlockSpec((tall, HD), lambda h, i, *_: (i, h))
    table = pl.BlockSpec((tall, 128), lambda h, i, *_: (i, 0))
    return pl.pallas_call(
        functools.partial(attend_back_kernel, wide=wide),
        grid_spec=pltpu.PrefetchScalarGridSpec(
            num_scalar_prefetch=2,
            grid=(heads, rows // tall),
            in_specs=[
                mine, pair(left), pair(own), pair(right), row, row,
                pl.BlockSpec((1, 1, tall), lambda h, i, *_: (h, 0, i)), mine, mine, table, table,
            ],
            out_specs=[mine, pair(left), pair(own), pair(right)],
            scratch_shapes=[
                pltpu.VMEM((extent, HD), bf16),
                pltpu.VMEM((extent, HD), bf16),
                pltpu.VMEM((HD, extent), bf16),
                pltpu.VMEM((extent, HD), f32),
                pltpu.VMEM((extent, HD), f32),
            ],
        ),
        out_shape=[
            jax.ShapeDtypeStruct((rows, width), bf16),
            jax.ShapeDtypeStruct(left.shape, bf16),
            jax.ShapeDtypeStruct(own.shape, f32),
            jax.ShapeDtypeStruct(right.shape, bf16),
        ],
        compiler_params=params(),
        cost_estimate=cost(16_000_000_000, 20_000_000, 3_000_000),
        name="attend_back",
    )(*key_blocks(low, high, tall, wide), q, left, own, right, low.reshape(1, rows), high.reshape(1, rows), lse, attended, grad, cos, sin)


def mixed_kernel(dq, own, later, earlier, cos, sin, out, sums):
    rows = dq.shape[0]
    near = earlier.shape[0]
    out[:, :HD] = dq[...]
    pairs = own[...] + later[...].astype(f32)
    top = pairs[:near] + earlier[...].astype(f32)
    for at, part in ((slice(0, near), top), (slice(near, rows), pairs[near:])):
        out[at, HD : HD + 128] = turn(part[:, :128], cos[at], sin[at], -1).astype(bf16)
        out[at, HD + 128 :] = part[:, 128:].astype(bf16)
    sums[...] = jnp.sum(out[...].astype(f32), axis=0, keepdims=True)


def mix(dq, own, later, earlier, cos, sin):
    rows, width = dq.shape
    heads = width // HD
    pair = lambda a: pl.BlockSpec((a.shape[0], 2 * HD), lambda h: (0, h))
    return pl.pallas_call(
        mixed_kernel,
        grid=(heads,),
        in_specs=[
            pl.BlockSpec((rows, HD), lambda h: (0, h)), pair(own), pair(later), pair(earlier),
            whole_spec(cos), whole_spec(sin),
        ],
        out_specs=[pl.BlockSpec((rows, 3 * HD), lambda h: (0, h)), pl.BlockSpec((1, 3 * HD), lambda h: (0, h))],
        out_shape=[
            jax.ShapeDtypeStruct((rows, 3 * width), bf16),
            jax.ShapeDtypeStruct((1, 3 * width), f32),
        ],
        compiler_params=params(),
        cost_estimate=cost(10_000_000, 14_000_000),
        name="mix",
    )(dq, own, later, earlier, cos, sin)


def input_kernel(mixed, w_a, w_b, second, tok, mean, inverse, gains, out_a, out_b, sums):
    step = pl.program_id(0)
    half = w_a.shape[0]
    grad_a = mul(mixed[...], w_a[...], NT)
    grad_b = mul(mixed[...], w_b[...], NT)
    scale = inverse[...]

    @pl.when(step == 0)
    def _():
        sums[...] = jnp.zeros_like(sums)

    pieces = []
    total = 0.0
    product = 0.0
    for number, grad in enumerate((grad_a, grad_b)):
        at = slice(number * half, (number + 1) * half)
        normed = (tok[:, at].astype(f32) - mean[...]) * scale
        other = second[:, at].astype(f32)
        both = grad * gains[0:1, at] + other * gains[2:3, at]
        sums[0:1, at] += jnp.sum(grad * normed, axis=0, keepdims=True)
        sums[1:2, at] += jnp.sum(grad, axis=0, keepdims=True)
        sums[2:3, at] += jnp.sum(other * normed, axis=0, keepdims=True)
        sums[3:4, at] += jnp.sum(other, axis=0, keepdims=True)
        total = total + jnp.sum(both, axis=1, keepdims=True)
        product = product + jnp.sum(both * normed, axis=1, keepdims=True)
        pieces.append((at, both, normed))
    total = total * (0.5 / half)
    product = product * (0.5 / half)
    for ref, chosen in ((out_a, step == 0), (out_b, step == 1)):

        @pl.when(chosen)
        def _(ref=ref):
            for at, both, normed in pieces:
                grad = (scale * (both - total - normed * product)).astype(bf16)
                for slab in range(half // 128):
                    ref[at.start // 128 + slab] = grad[:, slab * 128 : (slab + 1) * 128]


def input_back(mixed, w_a, w_b, second, tok, mean, inverse, gains, start, tile=256):
    width = tok.shape[1]
    depth = mixed.shape[1]
    row = lambda w: pl.BlockSpec((tile, w), lambda i: (i + start, 0))
    slabs = (width // 128, tile, 128)
    out = pl.BlockSpec(slabs, lambda i: (0, 0, 0))
    return pl.pallas_call(
        input_kernel,
        grid=(2,),
        in_specs=[
            row(depth), whole_spec(w_a), whole_spec(w_b), row(width), row(width), row(1), row(1), whole_spec(gains),
        ],
        out_specs=[out, out, pl.BlockSpec((8, width), lambda i: (0, 0))],
        out_shape=[jax.ShapeDtypeStruct(slabs, bf16)] * 2 + [jax.ShapeDtypeStruct((8, width), f32)],
        compiler_params=params(),
        cost_estimate=cost(4 * tile * depth * width, 14_000_000),
        name="input_back",
    )(mixed, w_a, w_b, second, tok, mean, inverse, gains)


def output_kernel(places, middle, tokens, bias, *refs):
    out = refs[-1]
    inside = middle[0] == 1
    for place in range(BLOCKS):
        settled, passed = refs[place % HALF], refs[HALF + place % HALF]
        for slab in range(BLOCK // 128):
            to = pl.ds(pl.multiple_of(places[place] * BLOCK + slab * 128, 128), 128)
            at = place // HALF * (BLOCK // 128) + slab
            total = jnp.where(inside, settled[at].astype(f32), passed[at].astype(f32))
            here = bias[0:1, place * BLOCK + slab * 128 : place * BLOCK + slab * 128 + 128]
            out[:, to] = (tokens[:, to].astype(f32) + total + here).astype(bf16)


def output_sum(places, middle, bias, settled, passed, tokens, tile=256):
    rows, width = tokens.shape
    row = lambda w: pl.BlockSpec((tile, w), lambda i, *_: (i, 0))
    slabs = pl.BlockSpec((width // 512, tile, 128), lambda i, *_: (0, i, 0))
    view = lambda a: a.reshape(width // 512, rows, 128)
    return pl.pallas_call(
        output_kernel,
        grid_spec=pltpu.PrefetchScalarGridSpec(
            num_scalar_prefetch=2,
            grid=(rows // tile,),
            in_specs=[row(width), whole_spec(bias)] + [slabs] * 8,
            out_specs=row(width),
        ),
        out_shape=jax.ShapeDtypeStruct((rows, width), bf16),
        compiler_params=params(),
        cost_estimate=cost(10_000_000, 17_000_000),
        name="output_sum",
    )(places, middle, tokens, bias, *map(view, settled), *map(view, passed))


def tokens_kernel(places, middle, upstream, settled, passed, *rest):
    out = rest[-1]
    inside = middle[0] == 1
    tile = out.shape[0]
    for slab in range(out.shape[1] // 128):
        per = BLOCK // 128
        at = slice(slab * tile, (slab + 1) * tile)
        to = pl.ds(pl.multiple_of(places[slab // per] * BLOCK + slab % per * 128, 128), 128)
        total = jnp.where(inside, settled[at].astype(f32), passed[at].astype(f32))
        out[:, to] = (upstream[:, to].astype(f32) + total).astype(bf16)


def tokens_sum(places, middle, upstream, settled, passed, number, earlier, tile=256):
    rows, width = upstream.shape
    row = pl.BlockSpec((tile, width), lambda i, *_: (number, 0))
    slabs = pl.BlockSpec((width // 128 * tile, 128), lambda i, *_: (0, 0))
    extra = [earlier]
    return pl.pallas_call(
        tokens_kernel,
        grid_spec=pltpu.PrefetchScalarGridSpec(
            num_scalar_prefetch=2,
            grid=(1,),
            in_specs=[row, slabs, slabs] + [pl.BlockSpec(memory_space=pl.ANY)] * len(extra),
            out_specs=row,
        ),
        out_shape=jax.ShapeDtypeStruct((rows, width), bf16),
        input_output_aliases={5: 0} if number else {},
        compiler_params=params(),
        cost_estimate=cost(2_000_000, 4_000_000),
        name="tokens_sum",
    )(places, middle, upstream, settled, passed, *extra)


class LineSum:
    def __init__(self, middle):
        self.middle = middle[0] == 1
        self.line = lax.axis_size("tensor") == 4
        self.pieces, self.joined, self.other, self.results = [], {}, {}, []

    def slot(self, piece, seen):
        number = len(self.pieces)
        shape = None if piece is None else piece.shape
        piece = None if piece is None else piece.reshape(-1, 128)
        self.pieces.append(piece)
        if not self.line:
            if piece is not None:
                total = lax.psum(piece, "tensor")
                self.results.append((total, total))
            return seen
        sent = []
        pairs, operand = [], None
        if piece is not None:
            operand = after(piece, seen)
            pairs += [(0, 1), (3, 2)]
        done = self.pieces[number - 2] if number >= 2 else None
        if done is not None:
            other = after(self.other[number - 2], (seen, self.inward))
            settled = (self.joined[number - 2] + other.astype(f32)).astype(bf16)
            if operand is None:
                operand = settled
            else:
                settled = jnp.pad(settled, ((0, operand.shape[0] - settled.shape[0]), (0, 0)))
                operand = jnp.where(self.middle, settled, operand)
            pairs += [(1, 0), (2, 3)]
        if number >= 1 and self.pieces[number - 1] is not None:
            inward = after(self.inward, seen).astype(f32)
            joined = (self.pieces[number - 1].astype(f32) + inward).astype(bf16)
            self.joined[number - 1] = joined.astype(f32)
            self.other[number - 1] = lax.ppermute(joined, "tensor", [(1, 2), (2, 1)])
            sent.append(joined)
        if operand is not None:
            self.inward = lax.ppermute(operand, "tensor", pairs)
            sent.append(operand)
        if done is not None:
            self.results.append((operand, self.inward))
        return tuple(sent)


def scatter_blocks(blocks, by_rows):
    if is_cube():
        return lax.psum_scatter(blocks, "dp", scatter_dimension=0, tiled=True)[0].astype(f32)
    if by_rows:
        full = blocks.reshape(-1, blocks.shape[2])
        return lax.psum_scatter(full, "dp", scatter_dimension=0, tiled=True).astype(f32)
    full = blocks.transpose(1, 0, 2).reshape(blocks.shape[1], -1)
    return lax.psum_scatter(full, "dp", scatter_dimension=1, tiled=True).astype(f32)


def ring(value, step):
    count = lax.axis_size("dp")
    pairs = [(i, i + step) for i in range(count) if 0 <= i + step < count]
    return lax.ppermute(value, "dp", pairs)


def locate(token_index, lengths, prefix):
    ends = jnp.cumsum(lengths)
    starts = ends - lengths
    inside = (token_index[:, None] >= starts[None, :]) & (token_index[:, None] < ends[None, :])
    begin = jnp.sum(jnp.where(inside, starts[None, :], 0), axis=1)
    limit = jnp.sum(jnp.where(inside, jnp.minimum(prefix, lengths)[None, :], 0), axis=1)
    return begin, limit


def rotary_tables(places):
    lane = jnp.arange(128, dtype=jnp.int32)
    exponents = (lane % (ROT // 2)).astype(f32) * (2.0 / ROT)
    angles = places.astype(f32)[:, None] * jnp.exp(exponents * -math.log(10000.0))[None, :]
    turned = (lane < ROT)[None, :]
    sign = jnp.where(lane < ROT // 2, -1.0, 1.0)[None, :]
    return jnp.where(turned, jnp.cos(angles), 1.0), jnp.where(turned, jnp.sin(angles) * sign, 0.0)


def on_device(
    tokens,
    project_weight,
    project_bias,
    dense_weight,
    dense_bias,
    expand_weight,
    expand_bias,
    shrink_weight,
    shrink_bias,
    first_gain,
    first_shift,
    second_gain,
    second_shift,
    lengths,
    prefix,
    upstream,
):
    rows, width = tokens.shape
    count = lax.axis_size("dp")
    me = lax.axis_index("dp")
    heads = project_bias.shape[0]
    places = natural_places()
    cube = is_cube()
    line = lax.axis_index("tensor")
    middle = ((line == 1) | (line == 2)).astype(jnp.int32).reshape(1)

    turned_width, hidden_width = dense_weight.shape[0], shrink_weight.shape[0]
    vectors = [first_gain, first_shift, second_gain, second_shift, dense_bias, shrink_bias]
    if cube:
        own = jnp.concatenate([v.reshape(-1).astype(bf16) for v in (*vectors, expand_bias, project_bias)])
        own = jnp.pad(own, (0, -own.size % 2048)).reshape(-1, 128)
        gathered = lax.all_gather(own, "dp", axis=0).reshape(count, -1)
        small = jnp.take(gathered, places, axis=0).astype(f32)
        wide = vectors[0].shape[0]
        rows_of = jnp.stack([small[:, k * wide : (k + 1) * wide].reshape(-1) for k in range(len(vectors))])
        at = len(vectors) * wide
        small = gathered.astype(f32)
        split = at + expand_bias.size
        full_expand_bias = small[:, at:split].reshape((count,) + expand_bias.shape).transpose(1, 0, 2).reshape(1, -1)
        full_project_bias = small[:, split : split + project_bias.size].reshape((count,) + project_bias.shape).transpose(1, 0, 2).reshape(1, -1)
    else:
        rows_of = lax.all_gather(jnp.stack(vectors).astype(bf16), "dp", axis=1, tiled=True).astype(f32)
        full_expand_bias = lax.all_gather(expand_bias.astype(bf16), "dp", axis=1, tiled=True).astype(f32).reshape(1, -1)
        full_project_bias = lax.all_gather(project_bias.astype(bf16), "dp", axis=1, tiled=True).astype(f32).reshape(1, -1)
    gains = jnp.concatenate([rows_of[:4], jnp.zeros((4, width), f32)], axis=0)
    bias_total = rows_of[4:5] + rows_of[5:6]

    def halved(vector, bit):
        keep = vector.shape[0] // 2
        return vector[:keep] + swap(vector[keep:], bit)

    def vector_parts(sums, grad_bias, expand_bias_sums, project_bias_sums):
        norms = sums[:4].reshape(4, BLOCKS, BLOCK).transpose(1, 0, 2).reshape(BLOCKS, -1)
        bias = grad_bias[0].reshape(BLOCKS, BLOCK)
        per_head = lambda v, like: v.reshape(heads, BLOCKS, like.shape[1]).transpose(1, 0, 2).reshape(BLOCKS, -1)
        heads_part = jnp.concatenate(
            [per_head(expand_bias_sums, expand_bias), per_head(project_bias_sums, project_bias)], axis=1
        )
        heads_part = jnp.take(heads_part, places, axis=0)
        return jnp.concatenate([norms, bias, heads_part], axis=1)

    token_index = me * rows + jnp.arange(rows, dtype=jnp.int32)
    begin, limit = locate(token_index, lengths, prefix)
    base = me * rows - SEQ_MAX
    low = begin - base
    high = jnp.maximum(token_index, begin + limit - 1) - base
    cos, sin = rotary_tables(token_index - begin)

    tok, one_a, one_b, two_a, two_b, up_a, up_b, mean, inverse, grad_bias = norm(places, tokens, upstream, gains)

    spread_expand = Spread(expand_weight.astype(bf16))
    spread_project = Spread(project_weight.astype(bf16))
    seen_expand = spread_expand.first()
    seen_project = spread_project.first()
    seen_expand_too = spread_expand.second(seen_expand, mean)
    seen_project_too = spread_project.second(seen_project, mean)
    down_weight = jnp.concatenate([dense_weight.astype(bf16), shrink_weight.astype(bf16)], axis=0)
    down_weight = after(down_weight, (mean, seen_expand, seen_project))
    project_a, project_b = spread_project.join(seen_project_too, down_weight)
    expand_a, expand_b = spread_expand.join(seen_expand_too, project_a)
    down_blocks = gather_columns(after(down_weight, (project_a, expand_a)))
    queries, pairs = project(after(one_a, expand_a), one_b, project_a, project_b, full_project_bias, cos, sin)
    left = ring(pairs, 1)
    right = ring(pairs[:PREFIX_MAX], -1)
    if cube:
        own_blocks = (down_weight, swap(after(down_weight, seen_expand_too), CORE))
    else:
        own_blocks = (down_blocks[0], down_blocks[HALF])
    active, slope = expand(after(two_a, (pairs, own_blocks)), two_b, expand_a, expand_b, full_expand_bias)
    attended, lse = attend(after(queries, active), left, pairs, right, low, high)

    line = LineSum(middle)
    pieces = [branch_piece(attended, active, *own_blocks)]
    seen = line.slot(pieces[0], ())
    column_blocks = column_grad(places, after(attended, (pieces[0], seen)), active, up_a, up_b)
    grad_attended = back(places, after(up_a, column_blocks), up_b, down_blocks, 0, turned_width)
    dq, dleft, down, dright = attend_back(
        queries, left, pairs, right, low, high, lse, attended, grad_attended, cos, sin
    )
    later = ring(dleft, -1)
    earlier = ring(dright, 1)
    last = dq
    for place in (1, 2, 3):
        pieces.append(branch_place(places, after(attended, last), active, down_blocks, place))
        last = pieces[-1]
        if place == 1:
            seen = line.slot(pieces[1], last)
            last = (last, seen, earlier)
    column_blocks, later, earlier, last = lax.optimization_barrier((column_blocks, later, earlier, last))
    grad_down = scatter_blocks(column_blocks, False)
    grad_hidden, expand_bias_sums = back(
        places, after(up_a, last), up_b, down_blocks, turned_width, hidden_width, slope
    )
    seen = line.slot(pieces[2], grad_hidden)
    grad_second = second_back(after(grad_hidden, seen), expand_a, expand_b)
    grad_mixed, project_bias_sums = mix(after(dq, grad_second), down, later, earlier, cos, sin)
    seen = line.slot(pieces[3], grad_mixed)
    *tails, sums = input_back(
        after(grad_mixed, seen), project_a, project_b, grad_second, tok, mean, inverse, gains, 0
    )
    seen = line.slot(tails[0], sums)
    *more, part = input_back(
        after(grad_mixed, (sums, seen)), project_a, project_b, grad_second, tok, mean, inverse, gains, 2
    )
    tails += more
    sums = sums + part
    seen = line.slot(tails[1], part)
    vector = part
    if cube:
        vector = after(vector_parts(sums, grad_bias, expand_bias_sums, project_bias_sums), seen)
        vector = halved(halved(halved(vector, CORE), ALONG_Y), ALONG_X)[0]
    widths = grad_hidden.shape[1], grad_mixed.shape[1]
    row_blocks = row_grad(places, two_a, two_b, after(grad_hidden, seen), sum(widths))
    row_blocks = row_grad(places, one_a, one_b, grad_mixed, sum(widths), widths[0], row_blocks)
    seen = line.slot(tails[2], row_blocks)
    row_blocks, grad_down, vector, seen = lax.optimization_barrier((row_blocks, grad_down, vector, seen))
    if cube:
        grad_rows = scatter_blocks(row_blocks, True)
        grad_expand, grad_project = grad_rows[:, : widths[0]], grad_rows[:, widths[0] :]
    else:
        grad_expand = scatter_blocks(row_blocks[:, :, : widths[0]], True)
        grad_project = scatter_blocks(row_blocks[:, :, widths[0] :], True)
    settled, passed = zip(*line.results[:4])
    output = output_sum(places, middle, after(bias_total, (row_blocks, seen)), settled, passed, tokens)
    tail = tails[3]
    if cube:
        norms = vector[: 4 * BLOCK].astype(bf16).reshape(-1, 128)
        tail = jnp.concatenate([tail.reshape(-1, 128), norms, jnp.zeros_like(norms)], axis=0)
    seen = line.slot(tail, output)
    tokens_grad = tokens_sum(places, middle, upstream, *line.results[4], 0, after(up_a, (output, seen)))
    seen = line.slot(None, tokens_grad)
    tokens_grad = tokens_sum(places, middle, upstream, *line.results[5], 1, after(tokens_grad, seen))
    line.slot(None, tokens_grad)
    for number in range(2, 4):
        tokens_grad = tokens_sum(places, middle, upstream, *line.results[4 + number], number, tokens_grad)
    grad_dense, grad_shrink = grad_down[:turned_width], grad_down[turned_width:]

    if cube:
        settled, passed = line.results[7]
        norms = jnp.where(middle[0] == 1, settled[-16:-8], passed[-16:-8]).astype(f32).reshape(4, BLOCK)
        at = 5 * BLOCK
        bias = vector[4 * BLOCK : at]
        expand_bias_grad = vector[at : at + expand_bias.size].reshape(expand_bias.shape)
        project_bias_grad = vector[at + expand_bias.size :].reshape(project_bias.shape)
    else:
        norms = lax.psum(lax.psum_scatter(sums[:4], "dp", scatter_dimension=1, tiled=True), "tensor")
        bias = lax.psum_scatter(grad_bias[0], "dp", scatter_dimension=0, tiled=True)
        split = lambda v: lax.psum_scatter(v.reshape(heads, -1), "dp", scatter_dimension=1, tiled=True)
        expand_bias_grad, project_bias_grad = split(expand_bias_sums), split(project_bias_sums)
    return (
        output,
        tokens_grad,
        grad_project,
        project_bias_grad,
        grad_dense,
        bias,
        grad_expand,
        expand_bias_grad,
        grad_shrink,
        bias,
        norms[0],
        norms[1],
        norms[2],
        norms[3],
    )


def solution(mesh):
    placed = (
        P("dp", None),
        P("dp", "tensor"),
        P("tensor", "dp"),
        P("tensor", "dp"),
        P("dp"),
        P("dp", "tensor"),
        P("tensor", "dp"),
        P("tensor", "dp"),
        P("dp"),
        P("dp"),
        P("dp"),
        P("dp"),
        P("dp"),
        P(),
        P(),
        P("dp", None),
    )
    return jax.shard_map(
        on_device,
        mesh=mesh,
        in_specs=placed,
        out_specs=(
            P("dp", None),
            P("dp", None),
            P("dp", "tensor"),
            P("tensor", "dp"),
            P("tensor", "dp"),
            P("dp"),
            P("dp", "tensor"),
            P("tensor", "dp"),
            P("tensor", "dp"),
            P("dp"),
            P("dp"),
            P("dp"),
            P("dp"),
            P("dp"),
        ),
        check_vma=False,
    )
```

time: 1160 us -> 595 us (0.51)
  waiting for transfers between devices: 420 us -> 99.7 us
  matrix products: 250 us -> 0 us
  Pallas kernels: 0 us -> 239 us
  blocking collectives: 171 us -> 41.4 us
  starting transfers between devices: 10.1 us -> 115 us
  other arithmetic: 141 us -> 40.1 us
  local copies, waits for them, and re-layouts: 136 us -> 35.9 us
    dot_general x26 -> x0, matrix products: 250 us -> none  [the longest x1 33.2 us: on_device(): jnp.einsum('td,fd->tf', upstream, full_shrink, preferred_element_type=f32)]
    pallas_call x0 -> x23, Pallas kernels: none -> 239 us  [the longest x2 26 us: row_grad(): pl.pallas_call(row_grad_kernel, grid_spec=pltpu.PrefetchScalarGridSpec(nu...]
    psum x1 -> x0, waiting for transfers between devices: 212 us -> none  [on_device(): lax.psum(partial_sum.astype(jnp.bfloat16), 'tensor').astype(jnp.float32)]
    reduce_scatter x4 -> x2, waiting for transfers between devices: 197 us -> 0.01 us  [scatter_blocks(): lax.psum_scatter(blocks, 'dp', scatter_dimension=0, tiled=True)[0]]
    ppermute x4 -> x36, starting transfers between devices: 9.65 us -> 115 us  [the longest x4 44.4 us: ring(): return lax.ppermute(value, 'dp', pairs)]
    ppermute x4 -> x36, waiting for transfers between devices: 0.01 us -> 99.6 us  [the longest x10 84.3 us: slot(): self.inward = lax.ppermute(operand, 'tensor', pairs)]
    all_gather x8 -> x1, blocking collectives: 133 us -> 41.4 us  [on_device(): gathered = lax.all_gather(own, 'dp', axis=0).reshape(count, -1)]
    convert_element_type x30 -> x27, other arithmetic: 66.9 us -> 19.5 us  [the longest x8 9.5 us: slot(): joined = (self.pieces[number - 1].astype(f32) + inward).astype(bf16)]
  transfers between devices with their start and end apart: 15 -> 39, of which waited for: 5 -> 12; matrix products, arithmetic and copies ran while one was open for 45% -> 10% of each run, Pallas kernels for 0% -> 41%
where the time goes in v1:
time: 595 us; the launch traced here: 586 us
  Pallas kernels  239 us (40%)
  starting transfers between devices  115 us (19%)
  waiting for transfers between devices  99.7 us (17%)
  blocking collectives  41.4 us (7%)
  other arithmetic  40.1 us (7%)
  local copies, waits for them, and re-layouts  35.9 us (6%)
  between operations  15 us (3%)
    ppermute x10, waiting for transfers between devices, slot(): self.inward = lax.ppermute(operand, 'tensor', pairs)  84.3 us
    ppermute x4, starting transfers between devices, ring(): return lax.ppermute(value, 'dp', pairs)  44.4 us
    all_gather x1, blocking collectives, on_device(): gathered = lax.all_gather(own, 'dp', axis=0).reshape(count, -1)  41.4 us
    ppermute x14, starting transfers between devices, swap(): return lax.ppermute(value, 'dp', [(i, i ^ bit) for i in range(count)])  36.4 us
    pallas_call x2, Pallas kernels, row_grad(): pl.pallas_call(row_grad_kernel, grid_spec=pltpu.PrefetchScalarGridSpec(nu...  26 us
    pallas_call x2, Pallas kernels, input_back(): pl.pallas_call(input_kernel, grid=(2,), in_specs=[row(depth), whole_spec(...  26 us
    ppermute x10, starting transfers between devices, slot(): self.inward = lax.ppermute(operand, 'tensor', pairs)  24.9 us
    pallas_call x2, Pallas kernels, back(): pl.pallas_call(body, grid_spec=pltpu.PrefetchScalarGridSpec(num_scalar_pr...  21.7 us
  transfers between devices with their start and end apart: 39, of which 12 were waited for; matrix products, arithmetic and copies ran while one was open for 10% of the time, Pallas kernels for 41%

profile of v1, /device:TPU:0, one launch (start us, length us, event | category | flops | bytes accessed | tf_op | source)
XLA Modules:
  0.0 585.9 jit_solution(4774294498197795296)
XLA Ops:
  9.0 3.0 collective-permute-start.5
  16.3 41.4 %all_gather.9 = bf16[8,16,128]{2,1,0:T(8,128)(2,1)S(1)} all-gather(bf16[1,16,128]{2,1,0:T(8,128)(2,1)S(1)} %pad_bitcast_fusion), channel_id=1, replica_groups=mesh['dp'=8,'tensor'=4] {'dp'}, dimensions={0}, use_global_device_ids=true | all-gather | bytes 36864 | tf_op jit(solution)/shard_map/all_gather | solution.py:845
  60.9 12.1 %norm.1 = (bf16[1024,2048]{1,0:T(8,128)(2,1)}, bf16[1024,1024]{1,0:T(8,128)(2,1)}, bf16[1024,1024]{1,0:T(8,128)(2,1)}, bf16[1024,1024]{1,0:T(8,128)(2,1)}, bf16[...) custom-call(s32[8]{0:T(128)} %fusion.17.places.where.w._, ...), custom_call_target="tpu_custom_call" | custom-call | flops 41943040 | bytes 41943040 | tf_op jit(solution)/shard_map/norm/pallas_call | solution.py:137
  82.9 5.0 collective-permute-done.6
  93.6 5.0 collective-permute-done.2
  100.1 2.3 constant_dynamic-update-slice_fusion.8
  107.7 3.1 fusion.7
  110.9 3.9 collective-permute-done.8.w_b
  114.8 12.1 %project.1 = (bf16[1024,512]{1,0:T(8,128)(2,1)}, bf16[1024,1024]{1,0:T(8,128)(2,1)}) custom-call(bf16[1024,1024]{1,0:T(8,128)(2,1)} %get-tuple-element.125.one_a.left_a, bf16[1024,1024]{1,0:T(8,128)(2,1)} %get-tuple-element.108.one_b.left_b, bf16[1024,1536]{1,0:T(8,128)(2,1)} %copy-done, bf16[1024,1536]{1,0:T(8,128)(2,1)} %collective-permute-done.8.w_b, ...), custom_call_target="tpu_custom_call" | custom-call | flops 6442450944 | bytes 14000000 | tf_op jit(solution)/shard_map/project/pallas_call | solution.py:178
  126.9 2.2 collective-permute-start.9
  130.7 12.5 %collective-permute-start.10 = (bf16[512,1024]{1,0:T(8,128)(2,1)S(1)}, bf16[512,1024]{1,0:T(8,128)(2,1)S(1)}, u32[]{:S(2)}, u32[]{:S(2)}) collective-permute-start(bf16[512,1024]{1,0:T(8,128)(2,1)S(1)} %slice.129), channel_id=1, source_target_pairs={{4,0},{8,4},{12,8},{16,12},{20,16},{24,20},{28,24},{5,1},{9,5},{13... | collective-permute-start | bytes 3145736 | tf_op jit(solution)/shard_map/ppermute | solution.py:792
  145.6 17.0 %expand.1 = (bf16[1024,2048]{1,0:T(8,128)(2,1)}, bf16[1024,2048]{1,0:T(8,128)(2,1)}) custom-call(bf16[1024,1024]{1,0:T(8,128)(2,1)} %get-tuple-element.130.two_a.left_a, bf16[1024,1024]{1,0:T(8,128)(2,1)} %get-tuple-element.131.two_b.left_b, bf16[1024,2048]{1,0:T(8,128)(2,1)} %constant_dynamic-update-slice_fusion.5.w_a, ...), custom_call_target="tpu_custom_call" | custom-call | flops 8589934592 | bytes 22000000 | tf_op jit(solution)/shard_map/expand/pallas_call | solution.py:216
  164.3 12.1 %attend.1 = (bf16[1024,512]{1,0:T(8,128)(2,1)}, f32[2,1,1024]{2,1,0:T(1,128)}) custom-call(s32[2]{0:T(128)} %get-tuple-element.225.first, s32[2]{0:T(128)} %get-tuple-element.224.last, bf16[1024,512]{1,0:T(8,128)(2,1)} %get-tuple-element.133.q, bf16[1024,1024]{1,0:T(8,128)(2,1)} %copy-done.38, bf16[1024,1024]{1,0:T(8,128)(2,1)} %get-tuple-element.127.own, ...), custom_call_target="tpu_custom_call" | custom-call | flops 8000000000 | bytes 10000000 | tf_op jit(solution)/shard_map/attend/pallas_call | solution.py:469
  176.4 6.4 %branch.4 = bf16[4,1024,128]{2,1,0:T(8,128)(2,1)} custom-call(bf16[1024,512]{1,0:T(8,128)(2,1)} %get-tuple-element.156.attended.first.refs_0_, bf16[1024,2048]{1,0:T(8,128)(2,1)} %get-tuple-element.132.active.second.refs_1_, bf16[2560,256]{1,0:T(8,128)(2,1)} %pad_maximum_fusion.mine, bf16[2560,256]{1,0:T(8,128)(2,1)} %collective-permute-done.11.theirs), custom_call_target="tpu_custom_call" | custom-call | flops 2684354560 | bytes 8912896 | tf_op jit(solution)/shard_map/branch/pallas_call | solution.py:242
  182.8 4.5 collective-permute-start.14
  187.3 17.4 %column_grad.1 = bf16[8,2560,256]{2,1,0:T(8,128)(2,1)} custom-call(s32[8]{0:T(128)} %fusion.17.places.where.w._, bf16[1024,512]{1,0:T(8,128)(2,1)} %get-tuple-element.156.attended.first.refs_0_, bf16[1024,2048]{1,0:T(8,128)(2,1)} %get-tuple-element.132.active.second.refs_1_, bf16[1024,1024]{1,0:T(8,128)(2,1)} %get-tuple-element.194.right_a.a.rest_0_, ...), custom_call_target="tpu_custom_call" | custom-call | flops 10737418240 | bytes 19922944 | tf_op jit(solution)/shard_map/column_grad/pallas_call | solution.py:401
  204.7 6.9 %back.2.grad = bf16[1024,512]{1,0:T(8,128)(2,1)} custom-call(s32[8]{0:T(128)} %fusion.17.places.where.w._, bf16[1024,1024]{1,0:T(8,128)(2,1)} %get-tuple-element.194.right_a.a.rest_0_, bf16[1024,1024]{1,0:T(8,128)(2,1)} %get-tuple-element.138.right_b.b, bf16[8,2560,256]{2,1,0:T(8,128)(2,1)} %bitcast.98), custom_call_target="tpu_custom_call" | custom-call | flops 2147483648 | bytes 8388608 | tf_op jit(solution)/shard_map/back/pallas_call | solution.py:307
  211.6 18.6 %attend_back.1 = (bf16[1024,512]{1,0:T(8,128)(2,1)}, bf16[1024,1024]{1,0:T(8,128)(2,1)}, f32[1024,1024]{1,0:T(8,128)}, bf16[512,1024]{1,0:T(8,128)(2,1)}) custom-call(s32[2]{0:T(128)} %get-tuple-element.225.first, s32[2]{0:T(128)} %get-tuple-element.224.last, bf16[1024,512]{1,0:T(8,128)(2,1)} %get-tuple-element.133.q, bf16[1024,1024]{1,0:T(8,128)(2,1)} %copy-done.38, ...), custom_call_target="tpu_custom_call" | custom-call | flops 16000000000 | bytes 20000000 | tf_op jit(solution)/shard_map/attend_back/pallas_call | solution.py:546
  231.6 28.3 %collective-permute-start.16 = (bf16[512,1024]{1,0:T(8,128)(2,1)}, bf16[512,1024]{1,0:T(8,128)(2,1)S(1)}, u32[]{:S(2)}, u32[]{:S(2)}) collective-permute-start(bf16[512,1024]{1,0:T(8,128)(2,1)} %get-tuple-element.149), channel_id=1, source_target_pairs={{0,4},{4,8},{8,12},{12,16},{16,20},{20,24},{24,28},{1,5},{5,9},{9,... | collective-permute-start | bytes 3145736 | tf_op jit(solution)/shard_map/ppermute | solution.py:792
  259.9 7.1 %branch.5 = bf16[4,1024,128]{2,1,0:T(8,128)(2,1)} custom-call(s32[8]{0:T(128)} %fusion.17.places.where.w._, bf16[1024,512]{1,0:T(8,128)(2,1)} %get-tuple-element.156.attended.first.refs_0_, bf16[1024,2048]{1,0:T(8,128)(2,1)} %get-tuple-element.132.active.second.refs_1_, bf16[8,2560,256]{2,1,0:T(8,128)(2,1)} %bitcast.99, bf16[8,2560,256]{2,1,0:T(8,128)(2,1)} %bitcast.100), custom_call_target="tpu_custom_call" | custom-call | flops 2684354560 | bytes 8912896 | tf_op jit(solution)/shard_map/branch/pallas_call | solution.py:260
  270.2 3.5 collective-permute-start.13
  273.7 7.1 %branch.6 = bf16[4,1024,128]{2,1,0:T(8,128)(2,1)} custom-call(s32[8]{0:T(128)} %fusion.17.places.where.w._, bf16[1024,512]{1,0:T(8,128)(2,1)} %get-tuple-element.156.attended.first.refs_0_, bf16[1024,2048]{1,0:T(8,128)(2,1)} %get-tuple-element.132.active.second.refs_1_, bf16[8,2560,256]{2,1,0:T(8,128)(2,1)} %bitcast.101, bf16[8,2560,256]{2,1,0:T(8,128)(2,1)} %bitcast.102), custom_call_target="tpu_custom_call" | custom-call | flops 2684354560 | bytes 8912896 | tf_op jit(solution)/shard_map/branch/pallas_call | solution.py:260
  280.7 7.1 %branch.7 = bf16[4,1024,128]{2,1,0:T(8,128)(2,1)} custom-call(s32[8]{0:T(128)} %fusion.17.places.where.w._, bf16[1024,512]{1,0:T(8,128)(2,1)} %get-tuple-element.156.attended.first.refs_0_, bf16[1024,2048]{1,0:T(8,128)(2,1)} %get-tuple-element.132.active.second.refs_1_, bf16[8,2560,256]{2,1,0:T(8,128)(2,1)} %bitcast.103, bf16[8,2560,256]{2,1,0:T(8,128)(2,1)} %bitcast.104), custom_call_target="tpu_custom_call" | custom-call | flops 2684354560 | bytes 8912896 | tf_op jit(solution)/shard_map/branch/pallas_call | solution.py:260
  288.1 14.8 %back.3 = (bf16[1024,2048]{1,0:T(8,128)(2,1)}, f32[1,2048]{1,0:T(1,128)}) custom-call(s32[8]{0:T(128)} %fusion.17.places.where.w._, bf16[1024,1024]{1,0:T(8,128)(2,1)} %get-tuple-element.194.right_a.a.rest_0_, bf16[1024,1024]{1,0:T(8,128)(2,1)} %get-tuple-element.138.right_b.b, bf16[8,2560,256]{2,1,0:T(8,128)(2,1)} %bitcast.105, ...), custom_call_target="tpu_custom_call" | custom-call | flops 8589934592 | bytes 20971520 | tf_op jit(solution)/shard_map/back/pallas_call | solution.py:307
  307.1 14.3 %second_back.1.second = bf16[1024,2048]{1,0:T(8,128)(2,1)} custom-call(bf16[1024,2048]{1,0:T(8,128)(2,1)} %get-tuple-element.177.grad.right, bf16[1024,2048]{1,0:T(8,128)(2,1)} %constant_dynamic-update-slice_fusion.5.w_a, bf16[1024,2048]{1,0:T(8,128)(2,1)} %collective-permute-done.12.w_b), custom_call_target="tpu_custom_call" | custom-call | flops 8589934592 | bytes 16777216 | tf_op jit(solution)/shard_map/second_back/pallas_call | solution.py:339
  321.4 7.6 %mix.1 = (bf16[1024,1536]{1,0:T(8,128)(2,1)}, f32[1,1536]{1,0:T(1,128)}) custom-call(bf16[1024,512]{1,0:T(8,128)(2,1)} %get-tuple-element.153.dq, f32[1024,1024]{1,0:T(8,128)} %get-tuple-element.154.own, bf16[1024,1024]{1,0:T(8,128)(2,1)} %collective-permute-done.17.later, bf16[512,1024]{1,0:T(8,128)(2,1)} %copy-done.26, ...), custom_call_target="tpu_custom_call" | custom-call | flops 10000000 | bytes 14000000 | tf_op jit(solution)/shard_map/mix/pallas_call | solution.py:592
  335.9 13.2 %input_back.2 = (bf16[16,256,128]{2,1,0:T(8,128)(2,1)}, bf16[16,256,128]{2,1,0:T(8,128)(2,1)}, f32[8,2048]{1,0:T(8,128)}) custom-call(bf16[1024,1536]{1,0:T(8,128)(2,1)} %get-tuple-element.171.mixed.right, bf16[1024,1536]{1,0:T(8,128)(2,1)} %copy-done, bf16[1024,1536]{1,0:T(8,128)(2,1)} %collective-permute-done.8.w_b, bf16[1024,2048]{1,0:T(8,128)(2,1)} %second_back.1.second, ...), custom_call_target="tpu_custom_call" | custom-call | flops 3221225472 | bytes 14000000 | tf_op jit(solution)/shard_map/input_back/pallas_call | solution.py:654
  349.1 7.3 %collective-permute-done.21 = bf16[4096,128]{1,0:T(8,128)(2,1)} collective-permute-done((bf16[4096,128]{1,0:T(8,128)(2,1)S(1)}, bf16[4096,128]{1,0:T(8,128)(2,1)}, u32[]{:S(2)}, u32[]{:S(2)}) %collective-permute-start.21) | collective-permute-done | bytes 1048608 | tf_op jit(solution)/shard_map/ppermute | solution.py:772
  356.4 2.2 fusion.2
  358.7 4.1 collective-permute-start.22
  365.0 12.8 %input_back.3 = (bf16[16,256,128]{2,1,0:T(8,128)(2,1)}, bf16[16,256,128]{2,1,0:T(8,128)(2,1)}, f32[8,2048]{1,0:T(8,128)}) custom-call(bf16[1024,1536]{1,0:T(8,128)(2,1)} %get-tuple-element.171.mixed.right, bf16[1024,1536]{1,0:T(8,128)(2,1)} %copy-done, bf16[1024,1536]{1,0:T(8,128)(2,1)} %collective-permute-done.8.w_b, bf16[1024,2048]{1,0:T(8,128)(2,1)} %second_back.1.second, ...), custom_call_target="tpu_custom_call" | custom-call | flops 3221225472 | bytes 14000000 | tf_op jit(solution)/shard_map/input_back/pallas_call | solution.py:654
  378.8 7.7 %collective-permute-done.22 = bf16[4096,128]{1,0:T(8,128)(2,1)S(1)} collective-permute-done((bf16[4096,128]{1,0:T(8,128)(2,1)S(1)}, bf16[4096,128]{1,0:T(8,128)(2,1)S(1)}, u32[]{:S(2)}, u32[]{:S(2)}) %collective-permute-start.22) | collective-permute-done | bytes 1048608 | tf_op jit(solution)/shard_map/ppermute | solution.py:772
  390.6 6.1 %collective-permute-start.27 = (bf16[4096,128]{1,0:T(8,128)(2,1)}, bf16[4096,128]{1,0:T(8,128)(2,1)}, u32[]{:S(2)}, u32[]{:S(2)}) collective-permute-start(bf16[4096,128]{1,0:T(8,128)(2,1)} %fusion.3), channel_id=1, source_target_pairs={{0,1},{3,2},{1,0},{2,3},{4,5},{7,6},{5,4},{6,7},{8,9},{11,10},{9,8... | collective-permute-start | bytes 3145736 | tf_op jit(solution)/shard_map/ppermute | solution.py:772
  396.7 25.8 %collective-permute-start.25 = (f32[2,1728]{1,0:T(2,128)S(1)}, f32[2,1728]{1,0:T(2,128)S(1)}, u32[]{:S(2)}, u32[]{:S(2)}) collective-permute-start(f32[2,1728]{1,0:T(2,128)S(1)} %slice.172), channel_id=1, source_target_pairs={{0,16},{4,20},{8,24},{12,28},{16,0},{20,4},{24,8},{28,12},{1,17},{... | collective-permute-start | bytes 41480 | tf_op jit(solution)/shard_map/ppermute | solution.py:47
  422.5 14.2 %row_grad.2.rest_0_ = bf16[8,256,3584]{2,1,0:T(8,128)(2,1)} custom-call(s32[8]{0:T(128)} %fusion.17.places.where.w._, bf16[1024,1024]{1,0:T(8,128)(2,1)} %get-tuple-element.130.two_a.left_a, bf16[1024,1024]{1,0:T(8,128)(2,1)} %get-tuple-element.131.two_b.left_b, bf16[1024,2048]{1,0:T(8,128)(2,1)} %get-tuple-element.177.grad.right), custom_call_target="tpu_custom_call" | custom-call | flops 8589934592 | bytes 16777216 | tf_op jit(solution)/shard_map/row_grad/pallas_call | solution.py:367
  436.8 11.8 %row_grad.3 = bf16[8,256,3584]{2,1,0:T(8,128)(2,1)} custom-call(s32[8]{0:T(128)} %fusion.17.places.where.w._, bf16[1024,1024]{1,0:T(8,128)(2,1)} %get-tuple-element.125.one_a.left_a, bf16[1024,1024]{1,0:T(8,128)(2,1)} %get-tuple-element.108.one_b.left_b, bf16[1024,1536]{1,0:T(8,128)(2,1)} %get-tuple-element.171.mixed.right, ...), custom_call_target="tpu_custom_call", output_to_operand_aliasing={{}: (4, {})} | custom-call | flops 6442450944 | bytes 13631488 | tf_op jit(solution)/shard_map/row_grad/pallas_call | solution.py:367
  448.7 2.5 add_convert_fusion.6
  451.2 2.6 fusion.4.settled
  459.6 10.2 %output_sum.1 = bf16[1024,2048]{1,0:T(8,128)(2,1)} custom-call(s32[8]{0:T(128)} %fusion.17.places.where.w._, s32[1]{0:T(128)} %bitcast.middle, bf16[1024,2048]{1,0:T(8,128)(2,1)} %tokens.3, f32[1,2048]{1,0:T(1,128)} %bitcast.123, bf16[4,1024,128]{2,1,0:T(8,128)(2,1)} %bitcast.112, bf16[4,1024,128]{2,1,0:T(8,128)(2,1)} %bitcast.114, ...), custom_call_target="tpu_custom_call" | custom-call | flops 10000000 | bytes 17000000 | tf_op jit(solution)/shard_map/output_sum/pallas_call | solution.py:686
  469.8 3.7 maximum_maximum_fusion
  473.5 9.3 %collective-permute-done.30.passed = bf16[4096,128]{1,0:T(8,128)(2,1)S(1)} collective-permute-done((bf16[4096,128]{1,0:T(8,128)(2,1)}, bf16[4096,128]{1,0:T(8,128)(2,1)S(1)}, u32[]{:S(2)}, u32[]{:S(2)}) %collective-permute-start.30) | collective-permute-done | bytes 1048608 | tf_op jit(solution)/shard_map/ppermute | solution.py:772
  488.2 4.0 tokens_sum.4.rest_0_
  492.2 16.4 %collective-permute-done.31.passed = bf16[4112,128]{1,0:T(8,128)(2,1)S(1)} collective-permute-done((bf16[4112,128]{1,0:T(8,128)(2,1)S(1)}, bf16[4112,128]{1,0:T(8,128)(2,1)S(1)}, u32[]{:S(2)}, u32[]{:S(2)}) %collective-permute-start.31) | collective-permute-done | bytes 1052704 | tf_op jit(solution)/shard_map/ppermute | solution.py:772
  512.9 4.1 tokens_sum.5.rest_0_
  517.0 26.1 %collective-permute-done.34.passed = bf16[4096,128]{1,0:T(8,128)(2,1)} collective-permute-done((bf16[4096,128]{1,0:T(8,128)(2,1)S(1)}, bf16[4096,128]{1,0:T(8,128)(2,1)}, u32[]{:S(2)}, u32[]{:S(2)}) %collective-permute-start.34) | collective-permute-done | bytes 1048608 | tf_op jit(solution)/shard_map/ppermute | solution.py:772
  549.1 4.0 tokens_sum.6.rest_0_
  553.1 15.6 %collective-permute-done.35.passed = bf16[4112,128]{1,0:T(8,128)(2,1)} collective-permute-done((bf16[4112,128]{1,0:T(8,128)(2,1)}, bf16[4112,128]{1,0:T(8,128)(2,1)}, u32[]{:S(2)}, u32[]{:S(2)}) %collective-permute-start.35) | collective-permute-done | bytes 1052704 | tf_op jit(solution)/shard_map/ppermute | solution.py:772
  568.7 4.0 tokens_sum.7
  (279 shorter events, 87.7 us)
Async XLA Ops:
  7.2 197.6 %all-gather.3.cloned.1.call-start = ((), (), s32[]{:S(2)}) async-start(), calls=%async_computation.4 | async-start | bytes 11796480 | tf_op jit(solution)/shard_map/all_gather | solution.py:96
  8.9 64.1 %copy-start.21 = (bf16[256,1536]{1,0:T(8,128)(2,1)}, bf16[256,1536]{1,0:T(8,128)(2,1)S(1)}, u32[]{:S(2)}) copy-start(bf16[256,1536]{1,0:T(8,128)(2,1)S(1)} %convert_element_type.246) | copy-start | bytes 2359300
  9.0 64.0 %collective-permute-start.5 = (bf16[256,1536]{1,0:T(8,128)(2,1)S(1)}, bf16[256,1536]{1,0:T(8,128)(2,1)}, u32[]{:S(2)}, u32[]{:S(2)}) collective-permute-start(bf16[256,1536]{1,0:T(8,128)(2,1)S(1)} %convert_element_type.246), channel_id=1, source_target_pairs={{0,16},{4,20},{8,24},{12,28},{16,0},{20,4},{24,8},{28,12},{1,17},{... | collective-permute-start | bytes 2359304 | tf_op jit(solution)/shard_map/ppermute | solution.py:47
  12.0 62.9 %collective-permute-start.4 = (bf16[256,1536]{1,0:T(8,128)(2,1)S(1)}, bf16[256,1536]{1,0:T(8,128)(2,1)}, u32[]{:S(2)}, u32[]{:S(2)}) collective-permute-start(bf16[256,1536]{1,0:T(8,128)(2,1)S(1)} %convert_element_type.246), channel_id=1, source_target_pairs={{0,8},{4,12},{8,0},{12,4},{16,24},{20,28},{24,16},{28,20},{1,9},{5... | collective-permute-start | bytes 2359304 | tf_op jit(solution)/shard_map/ppermute | solution.py:47
  13.7 59.3 %copy-start.13 = (bf16[256,2048]{1,0:T(8,128)(2,1)}, bf16[256,2048]{1,0:T(8,128)(2,1)S(1)}, u32[]{:S(2)}) copy-start(bf16[256,2048]{1,0:T(8,128)(2,1)S(1)} %convert_element_type.245) | copy-start | bytes 3145732
  13.7 64.6 %collective-permute-start.1 = (bf16[256,2048]{1,0:T(8,128)(2,1)S(1)}, bf16[256,2048]{1,0:T(8,128)(2,1)S(1)}, u32[]{:S(2)}, u32[]{:S(2)}) collective-permute-start(bf16[256,2048]{1,0:T(8,128)(2,1)S(1)} %convert_element_type.245), channel_id=1, source_target_pairs={{0,16},{4,20},{8,24},{12,28},{16,0},{20,4},{24,8},{28,12},{1,17},{... | collective-permute-start | bytes 3145736 | tf_op jit(solution)/shard_map/ppermute | solution.py:47
  14.2 64.0 %collective-permute-start = (bf16[256,2048]{1,0:T(8,128)(2,1)S(1)}, bf16[256,2048]{1,0:T(8,128)(2,1)}, u32[]{:S(2)}, u32[]{:S(2)}) collective-permute-start(bf16[256,2048]{1,0:T(8,128)(2,1)S(1)} %convert_element_type.245), channel_id=1, source_target_pairs={{0,8},{4,12},{8,0},{12,4},{16,24},{20,28},{24,16},{28,20},{1,9},{5... | collective-permute-start | bytes 3145736 | tf_op jit(solution)/shard_map/ppermute | solution.py:47
  76.0 12.0 %collective-permute-start.6 = (bf16[128,1536]{1,0:T(8,128)(2,1)S(1)}, bf16[128,1536]{1,0:T(8,128)(2,1)S(1)}, u32[]{:S(2)}, u32[]{:S(2)}) collective-permute-start(bf16[128,1536]{1,0:T(8,128)(2,1)S(1)} %slice.165), channel_id=1, source_target_pairs={{0,16},{4,20},{8,24},{12,28},{16,0},{20,4},{24,8},{28,12},{1,17},{... | collective-permute-start | bytes 1179656 | tf_op jit(solution)/shard_map/ppermute | solution.py:47
  76.5 12.3 %collective-permute-start.7 = (bf16[128,1536]{1,0:T(8,128)(2,1)}, bf16[128,1536]{1,0:T(8,128)(2,1)}, u32[]{:S(2)}, u32[]{:S(2)}) collective-permute-start(bf16[128,1536]{1,0:T(8,128)(2,1)} %slice.166), channel_id=1, source_target_pairs={{0,8},{4,12},{8,0},{12,4},{16,24},{20,28},{24,16},{28,20},{1,9},{5... | collective-permute-start | bytes 1179656 | tf_op jit(solution)/shard_map/ppermute | solution.py:47
  79.7 18.9 %collective-permute-start.2 = (bf16[128,2048]{1,0:T(8,128)(2,1)S(1)}, bf16[128,2048]{1,0:T(8,128)(2,1)S(1)}, u32[]{:S(2)}, u32[]{:S(2)}) collective-permute-start(bf16[128,2048]{1,0:T(8,128)(2,1)S(1)} %slice.163), channel_id=1, source_target_pairs={{0,16},{4,20},{8,24},{12,28},{16,0},{20,4},{24,8},{28,12},{1,17},{... | collective-permute-start | bytes 1572872 | tf_op jit(solution)/shard_map/ppermute | solution.py:47
  81.4 17.6 %collective-permute-start.3 = (bf16[128,2048]{1,0:T(8,128)(2,1)S(1)}, bf16[128,2048]{1,0:T(8,128)(2,1)S(1)}, u32[]{:S(2)}, u32[]{:S(2)}) collective-permute-start(bf16[128,2048]{1,0:T(8,128)(2,1)S(1)} %slice.164), channel_id=1, source_target_pairs={{0,8},{4,12},{8,0},{12,4},{16,24},{20,28},{24,16},{28,20},{1,9},{5... | collective-permute-start | bytes 1572872 | tf_op jit(solution)/shard_map/ppermute | solution.py:47
  105.1 348.7 %reduce-scatter.3.cloned.1.call-start = ((), (), s32[]{:S(2)}) async-start(), calls=%async_computation.2 | async-start | bytes 11796480 | tf_op jit(solution)/shard_map/reduce_scatter | solution.py:781
  105.2 9.6 %collective-permute-start.8 = (bf16[1024,1536]{1,0:T(8,128)(2,1)S(1)}, bf16[1024,1536]{1,0:T(8,128)(2,1)}, u32[]{:S(2)}, u32[]{:S(2)}) collective-permute-start(bf16[1024,1536]{1,0:T(8,128)(2,1)S(1)} %constant_dynamic-update-slice_fusion.w_a), channel_id=1, source_target_pairs={{0,4},{4,0},{8,12},{12,8},{16,20},{20,16},{24,28},{28,24},{1,5},{5... | collective-permute-start | bytes 9437192 | tf_op jit(solution)/shard_map/ppermute | solution.py:47
  105.3 40.4 %collective-permute-start.12 = (bf16[1024,2048]{1,0:T(8,128)(2,1)}, bf16[1024,2048]{1,0:T(8,128)(2,1)}, u32[]{:S(2)}, u32[]{:S(2)}) collective-permute-start(bf16[1024,2048]{1,0:T(8,128)(2,1)} %constant_dynamic-update-slice_fusion.5.w_a), channel_id=1, source_target_pairs={{0,4},{4,0},{8,12},{12,8},{16,20},{20,16},{24,28},{28,24},{1,5},{5... | collective-permute-start | bytes 12582920 | tf_op jit(solution)/shard_map/ppermute | solution.py:47
  107.7 21.5 %copy-start.32 = (s32[1024]{0:T(1024)}, s32[1024]{0:T(1024)S(1)}, u32[]{:S(2)}) copy-start(s32[1024]{0:T(1024)S(1)} %get-tuple-element.219) | copy-start | bytes 12292
  110.8 34.8 %collective-permute-start.11 = (bf16[2560,256]{1,0:T(8,128)(2,1)}, bf16[2560,256]{1,0:T(8,128)(2,1)}, u32[]{:S(2)}, u32[]{:S(2)}) collective-permute-start(bf16[2560,256]{1,0:T(8,128)(2,1)} %pad_maximum_fusion.mine), channel_id=1, source_target_pairs={{0,4},{4,0},{8,12},{12,8},{16,20},{20,16},{24,28},{28,24},{1,5},{5... | collective-permute-start | bytes 3932168 | tf_op jit(solution)/shard_map/ppermute | solution.py:47
  126.9 35.8 %collective-permute-start.9 = (bf16[1024,1024]{1,0:T(8,128)(2,1)}, bf16[1024,1024]{1,0:T(8,128)(2,1)S(1)}, u32[]{:S(2)}, u32[]{:S(2)}) collective-permute-start(bf16[1024,1024]{1,0:T(8,128)(2,1)} %get-tuple-element.127.own), channel_id=1, source_target_pairs={{0,4},{4,8},{8,12},{12,16},{16,20},{20,24},{24,28},{1,5},{5,9},{9,... | collective-permute-start | bytes 6291464 | tf_op jit(solution)/shard_map/ppermute | solution.py:792
  130.7 31.9 %collective-permute-start.10 = (bf16[512,1024]{1,0:T(8,128)(2,1)S(1)}, bf16[512,1024]{1,0:T(8,128)(2,1)S(1)}, u32[]{:S(2)}, u32[]{:S(2)}) collective-permute-start(bf16[512,1024]{1,0:T(8,128)(2,1)S(1)} %slice.129), channel_id=1, source_target_pairs={{4,0},{8,4},{12,8},{16,12},{20,16},{24,20},{28,24},{5,1},{9,5},{13... | collective-permute-start | bytes 3145736 | tf_op jit(solution)/shard_map/ppermute | solution.py:792
  182.8 84.1 %collective-permute-start.14 = (bf16[4096,128]{1,0:T(8,128)(2,1)}, bf16[4096,128]{1,0:T(8,128)(2,1)}, u32[]{:S(2)}, u32[]{:S(2)}) collective-permute-start(bf16[4096,128]{1,0:T(8,128)(2,1)} %bitcast.117), channel_id=1, source_target_pairs={{0,1},{3,2},{4,5},{7,6},{8,9},{11,10},{12,13},{15,14},{16,17},{19,... | collective-permute-start | bytes 3145736 | tf_op jit(solution)/shard_map/ppermute | solution.py:772
  230.2 57.6 %collective-permute-start.17 = (bf16[1024,1024]{1,0:T(8,128)(2,1)}, bf16[1024,1024]{1,0:T(8,128)(2,1)}, u32[]{:S(2)}, u32[]{:S(2)}) collective-permute-start(bf16[1024,1024]{1,0:T(8,128)(2,1)} %get-tuple-element.155), channel_id=1, source_target_pairs={{4,0},{8,4},{12,8},{16,12},{20,16},{24,20},{28,24},{5,1},{9,5},{13... | collective-permute-start | bytes 6291464 | tf_op jit(solution)/shard_map/ppermute | solution.py:792
  231.6 35.4 %copy-start.27 = (bf16[4,1024,128]{2,1,0:T(8,128)(2,1)S(1)}, bf16[4,1024,128]{2,1,0:T(8,128)(2,1)}, u32[]{:S(2)}) copy-start(bf16[4,1024,128]{2,1,0:T(8,128)(2,1)} %branch.4) | copy-start | bytes 3145732
  231.6 42.1 %collective-permute-start.16 = (bf16[512,1024]{1,0:T(8,128)(2,1)}, bf16[512,1024]{1,0:T(8,128)(2,1)S(1)}, u32[]{:S(2)}, u32[]{:S(2)}) collective-permute-start(bf16[512,1024]{1,0:T(8,128)(2,1)} %get-tuple-element.149), channel_id=1, source_target_pairs={{0,4},{4,8},{8,12},{12,16},{16,20},{20,24},{24,28},{1,5},{5,9},{9,... | collective-permute-start | bytes 3145736 | tf_op jit(solution)/shard_map/ppermute | solution.py:792
  268.6 34.4 %collective-permute-start.15 = (bf16[4096,128]{1,0:T(8,128)(2,1)S(1)}, bf16[4096,128]{1,0:T(8,128)(2,1)}, u32[]{:S(2)}, u32[]{:S(2)}) collective-permute-start(bf16[4096,128]{1,0:T(8,128)(2,1)S(1)} %add_convert_fusion.14), channel_id=1, source_target_pairs={{1,2},{2,1},{5,6},{6,5},{9,10},{10,9},{13,14},{14,13},{17,18},{18,... | collective-permute-start | bytes 3145736 | tf_op jit(solution)/shard_map/ppermute | solution.py:769
  270.2 32.8 %collective-permute-start.13 = (bf16[4096,128]{1,0:T(8,128)(2,1)S(1)}, bf16[4096,128]{1,0:T(8,128)(2,1)}, u32[]{:S(2)}, u32[]{:S(2)}) collective-permute-start(bf16[4096,128]{1,0:T(8,128)(2,1)S(1)} %bitcast.111), channel_id=1, source_target_pairs={{0,1},{3,2},{4,5},{7,6},{8,9},{11,10},{12,13},{15,14},{16,17},{19,... | collective-permute-start | bytes 3145736 | tf_op jit(solution)/shard_map/ppermute | solution.py:772
  287.8 286.1 %reduce-scatter.5.cloned.1.call-start = ((), (), s32[]{:S(2)}) async-start(), calls=%async_computation.3 | async-start | bytes 16515072 | tf_op jit(solution)/shard_map/reduce_scatter | solution.py:781
  304.6 24.4 %collective-permute-start.19 = (bf16[4096,128]{1,0:T(8,128)(2,1)S(1)}, bf16[4096,128]{1,0:T(8,128)(2,1)S(1)}, u32[]{:S(2)}, u32[]{:S(2)}) collective-permute-start(bf16[4096,128]{1,0:T(8,128)(2,1)S(1)} %add_convert_fusion.15), channel_id=1, source_target_pairs={{1,2},{2,1},{5,6},{6,5},{9,10},{10,9},{13,14},{14,13},{17,18},{18,... | collective-permute-start | bytes 3145736 | tf_op jit(solution)/shard_map/ppermute | solution.py:769
  307.0 23.9 %collective-permute-start.18 = (bf16[4096,128]{1,0:T(8,128)(2,1)S(1)}, bf16[4096,128]{1,0:T(8,128)(2,1)S(1)}, u32[]{:S(2)}, u32[]{:S(2)}) collective-permute-start(bf16[4096,128]{1,0:T(8,128)(2,1)S(1)} %fusion), channel_id=1, source_target_pairs={{0,1},{3,2},{1,0},{2,3},{4,5},{7,6},{5,4},{6,7},{8,9},{11,10},{9,8... | collective-permute-start | bytes 3145736 | tf_op jit(solution)/shard_map/ppermute | solution.py:772
  331.3 17.8 %copy-start.18 = (bf16[4096,128]{1,0:T(8,128)(2,1)}, bf16[4096,128]{1,0:T(8,128)(2,1)S(1)}, u32[]{:S(2)}) copy-start(bf16[4096,128]{1,0:T(8,128)(2,1)S(1)} %fusion.1) | copy-start | bytes 3145732
  331.3 25.1 %collective-permute-start.21 = (bf16[4096,128]{1,0:T(8,128)(2,1)S(1)}, bf16[4096,128]{1,0:T(8,128)(2,1)}, u32[]{:S(2)}, u32[]{:S(2)}) collective-permute-start(bf16[4096,128]{1,0:T(8,128)(2,1)S(1)} %fusion.1), channel_id=1, source_target_pairs={{0,1},{3,2},{1,0},{2,3},{4,5},{7,6},{5,4},{6,7},{8,9},{11,10},{9,8... | collective-permute-start | bytes 3145736 | tf_op jit(solution)/shard_map/ppermute | solution.py:772
  332.2 24.2 %collective-permute-start.20 = (bf16[4096,128]{1,0:T(8,128)(2,1)S(1)}, bf16[4096,128]{1,0:T(8,128)(2,1)}, u32[]{:S(2)}, u32[]{:S(2)}) collective-permute-start(bf16[4096,128]{1,0:T(8,128)(2,1)S(1)} %add_convert_fusion.12), channel_id=1, source_target_pairs={{1,2},{2,1},{5,6},{6,5},{9,10},{10,9},{13,14},{14,13},{17,18},{18,... | collective-permute-start | bytes 3145736 | tf_op jit(solution)/shard_map/ppermute | solution.py:769
  358.6 19.2 %copy-start.19 = (bf16[4096,128]{1,0:T(8,128)(2,1)}, bf16[4096,128]{1,0:T(8,128)(2,1)S(1)}, u32[]{:S(2)}) copy-start(bf16[4096,128]{1,0:T(8,128)(2,1)S(1)} %fusion.2) | copy-start | bytes 3145732
  358.7 27.9 %collective-permute-start.22 = (bf16[4096,128]{1,0:T(8,128)(2,1)S(1)}, bf16[4096,128]{1,0:T(8,128)(2,1)S(1)}, u32[]{:S(2)}, u32[]{:S(2)}) collective-permute-start(bf16[4096,128]{1,0:T(8,128)(2,1)S(1)} %fusion.2), channel_id=1, source_target_pairs={{0,1},{3,2},{1,0},{2,3},{4,5},{7,6},{5,4},{6,7},{8,9},{11,10},{9,8... | collective-permute-start | bytes 3145736 | tf_op jit(solution)/shard_map/ppermute | solution.py:772
  364.2 22.3 %collective-permute-start.23 = (bf16[4096,128]{1,0:T(8,128)(2,1)S(1)}, bf16[4096,128]{1,0:T(8,128)(2,1)S(1)}, u32[]{:S(2)}, u32[]{:S(2)}) collective-permute-start(bf16[4096,128]{1,0:T(8,128)(2,1)S(1)} %add_convert_fusion.9), channel_id=1, source_target_pairs={{1,2},{2,1},{5,6},{6,5},{9,10},{10,9},{13,14},{14,13},{17,18},{18,... | collective-permute-start | bytes 3145736 | tf_op jit(solution)/shard_map/ppermute | solution.py:769
  365.0 21.5 %copy-start.9 = (bf16[16,256,128]{2,1,0:T(8,128)(2,1)S(1)}, bf16[16,256,128]{2,1,0:T(8,128)(2,1)}, u32[]{:S(2)}) copy-start(bf16[16,256,128]{2,1,0:T(8,128)(2,1)} %get-tuple-element.166) | copy-start | bytes 3145732
  388.3 8.3 %collective-permute-start.24 = (f32[4,1728]{1,0:T(4,128)S(1)}, f32[4,1728]{1,0:T(4,128)S(1)}, u32[]{:S(2)}, u32[]{:S(2)}) collective-permute-start(f32[4,1728]{1,0:T(4,128)S(1)} %slice.134), channel_id=1, source_target_pairs={{0,4},{4,0},{8,12},{12,8},{16,20},{20,16},{24,28},{28,24},{1,5},{5... | collective-permute-start | bytes 82952 | tf_op jit(solution)/shard_map/ppermute | solution.py:47
  388.8 59.9 %collective-permute-start.28 = (bf16[4096,128]{1,0:T(8,128)(2,1)S(1)}, bf16[4096,128]{1,0:T(8,128)(2,1)}, u32[]{:S(2)}, u32[]{:S(2)}) collective-permute-start(bf16[4096,128]{1,0:T(8,128)(2,1)S(1)} %add_convert_fusion.8), channel_id=1, source_target_pairs={{1,2},{2,1},{5,6},{6,5},{9,10},{10,9},{13,14},{14,13},{17,18},{18,... | collective-permute-start | bytes 3145736 | tf_op jit(solution)/shard_map/ppermute | solution.py:769
  390.6 58.1 %collective-permute-start.27 = (bf16[4096,128]{1,0:T(8,128)(2,1)}, bf16[4096,128]{1,0:T(8,128)(2,1)}, u32[]{:S(2)}, u32[]{:S(2)}) collective-permute-start(bf16[4096,128]{1,0:T(8,128)(2,1)} %fusion.3), channel_id=1, source_target_pairs={{0,1},{3,2},{1,0},{2,3},{4,5},{7,6},{5,4},{6,7},{8,9},{11,10},{9,8... | collective-permute-start | bytes 3145736 | tf_op jit(solution)/shard_map/ppermute | solution.py:772
  396.7 40.0 %collective-permute-start.25 = (f32[2,1728]{1,0:T(2,128)S(1)}, f32[2,1728]{1,0:T(2,128)S(1)}, u32[]{:S(2)}, u32[]{:S(2)}) collective-permute-start(f32[2,1728]{1,0:T(2,128)S(1)} %slice.172), channel_id=1, source_target_pairs={{0,16},{4,20},{8,24},{12,28},{16,0},{20,4},{24,8},{28,12},{1,17},{... | collective-permute-start | bytes 41480 | tf_op jit(solution)/shard_map/ppermute | solution.py:47
  436.8 11.9 %collective-permute-start.26 = (f32[1,1728]{1,0:T(1,128)S(1)}, f32[1,1728]{1,0:T(1,128)S(1)}, u32[]{:S(2)}, u32[]{:S(2)}) collective-permute-start(f32[1,1728]{1,0:T(1,128)S(1)} %slice.174), channel_id=1, source_target_pairs={{0,8},{4,12},{8,0},{12,4},{16,24},{20,28},{24,16},{28,20},{1,9},{5... | collective-permute-start | bytes 20744 | tf_op jit(solution)/shard_map/ppermute | solution.py:47
  456.7 26.0 %collective-permute-start.29 = (bf16[4096,128]{1,0:T(8,128)(2,1)}, bf16[4096,128]{1,0:T(8,128)(2,1)S(1)}, u32[]{:S(2)}, u32[]{:S(2)}) collective-permute-start(bf16[4096,128]{1,0:T(8,128)(2,1)} %add_convert_fusion.6), channel_id=1, source_target_pairs={{1,2},{2,1},{5,6},{6,5},{9,10},{10,9},{13,14},{14,13},{17,18},{18,... | collective-permute-start | bytes 3145736 | tf_op jit(solution)/shard_map/ppermute | solution.py:769
  457.5 25.3 %collective-permute-start.30 = (bf16[4096,128]{1,0:T(8,128)(2,1)}, bf16[4096,128]{1,0:T(8,128)(2,1)S(1)}, u32[]{:S(2)}, u32[]{:S(2)}) collective-permute-start(bf16[4096,128]{1,0:T(8,128)(2,1)} %fusion.4.settled), channel_id=1, source_target_pairs={{0,1},{3,2},{1,0},{2,3},{4,5},{7,6},{5,4},{6,7},{8,9},{11,10},{9,8... | collective-permute-start | bytes 3145736 | tf_op jit(solution)/shard_map/ppermute | solution.py:772
  484.4 24.3 %collective-permute-start.31 = (bf16[4112,128]{1,0:T(8,128)(2,1)S(1)}, bf16[4112,128]{1,0:T(8,128)(2,1)S(1)}, u32[]{:S(2)}, u32[]{:S(2)}) collective-permute-start(bf16[4112,128]{1,0:T(8,128)(2,1)S(1)} %pad_select_fusion.settled), channel_id=1, source_target_pairs={{0,1},{3,2},{1,0},{2,3},{4,5},{7,6},{5,4},{6,7},{8,9},{11,10},{9,8... | collective-permute-start | bytes 3158024 | tf_op jit(solution)/shard_map/ppermute | solution.py:772
  487.5 4.7 collective-permute-start.33
  492.2 16.7 %copy-start.28 = (bf16[4096,128]{1,0:T(8,128)(2,1)}, bf16[4096,128]{1,0:T(8,128)(2,1)S(1)}, u32[]{:S(2)}) copy-start(bf16[4096,128]{1,0:T(8,128)(2,1)S(1)} %collective-permute-done.33) | copy-start | bytes 3145732
  508.9 34.2 %collective-permute-start.32 = (bf16[4112,128]{1,0:T(8,128)(2,1)S(1)}, bf16[4112,128]{1,0:T(8,128)(2,1)S(1)}, u32[]{:S(2)}, u32[]{:S(2)}) collective-permute-start(bf16[4112,128]{1,0:T(8,128)(2,1)S(1)} %add_convert_fusion.1), channel_id=1, source_target_pairs={{1,2},{2,1},{5,6},{6,5},{9,10},{10,9},{13,14},{14,13},{17,18},{18,... | collective-permute-start | bytes 3158024 | tf_op jit(solution)/shard_map/ppermute | solution.py:769
  511.6 31.5 %collective-permute-start.34 = (bf16[4096,128]{1,0:T(8,128)(2,1)S(1)}, bf16[4096,128]{1,0:T(8,128)(2,1)}, u32[]{:S(2)}, u32[]{:S(2)}) collective-permute-start(bf16[4096,128]{1,0:T(8,128)(2,1)S(1)} %add_convert_fusion.2.settled), channel_id=1, source_target_pairs={{1,0},{2,3},{5,4},{6,7},{9,8},{10,11},{13,12},{14,15},{17,16},{18,... | collective-permute-start | bytes 3145736 | tf_op jit(solution)/shard_map/ppermute | solution.py:772
  544.4 24.3 %collective-permute-start.35 = (bf16[4112,128]{1,0:T(8,128)(2,1)}, bf16[4112,128]{1,0:T(8,128)(2,1)}, u32[]{:S(2)}, u32[]{:S(2)}) collective-permute-start(bf16[4112,128]{1,0:T(8,128)(2,1)} %add_convert_fusion.settled), channel_id=1, source_target_pairs={{1,0},{2,3},{5,4},{6,7},{9,8},{10,11},{13,12},{14,15},{17,16},{18,... | collective-permute-start | bytes 3158024 | tf_op jit(solution)/shard_map/ppermute | solution.py:772
  549.1 29.4 %copy-start.35 = (f32[256]{0:T(256)}, f32[256]{0:T(256)S(1)}, u32[]{:S(2)}) copy-start(f32[256]{0:T(256)S(1)} %get-tuple-element.249) | copy-start | bytes 3076
  (39 other events, 227.2 us)
Sparse Core Ops, SparseCore 0:
  105.3 87.2 all-gather.2
  288.0 106.4 reduce-scatter.2
  455.5 102.5 reduce-scatter.4

commit v2 on v1

--- a/solution.py
+++ b/solution.py
@@ -63,15 +63,15 @@
 
 
 class Spread:
-    def __init__(self, weight):
-        self.weight = weight
+    def __init__(self, weight, by_rows):
+        self.weight, self.by_rows = weight, by_rows
 
     def first(self):
         if is_cube():
             self.from_x = swap(self.weight, ALONG_X)
             self.from_y = swap(self.weight, ALONG_Y)
             return self.from_x, self.from_y
-        self.full = lax.all_gather(self.weight, "dp", axis=0, tiled=True)
+        self.full = lax.all_gather(self.weight, "dp", axis=0 if self.by_rows else 1, tiled=True)
         return (self.full,)
 
     def second(self, *seen):
@@ -90,12 +90,26 @@
         half = self.full.shape[0] // 2
         return self.full[:half], self.full[half:]
 
-
-def gather_columns(weight):
-    if is_cube():
-        return lax.all_gather(weight, "dp", axis=0)
-    full = lax.all_gather(weight, "dp", axis=1, tiled=True)
-    return full.reshape(full.shape[0], BLOCKS, -1).transpose(1, 0, 2)
+    def begin_parts(self, *seen):
+        if is_cube():
+            self.near = [swap(after(part, seen), CORE) for part in (self.weight, self.from_x, self.from_y)]
+
+    def parts(self, *seen):
+        if is_cube():
+            far = [swap(after(part, seen), CORE) for part in (self.over_x, self.over_y)]
+            return [self.weight, self.from_x, self.from_y, self.over_x, self.over_y], self.near + far
+        half = self.full.shape[0] // 2
+        return [self.full[:half]], [self.full[half:]]
+
+    def pair(self, place, seen=()):
+        if is_cube():
+            if place == 3:
+                mine = jnp.concatenate([self.over_x, self.over_y], axis=0)
+            else:
+                mine = self.weight if place == 0 else (self.from_x, self.from_y)[place - 1]
+            return mine, swap(after(mine, seen), CORE)
+        blocks = self.full.reshape(self.full.shape[0], BLOCKS, -1)
+        return blocks[:, place], blocks[:, place + HALF]
 
 
 def after(value, seen):
@@ -198,31 +212,41 @@
     )(one_a, one_b, w_a, w_b, bias, cos, sin)
 
 
-def expand_kernel(two_a, two_b, w_a, w_b, bias, active, slope):
-    rows = two_a.shape[0]
+def lay(parts, joined):
+    at = 0
+    for part in parts:
+        joined[at : at + part.shape[0], :] = part[...]
+        at += part.shape[0]
+
+
+def expand_kernel(two_a, two_b, bias, *refs):
+    *parts, active, slope, weight = refs
+    lay(parts, weight)
+    rows, half = two_a.shape
     for start in range(0, rows, 512):
         at = slice(start, start + 512)
-        hidden = mul(two_a[at], w_a[...]) + mul(two_b[at], w_b[...]) + bias[...]
+        hidden = mul(two_a[at], weight[:half]) + mul(two_b[at], weight[half:]) + bias[...]
         below = 0.5 + 0.5 * lax.erf(hidden * (0.5**0.5))
         density = jnp.exp(hidden * hidden * -0.5) * (1.0 / math.sqrt(2.0 * math.pi))
         active[at] = (hidden * below).astype(bf16)
         slope[at] = (below + hidden * density).astype(bf16)
 
 
-def expand(two_a, two_b, w_a, w_b, bias, tile=512):
+def expand(two_a, two_b, parts, bias, tile=512):
     rows, half = two_a.shape
-    width = w_a.shape[1]
+    width = parts[0].shape[1]
     column = lambda r: pl.BlockSpec((r, tile), lambda n: (0, n))
     return pl.pallas_call(
         expand_kernel,
         grid=(width // tile,),
-        in_specs=[whole_spec(two_a), whole_spec(two_b), column(half), column(half), column(1)],
+        in_specs=[whole_spec(two_a), whole_spec(two_b), column(1)] + [column(part.shape[0]) for part in parts],
         out_specs=[column(rows), column(rows)],
         out_shape=[jax.ShapeDtypeStruct((rows, width), bf16)] * 2,
-        compiler_params=params(),
-        cost_estimate=cost(4 * rows * half * width, 22_000_000, 2 * rows * width),
+        scratch_shapes=[pltpu.VMEM((2 * half, tile), bf16)],
+        compiler_params=params(),
+        cost_estimate=cost(0, 0),
         name="expand",
-    )(two_a, two_b, w_a, w_b, bias)
+    )(two_a, two_b, bias, *parts)
 
 
 def branch_kernel(attended, active, mine, theirs, out):
@@ -251,30 +275,9 @@
     )(attended, active, mine, theirs)
 
 
-def branch_place(places, attended, active, weight, place, tile=512):
-    rows = attended.shape[0]
-    depth = weight.shape[1]
-    slabs = 2 * BLOCK // 128
-    row = lambda a: pl.BlockSpec((tile, a.shape[1]), lambda i, *_: (i, 0))
-    block = lambda p: pl.BlockSpec((None, depth, BLOCK), lambda i, w: (w[p], 0, 0))
-    return pl.pallas_call(
-        lambda _, *refs: branch_kernel(*refs),
-        grid_spec=pltpu.PrefetchScalarGridSpec(
-            num_scalar_prefetch=1,
-            grid=(rows // tile,),
-            in_specs=[row(attended), row(active), block(place), block(place + HALF)],
-            out_specs=pl.BlockSpec((slabs, tile, 128), lambda i, *_: (0, i, 0)),
-        ),
-        out_shape=jax.ShapeDtypeStruct((slabs, rows, 128), bf16),
-        compiler_params=params(),
-        cost_estimate=cost(4 * rows * depth * BLOCK, 2 * (rows * depth + 2 * (rows + depth) * BLOCK)),
-        name="branch",
-    )(places, attended, active, weight, weight)
-
-
-def back_kernel(places, up_a, up_b, blocks, slope, out, sums, joined):
+def back_kernel(up_a, up_b, blocks, slope, out, sums, joined):
     for place in range(BLOCKS):
-        joined[:, place * BLOCK : (place + 1) * BLOCK] = blocks[places[place]]
+        joined[:, place * BLOCK : (place + 1) * BLOCK] = blocks[place][...]
     half = HALF * BLOCK
     total = jnp.zeros((1, out.shape[1]), f32)
     for start in range(0, out.shape[0], 512):
@@ -290,66 +293,65 @@
         sums[...] = total
 
 
-def back(places, up_a, up_b, blocks, start, width, slope=None, tile=512):
+def back(up_a, up_b, blocks, start, width, slope=None, tile=512):
     rows, half = up_a.shape
-    weight = pl.BlockSpec((BLOCKS, tile, BLOCK), lambda n, *_: (0, n + start // tile, 0))
-    column = lambda r: pl.BlockSpec((r, tile), lambda n, *_: (0, n))
+    weight = pl.BlockSpec((tile, BLOCK), lambda n: (n + start // tile, 0))
+    column = lambda r: pl.BlockSpec((r, tile), lambda n: (0, n))
     scaled = slope is not None
 
-    def body(w, a, b, c, *rest):
+    def body(a, b, *rest):
+        blocks, rest = rest[:BLOCKS], rest[BLOCKS:]
         if scaled:
             s, out, sums, joined = rest
         else:
             (out, joined), s, sums = rest, None, None
-        back_kernel(w, a, b, c, s, out, sums, joined)
+        back_kernel(a, b, blocks, s, out, sums, joined)
 
     out = jax.ShapeDtypeStruct((rows, width), bf16)
     return pl.pallas_call(
         body,
-        grid_spec=pltpu.PrefetchScalarGridSpec(
-            num_scalar_prefetch=1,
-            grid=(width // tile,),
-            in_specs=[whole_spec(up_a), whole_spec(up_b), weight] + [column(rows)] * scaled,
-            out_specs=[column(rows), column(1)] if scaled else column(rows),
-            scratch_shapes=[pltpu.VMEM((tile, 2 * half), bf16)],
-        ),
+        grid=(width // tile,),
+        in_specs=[whole_spec(up_a), whole_spec(up_b)] + [weight] * BLOCKS + [column(rows)] * scaled,
+        out_specs=[column(rows), column(1)] if scaled else column(rows),
         out_shape=[out, jax.ShapeDtypeStruct((1, width), f32)] if scaled else out,
+        scratch_shapes=[pltpu.VMEM((tile, 2 * half), bf16)],
         compiler_params=params(),
         cost_estimate=cost(4 * rows * half * width, 4 * rows * half + 4 * half * width + 4 * rows * width),
         name="back",
-    )(places, up_a, up_b, blocks, *([slope] if scaled else []))
-
-
-def second_kernel(grad, w_a, w_b, out):
-    step = pl.program_id(0)
-
-    @pl.when(step < 2)
-    def _():
-        out[...] = mul(grad[...], w_a[...], NT).astype(bf16)
-
-    @pl.when(step >= 2)
-    def _():
-        out[...] = mul(grad[...], w_b[...], NT).astype(bf16)
-
-
-def second_back(grad, w_a, w_b):
+    )(up_a, up_b, *blocks, *([slope] if scaled else []))
+
+
+def second_kernel(grad, *refs):
+    *parts, out, weight = refs
+    tile = weight.shape[0]
+    taken, size = [[]], 0
+    for part in parts:
+        for start in range(0, part.shape[0], tile):
+            if size == tile:
+                taken.append([])
+                size = 0
+            rows = min(tile, part.shape[0] - start)
+            taken[-1].append(part.at[start : start + rows])
+            size += rows
+    for number, runs in enumerate(taken):
+        pl.when(pl.program_id(0) == number)(functools.partial(lay, runs, weight))
+    out[...] = mul(grad[...], weight[...], NT).astype(bf16)
+
+
+def second_back(grad, parts, tile=512):
     rows, width = grad.shape
-    half = w_a.shape[0]
-    tile = half // 2
+    depth = sum(part.shape[0] for part in parts)
     return pl.pallas_call(
         second_kernel,
-        grid=(4,),
-        in_specs=[
-            whole_spec(grad),
-            pl.BlockSpec((tile, width), lambda n: (jnp.minimum(n, 1), 0)),
-            pl.BlockSpec((tile, width), lambda n: (jnp.maximum(n - 2, 0), 0)),
-        ],
+        grid=(depth // tile,),
+        in_specs=[whole_spec(grad)] + [whole_spec(part) for part in parts],
         out_specs=pl.BlockSpec((rows, tile), lambda n: (0, n)),
-        out_shape=jax.ShapeDtypeStruct((rows, 2 * half), bf16),
-        compiler_params=params(),
-        cost_estimate=cost(4 * rows * half * width, 2 * rows * width + 4 * half * width + 4 * rows * half),
+        out_shape=jax.ShapeDtypeStruct((rows, depth), bf16),
+        scratch_shapes=[pltpu.VMEM((tile, width), bf16)],
+        compiler_params=params(),
+        cost_estimate=cost(2 * rows * depth * width, 2 * (rows + depth) * width + 2 * rows * depth),
         name="second_back",
-    )(grad, w_a, w_b)
+    )(grad, *parts)
 
 
 def row_grad_kernel(where, left_a, left_b, right, *rest):
@@ -381,99 +383,105 @@
     )(where, left_a, left_b, right, *extra)
 
 
-def column_grad_kernel(where, first, second, right_a, right_b, out):
-    def store(left):
-        for number, right in enumerate((right_a, right_b)):
-            full = mul(left[...], right[...], TN)
-            for place in range(HALF):
-                out[where[number * HALF + place]] = full[:, place * BLOCK : (place + 1) * BLOCK].astype(bf16)
-
-    ahead = first.shape[1] // out.shape[1]
-    assert ahead == 1
-    pl.when(pl.program_id(0) == 0)(lambda: store(first))
-    pl.when(pl.program_id(0) > 0)(lambda: store(second))
-
-
-def column_grad(where, first, second, right_a, right_b, tile=512):
-    rows = first.shape[0]
-    width = first.shape[1] + second.shape[1]
+def column_grad_kernel(where, left, right_a, right_b, *rest):
+    out = rest[-1]
+    for number, right in enumerate((right_a, right_b)):
+        full = mul(left[...], right[...], TN)
+        for place in range(HALF):
+            out[where[number * HALF + place]] = full[:, place * BLOCK : (place + 1) * BLOCK].astype(bf16)
+
+
+def column_grad(where, left, right_a, right_b, total, start=0, into=None, tile=512):
+    rows, width = left.shape
     blocks = 2 * HALF
+    extra = [] if into is None else [into]
     return pl.pallas_call(
         column_grad_kernel,
         grid_spec=pltpu.PrefetchScalarGridSpec(
             num_scalar_prefetch=1,
             grid=(width // tile,),
-            in_specs=[
-                pl.BlockSpec((rows, tile), lambda n, *_: (0, 0)),
-                pl.BlockSpec((rows, tile), lambda n, *_: (0, jnp.maximum(n - 1, 0))),
-                whole_spec(right_a),
-                whole_spec(right_b),
-            ],
-            out_specs=pl.BlockSpec((blocks, tile, BLOCK), lambda n, *_: (0, n, 0)),
+            in_specs=[pl.BlockSpec((rows, tile), lambda n, *_: (0, n)), whole_spec(right_a), whole_spec(right_b)]
+            + [pl.BlockSpec(memory_space=pl.ANY)] * len(extra),
+            out_specs=pl.BlockSpec((blocks, tile, BLOCK), lambda n, *_: (0, n + start // tile, 0)),
         ),
-        out_shape=jax.ShapeDtypeStruct((blocks, width, BLOCK), bf16),
-        compiler_params=params(),
-        cost_estimate=cost(2 * rows * blocks * BLOCK * width, 2 * blocks * BLOCK * (rows + width) + 2 * rows * width),
+        out_shape=jax.ShapeDtypeStruct((blocks, total, BLOCK), bf16),
+        input_output_aliases={4: 0} if extra else {},
+        compiler_params=params(),
+        cost_estimate=cost(0, 0),
         name="column_grad",
-    )(where, first, second, right_a, right_b)
+    )(where, left, right_a, right_b, *extra)
+
+
+def fill(refs, heads, place):
+    for head in range(heads):
+        at = 0
+        for ref in refs:
+            for start in range(0, ref.shape[0], 512):
+                rows = slice(start, start + 512)
+                place(head, at, ref[rows, 2 * head * HD : (2 * head + 1) * HD], ref[rows, (2 * head + 1) * HD : (2 * head + 2) * HD])
+                at += 512
 
 
 def attend_kernel(first, last, q, left, own, right, low, high, out, lse, keys, values_turned, *, wide):
-    step = pl.program_id(1)
+    step = pl.program_id(0)
     tall = q.shape[0]
+    heads = range(keys.shape[0])
 
     @pl.when(step == 0)
     def _():
-        at = 0
-        for ref in (left, own, right):
-            count = ref.shape[0]
-            keys[at : at + count, :] = ref[:, :HD]
-            for r in range(0, count, 512):
-                values_turned[:, at + r : at + r + 512] = jnp.transpose(ref[r : r + 512, HD:])
-            at += count
-
-    scaled = q[...] * jnp.asarray(HD**-0.5, bf16)
+        def place(head, at, k, v):
+            keys[head, at : at + 512, :] = k
+            values_turned[head, :, at : at + 512] = jnp.transpose(v)
+
+        fill((left, own, right), len(heads), place)
+
+    scaled = [q[:, h * HD : (h + 1) * HD] * jnp.asarray(HD**-0.5, bf16) for h in heads]
     low_row = low[...]
     high_row = high[...]
 
     def block(j, carry):
-        top, total, acc = carry
         rows = pl.ds(pl.multiple_of(j * wide, wide), wide)
-        scores = mul(keys[rows, :], scaled, NT)
         key = j * wide + lax.broadcasted_iota(jnp.int32, (wide, tall), 0)
-        scores = jnp.where((key >= low_row) & (key <= high_row), scores, MASKED)
-        new = jnp.maximum(top, jnp.max(scores, axis=0, keepdims=True))
-        weights = jnp.exp(scores - new)
-        fade = jnp.exp(top - new)
-        total = total * fade + jnp.sum(weights, axis=0, keepdims=True)
-        acc = acc * fade + mul(values_turned[:, rows], weights.astype(bf16))
-        return new, total, acc
+        seen = (key >= low_row) & (key <= high_row)
+        scores = [mul(keys[h, rows, :], scaled[h], NT) for h in heads]
+        after_block = []
+        for h in heads:
+            top, total, acc = carry[h]
+            masked = jnp.where(seen, scores[h], MASKED)
+            new = jnp.maximum(top, jnp.max(masked, axis=0, keepdims=True))
+            weights = jnp.exp(masked - new)
+            fade = jnp.exp(top - new)
+            total = total * fade + jnp.sum(weights, axis=0, keepdims=True)
+            acc = acc * fade + mul(values_turned[h, :, rows], weights.astype(bf16))
+            after_block.append((new, total, acc))
+        return tuple(after_block)
 
     start = (jnp.full((1, tall), MASKED, f32), jnp.zeros((1, tall), f32), jnp.zeros((HD, tall), f32))
-    top, total, acc = lax.fori_loop(first[step], last[step] + 1, block, start)
-    out[...] = jnp.transpose(acc / total).astype(bf16)
-    lse[0] = top + jnp.log(total)
+    done = lax.fori_loop(first[step], last[step] + 1, block, tuple(start for _ in heads))
+    for h in heads:
+        top, total, acc = done[h]
+        out[:, h * HD : (h + 1) * HD] = jnp.transpose(acc / total).astype(bf16)
+        lse[h] = top + jnp.log(total)
 
 
 def key_blocks(low, high, tall, wide):
     return jnp.min(low.reshape(-1, tall), axis=1) // wide, jnp.max(high.reshape(-1, tall), axis=1) // wide
 
 
-def attend(q, left, own, right, low, high, tall=512, wide=512):
+def attend(q, left, own, right, low, high, tall=256, wide=512):
     rows, width = q.shape
     heads = width // HD
     extent = left.shape[0] + rows + right.shape[0]
-    pair = lambda a: pl.BlockSpec((a.shape[0], 2 * HD), lambda h, i, *_: (0, h))
-    row = pl.BlockSpec((1, tall), lambda h, i, *_: (0, i))
-    mine = pl.BlockSpec((tall, HD), lambda h, i, *_: (i, h))
+    row = pl.BlockSpec((1, tall), lambda i, *_: (0, i))
+    mine = pl.BlockSpec((tall, width), lambda i, *_: (i, 0))
     return pl.pallas_call(
         functools.partial(attend_kernel, wide=wide),
         grid_spec=pltpu.PrefetchScalarGridSpec(
             num_scalar_prefetch=2,
-            grid=(heads, rows // tall),
-            in_specs=[mine, pair(left), pair(own), pair(right), row, row],
-            out_specs=[mine, pl.BlockSpec((1, 1, tall), lambda h, i, *_: (h, 0, i))],
-            scratch_shapes=[pltpu.VMEM((extent, HD), bf16), pltpu.VMEM((HD, extent), bf16)],
+            grid=(rows // tall,),
+            in_specs=[mine, whole_spec(left), whole_spec(own), whole_spec(right), row, row],
+            out_specs=[mine, pl.BlockSpec((heads, 1, tall), lambda i, *_: (0, 0, i))],
+            scratch_shapes=[pltpu.VMEM((heads, extent, HD), bf16), pltpu.VMEM((heads, HD, extent), bf16)],
         ),
         out_shape=[jax.ShapeDtypeStruct((rows, width), bf16), jax.ShapeDtypeStruct((heads, 1, rows), f32)],
         compiler_params=params(),
@@ -486,79 +494,85 @@
     first, last, q, left, own, right, low, high, lse, attended, grad, cos, sin,
     dq, dleft, down, dright, keys, values, keys_turned, dk, dv, *, wide,
 ):
-    step = pl.program_id(1)
+    step = pl.program_id(0)
     tall = q.shape[0]
+    heads = range(keys.shape[0])
 
     @pl.when(step == 0)
     def _():
-        at = 0
-        for ref in (left, own, right):
-            count = ref.shape[0]
-            keys[at : at + count, :] = ref[:, :HD]
-            values[at : at + count, :] = ref[:, HD:]
-            for r in range(0, count, 512):
-                keys_turned[:, at + r : at + r + 512] = jnp.transpose(ref[r : r + 512, :HD])
-            at += count
+        def place(head, at, k, v):
+            keys[head, at : at + 512, :] = k
+            values[head, at : at + 512, :] = v
+            keys_turned[head, :, at : at + 512] = jnp.transpose(k)
+
+        fill((left, own, right), len(heads), place)
         dk[...] = jnp.zeros_like(dk)
         dv[...] = jnp.zeros_like(dv)
 
-    scaled = q[...] * jnp.asarray(HD**-0.5, bf16)
+    cut = lambda ref, h: ref[:, h * HD : (h + 1) * HD]
+    scaled = [cut(q, h) * jnp.asarray(HD**-0.5, bf16) for h in heads]
+    given = [cut(grad, h) for h in heads]
     low_row = low[...]
     high_row = high[...]
-    log_total = lse[0]
-    given = grad[...]
-    delta = jnp.sum(jnp.transpose(given.astype(f32) * attended[...].astype(f32)), axis=0, keepdims=True)
-
-    def block(j, acc):
+    deltas = [
+        jnp.sum(jnp.transpose(given[h].astype(f32) * cut(attended, h).astype(f32)), axis=0, keepdims=True) for h in heads
+    ]
+
+    def block(j, accs):
         rows = pl.ds(pl.multiple_of(j * wide, wide), wide)
-        scores = mul(keys[rows, :], scaled, NT)
-        grad_probs = mul(values[rows, :], given, NT)
         key = j * wide + lax.broadcasted_iota(jnp.int32, (wide, tall), 0)
-        probs = jnp.exp(jnp.where((key >= low_row) & (key <= high_row), scores - log_total, MASKED))
-        grad_scores = (probs * (grad_probs - delta)).astype(bf16)
-        dv[rows, :] += mul(probs.astype(bf16), given)
-        dk[rows, :] += mul(grad_scores, scaled)
-        return acc + mul(keys_turned[:, rows], grad_scores)
-
-    acc = lax.fori_loop(first[step], last[step] + 1, block, jnp.zeros((HD, tall), f32))
-    full = jnp.transpose(acc) * (HD**-0.5)
-    dq[:, :128] = turn(full[:, :128], cos[...], sin[...], -1).astype(bf16)
-    dq[:, 128:] = full[:, 128:].astype(bf16)
-
-    @pl.when(step == pl.num_programs(1) - 1)
+        seen = (key >= low_row) & (key <= high_row)
+        scores = [mul(keys[h, rows, :], scaled[h], NT) for h in heads]
+        grad_probs = [mul(values[h, rows, :], given[h], NT) for h in heads]
+        after_block = []
+        for h in heads:
+            probs = jnp.exp(jnp.where(seen, scores[h] - lse[h], MASKED))
+            grad_scores = (probs * (grad_probs[h] - deltas[h])).astype(bf16)
+            dv[h, rows, :] += mul(probs.astype(bf16), given[h])
+            dk[h, rows, :] += mul(grad_scores, scaled[h])
+            after_block.append(accs[h] + mul(keys_turned[h, :, rows], grad_scores))
+        return tuple(after_block)
+
+    accs = lax.fori_loop(first[step], last[step] + 1, block, tuple(jnp.zeros((HD, tall), f32) for _ in heads))
+    for h in heads:
+        full = jnp.transpose(accs[h]) * (HD**-0.5)
+        dq[:, h * HD : h * HD + 128] = turn(full[:, :128], cos[...], sin[...], -1).astype(bf16)
+        dq[:, h * HD + 128 : (h + 1) * HD] = full[:, 128:].astype(bf16)
+
+    @pl.when(step == pl.num_programs(0) - 1)
     def _():
-        at = 0
-        for ref in (dleft, down, dright):
-            count = ref.shape[0]
-            ref[:, :HD] = dk[at : at + count, :].astype(ref.dtype)
-            ref[:, HD:] = dv[at : at + count, :].astype(ref.dtype)
-            at += count
-
-
-def attend_back(q, left, own, right, low, high, lse, attended, grad, cos, sin, tall=512, wide=512):
+        for h in heads:
+            at = 0
+            for ref in (dleft, down, dright):
+                count = ref.shape[0]
+                ref[:, 2 * h * HD : (2 * h + 1) * HD] = dk[h, at : at + count, :].astype(ref.dtype)
+                ref[:, (2 * h + 1) * HD : (2 * h + 2) * HD] = dv[h, at : at + count, :].astype(ref.dtype)
+                at += count
+
+
+def attend_back(q, left, own, right, low, high, lse, attended, grad, cos, sin, tall=256, wide=512):
     rows, width = q.shape
     heads = width // HD
     extent = left.shape[0] + rows + right.shape[0]
-    pair = lambda a: pl.BlockSpec((a.shape[0], 2 * HD), lambda h, i, *_: (0, h))
-    row = pl.BlockSpec((1, tall), lambda h, i, *_: (0, i))
-    mine = pl.BlockSpec((tall, HD), lambda h, i, *_: (i, h))
-    table = pl.BlockSpec((tall, 128), lambda h, i, *_: (i, 0))
+    row = pl.BlockSpec((1, tall), lambda i, *_: (0, i))
+    mine = pl.BlockSpec((tall, width), lambda i, *_: (i, 0))
+    table = pl.BlockSpec((tall, 128), lambda i, *_: (i, 0))
     return pl.pallas_call(
         functools.partial(attend_back_kernel, wide=wide),
         grid_spec=pltpu.PrefetchScalarGridSpec(
             num_scalar_prefetch=2,
-            grid=(heads, rows // tall),
+            grid=(rows // tall,),
             in_specs=[
-                mine, pair(left), pair(own), pair(right), row, row,
-                pl.BlockSpec((1, 1, tall), lambda h, i, *_: (h, 0, i)), mine, mine, table, table,
+                mine, whole_spec(left), whole_spec(own), whole_spec(right), row, row,
+                pl.BlockSpec((heads, 1, tall), lambda i, *_: (0, 0, i)), mine, mine, table, table,
             ],
-            out_specs=[mine, pair(left), pair(own), pair(right)],
+            out_specs=[mine, whole_spec(left), whole_spec(own), whole_spec(right)],
             scratch_shapes=[
-                pltpu.VMEM((extent, HD), bf16),
-                pltpu.VMEM((extent, HD), bf16),
-                pltpu.VMEM((HD, extent), bf16),
-                pltpu.VMEM((extent, HD), f32),
-                pltpu.VMEM((extent, HD), f32),
+                pltpu.VMEM((heads, extent, HD), bf16),
+                pltpu.VMEM((heads, extent, HD), bf16),
+                pltpu.VMEM((heads, HD, extent), bf16),
+                pltpu.VMEM((heads, extent, HD), f32),
+                pltpu.VMEM((heads, extent, HD), f32),
             ],
         ),
         out_shape=[
@@ -693,7 +707,7 @@
         ),
         out_shape=jax.ShapeDtypeStruct((rows, width), bf16),
         compiler_params=params(),
-        cost_estimate=cost(10_000_000, 17_000_000),
+        cost_estimate=cost(36_000_000_000, 17_000_000),
         name="output_sum",
     )(places, middle, tokens, bias, *map(view, settled), *map(view, passed))
 
@@ -726,7 +740,7 @@
         out_shape=jax.ShapeDtypeStruct((rows, width), bf16),
         input_output_aliases={5: 0} if number else {},
         compiler_params=params(),
-        cost_estimate=cost(2_000_000, 4_000_000),
+        cost_estimate=cost(36_000_000_000, 4_000_000),
         name="tokens_sum",
     )(places, middle, upstream, settled, passed, *extra)
 
@@ -852,7 +866,8 @@
         full_expand_bias = small[:, at:split].reshape((count,) + expand_bias.shape).transpose(1, 0, 2).reshape(1, -1)
         full_project_bias = small[:, split : split + project_bias.size].reshape((count,) + project_bias.shape).transpose(1, 0, 2).reshape(1, -1)
     else:
-        rows_of = lax.all_gather(jnp.stack(vectors).astype(bf16), "dp", axis=1, tiled=True).astype(f32)
+        gathered = lax.all_gather(jnp.stack(vectors).astype(bf16), "dp", axis=1, tiled=True)
+        rows_of = gathered.astype(f32)
         full_expand_bias = lax.all_gather(expand_bias.astype(bf16), "dp", axis=1, tiled=True).astype(f32).reshape(1, -1)
         full_project_bias = lax.all_gather(project_bias.astype(bf16), "dp", axis=1, tiled=True).astype(f32).reshape(1, -1)
     gains = jnp.concatenate([rows_of[:4], jnp.zeros((4, width), f32)], axis=0)
@@ -879,34 +894,43 @@
     high = jnp.maximum(token_index, begin + limit - 1) - base
     cos, sin = rotary_tables(token_index - begin)
 
-    tok, one_a, one_b, two_a, two_b, up_a, up_b, mean, inverse, grad_bias = norm(places, tokens, upstream, gains)
-
-    spread_expand = Spread(expand_weight.astype(bf16))
-    spread_project = Spread(project_weight.astype(bf16))
+    spread_project = Spread(project_weight.astype(bf16), True)
+    seen_project = spread_project.first()
+    seen_project_too = spread_project.second(seen_project, gathered)
+    spread_expand = Spread(after(expand_weight.astype(bf16), (gathered, seen_project)), True)
     seen_expand = spread_expand.first()
-    seen_project = spread_project.first()
-    seen_expand_too = spread_expand.second(seen_expand, mean)
-    seen_project_too = spread_project.second(seen_project, mean)
+    project_a, project_b = spread_project.join(seen_project_too)
+    tok, one_a, one_b, two_a, two_b, up_a, up_b, mean, inverse, grad_bias = norm(
+        places, tokens, upstream, after(gains, project_a)
+    )
+    seen_expand_too = spread_expand.second(seen_expand, project_a)
+    queries, pairs = project(after(one_a, seen_expand), one_b, project_a, project_b, full_project_bias, cos, sin)
+    sent = after(pairs, seen_expand_too)
+    left = ring(sent, 1)
+    right = ring(sent[:PREFIX_MAX], -1)
+    spread_expand.begin_parts(seen_expand_too)
+    expand_mine, expand_theirs = spread_expand.parts(pairs)
     down_weight = jnp.concatenate([dense_weight.astype(bf16), shrink_weight.astype(bf16)], axis=0)
-    down_weight = after(down_weight, (mean, seen_expand, seen_project))
-    project_a, project_b = spread_project.join(seen_project_too, down_weight)
-    expand_a, expand_b = spread_expand.join(seen_expand_too, project_a)
-    down_blocks = gather_columns(after(down_weight, (project_a, expand_a)))
-    queries, pairs = project(after(one_a, expand_a), one_b, project_a, project_b, full_project_bias, cos, sin)
-    left = ring(pairs, 1)
-    right = ring(pairs[:PREFIX_MAX], -1)
-    if cube:
-        own_blocks = (down_weight, swap(after(down_weight, seen_expand_too), CORE))
-    else:
-        own_blocks = (down_blocks[0], down_blocks[HALF])
-    active, slope = expand(after(two_a, (pairs, own_blocks)), two_b, expand_a, expand_b, full_expand_bias)
-    attended, lse = attend(after(queries, active), left, pairs, right, low, high)
+    spread_down = Spread(after(down_weight, (mean, seen_project)), False)
+    active, slope = expand(after(two_a, sent), two_b, expand_mine + expand_theirs, full_expand_bias)
+    depth = turned_width + hidden_width
+    column_blocks = column_grad(places, active, up_a, up_b, depth, turned_width)
+    blocks = [spread_down.pair(0, active)] if cube else []
+    spread_down.weight = after(spread_down.weight, (left, active))
+    seen_down = spread_down.first()
+    if not cube:
+        blocks = [spread_down.pair(0)]
+    attended, lse = attend(after(queries, column_blocks), left, pairs, right, low, high)
 
     line = LineSum(middle)
-    pieces = [branch_piece(attended, active, *own_blocks)]
+    seen_down_too = spread_down.second(seen_down, attended)
+    blocks += [spread_down.pair(place, (attended, seen_down)) for place in range(len(blocks), HALF - 1)]
+    pieces = [branch_piece(attended, active, *blocks[0])]
     seen = line.slot(pieces[0], ())
-    column_blocks = column_grad(places, after(attended, (pieces[0], seen)), active, up_a, up_b)
-    grad_attended = back(places, after(up_a, column_blocks), up_b, down_blocks, 0, turned_width)
+    column_blocks = column_grad(places, after(attended, (pieces[0], seen)), up_a, up_b, depth, 0, column_blocks)
+    blocks.append(spread_down.pair(3, (column_blocks, seen_down_too)))
+    down_blocks = [b for b, _ in blocks] + [b for _, b in blocks]
+    grad_attended = back(after(up_a, column_blocks), up_b, down_blocks, 0, turned_width)
     dq, dleft, down, dright = attend_back(
         queries, left, pairs, right, low, high, lse, attended, grad_attended, cos, sin
     )
@@ -914,18 +938,18 @@
     earlier = ring(dright, 1)
     last = dq
     for place in (1, 2, 3):
-        pieces.append(branch_place(places, after(attended, last), active, down_blocks, place))
+        pieces.append(branch_piece(after(attended, last), active, *blocks[place]))
         last = pieces[-1]
         if place == 1:
             seen = line.slot(pieces[1], last)
-            last = (last, seen, earlier)
-    column_blocks, later, earlier, last = lax.optimization_barrier((column_blocks, later, earlier, last))
+            last = (last, seen)
+    grad_hidden, expand_bias_sums = back(
+        after(up_a, pieces[-1]), up_b, down_blocks, turned_width, hidden_width, slope
+    )
+    column_blocks, later, earlier, grad_hidden = lax.optimization_barrier((column_blocks, later, earlier, grad_hidden))
     grad_down = scatter_blocks(column_blocks, False)
-    grad_hidden, expand_bias_sums = back(
-        places, after(up_a, last), up_b, down_blocks, turned_width, hidden_width, slope
-    )
     seen = line.slot(pieces[2], grad_hidden)
-    grad_second = second_back(after(grad_hidden, seen), expand_a, expand_b)
+    grad_second = second_back(after(grad_hidden, seen), expand_mine + expand_theirs)
     grad_mixed, project_bias_sums = mix(after(dq, grad_second), down, later, earlier, cos, sin)
     seen = line.slot(pieces[3], grad_mixed)
     *tails, sums = input_back(
@@ -938,15 +962,16 @@
     tails += more
     sums = sums + part
     seen = line.slot(tails[1], part)
+    widths = grad_hidden.shape[1], grad_mixed.shape[1]
+    row_blocks = row_grad(places, two_a, two_b, after(grad_hidden, seen), sum(widths))
     vector = part
     if cube:
         vector = after(vector_parts(sums, grad_bias, expand_bias_sums, project_bias_sums), seen)
-        vector = halved(halved(halved(vector, CORE), ALONG_Y), ALONG_X)[0]
-    widths = grad_hidden.shape[1], grad_mixed.shape[1]
-    row_blocks = row_grad(places, two_a, two_b, after(grad_hidden, seen), sum(widths))
-    row_blocks = row_grad(places, one_a, one_b, grad_mixed, sum(widths), widths[0], row_blocks)
+        vector = halved(halved(vector, CORE), ALONG_Y)
+        vector = halved(after(vector, row_blocks), ALONG_X)[0]
     seen = line.slot(tails[2], row_blocks)
-    row_blocks, grad_down, vector, seen = lax.optimization_barrier((row_blocks, grad_down, vector, seen))
+    row_blocks = row_grad(places, one_a, one_b, after(grad_mixed, seen), sum(widths), widths[0], row_blocks)
+    row_blocks, grad_down, vector = lax.optimization_barrier((row_blocks, grad_down, vector))
     if cube:
         grad_rows = scatter_blocks(row_blocks, True)
         grad_expand, grad_project = grad_rows[:, : widths[0]], grad_rows[:, widths[0] :]

time: 595 us -> 534 us (0.90)
  starting transfers between devices: 115 us -> 82.3 us
  blocking collectives: 41.4 us -> 18.7 us
  local copies, waits for them, and re-layouts: 35.9 us -> 29.9 us
    ppermute x4, starting transfers between devices: 44.4 us -> 10.1 us  [ring(): return lax.ppermute(value, 'dp', pairs)]
    all_gather x1, blocking collectives: 41.4 us -> 18.7 us  [on_device(): gathered = lax.all_gather(own, 'dp', axis=0).reshape(count, -1)]
    pallas_call x1 -> x4, Pallas kernels: 6.4 us -> 25.6 us  [branch_piece(): pl.pallas_call(branch_kernel, grid=(rows // tile,), in_specs=[row(attende...]
    pallas_call x6 -> x3, Pallas kernels: 57.2 us -> 38.8 us  [the longest x2 20.6 us: back(): pl.pallas_call(body, grid=(width // tile,), in_specs=[whole_spec(up_a), w...]
    ppermute x10, waiting for transfers between devices: 84.3 us -> 68.6 us  [slot(): self.inward = lax.ppermute(operand, 'tensor', pairs)]
    ppermute x14 -> x25, waiting for transfers between devices: 15.3 us -> 23 us  [swap(): return lax.ppermute(value, 'dp', [(i, i ^ bit) for i in range(count)])]
    ppermute x14 -> x25, starting transfers between devices: 36.4 us -> 32.2 us  [swap(): return lax.ppermute(value, 'dp', [(i, i ^ bit) for i in range(count)])]
    pallas_call x1 -> x2, Pallas kernels: 17.4 us -> 21.5 us  [column_grad(): pl.pallas_call(column_grad_kernel, grid_spec=pltpu.PrefetchScalarGridSpec...]
  transfers between devices with their start and end apart: 39 -> 49, of which waited for: 12 -> 15; matrix products, arithmetic and copies ran while one was open for 10% -> 11% of each run, Pallas kernels for 41% -> 46%
where the time goes in v2:
time: 534 us; the launch traced here: 526 us
  Pallas kernels  241 us (45%)
  waiting for transfers between devices  95.4 us (18%)
  starting transfers between devices  82.3 us (15%)
  other arithmetic  43 us (8%)
  local copies, waits for them, and re-layouts  29.9 us (6%)
  blocking collectives  18.7 us (4%)
  between operations  15.7 us (3%)
    ppermute x10, waiting for transfers between devices, slot(): self.inward = lax.ppermute(operand, 'tensor', pairs)  68.6 us
    ppermute x25, starting transfers between devices, swap(): return lax.ppermute(value, 'dp', [(i, i ^ bit) for i in range(count)])  32.2 us
    ppermute x10, starting transfers between devices, slot(): self.inward = lax.ppermute(operand, 'tensor', pairs)  29.8 us
    pallas_call x2, Pallas kernels, row_grad(): pl.pallas_call(row_grad_kernel, grid_spec=pltpu.PrefetchScalarGridSpec(nu...  26 us
    pallas_call x2, Pallas kernels, input_back(): pl.pallas_call(input_kernel, grid=(2,), in_specs=[row(depth), whole_spec(...  25.7 us
    pallas_call x4, Pallas kernels, branch_piece(): pl.pallas_call(branch_kernel, grid=(rows // tile,), in_specs=[row(attende...  25.6 us
    ppermute x25, waiting for transfers between devices, swap(): return lax.ppermute(value, 'dp', [(i, i ^ bit) for i in range(count)])  23 us
    pallas_call x2, Pallas kernels, column_grad(): pl.pallas_call(column_grad_kernel, grid_spec=pltpu.PrefetchScalarGridSpec...  21.5 us
  transfers between devices with their start and end apart: 49, of which 15 were waited for; matrix products, arithmetic and copies ran while one was open for 11% of the time, Pallas kernels for 46%

profile of v2, /device:TPU:0, one launch (start us, length us, event | category | flops | bytes accessed | tf_op | source)
XLA Modules:
  0.0 525.6 jit_solution(11852708261838119334)
XLA Ops:
  8.8 3.0 collective-permute-start
  15.2 18.7 %all_gather.3 = bf16[8,16,128]{2,1,0:T(8,128)(2,1)S(1)} all-gather(bf16[1,16,128]{2,1,0:T(8,128)(2,1)S(1)} %pad_bitcast_fusion), channel_id=1, replica_groups=mesh['dp'=8,'tensor'=4] {'dp'}, dimensions={0}, use_global_device_ids=true | all-gather | bytes 36864 | tf_op jit(solution)/shard_map/all_gather | solution.py:859
  37.3 8.1 %collective-permute-done.2 = bf16[128,1536]{1,0:T(8,128)(2,1)S(1)} collective-permute-done((bf16[128,1536]{1,0:T(8,128)(2,1)S(1)}, bf16[128,1536]{1,0:T(8,128)(2,1)S(1)}, u32[]{:S(2)}, u32[]{:S(2)}) %collective-permute-start.2) | collective-permute-done | bytes 393248 | tf_op jit(solution)/shard_map/ppermute | solution.py:47
  49.4 3.1 convert_element_type.246.refs_0_
  57.1 3.1 fusion.7
  60.3 12.0 %norm.1 = (bf16[1024,2048]{1,0:T(8,128)(2,1)}, bf16[1024,1024]{1,0:T(8,128)(2,1)}, bf16[1024,1024]{1,0:T(8,128)(2,1)}, bf16[1024,1024]{1,0:T(8,128)(2,1)}, bf16[...) custom-call(s32[8]{0:T(128)} %fusion.16.places.where, ...), custom_call_target="tpu_custom_call" | custom-call | flops 41943040 | bytes 41943040 | tf_op jit(solution)/shard_map/norm/pallas_call | solution.py:151
  72.3 6.4 %collective-permute-done.4.refs_1_ = bf16[256,2048]{1,0:T(8,128)(2,1)} collective-permute-done((bf16[256,2048]{1,0:T(8,128)(2,1)}, bf16[256,2048]{1,0:T(8,128)(2,1)}, u32[]{:S(2)}, u32[]{:S(2)}) %collective-permute-start.4) | collective-permute-done | bytes 1048608 | tf_op jit(solution)/shard_map/ppermute | solution.py:47
  83.1 11.9 %project.1 = (bf16[1024,512]{1,0:T(8,128)(2,1)}, bf16[1024,1024]{1,0:T(8,128)(2,1)}) custom-call(bf16[1024,1024]{1,0:T(8,128)(2,1)} %get-tuple-element.130.one_a.left_a, bf16[1024,1024]{1,0:T(8,128)(2,1)} %get-tuple-element.128.one_b.left_b, bf16[1024,1536]{1,0:T(8,128)(2,1)} %copy-done, bf16[1024,1536]{1,0:T(8,128)(2,1)} %collective-permute-done.6.w_b, ...), custom_call_target="tpu_custom_call" | custom-call | flops 6442450944 | bytes 14000000 | tf_op jit(solution)/shard_map/project/pallas_call | solution.py:192
  95.3 2.7 collective-permute-start.9
  99.5 2.8 collective-permute-done.11.refs_5_
  108.5 17.4 %expand.1 = (bf16[1024,2048]{1,0:T(8,128)(2,1)}, bf16[1024,2048]{1,0:T(8,128)(2,1)}) custom-call(bf16[1024,1024]{1,0:T(8,128)(2,1)} %get-tuple-element.137.two_a.left_a, bf16[1024,1024]{1,0:T(8,128)(2,1)} %get-tuple-element.138.two_b.left_b, f32[1,2048]{1,0:T(1,128)} %bitcast.120, bf16[256,2048]{1,0:T(8,128)(2,1)} %convert_element_type.246.refs_0_, ...), custom_call_target="tpu_custom_call" | custom-call | tf_op jit(solution)/shard_map/expand/pallas_call | solution.py:239
  125.9 2.7 collective-permute-start.17
  128.6 10.1 %collective-permute-start.18 = (bf16[2560,256]{1,0:T(8,128)(2,1)S(1)}, bf16[2560,256]{1,0:T(8,128)(2,1)S(1)}, u32[]{:S(2)}, u32[]{:S(2)}) collective-permute-start(bf16[2560,256]{1,0:T(8,128)(2,1)S(1)} %pad_maximum_fusion.mine.rest_0_), channel_id=1, source_target_pairs={{0,16},{4,20},{8,24},{12,28},{16,0},{20,4},{24,8},{28,12},{1,17},{... | collective-permute-start | bytes 3932168 | tf_op jit(solution)/shard_map/ppermute | solution.py:47
  140.0 14.5 %column_grad.2.rest_0_ = bf16[8,2560,256]{2,1,0:T(8,128)(2,1)} custom-call(s32[8]{0:T(128)} %fusion.16.places.where, bf16[1024,2048]{1,0:T(8,128)(2,1)} %get-tuple-element.144.left.active, bf16[1024,1024]{1,0:T(8,128)(2,1)} %get-tuple-element.218.right_a.a.rest_0_, bf16[1024,1024]{1,0:T(8,128)(2,1)} %get-tuple-element.146.right_b.b), custom_call_target="tpu_custom_call" | custom-call | tf_op jit(solution)/shard_map/column_grad/pallas_call | solution.py:398
  154.5 11.9 %attend.1 = (bf16[1024,512]{1,0:T(8,128)(2,1)}, f32[2,1,1024]{2,1,0:T(1,128)}) custom-call(s32[4]{0:T(128)} %get-tuple-element.249.first, s32[4]{0:T(128)} %get-tuple-element.248.last, bf16[1024,512]{1,0:T(8,128)(2,1)} %get-tuple-element.147.q, bf16[1024,1024]{1,0:T(8,128)(2,1)} %collective-permute-done.9.left, bf16[1024,1024]{1,0:T(8,128)(2,1)} %get-tuple-element.135.own, ...), custom_call_target="tpu_custom_call" | custom-call | flops 8000000000 | bytes 10000000 | tf_op jit(solution)/shard_map/attend/pallas_call | solution.py:477
  172.4 6.4 %branch.4 = bf16[4,1024,128]{2,1,0:T(8,128)(2,1)} custom-call(bf16[1024,512]{1,0:T(8,128)(2,1)} %get-tuple-element.168.attended.left, bf16[1024,2048]{1,0:T(8,128)(2,1)} %get-tuple-element.144.left.active, bf16[2560,256]{1,0:T(8,128)(2,1)} %copy-done.2, bf16[2560,256]{1,0:T(8,128)(2,1)} %copy-done.19), custom_call_target="tpu_custom_call" | custom-call | flops 2684354560 | bytes 8912896 | tf_op jit(solution)/shard_map/branch/pallas_call | solution.py:266
  178.8 7.0 %column_grad.3 = bf16[8,2560,256]{2,1,0:T(8,128)(2,1)} custom-call(s32[8]{0:T(128)} %fusion.16.places.where, bf16[1024,512]{1,0:T(8,128)(2,1)} %get-tuple-element.168.attended.left, bf16[1024,1024]{1,0:T(8,128)(2,1)} %get-tuple-element.218.right_a.a.rest_0_, bf16[1024,1024]{1,0:T(8,128)(2,1)} %get-tuple-element.146.right_b.b, ...), custom_call_target="tpu_custom_call", output_to_operand_aliasing={{}: (4, {})} | custom-call | tf_op jit(solution)/shard_map/column_grad/pallas_call | solution.py:398
  188.9 4.8 collective-permute-start.26
  195.3 6.1 %back.2.grad = bf16[1024,512]{1,0:T(8,128)(2,1)} custom-call(bf16[1024,1024]{1,0:T(8,128)(2,1)} %get-tuple-element.218.right_a.a.rest_0_, bf16[1024,1024]{1,0:T(8,128)(2,1)} %get-tuple-element.146.right_b.b, bf16[2560,256]{1,0:T(8,128)(2,1)} %copy-done.2, bf16[2560,256]{1,0:T(8,128)(2,1)} %copy-done.10, bf16[2560,256]{1,0:T(8,128)(2,1)} %copy-done.11, ...), custom_call_target="tpu_custom_call" | custom-call | flops 2147483648 | bytes 8388608 | tf_op jit(solution)/shard_map/back/pallas_call | solution.py:311
  201.3 18.9 %attend_back.1 = (bf16[1024,512]{1,0:T(8,128)(2,1)}, bf16[1024,1024]{1,0:T(8,128)(2,1)}, f32[1024,1024]{1,0:T(8,128)}, bf16[512,1024]{1,0:T(8,128)(2,1)}) custom-call(s32[4]{0:T(128)} %get-tuple-element.249.first, s32[4]{0:T(128)} %get-tuple-element.248.last, bf16[1024,512]{1,0:T(8,128)(2,1)} %get-tuple-element.147.q, ...), custom_call_target="tpu_custom_call" | custom-call | flops 16000000000 | bytes 20000000 | tf_op jit(solution)/shard_map/attend_back/pallas_call | solution.py:560
  221.6 6.4 %branch.5 = bf16[4,1024,128]{2,1,0:T(8,128)(2,1)} custom-call(bf16[1024,512]{1,0:T(8,128)(2,1)} %get-tuple-element.168.attended.left, bf16[1024,2048]{1,0:T(8,128)(2,1)} %get-tuple-element.144.left.active, bf16[2560,256]{1,0:T(8,128)(2,1)} %copy-done.10, bf16[2560,256]{1,0:T(8,128)(2,1)} %copy-done.20), custom_call_target="tpu_custom_call" | custom-call | flops 2684354560 | bytes 8912896 | tf_op jit(solution)/shard_map/branch/pallas_call | solution.py:266
  233.9 4.6 collective-permute-start.25
  238.5 6.5 %branch.6 = bf16[4,1024,128]{2,1,0:T(8,128)(2,1)} custom-call(bf16[1024,512]{1,0:T(8,128)(2,1)} %get-tuple-element.168.attended.left, bf16[1024,2048]{1,0:T(8,128)(2,1)} %get-tuple-element.144.left.active, bf16[2560,256]{1,0:T(8,128)(2,1)} %copy-done.11, bf16[2560,256]{1,0:T(8,128)(2,1)} %copy-done.21), custom_call_target="tpu_custom_call" | custom-call | flops 2684354560 | bytes 8912896 | tf_op jit(solution)/shard_map/branch/pallas_call | solution.py:266
  244.9 6.4 %branch.7 = bf16[4,1024,128]{2,1,0:T(8,128)(2,1)} custom-call(bf16[1024,512]{1,0:T(8,128)(2,1)} %get-tuple-element.168.attended.left, bf16[1024,2048]{1,0:T(8,128)(2,1)} %get-tuple-element.144.left.active, bf16[2560,256]{1,0:T(8,128)(2,1)} %copy-done.12, bf16[2560,256]{1,0:T(8,128)(2,1)} %collective-permute-done.23.rest_7_.theirs), custom_call_target="tpu_custom_call" | custom-call | flops 2684354560 | bytes 8912896 | tf_op jit(solution)/shard_map/branch/pallas_call | solution.py:266
  251.3 14.5 %back.3 = (bf16[1024,2048]{1,0:T(8,128)(2,1)}, f32[1,2048]{1,0:T(1,128)}) custom-call(bf16[1024,1024]{1,0:T(8,128)(2,1)} %get-tuple-element.218.right_a.a.rest_0_, bf16[1024,1024]{1,0:T(8,128)(2,1)} %get-tuple-element.146.right_b.b, bf16[2560,256]{1,0:T(8,128)(2,1)} %copy-done.2, bf16[2560,256]{1,0:T(8,128)(2,1)} %copy-done.10, ...), custom_call_target="tpu_custom_call" | custom-call | flops 8589934592 | bytes 20971520 | tf_op jit(solution)/shard_map/back/pallas_call | solution.py:311
  273.0 18.2 %second_back.1.second = bf16[1024,2048]{1,0:T(8,128)(2,1)} custom-call(bf16[1024,2048]{1,0:T(8,128)(2,1)} %get-tuple-element.199.grad.right, bf16[256,2048]{1,0:T(8,128)(2,1)} %convert_element_type.246.refs_0_, bf16[256,2048]{1,0:T(8,128)(2,1)} %collective-permute-done.4.refs_1_, bf16[256,2048]{1,0:T(8,128)(2,1)} %collective-permute-done.5.refs_2_, ...), custom_call_target="tpu_custom_call" | custom-call | flops 8589934592 | bytes 16777216 | tf_op jit(solution)/shard_map/second_back/pallas_call | solution.py:344
  291.1 5.5 %mix.1 = (bf16[1024,1536]{1,0:T(8,128)(2,1)}, f32[1,1536]{1,0:T(1,128)}) custom-call(bf16[1024,512]{1,0:T(8,128)(2,1)} %get-tuple-element.177.dq, f32[1024,1024]{1,0:T(8,128)} %get-tuple-element.178.own, bf16[1024,1024]{1,0:T(8,128)(2,1)} %copy-done.14, bf16[512,1024]{1,0:T(8,128)(2,1)} %copy-done.29, f32[1024,128]{1,0:T(8,128)} %get-tuple-element.236.cos, ...), custom_call_target="tpu_custom_call" | custom-call | flops 10000000 | bytes 14000000 | tf_op jit(solution)/shard_map/mix/pallas_call | solution.py:606
  298.1 5.8 %collective-permute-start.31 = (bf16[4096,128]{1,0:T(8,128)(2,1)}, bf16[4096,128]{1,0:T(8,128)(2,1)}, u32[]{:S(2)}, u32[]{:S(2)}) collective-permute-start(bf16[4096,128]{1,0:T(8,128)(2,1)} %fusion.1), channel_id=1, source_target_pairs={{0,1},{3,2},{1,0},{2,3},{4,5},{7,6},{5,4},{6,7},{8,9},{11,10},{9,8... | collective-permute-start | bytes 3145736 | tf_op jit(solution)/shard_map/ppermute | solution.py:786
  307.5 13.0 %input_back.2 = (bf16[16,256,128]{2,1,0:T(8,128)(2,1)}, bf16[16,256,128]{2,1,0:T(8,128)(2,1)}, f32[8,2048]{1,0:T(8,128)}) custom-call(bf16[1024,1536]{1,0:T(8,128)(2,1)} %get-tuple-element.204.mixed.right, bf16[1024,1536]{1,0:T(8,128)(2,1)} %copy-done, bf16[1024,1536]{1,0:T(8,128)(2,1)} %collective-permute-done.6.w_b, bf16[1024,2048]{1,0:T(8,128)(2,1)} %second_back.1.second, ...), custom_call_target="tpu_custom_call" | custom-call | flops 3221225472 | bytes 14000000 | tf_op jit(solution)/shard_map/input_back/pallas_call | solution.py:668
  320.5 7.5 %collective-permute-done.31 = bf16[4096,128]{1,0:T(8,128)(2,1)} collective-permute-done((bf16[4096,128]{1,0:T(8,128)(2,1)}, bf16[4096,128]{1,0:T(8,128)(2,1)}, u32[]{:S(2)}, u32[]{:S(2)}) %collective-permute-start.31) | collective-permute-done | bytes 1048608 | tf_op jit(solution)/shard_map/ppermute | solution.py:786
  330.0 3.5 collective-permute-start.34
  336.1 12.8 %input_back.3 = (bf16[16,256,128]{2,1,0:T(8,128)(2,1)}, bf16[16,256,128]{2,1,0:T(8,128)(2,1)}, f32[8,2048]{1,0:T(8,128)}) custom-call(bf16[1024,1536]{1,0:T(8,128)(2,1)} %get-tuple-element.204.mixed.right, bf16[1024,1536]{1,0:T(8,128)(2,1)} %copy-done, bf16[1024,1536]{1,0:T(8,128)(2,1)} %collective-permute-done.6.w_b, bf16[1024,2048]{1,0:T(8,128)(2,1)} %second_back.1.second, ...), custom_call_target="tpu_custom_call" | custom-call | flops 3221225472 | bytes 14000000 | tf_op jit(solution)/shard_map/input_back/pallas_call | solution.py:668
  349.8 6.8 %collective-permute-done.34 = bf16[4096,128]{1,0:T(8,128)(2,1)S(1)} collective-permute-done((bf16[4096,128]{1,0:T(8,128)(2,1)S(1)}, bf16[4096,128]{1,0:T(8,128)(2,1)S(1)}, u32[]{:S(2)}, u32[]{:S(2)}) %collective-permute-start.34) | collective-permute-done | bytes 1048608 | tf_op jit(solution)/shard_map/ppermute | solution.py:786
  357.7 5.5 %collective-permute-start.35 = (bf16[4096,128]{1,0:T(8,128)(2,1)S(1)}, bf16[4096,128]{1,0:T(8,128)(2,1)S(1)}, u32[]{:S(2)}, u32[]{:S(2)}) collective-permute-start(bf16[4096,128]{1,0:T(8,128)(2,1)S(1)} %fusion.3), channel_id=1, source_target_pairs={{0,1},{3,2},{1,0},{2,3},{4,5},{7,6},{5,4},{6,7},{8,9},{11,10},{9,8... | collective-permute-start | bytes 3145736 | tf_op jit(solution)/shard_map/ppermute | solution.py:786
  365.5 14.2 %row_grad.2.rest_0_ = bf16[8,256,3584]{2,1,0:T(8,128)(2,1)} custom-call(s32[8]{0:T(128)} %fusion.16.places.where, bf16[1024,1024]{1,0:T(8,128)(2,1)} %get-tuple-element.137.two_a.left_a, bf16[1024,1024]{1,0:T(8,128)(2,1)} %get-tuple-element.138.two_b.left_b, bf16[1024,2048]{1,0:T(8,128)(2,1)} %get-tuple-element.199.grad.right), custom_call_target="tpu_custom_call" | custom-call | flops 8589934592 | bytes 16777216 | tf_op jit(solution)/shard_map/row_grad/pallas_call | solution.py:369
  383.4 3.6 collective-permute-done.35
  391.6 5.0 collective-permute-start.41
  396.7 11.8 %row_grad.3 = bf16[8,256,3584]{2,1,0:T(8,128)(2,1)} custom-call(s32[8]{0:T(128)} %fusion.16.places.where, bf16[1024,1024]{1,0:T(8,128)(2,1)} %get-tuple-element.130.one_a.left_a, bf16[1024,1024]{1,0:T(8,128)(2,1)} %get-tuple-element.128.one_b.left_b, bf16[1024,1536]{1,0:T(8,128)(2,1)} %get-tuple-element.204.mixed.right, ...), custom_call_target="tpu_custom_call", output_to_operand_aliasing={{}: (4, {})} | custom-call | flops 6442450944 | bytes 13631488 | tf_op jit(solution)/shard_map/row_grad/pallas_call | solution.py:369
  410.1 9.2 %output_sum.1 = bf16[1024,2048]{1,0:T(8,128)(2,1)} custom-call(s32[8]{0:T(128)} %fusion.16.places.where, s32[1]{0:T(128)} %bitcast.middle, bf16[1024,2048]{1,0:T(8,128)(2,1)} %tokens.3, f32[1,2048]{1,0:T(1,128)} %bitcast.123, bf16[4,1024,128]{2,1,0:T(8,128)(2,1)} %bitcast.102, bf16[4,1024,128]{2,1,0:T(8,128)(2,1)} %bitcast.26.refs_1_, ...), custom_call_target="tpu_custom_call" | custom-call | flops 35999997952 | bytes 17000000 | tf_op jit(solution)/shard_map/output_sum/pallas_call | solution.py:700
  426.3 2.8 add_convert_fusion.3
  430.8 4.2 tokens_sum.4.rest_0_
  438.5 11.7 %collective-permute-done.42.passed = bf16[4112,128]{1,0:T(8,128)(2,1)} collective-permute-done((bf16[4112,128]{1,0:T(8,128)(2,1)}, bf16[4112,128]{1,0:T(8,128)(2,1)}, u32[]{:S(2)}, u32[]{:S(2)}) %collective-permute-start.42) | collective-permute-done | bytes 1052704 | tf_op jit(solution)/shard_map/ppermute | solution.py:786
  455.9 4.0 tokens_sum.5.rest_0_
  459.9 21.1 %collective-permute-done.45.passed = bf16[4096,128]{1,0:T(8,128)(2,1)S(1)} collective-permute-done((bf16[4096,128]{1,0:T(8,128)(2,1)S(1)}, bf16[4096,128]{1,0:T(8,128)(2,1)S(1)}, u32[]{:S(2)}, u32[]{:S(2)}) %collective-permute-start.45) | collective-permute-done | bytes 1048608 | tf_op jit(solution)/shard_map/ppermute | solution.py:786
  482.6 4.1 tokens_sum.6.rest_0_
  486.6 17.9 %collective-permute-done.46.passed = bf16[4112,128]{1,0:T(8,128)(2,1)S(1)} collective-permute-done((bf16[4112,128]{1,0:T(8,128)(2,1)S(1)}, bf16[4112,128]{1,0:T(8,128)(2,1)S(1)}, u32[]{:S(2)}, u32[]{:S(2)}) %collective-permute-start.46) | collective-permute-done | bytes 1052704 | tf_op jit(solution)/shard_map/ppermute | solution.py:786
  505.5 4.0 tokens_sum.7
  509.5 3.7 reduce-scatter.5.cloned.1.call-done
  (304 shorter events, 104.1 us)
Async XLA Ops:
  7.3 401.2 %reduce-scatter.3.cloned.1.call-start = ((), (), s32[]{:S(2)}) async-start(), calls=%async_computation.2 | async-start | bytes 11796480 | tf_op jit(solution)/shard_map/reduce_scatter | solution.py:795
  8.8 25.1 %collective-permute-start = (bf16[256,1536]{1,0:T(8,128)(2,1)S(1)}, bf16[256,1536]{1,0:T(8,128)(2,1)S(1)}, u32[]{:S(2)}, u32[]{:S(2)}) collective-permute-start(bf16[256,1536]{1,0:T(8,128)(2,1)S(1)} %convert_element_type.245), channel_id=1, source_target_pairs={{0,8},{4,12},{8,0},{12,4},{16,24},{20,28},{24,16},{28,20},{1,9},{5... | collective-permute-start | bytes 2359304 | tf_op jit(solution)/shard_map/ppermute | solution.py:47
  11.8 22.2 %collective-permute-start.1 = (bf16[256,1536]{1,0:T(8,128)(2,1)S(1)}, bf16[256,1536]{1,0:T(8,128)(2,1)S(1)}, u32[]{:S(2)}, u32[]{:S(2)}) collective-permute-start(bf16[256,1536]{1,0:T(8,128)(2,1)S(1)} %convert_element_type.245), channel_id=1, source_target_pairs={{0,16},{4,20},{8,24},{12,28},{16,0},{20,4},{24,8},{28,12},{1,17},{... | collective-permute-start | bytes 2359304 | tf_op jit(solution)/shard_map/ppermute | solution.py:47
  34.0 11.4 %collective-permute-start.2 = (bf16[128,1536]{1,0:T(8,128)(2,1)S(1)}, bf16[128,1536]{1,0:T(8,128)(2,1)S(1)}, u32[]{:S(2)}, u32[]{:S(2)}) collective-permute-start(bf16[128,1536]{1,0:T(8,128)(2,1)S(1)} %slice.171), channel_id=1, source_target_pairs={{0,16},{4,20},{8,24},{12,28},{16,0},{20,4},{24,8},{28,12},{1,17},{... | collective-permute-start | bytes 1179656 | tf_op jit(solution)/shard_map/ppermute | solution.py:47
  35.8 11.1 %collective-permute-start.3 = (bf16[128,1536]{1,0:T(8,128)(2,1)S(1)}, bf16[128,1536]{1,0:T(8,128)(2,1)S(1)}, u32[]{:S(2)}, u32[]{:S(2)}) collective-permute-start(bf16[128,1536]{1,0:T(8,128)(2,1)S(1)} %slice.172), channel_id=1, source_target_pairs={{0,8},{4,12},{8,0},{12,4},{16,24},{20,28},{24,16},{28,20},{1,9},{5... | collective-permute-start | bytes 1179656 | tf_op jit(solution)/shard_map/ppermute | solution.py:47
  48.7 34.4 %collective-permute-start.6 = (bf16[1024,1536]{1,0:T(8,128)(2,1)S(1)}, bf16[1024,1536]{1,0:T(8,128)(2,1)}, u32[]{:S(2)}, u32[]{:S(2)}) collective-permute-start(bf16[1024,1536]{1,0:T(8,128)(2,1)S(1)} %constant_dynamic-update-slice_fusion.w_a), channel_id=1, source_target_pairs={{0,4},{4,0},{8,12},{12,8},{16,20},{20,16},{24,28},{28,24},{1,5},{5... | collective-permute-start | bytes 9437192 | tf_op jit(solution)/shard_map/ppermute | solution.py:47
  53.1 25.5 %collective-permute-start.4 = (bf16[256,2048]{1,0:T(8,128)(2,1)}, bf16[256,2048]{1,0:T(8,128)(2,1)}, u32[]{:S(2)}, u32[]{:S(2)}) collective-permute-start(bf16[256,2048]{1,0:T(8,128)(2,1)} %convert_element_type.246.refs_0_), channel_id=1, source_target_pairs={{0,8},{4,12},{8,0},{12,4},{16,24},{20,28},{24,16},{28,20},{1,9},{5... | collective-permute-start | bytes 3145736 | tf_op jit(solution)/shard_map/ppermute | solution.py:47
  54.7 25.2 %collective-permute-start.5 = (bf16[256,2048]{1,0:T(8,128)(2,1)}, bf16[256,2048]{1,0:T(8,128)(2,1)}, u32[]{:S(2)}, u32[]{:S(2)}) collective-permute-start(bf16[256,2048]{1,0:T(8,128)(2,1)} %convert_element_type.246.refs_0_), channel_id=1, source_target_pairs={{0,16},{4,20},{8,24},{12,28},{16,0},{20,4},{24,8},{28,12},{1,17},{... | collective-permute-start | bytes 3145736 | tf_op jit(solution)/shard_map/ppermute | solution.py:47
  81.0 14.1 %collective-permute-start.7 = (bf16[128,2048]{1,0:T(8,128)(2,1)S(1)}, bf16[128,2048]{1,0:T(8,128)(2,1)}, u32[]{:S(2)}, u32[]{:S(2)}) collective-permute-start(bf16[128,2048]{1,0:T(8,128)(2,1)S(1)} %slice.174), channel_id=1, source_target_pairs={{0,16},{4,20},{8,24},{12,28},{16,0},{20,4},{24,8},{28,12},{1,17},{... | collective-permute-start | bytes 1572872 | tf_op jit(solution)/shard_map/ppermute | solution.py:47
  82.6 12.7 %collective-permute-start.8 = (bf16[128,2048]{1,0:T(8,128)(2,1)S(1)}, bf16[128,2048]{1,0:T(8,128)(2,1)}, u32[]{:S(2)}, u32[]{:S(2)}) collective-permute-start(bf16[128,2048]{1,0:T(8,128)(2,1)S(1)} %slice.175), channel_id=1, source_target_pairs={{0,8},{4,12},{8,0},{12,4},{16,24},{20,28},{24,16},{28,20},{1,9},{5... | collective-permute-start | bytes 1572872 | tf_op jit(solution)/shard_map/ppermute | solution.py:47
  95.3 30.6 %collective-permute-start.9 = (bf16[1024,1024]{1,0:T(8,128)(2,1)}, bf16[1024,1024]{1,0:T(8,128)(2,1)}, u32[]{:S(2)}, u32[]{:S(2)}) collective-permute-start(bf16[1024,1024]{1,0:T(8,128)(2,1)} %get-tuple-element.135.own), channel_id=1, source_target_pairs={{0,4},{4,8},{8,12},{12,16},{16,20},{20,24},{24,28},{1,5},{5,9},{9,... | collective-permute-start | bytes 6291464 | tf_op jit(solution)/shard_map/ppermute | solution.py:806
  98.0 4.3 collective-permute-start.11
  98.9 6.0 %collective-permute-start.12 = (bf16[256,2048]{1,0:T(8,128)(2,1)}, bf16[256,2048]{1,0:T(8,128)(2,1)}, u32[]{:S(2)}, u32[]{:S(2)}) collective-permute-start(bf16[256,2048]{1,0:T(8,128)(2,1)} %collective-permute-done.4.refs_1_), channel_id=1, source_target_pairs={{0,4},{4,0},{8,12},{12,8},{16,20},{20,16},{24,28},{28,24},{1,5},{5... | collective-permute-start | bytes 3145736 | tf_op jit(solution)/shard_map/ppermute | solution.py:47
  99.0 9.5 %collective-permute-start.13 = (bf16[256,2048]{1,0:T(8,128)(2,1)}, bf16[256,2048]{1,0:T(8,128)(2,1)}, u32[]{:S(2)}, u32[]{:S(2)}) collective-permute-start(bf16[256,2048]{1,0:T(8,128)(2,1)} %collective-permute-done.5.refs_2_), channel_id=1, source_target_pairs={{0,4},{4,0},{8,12},{12,8},{16,20},{20,16},{24,28},{28,24},{1,5},{5... | collective-permute-start | bytes 3145736 | tf_op jit(solution)/shard_map/ppermute | solution.py:47
  99.4 9.1 %collective-permute-start.14 = (bf16[128,2048]{1,0:T(8,128)(2,1)}, bf16[128,2048]{1,0:T(8,128)(2,1)}, u32[]{:S(2)}, u32[]{:S(2)}) collective-permute-start(bf16[128,2048]{1,0:T(8,128)(2,1)} %collective-permute-done.7.refs_3_), channel_id=1, source_target_pairs={{0,4},{4,0},{8,12},{12,8},{16,20},{20,16},{24,28},{28,24},{1,5},{5... | collective-permute-start | bytes 1572872 | tf_op jit(solution)/shard_map/ppermute | solution.py:47
  102.3 6.2 %collective-permute-start.15 = (bf16[128,2048]{1,0:T(8,128)(2,1)}, bf16[128,2048]{1,0:T(8,128)(2,1)}, u32[]{:S(2)}, u32[]{:S(2)}) collective-permute-start(bf16[128,2048]{1,0:T(8,128)(2,1)} %collective-permute-done.8.refs_4_), channel_id=1, source_target_pairs={{0,4},{4,0},{8,12},{12,8},{16,20},{20,16},{24,28},{28,24},{1,5},{5... | collective-permute-start | bytes 1572872 | tf_op jit(solution)/shard_map/ppermute | solution.py:47
  105.0 49.5 %collective-permute-start.10 = (bf16[512,1024]{1,0:T(8,128)(2,1)}, bf16[512,1024]{1,0:T(8,128)(2,1)}, u32[]{:S(2)}, u32[]{:S(2)}) collective-permute-start(bf16[512,1024]{1,0:T(8,128)(2,1)} %slice.135), channel_id=1, source_target_pairs={{4,0},{8,4},{12,8},{16,12},{20,16},{24,20},{28,24},{5,1},{9,5},{13... | collective-permute-start | bytes 3145736 | tf_op jit(solution)/shard_map/ppermute | solution.py:806
  125.9 40.5 %collective-permute-start.17 = (bf16[2560,256]{1,0:T(8,128)(2,1)S(1)}, bf16[2560,256]{1,0:T(8,128)(2,1)S(1)}, u32[]{:S(2)}, u32[]{:S(2)}) collective-permute-start(bf16[2560,256]{1,0:T(8,128)(2,1)S(1)} %pad_maximum_fusion.mine.rest_0_), channel_id=1, source_target_pairs={{0,8},{4,12},{8,0},{12,4},{16,24},{20,28},{24,16},{28,20},{1,9},{5... | collective-permute-start | bytes 3932168 | tf_op jit(solution)/shard_map/ppermute | solution.py:47
  128.6 38.7 %collective-permute-start.18 = (bf16[2560,256]{1,0:T(8,128)(2,1)S(1)}, bf16[2560,256]{1,0:T(8,128)(2,1)S(1)}, u32[]{:S(2)}, u32[]{:S(2)}) collective-permute-start(bf16[2560,256]{1,0:T(8,128)(2,1)S(1)} %pad_maximum_fusion.mine.rest_0_), channel_id=1, source_target_pairs={{0,16},{4,20},{8,24},{12,28},{16,0},{20,4},{24,8},{28,12},{1,17},{... | collective-permute-start | bytes 3932168 | tf_op jit(solution)/shard_map/ppermute | solution.py:47
  139.4 31.9 %collective-permute-start.16 = (bf16[2560,256]{1,0:T(8,128)(2,1)S(1)}, bf16[2560,256]{1,0:T(8,128)(2,1)S(1)}, u32[]{:S(2)}, u32[]{:S(2)}) collective-permute-start(bf16[2560,256]{1,0:T(8,128)(2,1)S(1)} %pad_maximum_fusion.mine.rest_0_), channel_id=1, source_target_pairs={{0,4},{4,0},{8,12},{12,8},{16,20},{20,16},{24,28},{28,24},{1,5},{5... | collective-permute-start | bytes 3932168 | tf_op jit(solution)/shard_map/ppermute | solution.py:47
  167.3 19.0 %collective-permute-start.19 = (bf16[1280,256]{1,0:T(8,128)(2,1)S(1)}, bf16[1280,256]{1,0:T(8,128)(2,1)}, u32[]{:S(2)}, u32[]{:S(2)}) collective-permute-start(bf16[1280,256]{1,0:T(8,128)(2,1)S(1)} %slice.177), channel_id=1, source_target_pairs={{0,16},{4,20},{8,24},{12,28},{16,0},{20,4},{24,8},{28,12},{1,17},{... | collective-permute-start | bytes 1966088 | tf_op jit(solution)/shard_map/ppermute | solution.py:47
  169.1 18.3 %collective-permute-start.20 = (bf16[1280,256]{1,0:T(8,128)(2,1)}, bf16[1280,256]{1,0:T(8,128)(2,1)}, u32[]{:S(2)}, u32[]{:S(2)}) collective-permute-start(bf16[1280,256]{1,0:T(8,128)(2,1)} %slice.178), channel_id=1, source_target_pairs={{0,8},{4,12},{8,0},{12,4},{16,24},{20,28},{24,16},{28,20},{1,9},{5... | collective-permute-start | bytes 1966088 | tf_op jit(solution)/shard_map/ppermute | solution.py:47
  185.8 7.9 %collective-permute-start.21 = (bf16[2560,256]{1,0:T(8,128)(2,1)S(1)}, bf16[2560,256]{1,0:T(8,128)(2,1)S(1)}, u32[]{:S(2)}, u32[]{:S(2)}) collective-permute-start(bf16[2560,256]{1,0:T(8,128)(2,1)S(1)} %collective-permute-done.17.rest_1_.mine), channel_id=1, source_target_pairs={{0,4},{4,0},{8,12},{12,8},{16,20},{20,16},{24,28},{28,24},{1,5},{5... | collective-permute-start | bytes 3932168 | tf_op jit(solution)/shard_map/ppermute | solution.py:47
  186.0 7.7 %collective-permute-start.22 = (bf16[2560,256]{1,0:T(8,128)(2,1)S(1)}, bf16[2560,256]{1,0:T(8,128)(2,1)S(1)}, u32[]{:S(2)}, u32[]{:S(2)}) collective-permute-start(bf16[2560,256]{1,0:T(8,128)(2,1)S(1)} %collective-permute-done.18.rest_2_.mine), channel_id=1, source_target_pairs={{0,4},{4,0},{8,12},{12,8},{16,20},{20,16},{24,28},{28,24},{1,5},{5... | collective-permute-start | bytes 3932168 | tf_op jit(solution)/shard_map/ppermute | solution.py:47
  188.6 5.2 collective-permute-start.23
  188.9 39.1 %collective-permute-start.26 = (bf16[4096,128]{1,0:T(8,128)(2,1)}, bf16[4096,128]{1,0:T(8,128)(2,1)}, u32[]{:S(2)}, u32[]{:S(2)}) collective-permute-start(bf16[4096,128]{1,0:T(8,128)(2,1)} %bitcast.11), channel_id=1, source_target_pairs={{0,1},{3,2},{4,5},{7,6},{8,9},{11,10},{12,13},{15,14},{16,17},{19,... | collective-permute-start | bytes 3145736 | tf_op jit(solution)/shard_map/ppermute | solution.py:786
  220.3 45.6 %collective-permute-start.24 = (bf16[1024,1024]{1,0:T(8,128)(2,1)}, bf16[1024,1024]{1,0:T(8,128)(2,1)S(1)}, u32[]{:S(2)}, u32[]{:S(2)}) collective-permute-start(bf16[1024,1024]{1,0:T(8,128)(2,1)} %get-tuple-element.162), channel_id=1, source_target_pairs={{4,0},{8,4},{12,8},{16,12},{20,16},{24,20},{28,24},{5,1},{9,5},{13... | collective-permute-start | bytes 6291464 | tf_op jit(solution)/shard_map/ppermute | solution.py:806
  228.0 39.4 %collective-permute-start.27 = (bf16[4096,128]{1,0:T(8,128)(2,1)}, bf16[4096,128]{1,0:T(8,128)(2,1)}, u32[]{:S(2)}, u32[]{:S(2)}) collective-permute-start(bf16[4096,128]{1,0:T(8,128)(2,1)} %bitcast.108), channel_id=1, source_target_pairs={{0,1},{3,2},{4,5},{7,6},{8,9},{11,10},{12,13},{15,14},{16,17},{19,... | collective-permute-start | bytes 3145736 | tf_op jit(solution)/shard_map/ppermute | solution.py:786
  232.2 35.2 %collective-permute-start.28 = (bf16[4096,128]{1,0:T(8,128)(2,1)S(1)}, bf16[4096,128]{1,0:T(8,128)(2,1)}, u32[]{:S(2)}, u32[]{:S(2)}) collective-permute-start(bf16[4096,128]{1,0:T(8,128)(2,1)S(1)} %add_convert_fusion.15), channel_id=1, source_target_pairs={{1,2},{2,1},{5,6},{6,5},{9,10},{10,9},{13,14},{14,13},{17,18},{18,... | collective-permute-start | bytes 3145736 | tf_op jit(solution)/shard_map/ppermute | solution.py:783
  233.9 32.0 %collective-permute-start.25 = (bf16[512,1024]{1,0:T(8,128)(2,1)S(1)}, bf16[512,1024]{1,0:T(8,128)(2,1)S(1)}, u32[]{:S(2)}, u32[]{:S(2)}) collective-permute-start(bf16[512,1024]{1,0:T(8,128)(2,1)S(1)} %copy-done.41), channel_id=1, source_target_pairs={{0,4},{4,8},{8,12},{12,16},{16,20},{20,24},{24,28},{1,5},{5,9},{9,... | collective-permute-start | bytes 3145736 | tf_op jit(solution)/shard_map/ppermute | solution.py:806
  267.3 245.8 %reduce-scatter.5.cloned.1.call-start = ((), (), s32[]{:S(2)}) async-start(), calls=%async_computation.3 | async-start | bytes 16515072 | tf_op jit(solution)/shard_map/reduce_scatter | solution.py:795
  270.2 26.5 %collective-permute-start.29 = (bf16[4096,128]{1,0:T(8,128)(2,1)S(1)}, bf16[4096,128]{1,0:T(8,128)(2,1)S(1)}, u32[]{:S(2)}, u32[]{:S(2)}) collective-permute-start(bf16[4096,128]{1,0:T(8,128)(2,1)S(1)} %fusion), channel_id=1, source_target_pairs={{0,1},{3,2},{1,0},{2,3},{4,5},{7,6},{5,4},{6,7},{8,9},{11,10},{9,8... | collective-permute-start | bytes 3145736 | tf_op jit(solution)/shard_map/ppermute | solution.py:786
  272.0 24.6 %collective-permute-start.30 = (bf16[4096,128]{1,0:T(8,128)(2,1)S(1)}, bf16[4096,128]{1,0:T(8,128)(2,1)S(1)}, u32[]{:S(2)}, u32[]{:S(2)}) collective-permute-start(bf16[4096,128]{1,0:T(8,128)(2,1)S(1)} %add_convert_fusion.14), channel_id=1, source_target_pairs={{1,2},{2,1},{5,6},{6,5},{9,10},{10,9},{13,14},{14,13},{17,18},{18,... | collective-permute-start | bytes 3145736 | tf_op jit(solution)/shard_map/ppermute | solution.py:783
  298.1 30.0 %collective-permute-start.31 = (bf16[4096,128]{1,0:T(8,128)(2,1)}, bf16[4096,128]{1,0:T(8,128)(2,1)}, u32[]{:S(2)}, u32[]{:S(2)}) collective-permute-start(bf16[4096,128]{1,0:T(8,128)(2,1)} %fusion.1), channel_id=1, source_target_pairs={{0,1},{3,2},{1,0},{2,3},{4,5},{7,6},{5,4},{6,7},{8,9},{11,10},{9,8... | collective-permute-start | bytes 3145736 | tf_op jit(solution)/shard_map/ppermute | solution.py:786
  304.2 23.8 %collective-permute-start.33 = (bf16[4096,128]{1,0:T(8,128)(2,1)S(1)}, bf16[4096,128]{1,0:T(8,128)(2,1)}, u32[]{:S(2)}, u32[]{:S(2)}) collective-permute-start(bf16[4096,128]{1,0:T(8,128)(2,1)S(1)} %add_convert_fusion.12), channel_id=1, source_target_pairs={{1,2},{2,1},{5,6},{6,5},{9,10},{10,9},{13,14},{14,13},{17,18},{18,... | collective-permute-start | bytes 3145736 | tf_op jit(solution)/shard_map/ppermute | solution.py:783
  330.0 26.6 %collective-permute-start.34 = (bf16[4096,128]{1,0:T(8,128)(2,1)S(1)}, bf16[4096,128]{1,0:T(8,128)(2,1)S(1)}, u32[]{:S(2)}, u32[]{:S(2)}) collective-permute-start(bf16[4096,128]{1,0:T(8,128)(2,1)S(1)} %fusion.2), channel_id=1, source_target_pairs={{0,1},{3,2},{1,0},{2,3},{4,5},{7,6},{5,4},{6,7},{8,9},{11,10},{9,8... | collective-permute-start | bytes 3145736 | tf_op jit(solution)/shard_map/ppermute | solution.py:786
  335.1 21.6 %collective-permute-start.32 = (bf16[4096,128]{1,0:T(8,128)(2,1)S(1)}, bf16[4096,128]{1,0:T(8,128)(2,1)S(1)}, u32[]{:S(2)}, u32[]{:S(2)}) collective-permute-start(bf16[4096,128]{1,0:T(8,128)(2,1)S(1)} %add_convert_fusion.10), channel_id=1, source_target_pairs={{1,2},{2,1},{5,6},{6,5},{9,10},{10,9},{13,14},{14,13},{17,18},{18,... | collective-permute-start | bytes 3145736 | tf_op jit(solution)/shard_map/ppermute | solution.py:783
  357.6 6.3 %collective-permute-start.37 = (f32[4,1728]{1,0:T(4,128)S(1)}, f32[4,1728]{1,0:T(4,128)S(1)}, u32[]{:S(2)}, u32[]{:S(2)}) collective-permute-start(f32[4,1728]{1,0:T(4,128)S(1)} %slice.142), channel_id=1, source_target_pairs={{0,4},{4,0},{8,12},{12,8},{16,20},{20,16},{24,28},{28,24},{1,5},{5... | collective-permute-start | bytes 82952 | tf_op jit(solution)/shard_map/ppermute | solution.py:47
  357.7 29.3 %collective-permute-start.35 = (bf16[4096,128]{1,0:T(8,128)(2,1)S(1)}, bf16[4096,128]{1,0:T(8,128)(2,1)S(1)}, u32[]{:S(2)}, u32[]{:S(2)}) collective-permute-start(bf16[4096,128]{1,0:T(8,128)(2,1)S(1)} %fusion.3), channel_id=1, source_target_pairs={{0,1},{3,2},{1,0},{2,3},{4,5},{7,6},{5,4},{6,7},{8,9},{11,10},{9,8... | collective-permute-start | bytes 3145736 | tf_op jit(solution)/shard_map/ppermute | solution.py:786
  363.2 23.8 %collective-permute-start.36 = (bf16[4096,128]{1,0:T(8,128)(2,1)S(1)}, bf16[4096,128]{1,0:T(8,128)(2,1)S(1)}, u32[]{:S(2)}, u32[]{:S(2)}) collective-permute-start(bf16[4096,128]{1,0:T(8,128)(2,1)S(1)} %add_convert_fusion.7), channel_id=1, source_target_pairs={{1,2},{2,1},{5,6},{6,5},{9,10},{10,9},{13,14},{14,13},{17,18},{18,... | collective-permute-start | bytes 3145736 | tf_op jit(solution)/shard_map/ppermute | solution.py:783
  364.0 15.6 %collective-permute-start.38 = (f32[2,1728]{1,0:T(2,128)S(1)}, f32[2,1728]{1,0:T(2,128)S(1)}, u32[]{:S(2)}, u32[]{:S(2)}) collective-permute-start(f32[2,1728]{1,0:T(2,128)S(1)} %slice.182), channel_id=1, source_target_pairs={{0,16},{4,20},{8,24},{12,28},{16,0},{20,4},{24,8},{28,12},{1,17},{... | collective-permute-start | bytes 41480 | tf_op jit(solution)/shard_map/ppermute | solution.py:47
  388.3 33.5 %collective-permute-start.40 = (bf16[4096,128]{1,0:T(8,128)(2,1)}, bf16[4096,128]{1,0:T(8,128)(2,1)}, u32[]{:S(2)}, u32[]{:S(2)}) collective-permute-start(bf16[4096,128]{1,0:T(8,128)(2,1)} %add_convert_fusion.6), channel_id=1, source_target_pairs={{1,2},{2,1},{5,6},{6,5},{9,10},{10,9},{13,14},{14,13},{17,18},{18,... | collective-permute-start | bytes 3145736 | tf_op jit(solution)/shard_map/ppermute | solution.py:783
  391.6 30.2 %collective-permute-start.41 = (bf16[4096,128]{1,0:T(8,128)(2,1)}, bf16[4096,128]{1,0:T(8,128)(2,1)}, u32[]{:S(2)}, u32[]{:S(2)}) collective-permute-start(bf16[4096,128]{1,0:T(8,128)(2,1)} %fusion.4.settled), channel_id=1, source_target_pairs={{0,1},{3,2},{1,0},{2,3},{4,5},{7,6},{5,4},{6,7},{8,9},{11,10},{9,8... | collective-permute-start | bytes 3145736 | tf_op jit(solution)/shard_map/ppermute | solution.py:786
  425.8 24.4 %collective-permute-start.42 = (bf16[4112,128]{1,0:T(8,128)(2,1)}, bf16[4112,128]{1,0:T(8,128)(2,1)}, u32[]{:S(2)}, u32[]{:S(2)}) collective-permute-start(bf16[4112,128]{1,0:T(8,128)(2,1)} %pad_select_fusion.settled), channel_id=1, source_target_pairs={{0,1},{3,2},{1,0},{2,3},{4,5},{7,6},{5,4},{6,7},{8,9},{11,10},{9,8... | collective-permute-start | bytes 3158024 | tf_op jit(solution)/shard_map/ppermute | solution.py:786
  429.2 23.6 %collective-permute-start.44 = (bf16[4096,128]{1,0:T(8,128)(2,1)}, bf16[4096,128]{1,0:T(8,128)(2,1)}, u32[]{:S(2)}, u32[]{:S(2)}) collective-permute-start(bf16[4096,128]{1,0:T(8,128)(2,1)} %add_convert_fusion.3), channel_id=1, source_target_pairs={{1,2},{2,1},{5,6},{6,5},{9,10},{10,9},{13,14},{14,13},{17,18},{18,... | collective-permute-start | bytes 3145736 | tf_op jit(solution)/shard_map/ppermute | solution.py:783
  452.0 28.9 %collective-permute-start.43 = (bf16[4112,128]{1,0:T(8,128)(2,1)S(1)}, bf16[4112,128]{1,0:T(8,128)(2,1)S(1)}, u32[]{:S(2)}, u32[]{:S(2)}) collective-permute-start(bf16[4112,128]{1,0:T(8,128)(2,1)S(1)} %add_convert_fusion.1), channel_id=1, source_target_pairs={{1,2},{2,1},{5,6},{6,5},{9,10},{10,9},{13,14},{14,13},{17,18},{18,... | collective-permute-start | bytes 3158024 | tf_op jit(solution)/shard_map/ppermute | solution.py:783
  454.6 26.4 %collective-permute-start.45 = (bf16[4096,128]{1,0:T(8,128)(2,1)S(1)}, bf16[4096,128]{1,0:T(8,128)(2,1)S(1)}, u32[]{:S(2)}, u32[]{:S(2)}) collective-permute-start(bf16[4096,128]{1,0:T(8,128)(2,1)S(1)} %add_convert_fusion.2.settled), channel_id=1, source_target_pairs={{1,0},{2,3},{5,4},{6,7},{9,8},{10,11},{13,12},{14,15},{17,16},{18,... | collective-permute-start | bytes 3145736 | tf_op jit(solution)/shard_map/ppermute | solution.py:786
  481.3 23.2 %collective-permute-start.46 = (bf16[4112,128]{1,0:T(8,128)(2,1)S(1)}, bf16[4112,128]{1,0:T(8,128)(2,1)S(1)}, u32[]{:S(2)}, u32[]{:S(2)}) collective-permute-start(bf16[4112,128]{1,0:T(8,128)(2,1)S(1)} %add_convert_fusion.settled), channel_id=1, source_target_pairs={{1,0},{2,3},{5,4},{6,7},{9,8},{10,11},{13,12},{14,15},{17,16},{18,... | collective-permute-start | bytes 3158024 | tf_op jit(solution)/shard_map/ppermute | solution.py:786
  (52 other events, 574.3 us)
Sparse Core Ops, SparseCore 0:
  267.4 82.7 reduce-scatter.2
  410.2 102.9 reduce-scatter.4

commit v3 on v2

--- a/solution.py
+++ b/solution.py
@@ -249,30 +249,60 @@
     )(two_a, two_b, bias, *parts)
 
 
-def branch_kernel(attended, active, mine, theirs, out):
-    depth = attended.shape[1]
+def branch_kernel(attended, active, dense_a, dense_b, mine, theirs, out):
     slabs = BLOCK // 128
-    for number, weight in enumerate((mine, theirs)):
-        full = (mul(attended[...], weight[:depth]) + mul(active[...], weight[depth:])).astype(bf16)
+    for number, (dense, weight) in enumerate(((dense_a, mine), (dense_b, theirs))):
+        full = mul(active[...], weight[...])
+        for at in range(0, attended.shape[1], BLOCK):
+            full = full + mul(attended[:, at : at + BLOCK], dense[:, at : at + BLOCK])
+        full = full.astype(bf16)
         for slab in range(slabs):
             out[number * slabs + slab] = full[:, slab * 128 : (slab + 1) * 128]
 
 
-def branch_piece(attended, active, mine, theirs, tile=512):
-    rows = attended.shape[0]
-    depth = mine.shape[0]
+def branch_piece(attended, active, w_a, w_b, pair, place, tile=512):
+    rows, turned = attended.shape
     slabs = 2 * BLOCK // 128
     row = lambda a: pl.BlockSpec((tile, a.shape[1]), lambda i: (i, 0))
+    dense = pl.BlockSpec((BLOCK, turned), lambda i: (place, w_a.shape[1] // turned - 1))
     return pl.pallas_call(
         branch_kernel,
         grid=(rows // tile,),
-        in_specs=[row(attended), row(active), whole_spec(mine), whole_spec(theirs)],
+        in_specs=[row(attended), row(active), dense, dense, whole_spec(pair[0]), whole_spec(pair[1])],
         out_specs=pl.BlockSpec((slabs, tile, 128), lambda i: (0, i, 0)),
         out_shape=jax.ShapeDtypeStruct((slabs, rows, 128), bf16),
         compiler_params=params(),
-        cost_estimate=cost(4 * rows * depth * BLOCK, 2 * (rows * depth + 2 * (rows + depth) * BLOCK)),
+        cost_estimate=cost(0, 0),
         name="branch",
-    )(attended, active, mine, theirs)
+    )(attended, active, w_a, w_b, *pair)
+
+
+def dense_kernel(up_a, up_b, w_a, w_b, out, joined):
+    for place in range(BLOCKS):
+        ref = w_a if place < HALF else w_b
+        rows = slice(place % HALF * BLOCK, (place % HALF + 1) * BLOCK)
+        for at in range(0, out.shape[1], BLOCK):
+            joined[at : at + BLOCK, place * BLOCK : (place + 1) * BLOCK] = ref[rows, at : at + BLOCK]
+    half = up_a.shape[1]
+    for start in range(0, out.shape[0], 512):
+        at = slice(start, start + 512)
+        out[at] = (mul(up_a[at], joined[:, :half], NT) + mul(up_b[at], joined[:, half:], NT)).astype(bf16)
+
+
+def dense_back(up_a, up_b, w_a, w_b, turned):
+    rows, half = up_a.shape
+    dense = pl.BlockSpec((half, turned), lambda i: (0, w_a.shape[1] // turned - 1))
+    return pl.pallas_call(
+        dense_kernel,
+        grid=(1,),
+        in_specs=[whole_spec(up_a), whole_spec(up_b), dense, dense],
+        out_specs=pl.BlockSpec((rows, turned), lambda i: (0, 0)),
+        out_shape=jax.ShapeDtypeStruct((rows, turned), bf16),
+        scratch_shapes=[pltpu.VMEM((turned, 2 * half), bf16)],
+        compiler_params=params(),
+        cost_estimate=cost(0, 0),
+        name="dense_back",
+    )(up_a, up_b, w_a, w_b)
 
 
 def back_kernel(up_a, up_b, blocks, slope, out, sums, joined):
@@ -322,20 +352,35 @@
 
 
 def second_kernel(grad, *refs):
-    *parts, out, weight = refs
-    tile = weight.shape[0]
-    taken, size = [[]], 0
-    for part in parts:
-        for start in range(0, part.shape[0], tile):
-            if size == tile:
-                taken.append([])
-                size = 0
-            rows = min(tile, part.shape[0] - start)
-            taken[-1].append(part.at[start : start + rows])
-            size += rows
-    for number, runs in enumerate(taken):
-        pl.when(pl.program_id(0) == number)(functools.partial(lay, runs, weight))
-    out[...] = mul(grad[...], weight[...], NT).astype(bf16)
+    count = len(refs) - 3
+    parts, out, weight, arrived = refs[:count], *refs[count:]
+    tile = out.shape[1]
+    step = pl.program_id(0)
+    copies, ends, at = [], [], 0
+    for number, part in enumerate(parts):
+        to = weight.at[at : at + part.shape[0]]
+        copies.append(pltpu.make_async_copy(part, to, arrived.at[number]))
+        at += part.shape[0]
+        ends.append(at)
+
+    @pl.when(step == 0)
+    def _():
+        for copy in copies:
+            copy.start()
+
+    for number in range(weight.shape[0] // tile):
+
+        @pl.when(step == number)
+        def _(number=number):
+            before = 0
+            for copy, end in zip(copies, ends):
+                last_needed_at = before // tile
+                if last_needed_at == number:
+                    copy.wait()
+                before = end
+
+    rows = pl.ds(pl.multiple_of(step * tile, tile), tile)
+    out[...] = mul(grad[...], weight[rows], NT).astype(bf16)
 
 
 def second_back(grad, parts, tile=512):
@@ -344,10 +389,10 @@
     return pl.pallas_call(
         second_kernel,
         grid=(depth // tile,),
-        in_specs=[whole_spec(grad)] + [whole_spec(part) for part in parts],
+        in_specs=[whole_spec(grad)] + [pl.BlockSpec(memory_space=pl.ANY)] * len(parts),
         out_specs=pl.BlockSpec((rows, tile), lambda n: (0, n)),
         out_shape=jax.ShapeDtypeStruct((rows, depth), bf16),
-        scratch_shapes=[pltpu.VMEM((tile, width), bf16)],
+        scratch_shapes=[pltpu.VMEM((depth, width), bf16), pltpu.SemaphoreType.DMA((len(parts),))],
         compiler_params=params(),
         cost_estimate=cost(2 * rows * depth * width, 2 * (rows + depth) * width + 2 * rows * depth),
         name="second_back",
@@ -578,7 +623,7 @@
         out_shape=[
             jax.ShapeDtypeStruct((rows, width), bf16),
             jax.ShapeDtypeStruct(left.shape, bf16),
-            jax.ShapeDtypeStruct(own.shape, f32),
+            jax.ShapeDtypeStruct(own.shape, bf16),
             jax.ShapeDtypeStruct(right.shape, bf16),
         ],
         compiler_params=params(),
@@ -591,7 +636,7 @@
     rows = dq.shape[0]
     near = earlier.shape[0]
     out[:, :HD] = dq[...]
-    pairs = own[...] + later[...].astype(f32)
+    pairs = own[...].astype(f32) + later[...].astype(f32)
     top = pairs[:near] + earlier[...].astype(f32)
     for at, part in ((slice(0, near), top), (slice(near, rows), pairs[near:])):
         out[at, HD : HD + 128] = turn(part[:, :128], cos[at], sin[at], -1).astype(bf16)
@@ -621,7 +666,8 @@
     )(dq, own, later, earlier, cos, sin)
 
 
-def input_kernel(mixed, w_a, w_b, second, tok, mean, inverse, gains, out_a, out_b, sums):
+def input_kernel(mixed, w_a, w_b, second, tok, mean, inverse, gains, *outs):
+    *outs, sums = outs
     step = pl.program_id(0)
     half = w_a.shape[0]
     grad_a = mul(mixed[...], w_a[...], NT)
@@ -649,32 +695,37 @@
         pieces.append((at, both, normed))
     total = total * (0.5 / half)
     product = product * (0.5 / half)
-    for ref, chosen in ((out_a, step == 0), (out_b, step == 1)):
-
-        @pl.when(chosen)
-        def _(ref=ref):
-            for at, both, normed in pieces:
-                grad = (scale * (both - total - normed * product)).astype(bf16)
-                for slab in range(half // 128):
-                    ref[at.start // 128 + slab] = grad[:, slab * 128 : (slab + 1) * 128]
-
-
-def input_back(mixed, w_a, w_b, second, tok, mean, inverse, gains, start, tile=256):
+
+    def store(ref):
+        for at, both, normed in pieces:
+            grad = (scale * (both - total - normed * product)).astype(bf16)
+            for slab in range(half // 128):
+                ref[at.start // 128 + slab] = grad[:, slab * 128 : (slab + 1) * 128]
+
+    if len(outs) == 1:
+        store(outs[0])
+    else:
+        for number, ref in enumerate(outs):
+            pl.when(step == number)(functools.partial(store, ref))
+
+
+def input_back(mixed, w_a, w_b, second, tok, mean, inverse, gains, start, count, tile=256):
     width = tok.shape[1]
     depth = mixed.shape[1]
     row = lambda w: pl.BlockSpec((tile, w), lambda i: (i + start, 0))
+    weight = pl.BlockSpec((w_a.shape[0], depth), lambda i: (0, 0))
     slabs = (width // 128, tile, 128)
     out = pl.BlockSpec(slabs, lambda i: (0, 0, 0))
     return pl.pallas_call(
         input_kernel,
-        grid=(2,),
+        grid=(count,),
         in_specs=[
-            row(depth), whole_spec(w_a), whole_spec(w_b), row(width), row(width), row(1), row(1), whole_spec(gains),
+            row(depth), weight, weight, row(width), row(width), row(1), row(1), whole_spec(gains),
         ],
-        out_specs=[out, out, pl.BlockSpec((8, width), lambda i: (0, 0))],
-        out_shape=[jax.ShapeDtypeStruct(slabs, bf16)] * 2 + [jax.ShapeDtypeStruct((8, width), f32)],
-        compiler_params=params(),
-        cost_estimate=cost(4 * tile * depth * width, 14_000_000),
+        out_specs=[out] * count + [pl.BlockSpec((8, width), lambda i: (0, 0))],
+        out_shape=[jax.ShapeDtypeStruct(slabs, bf16)] * count + [jax.ShapeDtypeStruct((8, width), f32)],
+        compiler_params=params(),
+        cost_estimate=cost(2 * count * tile * depth * width, 14_000_000),
         name="input_back",
     )(mixed, w_a, w_b, second, tok, mean, inverse, gains)
 
@@ -792,12 +843,12 @@
 
 def scatter_blocks(blocks, by_rows):
     if is_cube():
-        return lax.psum_scatter(blocks, "dp", scatter_dimension=0, tiled=True)[0].astype(f32)
+        return lax.psum_scatter(blocks, "dp", scatter_dimension=0, tiled=True)[0]
     if by_rows:
         full = blocks.reshape(-1, blocks.shape[2])
-        return lax.psum_scatter(full, "dp", scatter_dimension=0, tiled=True).astype(f32)
+        return lax.psum_scatter(full, "dp", scatter_dimension=0, tiled=True)
     full = blocks.transpose(1, 0, 2).reshape(blocks.shape[1], -1)
-    return lax.psum_scatter(full, "dp", scatter_dimension=1, tiled=True).astype(f32)
+    return lax.psum_scatter(full, "dp", scatter_dimension=1, tiled=True)
 
 
 def ring(value, step):
@@ -851,7 +902,6 @@
     line = lax.axis_index("tensor")
     middle = ((line == 1) | (line == 2)).astype(jnp.int32).reshape(1)
 
-    turned_width, hidden_width = dense_weight.shape[0], shrink_weight.shape[0]
     vectors = [first_gain, first_shift, second_gain, second_shift, dense_bias, shrink_bias]
     if cube:
         own = jnp.concatenate([v.reshape(-1).astype(bf16) for v in (*vectors, expand_bias, project_bias)])
@@ -894,12 +944,24 @@
     high = jnp.maximum(token_index, begin + limit - 1) - base
     cos, sin = rotary_tables(token_index - begin)
 
-    spread_project = Spread(project_weight.astype(bf16), True)
-    seen_project = spread_project.first()
-    seen_project_too = spread_project.second(seen_project, gathered)
+    turned_width, hidden_width = dense_weight.shape[0], shrink_weight.shape[0]
+    project_low, dense_low = project_weight.astype(bf16), dense_weight.astype(bf16)
+    if cube:
+        dense_low = dense_low.reshape(-1, BLOCK, BLOCK).transpose(1, 0, 2).reshape(BLOCK, -1)
+        spread_project = Spread(jnp.concatenate([project_low, dense_low], axis=1), True)
+        seen_project = spread_project.first()
+        seen_project_too = spread_project.second(seen_project, gathered)
+    else:
+        seen_project = seen_project_too = ()
     spread_expand = Spread(after(expand_weight.astype(bf16), (gathered, seen_project)), True)
     seen_expand = spread_expand.first()
-    project_a, project_b = spread_project.join(seen_project_too)
+    if cube:
+        project_a, project_b = spread_project.join(seen_project_too, spread_expand.weight)
+    else:
+        dense_full = lax.all_gather(dense_low, "dp", axis=1, tiled=True)
+        dense_full = dense_full.reshape(-1, BLOCK, BLOCKS, BLOCK).transpose(2, 1, 0, 3).reshape(width, -1)
+        both = jnp.concatenate([lax.all_gather(project_low, "dp", axis=0, tiled=True), dense_full], axis=1)
+        project_a, project_b = both[: width // 2], both[width // 2 :]
     tok, one_a, one_b, two_a, two_b, up_a, up_b, mean, inverse, grad_bias = norm(
         places, tokens, upstream, after(gains, project_a)
     )
@@ -910,54 +972,49 @@
     right = ring(sent[:PREFIX_MAX], -1)
     spread_expand.begin_parts(seen_expand_too)
     expand_mine, expand_theirs = spread_expand.parts(pairs)
-    down_weight = jnp.concatenate([dense_weight.astype(bf16), shrink_weight.astype(bf16)], axis=0)
-    spread_down = Spread(after(down_weight, (mean, seen_project)), False)
+    spread_down = Spread(after(shrink_weight.astype(bf16), (mean, seen_project)), False)
     active, slope = expand(after(two_a, sent), two_b, expand_mine + expand_theirs, full_expand_bias)
-    depth = turned_width + hidden_width
-    column_blocks = column_grad(places, active, up_a, up_b, depth, turned_width)
+    grad_attended = dense_back(after(up_a, active), up_b, project_a, project_b, turned_width)
     blocks = [spread_down.pair(0, active)] if cube else []
     spread_down.weight = after(spread_down.weight, (left, active))
     seen_down = spread_down.first()
     if not cube:
         blocks = [spread_down.pair(0)]
-    attended, lse = attend(after(queries, column_blocks), left, pairs, right, low, high)
-
-    line = LineSum(middle)
+    attended, lse = attend(after(queries, grad_attended), left, pairs, right, low, high)
     seen_down_too = spread_down.second(seen_down, attended)
     blocks += [spread_down.pair(place, (attended, seen_down)) for place in range(len(blocks), HALF - 1)]
-    pieces = [branch_piece(attended, active, *blocks[0])]
-    seen = line.slot(pieces[0], ())
-    column_blocks = column_grad(places, after(attended, (pieces[0], seen)), up_a, up_b, depth, 0, column_blocks)
-    blocks.append(spread_down.pair(3, (column_blocks, seen_down_too)))
-    down_blocks = [b for b, _ in blocks] + [b for _, b in blocks]
-    grad_attended = back(after(up_a, column_blocks), up_b, down_blocks, 0, turned_width)
     dq, dleft, down, dright = attend_back(
         queries, left, pairs, right, low, high, lse, attended, grad_attended, cos, sin
     )
     later = ring(dleft, -1)
     earlier = ring(dright, 1)
-    last = dq
-    for place in (1, 2, 3):
-        pieces.append(branch_piece(after(attended, last), active, *blocks[place]))
-        last = pieces[-1]
-        if place == 1:
-            seen = line.slot(pieces[1], last)
-            last = (last, seen)
-    grad_hidden, expand_bias_sums = back(
-        after(up_a, pieces[-1]), up_b, down_blocks, turned_width, hidden_width, slope
-    )
-    column_blocks, later, earlier, grad_hidden = lax.optimization_barrier((column_blocks, later, earlier, grad_hidden))
+    blocks.append(spread_down.pair(3, (dq, seen_down_too)))
+
+    line = LineSum(middle)
+    branch = lambda place, *seen: branch_piece(after(attended, seen), active, project_a, project_b, blocks[place], place)
+    pieces = [branch(0, dq, seen_down_too)]
+    seen = line.slot(pieces[0], ())
+    depth = turned_width + hidden_width
+    pieces.append(branch(1, pieces[0], seen))
+    column_blocks = column_grad(places, after(attended, pieces[1]), up_a, up_b, depth)
+    seen = line.slot(pieces[1], column_blocks)
+    column_blocks = column_grad(places, after(active, seen), up_a, up_b, depth, turned_width, column_blocks)
+    pieces.append(branch(2, column_blocks))
+    seen = line.slot(pieces[2], pieces[2])
+    column_blocks, later, earlier, last = lax.optimization_barrier((column_blocks, later, earlier, pieces[2]))
     grad_down = scatter_blocks(column_blocks, False)
-    seen = line.slot(pieces[2], grad_hidden)
-    grad_second = second_back(after(grad_hidden, seen), expand_mine + expand_theirs)
+    down_blocks = [b for b, _ in blocks] + [b for _, b in blocks]
+    grad_hidden, expand_bias_sums = back(after(up_a, (last, seen)), up_b, down_blocks, 0, hidden_width, slope)
+    pieces.append(branch(3, grad_hidden))
+    seen = line.slot(pieces[3], pieces[3])
+    grad_second = second_back(after(grad_hidden, (pieces[3], seen)), expand_mine + expand_theirs)
     grad_mixed, project_bias_sums = mix(after(dq, grad_second), down, later, earlier, cos, sin)
-    seen = line.slot(pieces[3], grad_mixed)
     *tails, sums = input_back(
-        after(grad_mixed, seen), project_a, project_b, grad_second, tok, mean, inverse, gains, 0
+        grad_mixed, project_a, project_b, grad_second, tok, mean, inverse, gains, 0, 1
     )
     seen = line.slot(tails[0], sums)
     *more, part = input_back(
-        after(grad_mixed, (sums, seen)), project_a, project_b, grad_second, tok, mean, inverse, gains, 2
+        after(grad_mixed, (sums, seen)), project_a, project_b, grad_second, tok, mean, inverse, gains, 1, 3
     )
     tails += more
     sums = sums + part
@@ -974,10 +1031,10 @@
     row_blocks, grad_down, vector = lax.optimization_barrier((row_blocks, grad_down, vector))
     if cube:
         grad_rows = scatter_blocks(row_blocks, True)
-        grad_expand, grad_project = grad_rows[:, : widths[0]], grad_rows[:, widths[0] :]
+        grad_expand, grad_project = grad_rows[:, : widths[0]].astype(f32), grad_rows[:, widths[0] :].astype(f32)
     else:
-        grad_expand = scatter_blocks(row_blocks[:, :, : widths[0]], True)
-        grad_project = scatter_blocks(row_blocks[:, :, widths[0] :], True)
+        grad_expand = scatter_blocks(row_blocks[:, :, : widths[0]], True).astype(f32)
+        grad_project = scatter_blocks(row_blocks[:, :, widths[0] :], True).astype(f32)
     settled, passed = zip(*line.results[:4])
     output = output_sum(places, middle, after(bias_total, (row_blocks, seen)), settled, passed, tokens)
     tail = tails[3]
@@ -991,7 +1048,7 @@
     line.slot(None, tokens_grad)
     for number in range(2, 4):
         tokens_grad = tokens_sum(places, middle, upstream, *line.results[4 + number], number, tokens_grad)
-    grad_dense, grad_shrink = grad_down[:turned_width], grad_down[turned_width:]
+    grad_dense, grad_shrink = grad_down[:turned_width].astype(f32), grad_down[turned_width:].astype(f32)
 
     if cube:
         settled, passed = line.results[7]

time: 534 us -> 525 us (0.983)
  Pallas kernels: 241 us -> 235 us
  blocking collectives: 18.7 us -> 24.3 us
    ppermute x10, waiting for transfers between devices: 68.6 us -> 52.1 us  [slot(): self.inward = lax.ppermute(operand, 'tensor', pairs)]
    reduce_scatter x2, waiting for transfers between devices: 3.67 us -> 11.1 us  [scatter_blocks(): return lax.psum_scatter(blocks, 'dp', scatter_dimension=0, tiled=True)[0]]
    ppermute x25, waiting for transfers between devices: 23 us -> 29.9 us  [swap(): return lax.ppermute(value, 'dp', [(i, i ^ bit) for i in range(count)])]
    ppermute x10, starting transfers between devices: 29.8 us -> 23.6 us  [slot(): self.inward = lax.ppermute(operand, 'tensor', pairs)]
    all_gather x1, blocking collectives: 18.7 us -> 24.3 us  [on_device(): gathered = lax.all_gather(own, 'dp', axis=0).reshape(count, -1)]
    pallas_call x2 -> x3, Pallas kernels: 25.7 us -> 30.3 us  [the longest x2 24.2 us: input_back(): pl.pallas_call(input_kernel, grid=(count,), in_specs=[row(depth), weight,...]
    pallas_call x2 -> x1, Pallas kernels: 20.6 us -> 16.6 us  [back(): pl.pallas_call(body, grid=(width // tile,), in_specs=[whole_spec(up_a), w...]
    unnamed x121 -> x122, local copies, waits for them, and re-layouts: 11.7 us -> 14.2 us
  transfers between devices with their start and end apart: 49 -> 49, of which waited for: 15 -> 15; matrix products, arithmetic and copies ran while one was open for 11% -> 10% of each run, Pallas kernels for 46% -> 46%
where the time goes in v3:
time: 525 us; the launch traced here: 516 us
  Pallas kernels  235 us (45%)
  waiting for transfers between devices  93.2 us (18%)
  starting transfers between devices  78.9 us (15%)
  other arithmetic  42.5 us (8%)
  local copies, waits for them, and re-layouts  26.3 us (5%)
  blocking collectives  24.3 us (5%)
  between operations  15.6 us (3%)
    ppermute x10, waiting for transfers between devices, slot(): self.inward = lax.ppermute(operand, 'tensor', pairs)  52.1 us
    ppermute x25, starting transfers between devices, swap(): return lax.ppermute(value, 'dp', [(i, i ^ bit) for i in range(count)])  34.4 us
    ppermute x25, waiting for transfers between devices, swap(): return lax.ppermute(value, 'dp', [(i, i ^ bit) for i in range(count)])  29.9 us
    pallas_call x2, Pallas kernels, row_grad(): pl.pallas_call(row_grad_kernel, grid_spec=pltpu.PrefetchScalarGridSpec(nu...  26 us
    pallas_call x4, Pallas kernels, branch_piece(): pl.pallas_call(branch_kernel, grid=(rows // tile,), in_specs=[row(attende...  25.5 us
    all_gather x1, blocking collectives, on_device(): gathered = lax.all_gather(own, 'dp', axis=0).reshape(count, -1)  24.3 us
    pallas_call x2, Pallas kernels, input_back(): pl.pallas_call(input_kernel, grid=(count,), in_specs=[row(depth), weight,...  24.2 us
    ppermute x10, starting transfers between devices, slot(): self.inward = lax.ppermute(operand, 'tensor', pairs)  23.6 us
  transfers between devices with their start and end apart: 49, of which 15 were waited for; matrix products, arithmetic and copies ran while one was open for 10% of the time, Pallas kernels for 46%

profile of v3, /device:TPU:0, one launch (start us, length us, event | category | flops | bytes accessed | tf_op | source)
XLA Modules:
  0.0 515.9 jit_solution(12670123830030992869)
XLA Ops:
  9.1 3.0 collective-permute-start
  15.4 24.3 %all_gather.3 = bf16[8,16,128]{2,1,0:T(8,128)(2,1)S(1)} all-gather(bf16[1,16,128]{2,1,0:T(8,128)(2,1)S(1)} %pad_bitcast_fusion), channel_id=1, replica_groups=mesh['dp'=8,'tensor'=4] {'dp'}, dimensions={0}, use_global_device_ids=true | all-gather | bytes 36864 | tf_op jit(solution)/shard_map/all_gather | solution.py:909
  43.4 10.7 %collective-permute-done.2 = bf16[128,2048]{1,0:T(8,128)(2,1)S(1)} collective-permute-done((bf16[128,2048]{1,0:T(8,128)(2,1)S(1)}, bf16[128,2048]{1,0:T(8,128)(2,1)S(1)}, u32[]{:S(2)}, u32[]{:S(2)}) %collective-permute-start.2) | collective-permute-done | bytes 524320 | tf_op jit(solution)/shard_map/ppermute | solution.py:47
  66.5 3.1 fusion.7
  69.6 12.0 %norm.1 = (bf16[1024,2048]{1,0:T(8,128)(2,1)}, bf16[1024,1024]{1,0:T(8,128)(2,1)}, bf16[1024,1024]{1,0:T(8,128)(2,1)}, bf16[1024,1024]{1,0:T(8,128)(2,1)}, bf16[...) custom-call(s32[8]{0:T(128)} %fusion.16.places.where, ...), custom_call_target="tpu_custom_call" | custom-call | flops 41943040 | bytes 41943040 | tf_op jit(solution)/shard_map/norm/pallas_call | solution.py:151
  81.6 5.7 %collective-permute-done.4.refs_1_ = bf16[256,2048]{1,0:T(8,128)(2,1)S(1)} collective-permute-done((bf16[256,2048]{1,0:T(8,128)(2,1)S(1)}, bf16[256,2048]{1,0:T(8,128)(2,1)S(1)}, u32[]{:S(2)}, u32[]{:S(2)}) %collective-permute-start.4) | collective-permute-done | bytes 1048608 | tf_op jit(solution)/shard_map/ppermute | solution.py:47
  91.7 11.4 %project.1 = (bf16[1024,512]{1,0:T(8,128)(2,1)}, bf16[1024,1024]{1,0:T(8,128)(2,1)}) custom-call(bf16[1024,1024]{1,0:T(8,128)(2,1)} %get-tuple-element.130.one_a.left_a, bf16[1024,1024]{1,0:T(8,128)(2,1)} %get-tuple-element.129.one_b.left_b, bf16[1024,2048]{1,0:T(8,128)(2,1)} %constant_dynamic-update-slice_fusion.w_a.dense_a, ...), custom_call_target="tpu_custom_call" | custom-call | flops 8589934592 | bytes 14000000 | tf_op jit(solution)/shard_map/project/pallas_call | solution.py:192
  104.2 2.6 collective-permute-start.9
  118.5 16.9 %expand.1 = (bf16[1024,2048]{1,0:T(8,128)(2,1)}, bf16[1024,2048]{1,0:T(8,128)(2,1)}) custom-call(bf16[1024,1024]{1,0:T(8,128)(2,1)} %get-tuple-element.138.two_a.left_a, bf16[1024,1024]{1,0:T(8,128)(2,1)} %get-tuple-element.139.two_b.left_b, f32[1,2048]{1,0:T(1,128)} %bitcast.127, bf16[256,2048]{1,0:T(8,128)(2,1)} %copy-done.8, ...), custom_call_target="tpu_custom_call" | custom-call | tf_op jit(solution)/shard_map/expand/pallas_call | solution.py:239
  136.7 12.0 %collective-permute-start.17 = (bf16[2048,256]{1,0:T(8,128)(2,1)S(1)}, bf16[2048,256]{1,0:T(8,128)(2,1)S(1)}, u32[]{:S(2)}, u32[]{:S(2)}) collective-permute-start(bf16[2048,256]{1,0:T(8,128)(2,1)S(1)} %convert_element_type.251.mine.rest_0_), channel_id=1, source_target_pairs={{0,16},{4,20},{8,24},{12,28},{16,0},{20,4},{24,8},{28,12},{1,17},{... | collective-permute-start | bytes 3145736 | tf_op jit(solution)/shard_map/ppermute | solution.py:47
  149.9 6.1 %dense_back.1.grad = bf16[1024,512]{1,0:T(8,128)(2,1)} custom-call(bf16[1024,1024]{1,0:T(8,128)(2,1)} %get-tuple-element.218.up_a.right_a.a.rest_0_, bf16[1024,1024]{1,0:T(8,128)(2,1)} %get-tuple-element.147.up_b.right_b.b, bf16[1024,2048]{1,0:T(8,128)(2,1)} %constant_dynamic-update-slice_fusion.w_a.dense_a, ...), custom_call_target="tpu_custom_call" | custom-call | tf_op jit(solution)/shard_map/dense_back/pallas_call | solution.py:295
  156.0 11.9 %attend.1 = (bf16[1024,512]{1,0:T(8,128)(2,1)}, f32[2,1,1024]{2,1,0:T(1,128)}) custom-call(s32[4]{0:T(128)} %get-tuple-element.249.first, s32[4]{0:T(128)} %get-tuple-element.248.last, bf16[1024,512]{1,0:T(8,128)(2,1)} %get-tuple-element.148.q, bf16[1024,1024]{1,0:T(8,128)(2,1)} %collective-permute-done.9.left, bf16[1024,1024]{1,0:T(8,128)(2,1)} %get-tuple-element.135.own, ...), custom_call_target="tpu_custom_call" | custom-call | flops 8000000000 | bytes 10000000 | tf_op jit(solution)/shard_map/attend/pallas_call | solution.py:522
  168.0 3.7 collective-permute-done.17.mine.rest_2_
  172.4 18.3 %attend_back.1 = (bf16[1024,512]{1,0:T(8,128)(2,1)}, bf16[1024,1024]{1,0:T(8,128)(2,1)}, bf16[1024,1024]{1,0:T(8,128)(2,1)}, bf16[512,1024]{1,0:T(8,128)(2,1)}) custom-call(s32[4]{0:T(128)} %get-tuple-element.249.first, s32[4]{0:T(128)} %get-tuple-element.248.last, bf16[1024,512]{1,0:T(8,128)(2,1)} %get-tuple-element.148.q, ...), custom_call_target="tpu_custom_call" | custom-call | flops 16000000000 | bytes 20000000 | tf_op jit(solution)/shard_map/attend_back/pallas_call | solution.py:605
  191.8 6.4 %branch.4 = bf16[4,1024,128]{2,1,0:T(8,128)(2,1)} custom-call(bf16[1024,512]{1,0:T(8,128)(2,1)} %get-tuple-element.174.attended.left, bf16[1024,2048]{1,0:T(8,128)(2,1)} %get-tuple-element.164.active.left, bf16[1024,2048]{1,0:T(8,128)(2,1)} %constant_dynamic-update-slice_fusion.w_a.dense_a, bf16[1024,2048]{1,0:T(8,128)(2,1)} %collective-permute-done.6.w_b.dense_b, ...), custom_call_target="tpu_custom_call" | custom-call | tf_op jit(solution)/shard_map/branch/pallas_call | solution.py:268
  198.2 3.5 collective-permute-start.23
  203.0 5.9 %collective-permute-start.30 = (bf16[512,1024]{1,0:T(8,128)(2,1)}, bf16[512,1024]{1,0:T(8,128)(2,1)}, u32[]{:S(2)}, u32[]{:S(2)}) collective-permute-start(bf16[512,1024]{1,0:T(8,128)(2,1)} %get-tuple-element.182), channel_id=1, source_target_pairs={{0,4},{4,8},{8,12},{12,16},{16,20},{20,24},{24,28},{1,5},{5,9},{9,... | collective-permute-start | bytes 3145736 | tf_op jit(solution)/shard_map/ppermute | solution.py:857
  210.8 6.3 %branch.5 = bf16[4,1024,128]{2,1,0:T(8,128)(2,1)} custom-call(bf16[1024,512]{1,0:T(8,128)(2,1)} %get-tuple-element.174.attended.left, bf16[1024,2048]{1,0:T(8,128)(2,1)} %get-tuple-element.164.active.left, bf16[1024,2048]{1,0:T(8,128)(2,1)} %constant_dynamic-update-slice_fusion.w_a.dense_a, bf16[1024,2048]{1,0:T(8,128)(2,1)} %collective-permute-done.6.w_b.dense_b, ...), custom_call_target="tpu_custom_call" | custom-call | tf_op jit(solution)/shard_map/branch/pallas_call | solution.py:268
  217.2 7.1 %column_grad.2.rest_0_ = bf16[8,2560,256]{2,1,0:T(8,128)(2,1)} custom-call(s32[8]{0:T(128)} %fusion.16.places.where, bf16[1024,512]{1,0:T(8,128)(2,1)} %get-tuple-element.174.attended.left, bf16[1024,1024]{1,0:T(8,128)(2,1)} %get-tuple-element.218.up_a.right_a.a.rest_0_, bf16[1024,1024]{1,0:T(8,128)(2,1)} %get-tuple-element.147.up_b.right_b.b), custom_call_target="tpu_custom_call" | custom-call | tf_op jit(solution)/shard_map/column_grad/pallas_call | solution.py:443
  232.6 14.5 %column_grad.3 = bf16[8,2560,256]{2,1,0:T(8,128)(2,1)} custom-call(s32[8]{0:T(128)} %fusion.16.places.where, bf16[1024,2048]{1,0:T(8,128)(2,1)} %get-tuple-element.164.active.left, bf16[1024,1024]{1,0:T(8,128)(2,1)} %get-tuple-element.218.up_a.right_a.a.rest_0_, ...), custom_call_target="tpu_custom_call", output_to_operand_aliasing={{}: (4, {})} | custom-call | tf_op jit(solution)/shard_map/column_grad/pallas_call | solution.py:443
  247.2 6.4 %branch.6 = bf16[4,1024,128]{2,1,0:T(8,128)(2,1)} custom-call(bf16[1024,512]{1,0:T(8,128)(2,1)} %get-tuple-element.174.attended.left, bf16[1024,2048]{1,0:T(8,128)(2,1)} %get-tuple-element.164.active.left, bf16[1024,2048]{1,0:T(8,128)(2,1)} %constant_dynamic-update-slice_fusion.w_a.dense_a, bf16[1024,2048]{1,0:T(8,128)(2,1)} %collective-permute-done.6.w_b.dense_b, ...), custom_call_target="tpu_custom_call" | custom-call | tf_op jit(solution)/shard_map/branch/pallas_call | solution.py:268
  254.8 2.6 fusion
  263.0 16.6 %back.1 = (bf16[1024,2048]{1,0:T(8,128)(2,1)}, f32[1,2048]{1,0:T(1,128)}) custom-call(bf16[1024,1024]{1,0:T(8,128)(2,1)} %get-tuple-element.218.up_a.right_a.a.rest_0_, bf16[1024,1024]{1,0:T(8,128)(2,1)} %get-tuple-element.147.up_b.right_b.b, bf16[2048,256]{1,0:T(8,128)(2,1)} %copy-done.2, bf16[2048,256]{1,0:T(8,128)(2,1)} %copy-done.9, ...), custom_call_target="tpu_custom_call" | custom-call | flops 8589934592 | bytes 20971520 | tf_op jit(solution)/shard_map/back/pallas_call | solution.py:341
  279.5 6.4 %branch.7 = bf16[4,1024,128]{2,1,0:T(8,128)(2,1)} custom-call(bf16[1024,512]{1,0:T(8,128)(2,1)} %get-tuple-element.174.attended.left, bf16[1024,2048]{1,0:T(8,128)(2,1)} %get-tuple-element.164.active.left, bf16[1024,2048]{1,0:T(8,128)(2,1)} %constant_dynamic-update-slice_fusion.w_a.dense_a, bf16[1024,2048]{1,0:T(8,128)(2,1)} %collective-permute-done.6.w_b.dense_b, ...), custom_call_target="tpu_custom_call" | custom-call | tf_op jit(solution)/shard_map/branch/pallas_call | solution.py:268
  286.0 2.6 fusion.1
  293.2 14.7 %second_back.1.second = bf16[1024,2048]{1,0:T(8,128)(2,1)} custom-call(bf16[1024,2048]{1,0:T(8,128)(2,1)} %get-tuple-element.199.grad.right, bf16[256,2048]{1,0:T(8,128)(2,1)} %copy-done.8, bf16[256,2048]{1,0:T(8,128)(2,1)} %copy-done.15, bf16[256,2048]{1,0:T(8,128)(2,1)} %collective-permute-done.5.refs_2_, ...), custom_call_target="tpu_custom_call" | custom-call | flops 8589934592 | bytes 16777216 | tf_op jit(solution)/shard_map/second_back/pallas_call | solution.py:389
  307.9 4.9 mix.1
  314.2 7.5 %input_back.2 = (bf16[16,256,128]{2,1,0:T(8,128)(2,1)}, f32[8,2048]{1,0:T(8,128)}) custom-call(bf16[1024,1536]{1,0:T(8,128)(2,1)} %get-tuple-element.204.mixed.right, bf16[1024,2048]{1,0:T(8,128)(2,1)} %constant_dynamic-update-slice_fusion.w_a.dense_a, bf16[1024,2048]{1,0:T(8,128)(2,1)} %collective-permute-done.6.w_b.dense_b, ...), custom_call_target="tpu_custom_call" | custom-call | flops 1610612736 | bytes 14000000 | tf_op jit(solution)/shard_map/input_back/pallas_call | solution.py:719
  326.6 16.7 %input_back.3 = (bf16[16,256,128]{2,1,0:T(8,128)(2,1)}, bf16[16,256,128]{2,1,0:T(8,128)(2,1)}, bf16[16,256,128]{2,1,0:T(8,128)(2,1)}, f32[8,2048]{1,0:T(8,128)}) custom-call(bf16[1024,1536]{1,0:T(8,128)(2,1)} %get-tuple-element.204.mixed.right, bf16[1024,2048]{1,0:T(8,128)(2,1)} %constant_dynamic-update-slice_fusion.w_a.dense_a, ...), custom_call_target="tpu_custom_call" | custom-call | flops 4831838208 | bytes 14000000 | tf_op jit(solution)/shard_map/input_back/pallas_call | solution.py:719
  344.3 4.4 collective-permute-done.34
  349.8 4.0 collective-permute-start.35
  354.8 5.4 %collective-permute-start.38 = (f32[2,1728]{1,0:T(2,128)S(1)}, f32[2,1728]{1,0:T(2,128)S(1)}, u32[]{:S(2)}, u32[]{:S(2)}) collective-permute-start(f32[2,1728]{1,0:T(2,128)S(1)} %slice.182), channel_id=1, source_target_pairs={{0,16},{4,20},{8,24},{12,28},{16,0},{20,4},{24,8},{28,12},{1,17},{... | collective-permute-start | bytes 41480 | tf_op jit(solution)/shard_map/ppermute | solution.py:47
  360.2 14.2 %row_grad.2.rest_0_ = bf16[8,256,3584]{2,1,0:T(8,128)(2,1)} custom-call(s32[8]{0:T(128)} %fusion.16.places.where, bf16[1024,1024]{1,0:T(8,128)(2,1)} %get-tuple-element.138.two_a.left_a, bf16[1024,1024]{1,0:T(8,128)(2,1)} %get-tuple-element.139.two_b.left_b, bf16[1024,2048]{1,0:T(8,128)(2,1)} %get-tuple-element.199.grad.right), custom_call_target="tpu_custom_call" | custom-call | flops 8589934592 | bytes 16777216 | tf_op jit(solution)/shard_map/row_grad/pallas_call | solution.py:414
  375.2 2.9 collective-permute-done.39
  381.6 4.5 collective-permute-start.41
  386.1 11.8 %row_grad.3 = bf16[8,256,3584]{2,1,0:T(8,128)(2,1)} custom-call(s32[8]{0:T(128)} %fusion.16.places.where, bf16[1024,1024]{1,0:T(8,128)(2,1)} %get-tuple-element.130.one_a.left_a, bf16[1024,1024]{1,0:T(8,128)(2,1)} %get-tuple-element.129.one_b.left_b, bf16[1024,1536]{1,0:T(8,128)(2,1)} %get-tuple-element.204.mixed.right, ...), custom_call_target="tpu_custom_call", output_to_operand_aliasing={{}: (4, {})} | custom-call | flops 6442450944 | bytes 13631488 | tf_op jit(solution)/shard_map/row_grad/pallas_call | solution.py:414
  397.9 8.3 %output_sum.1 = bf16[1024,2048]{1,0:T(8,128)(2,1)} custom-call(s32[8]{0:T(128)} %fusion.16.places.where, s32[1]{0:T(128)} %bitcast.middle, bf16[1024,2048]{1,0:T(8,128)(2,1)} %tokens.3, f32[1,2048]{1,0:T(1,128)} %bitcast.130, bf16[4,1024,128]{2,1,0:T(8,128)(2,1)} %bitcast.27.refs_0_, bf16[4,1024,128]{2,1,0:T(8,128)(2,1)} %bitcast.28.refs_1_, ...), custom_call_target="tpu_custom_call" | custom-call | flops 35999997952 | bytes 17000000 | tf_op jit(solution)/shard_map/output_sum/pallas_call | solution.py:751
  406.2 2.5 maximum_maximum_fusion
  416.5 4.8 tokens_sum.4.rest_0_
  424.3 2.7 slice_convert_fusion.1
  427.0 9.3 %collective-permute-done.42.passed = bf16[4112,128]{1,0:T(8,128)(2,1)} collective-permute-done((bf16[4112,128]{1,0:T(8,128)(2,1)}, bf16[4112,128]{1,0:T(8,128)(2,1)}, u32[]{:S(2)}, u32[]{:S(2)}) %collective-permute-start.42) | collective-permute-done | bytes 1052704 | tf_op jit(solution)/shard_map/ppermute | solution.py:837
  440.1 4.0 tokens_sum.5.rest_0_
  444.1 19.7 %collective-permute-done.45.passed = bf16[4096,128]{1,0:T(8,128)(2,1)S(1)} collective-permute-done((bf16[4096,128]{1,0:T(8,128)(2,1)S(1)}, bf16[4096,128]{1,0:T(8,128)(2,1)S(1)}, u32[]{:S(2)}, u32[]{:S(2)}) %collective-permute-start.45) | collective-permute-done | bytes 1048608 | tf_op jit(solution)/shard_map/ppermute | solution.py:837
  465.4 4.0 tokens_sum.6.rest_0_
  469.4 18.4 %collective-permute-done.46.passed = bf16[4112,128]{1,0:T(8,128)(2,1)S(1)} collective-permute-done((bf16[4112,128]{1,0:T(8,128)(2,1)S(1)}, bf16[4112,128]{1,0:T(8,128)(2,1)S(1)}, u32[]{:S(2)}, u32[]{:S(2)}) %collective-permute-start.46) | collective-permute-done | bytes 1052704 | tf_op jit(solution)/shard_map/ppermute | solution.py:837
  488.8 4.0 tokens_sum.7
  492.8 11.1 %reduce-scatter.5.cloned.1.call-done = bf16[1,256,3584]{2,1,0:T(8,128)(2,1)} async-done(((bf16[8,256,3584]{2,1,0:T(8,128)(2,1)}), bf16[1,256,3584]{2,1,0:T(8,128)(2,1)}) %reduce-scatter.5.cloned.1.call-update) | async-done | bytes 1835024 | tf_op jit(solution)/shard_map/reduce_scatter | solution.py:846
  503.9 2.6 slice_convert_fusion.2
  (304 shorter events, 97.8 us)
Async XLA Ops:
  7.2 390.7 %reduce-scatter.3.cloned.1.call-start = ((), (), s32[]{:S(2)}) async-start(), calls=%async_computation.2 | async-start | bytes 11796480 | tf_op jit(solution)/shard_map/reduce_scatter | solution.py:846
  9.1 30.7 %collective-permute-start = (bf16[256,2048]{1,0:T(8,128)(2,1)S(1)}, bf16[256,2048]{1,0:T(8,128)(2,1)S(1)}, u32[]{:S(2)}, u32[]{:S(2)}) collective-permute-start(bf16[256,2048]{1,0:T(8,128)(2,1)S(1)} %pad_maximum_fusion), channel_id=1, source_target_pairs={{0,8},{4,12},{8,0},{12,4},{16,24},{20,28},{24,16},{28,20},{1,9},{5... | collective-permute-start | bytes 3145736 | tf_op jit(solution)/shard_map/ppermute | solution.py:47
  12.1 27.8 %collective-permute-start.1 = (bf16[256,2048]{1,0:T(8,128)(2,1)S(1)}, bf16[256,2048]{1,0:T(8,128)(2,1)S(1)}, u32[]{:S(2)}, u32[]{:S(2)}) collective-permute-start(bf16[256,2048]{1,0:T(8,128)(2,1)S(1)} %pad_maximum_fusion), channel_id=1, source_target_pairs={{0,16},{4,20},{8,24},{12,28},{16,0},{20,4},{24,8},{28,12},{1,17},{... | collective-permute-start | bytes 3145736 | tf_op jit(solution)/shard_map/ppermute | solution.py:47
  39.9 14.2 %collective-permute-start.2 = (bf16[128,2048]{1,0:T(8,128)(2,1)S(1)}, bf16[128,2048]{1,0:T(8,128)(2,1)S(1)}, u32[]{:S(2)}, u32[]{:S(2)}) collective-permute-start(bf16[128,2048]{1,0:T(8,128)(2,1)S(1)} %slice.171), channel_id=1, source_target_pairs={{0,16},{4,20},{8,24},{12,28},{16,0},{20,4},{24,8},{28,12},{1,17},{... | collective-permute-start | bytes 1572872 | tf_op jit(solution)/shard_map/ppermute | solution.py:47
  41.7 13.9 %collective-permute-start.3 = (bf16[128,2048]{1,0:T(8,128)(2,1)S(1)}, bf16[128,2048]{1,0:T(8,128)(2,1)S(1)}, u32[]{:S(2)}, u32[]{:S(2)}) collective-permute-start(bf16[128,2048]{1,0:T(8,128)(2,1)S(1)} %slice.172), channel_id=1, source_target_pairs={{0,8},{4,12},{8,0},{12,4},{16,24},{20,28},{24,16},{28,20},{1,9},{5... | collective-permute-start | bytes 1572872 | tf_op jit(solution)/shard_map/ppermute | solution.py:47
  60.4 31.3 %collective-permute-start.6 = (bf16[1024,2048]{1,0:T(8,128)(2,1)}, bf16[1024,2048]{1,0:T(8,128)(2,1)}, u32[]{:S(2)}, u32[]{:S(2)}) collective-permute-start(bf16[1024,2048]{1,0:T(8,128)(2,1)} %constant_dynamic-update-slice_fusion.w_a.dense_a), channel_id=1, source_target_pairs={{0,4},{4,0},{8,12},{12,8},{16,20},{20,16},{24,28},{28,24},{1,5},{5... | collective-permute-start | bytes 12582920 | tf_op jit(solution)/shard_map/ppermute | solution.py:47
  61.6 25.6 %collective-permute-start.4 = (bf16[256,2048]{1,0:T(8,128)(2,1)S(1)}, bf16[256,2048]{1,0:T(8,128)(2,1)S(1)}, u32[]{:S(2)}, u32[]{:S(2)}) collective-permute-start(bf16[256,2048]{1,0:T(8,128)(2,1)S(1)} %convert_element_type.247.refs_0_), channel_id=1, source_target_pairs={{0,8},{4,12},{8,0},{12,4},{16,24},{20,28},{24,16},{28,20},{1,9},{5... | collective-permute-start | bytes 3145736 | tf_op jit(solution)/shard_map/ppermute | solution.py:47
  63.2 25.4 %collective-permute-start.5 = (bf16[256,2048]{1,0:T(8,128)(2,1)S(1)}, bf16[256,2048]{1,0:T(8,128)(2,1)}, u32[]{:S(2)}, u32[]{:S(2)}) collective-permute-start(bf16[256,2048]{1,0:T(8,128)(2,1)S(1)} %convert_element_type.247.refs_0_), channel_id=1, source_target_pairs={{0,16},{4,20},{8,24},{12,28},{16,0},{20,4},{24,8},{28,12},{1,17},{... | collective-permute-start | bytes 3145736 | tf_op jit(solution)/shard_map/ppermute | solution.py:47
  88.6 14.5 %collective-permute-start.7 = (bf16[128,2048]{1,0:T(8,128)(2,1)S(1)}, bf16[128,2048]{1,0:T(8,128)(2,1)}, u32[]{:S(2)}, u32[]{:S(2)}) collective-permute-start(bf16[128,2048]{1,0:T(8,128)(2,1)S(1)} %slice.174), channel_id=1, source_target_pairs={{0,16},{4,20},{8,24},{12,28},{16,0},{20,4},{24,8},{28,12},{1,17},{... | collective-permute-start | bytes 1572872 | tf_op jit(solution)/shard_map/ppermute | solution.py:47
  91.1 13.1 %collective-permute-start.8 = (bf16[128,2048]{1,0:T(8,128)(2,1)S(1)}, bf16[128,2048]{1,0:T(8,128)(2,1)}, u32[]{:S(2)}, u32[]{:S(2)}) collective-permute-start(bf16[128,2048]{1,0:T(8,128)(2,1)S(1)} %slice.175), channel_id=1, source_target_pairs={{0,8},{4,12},{8,0},{12,4},{16,24},{20,28},{24,16},{28,20},{1,9},{5... | collective-permute-start | bytes 1572872 | tf_op jit(solution)/shard_map/ppermute | solution.py:47
  104.2 31.2 %collective-permute-start.9 = (bf16[1024,1024]{1,0:T(8,128)(2,1)}, bf16[1024,1024]{1,0:T(8,128)(2,1)}, u32[]{:S(2)}, u32[]{:S(2)}) collective-permute-start(bf16[1024,1024]{1,0:T(8,128)(2,1)} %get-tuple-element.135.own), channel_id=1, source_target_pairs={{0,4},{4,8},{8,12},{12,16},{16,20},{20,24},{24,28},{1,5},{5,9},{9,... | collective-permute-start | bytes 6291464 | tf_op jit(solution)/shard_map/ppermute | solution.py:857
  106.9 5.4 %collective-permute-start.11 = (bf16[256,2048]{1,0:T(8,128)(2,1)S(1)}, bf16[256,2048]{1,0:T(8,128)(2,1)S(1)}, u32[]{:S(2)}, u32[]{:S(2)}) collective-permute-start(bf16[256,2048]{1,0:T(8,128)(2,1)S(1)} %convert_element_type.247.refs_0_), channel_id=1, source_target_pairs={{0,4},{4,0},{8,12},{12,8},{16,20},{20,16},{24,28},{28,24},{1,5},{5... | collective-permute-start | bytes 3145736 | tf_op jit(solution)/shard_map/ppermute | solution.py:47
  106.9 6.9 %collective-permute-start.12 = (bf16[256,2048]{1,0:T(8,128)(2,1)S(1)}, bf16[256,2048]{1,0:T(8,128)(2,1)S(1)}, u32[]{:S(2)}, u32[]{:S(2)}) collective-permute-start(bf16[256,2048]{1,0:T(8,128)(2,1)S(1)} %collective-permute-done.4.refs_1_), channel_id=1, source_target_pairs={{0,4},{4,0},{8,12},{12,8},{16,20},{20,16},{24,28},{28,24},{1,5},{5... | collective-permute-start | bytes 3145736 | tf_op jit(solution)/shard_map/ppermute | solution.py:47
  107.4 10.0 %collective-permute-start.13 = (bf16[256,2048]{1,0:T(8,128)(2,1)}, bf16[256,2048]{1,0:T(8,128)(2,1)}, u32[]{:S(2)}, u32[]{:S(2)}) collective-permute-start(bf16[256,2048]{1,0:T(8,128)(2,1)} %collective-permute-done.5.refs_2_), channel_id=1, source_target_pairs={{0,4},{4,0},{8,12},{12,8},{16,20},{20,16},{24,28},{28,24},{1,5},{5... | collective-permute-start | bytes 3145736 | tf_op jit(solution)/shard_map/ppermute | solution.py:47
  108.7 47.3 %collective-permute-start.10 = (bf16[512,1024]{1,0:T(8,128)(2,1)S(1)}, bf16[512,1024]{1,0:T(8,128)(2,1)}, u32[]{:S(2)}, u32[]{:S(2)}) collective-permute-start(bf16[512,1024]{1,0:T(8,128)(2,1)S(1)} %slice.135), channel_id=1, source_target_pairs={{4,0},{8,4},{12,8},{16,12},{20,16},{24,20},{28,24},{5,1},{9,5},{13... | collective-permute-start | bytes 3145736 | tf_op jit(solution)/shard_map/ppermute | solution.py:857
  112.3 5.1 collective-permute-start.14
  135.4 32.6 %collective-permute-start.16 = (bf16[2048,256]{1,0:T(8,128)(2,1)S(1)}, bf16[2048,256]{1,0:T(8,128)(2,1)S(1)}, u32[]{:S(2)}, u32[]{:S(2)}) collective-permute-start(bf16[2048,256]{1,0:T(8,128)(2,1)S(1)} %convert_element_type.251.mine.rest_0_), channel_id=1, source_target_pairs={{0,8},{4,12},{8,0},{12,4},{16,24},{20,28},{24,16},{28,20},{1,9},{5... | collective-permute-start | bytes 3145736 | tf_op jit(solution)/shard_map/ppermute | solution.py:47
  136.7 35.0 %collective-permute-start.17 = (bf16[2048,256]{1,0:T(8,128)(2,1)S(1)}, bf16[2048,256]{1,0:T(8,128)(2,1)S(1)}, u32[]{:S(2)}, u32[]{:S(2)}) collective-permute-start(bf16[2048,256]{1,0:T(8,128)(2,1)S(1)} %convert_element_type.251.mine.rest_0_), channel_id=1, source_target_pairs={{0,16},{4,20},{8,24},{12,28},{16,0},{20,4},{24,8},{28,12},{1,17},{... | collective-permute-start | bytes 3145736 | tf_op jit(solution)/shard_map/ppermute | solution.py:47
  156.0 34.7 %collective-permute-start.20 = (bf16[2048,256]{1,0:T(8,128)(2,1)S(1)}, bf16[2048,256]{1,0:T(8,128)(2,1)S(1)}, u32[]{:S(2)}, u32[]{:S(2)}) collective-permute-start(bf16[2048,256]{1,0:T(8,128)(2,1)S(1)} %convert_element_type.251.mine.rest_0_), channel_id=1, source_target_pairs={{0,4},{4,0},{8,12},{12,8},{16,20},{20,16},{24,28},{28,24},{1,5},{5... | collective-permute-start | bytes 3145736 | tf_op jit(solution)/shard_map/ppermute | solution.py:47
  171.7 19.0 %collective-permute-start.18 = (bf16[1024,256]{1,0:T(8,128)(2,1)S(1)}, bf16[1024,256]{1,0:T(8,128)(2,1)S(1)}, u32[]{:S(2)}, u32[]{:S(2)}) collective-permute-start(bf16[1024,256]{1,0:T(8,128)(2,1)S(1)} %slice.177), channel_id=1, source_target_pairs={{0,16},{4,20},{8,24},{12,28},{16,0},{20,4},{24,8},{28,12},{1,17},{... | collective-permute-start | bytes 1572872 | tf_op jit(solution)/shard_map/ppermute | solution.py:47
  172.1 18.7 %collective-permute-start.19 = (bf16[1024,256]{1,0:T(8,128)(2,1)S(1)}, bf16[1024,256]{1,0:T(8,128)(2,1)S(1)}, u32[]{:S(2)}, u32[]{:S(2)}) collective-permute-start(bf16[1024,256]{1,0:T(8,128)(2,1)S(1)} %slice.178), channel_id=1, source_target_pairs={{0,8},{4,12},{8,0},{12,4},{16,24},{20,28},{24,16},{28,20},{1,9},{5... | collective-permute-start | bytes 1572872 | tf_op jit(solution)/shard_map/ppermute | solution.py:47
  172.4 37.4 %collective-permute-start.21 = (bf16[2048,256]{1,0:T(8,128)(2,1)S(1)}, bf16[2048,256]{1,0:T(8,128)(2,1)S(1)}, u32[]{:S(2)}, u32[]{:S(2)}) collective-permute-start(bf16[2048,256]{1,0:T(8,128)(2,1)S(1)} %collective-permute-done.16.mine.rest_1_), channel_id=1, source_target_pairs={{0,4},{4,0},{8,12},{12,8},{16,20},{20,16},{24,28},{28,24},{1,5},{5... | collective-permute-start | bytes 3145736 | tf_op jit(solution)/shard_map/ppermute | solution.py:47
  198.2 28.7 %collective-permute-start.23 = (bf16[4096,128]{1,0:T(8,128)(2,1)}, bf16[4096,128]{1,0:T(8,128)(2,1)S(1)}, u32[]{:S(2)}, u32[]{:S(2)}) collective-permute-start(bf16[4096,128]{1,0:T(8,128)(2,1)} %bitcast.103), channel_id=1, source_target_pairs={{0,1},{3,2},{4,5},{7,6},{8,9},{11,10},{12,13},{15,14},{16,17},{19,... | collective-permute-start | bytes 3145736 | tf_op jit(solution)/shard_map/ppermute | solution.py:837
  201.7 51.8 %collective-permute-start.29 = (bf16[1024,1024]{1,0:T(8,128)(2,1)}, bf16[1024,1024]{1,0:T(8,128)(2,1)}, u32[]{:S(2)}, u32[]{:S(2)}) collective-permute-start(bf16[1024,1024]{1,0:T(8,128)(2,1)} %get-tuple-element.181), channel_id=1, source_target_pairs={{4,0},{8,4},{12,8},{16,12},{20,16},{24,20},{28,24},{5,1},{9,5},{13... | collective-permute-start | bytes 6291464 | tf_op jit(solution)/shard_map/ppermute | solution.py:857
  203.0 50.5 %collective-permute-start.30 = (bf16[512,1024]{1,0:T(8,128)(2,1)}, bf16[512,1024]{1,0:T(8,128)(2,1)}, u32[]{:S(2)}, u32[]{:S(2)}) collective-permute-start(bf16[512,1024]{1,0:T(8,128)(2,1)} %get-tuple-element.182), channel_id=1, source_target_pairs={{0,4},{4,8},{8,12},{12,16},{16,20},{20,24},{24,28},{1,5},{5,9},{9,... | collective-permute-start | bytes 3145736 | tf_op jit(solution)/shard_map/ppermute | solution.py:857
  208.9 38.2 %collective-permute-start.24 = (bf16[2048,256]{1,0:T(8,128)(2,1)S(1)}, bf16[2048,256]{1,0:T(8,128)(2,1)}, u32[]{:S(2)}, u32[]{:S(2)}) collective-permute-start(bf16[2048,256]{1,0:T(8,128)(2,1)S(1)} %collective-permute-done.17.mine.rest_2_), channel_id=1, source_target_pairs={{0,4},{4,0},{8,12},{12,8},{16,20},{20,16},{24,28},{28,24},{1,5},{5... | collective-permute-start | bytes 3145736 | tf_op jit(solution)/shard_map/ppermute | solution.py:47
  224.3 29.3 %collective-permute-start.22 = (bf16[4096,128]{1,0:T(8,128)(2,1)S(1)}, bf16[4096,128]{1,0:T(8,128)(2,1)}, u32[]{:S(2)}, u32[]{:S(2)}) collective-permute-start(bf16[4096,128]{1,0:T(8,128)(2,1)S(1)} %bitcast.101), channel_id=1, source_target_pairs={{0,1},{3,2},{4,5},{7,6},{8,9},{11,10},{12,13},{15,14},{16,17},{19,... | collective-permute-start | bytes 3145736 | tf_op jit(solution)/shard_map/ppermute | solution.py:837
  227.2 26.5 %collective-permute-start.25 = (bf16[4096,128]{1,0:T(8,128)(2,1)S(1)}, bf16[4096,128]{1,0:T(8,128)(2,1)}, u32[]{:S(2)}, u32[]{:S(2)}) collective-permute-start(bf16[4096,128]{1,0:T(8,128)(2,1)S(1)} %add_convert_fusion.15), channel_id=1, source_target_pairs={{1,2},{2,1},{5,6},{6,5},{9,10},{10,9},{13,14},{14,13},{17,18},{18,... | collective-permute-start | bytes 3145736 | tf_op jit(solution)/shard_map/ppermute | solution.py:834
  247.2 15.8 %collective-permute-start.26 = (bf16[2048,256]{1,0:T(8,128)(2,1)}, bf16[2048,256]{1,0:T(8,128)(2,1)}, u32[]{:S(2)}, u32[]{:S(2)}) collective-permute-start(bf16[2048,256]{1,0:T(8,128)(2,1)} %constant_dynamic-update-slice_fusion.5.rest_3_.mine), channel_id=1, source_target_pairs={{0,4},{4,0},{8,12},{12,8},{16,20},{20,16},{24,28},{28,24},{1,5},{5... | collective-permute-start | bytes 3145736 | tf_op jit(solution)/shard_map/ppermute | solution.py:47
  253.6 250.3 %reduce-scatter.5.cloned.1.call-start = ((), (), s32[]{:S(2)}) async-start(), calls=%async_computation.3 | async-start | bytes 16515072 | tf_op jit(solution)/shard_map/reduce_scatter | solution.py:846
  257.4 28.6 %collective-permute-start.27 = (bf16[4096,128]{1,0:T(8,128)(2,1)}, bf16[4096,128]{1,0:T(8,128)(2,1)}, u32[]{:S(2)}, u32[]{:S(2)}) collective-permute-start(bf16[4096,128]{1,0:T(8,128)(2,1)} %fusion), channel_id=1, source_target_pairs={{0,1},{3,2},{1,0},{2,3},{4,5},{7,6},{5,4},{6,7},{8,9},{11,10},{9,8... | collective-permute-start | bytes 3145736 | tf_op jit(solution)/shard_map/ppermute | solution.py:837
  261.4 24.6 %collective-permute-start.28 = (bf16[4096,128]{1,0:T(8,128)(2,1)S(1)}, bf16[4096,128]{1,0:T(8,128)(2,1)S(1)}, u32[]{:S(2)}, u32[]{:S(2)}) collective-permute-start(bf16[4096,128]{1,0:T(8,128)(2,1)S(1)} %add_convert_fusion.14), channel_id=1, source_target_pairs={{1,2},{2,1},{5,6},{6,5},{9,10},{10,9},{13,14},{14,13},{17,18},{18,... | collective-permute-start | bytes 3145736 | tf_op jit(solution)/shard_map/ppermute | solution.py:834
  288.6 33.2 %collective-permute-start.31 = (bf16[4096,128]{1,0:T(8,128)(2,1)}, bf16[4096,128]{1,0:T(8,128)(2,1)S(1)}, u32[]{:S(2)}, u32[]{:S(2)}) collective-permute-start(bf16[4096,128]{1,0:T(8,128)(2,1)} %fusion.1), channel_id=1, source_target_pairs={{0,1},{3,2},{1,0},{2,3},{4,5},{7,6},{5,4},{6,7},{8,9},{11,10},{9,8... | collective-permute-start | bytes 3145736 | tf_op jit(solution)/shard_map/ppermute | solution.py:837
  291.4 30.4 %collective-permute-start.32 = (bf16[4096,128]{1,0:T(8,128)(2,1)S(1)}, bf16[4096,128]{1,0:T(8,128)(2,1)}, u32[]{:S(2)}, u32[]{:S(2)}) collective-permute-start(bf16[4096,128]{1,0:T(8,128)(2,1)S(1)} %add_convert_fusion.12), channel_id=1, source_target_pairs={{1,2},{2,1},{5,6},{6,5},{9,10},{10,9},{13,14},{14,13},{17,18},{18,... | collective-permute-start | bytes 3145736 | tf_op jit(solution)/shard_map/ppermute | solution.py:834
  324.2 24.5 %collective-permute-start.34 = (bf16[4096,128]{1,0:T(8,128)(2,1)S(1)}, bf16[4096,128]{1,0:T(8,128)(2,1)S(1)}, u32[]{:S(2)}, u32[]{:S(2)}) collective-permute-start(bf16[4096,128]{1,0:T(8,128)(2,1)S(1)} %fusion.2), channel_id=1, source_target_pairs={{0,1},{3,2},{1,0},{2,3},{4,5},{7,6},{5,4},{6,7},{8,9},{11,10},{9,8... | collective-permute-start | bytes 3145736 | tf_op jit(solution)/shard_map/ppermute | solution.py:837
  325.7 23.0 %collective-permute-start.33 = (bf16[4096,128]{1,0:T(8,128)(2,1)S(1)}, bf16[4096,128]{1,0:T(8,128)(2,1)S(1)}, u32[]{:S(2)}, u32[]{:S(2)}) collective-permute-start(bf16[4096,128]{1,0:T(8,128)(2,1)S(1)} %add_convert_fusion.10), channel_id=1, source_target_pairs={{1,2},{2,1},{5,6},{6,5},{9,10},{10,9},{13,14},{14,13},{17,18},{18,... | collective-permute-start | bytes 3145736 | tf_op jit(solution)/shard_map/ppermute | solution.py:834
  349.7 5.0 collective-permute-start.37
  349.8 28.3 %collective-permute-start.35 = (bf16[4096,128]{1,0:T(8,128)(2,1)S(1)}, bf16[4096,128]{1,0:T(8,128)(2,1)S(1)}, u32[]{:S(2)}, u32[]{:S(2)}) collective-permute-start(bf16[4096,128]{1,0:T(8,128)(2,1)S(1)} %fusion.3), channel_id=1, source_target_pairs={{0,1},{3,2},{1,0},{2,3},{4,5},{7,6},{5,4},{6,7},{8,9},{11,10},{9,8... | collective-permute-start | bytes 3145736 | tf_op jit(solution)/shard_map/ppermute | solution.py:837
  353.8 24.4 %collective-permute-start.36 = (bf16[4096,128]{1,0:T(8,128)(2,1)S(1)}, bf16[4096,128]{1,0:T(8,128)(2,1)S(1)}, u32[]{:S(2)}, u32[]{:S(2)}) collective-permute-start(bf16[4096,128]{1,0:T(8,128)(2,1)S(1)} %add_convert_fusion.7), channel_id=1, source_target_pairs={{1,2},{2,1},{5,6},{6,5},{9,10},{10,9},{13,14},{14,13},{17,18},{18,... | collective-permute-start | bytes 3145736 | tf_op jit(solution)/shard_map/ppermute | solution.py:834
  354.8 19.6 %collective-permute-start.38 = (f32[2,1728]{1,0:T(2,128)S(1)}, f32[2,1728]{1,0:T(2,128)S(1)}, u32[]{:S(2)}, u32[]{:S(2)}) collective-permute-start(f32[2,1728]{1,0:T(2,128)S(1)} %slice.182), channel_id=1, source_target_pairs={{0,16},{4,20},{8,24},{12,28},{16,0},{20,4},{24,8},{28,12},{1,17},{... | collective-permute-start | bytes 41480 | tf_op jit(solution)/shard_map/ppermute | solution.py:47
  374.4 3.7 collective-permute-start.39
  378.5 30.2 %collective-permute-start.40 = (bf16[4096,128]{1,0:T(8,128)(2,1)S(1)}, bf16[4096,128]{1,0:T(8,128)(2,1)}, u32[]{:S(2)}, u32[]{:S(2)}) collective-permute-start(bf16[4096,128]{1,0:T(8,128)(2,1)S(1)} %add_convert_fusion.6), channel_id=1, source_target_pairs={{1,2},{2,1},{5,6},{6,5},{9,10},{10,9},{13,14},{14,13},{17,18},{18,... | collective-permute-start | bytes 3145736 | tf_op jit(solution)/shard_map/ppermute | solution.py:834
  381.6 27.5 %collective-permute-start.41 = (bf16[4096,128]{1,0:T(8,128)(2,1)}, bf16[4096,128]{1,0:T(8,128)(2,1)}, u32[]{:S(2)}, u32[]{:S(2)}) collective-permute-start(bf16[4096,128]{1,0:T(8,128)(2,1)} %fusion.4.settled), channel_id=1, source_target_pairs={{0,1},{3,2},{1,0},{2,3},{4,5},{7,6},{5,4},{6,7},{8,9},{11,10},{9,8... | collective-permute-start | bytes 3145736 | tf_op jit(solution)/shard_map/ppermute | solution.py:837
  412.2 24.1 %collective-permute-start.42 = (bf16[4112,128]{1,0:T(8,128)(2,1)}, bf16[4112,128]{1,0:T(8,128)(2,1)}, u32[]{:S(2)}, u32[]{:S(2)}) collective-permute-start(bf16[4112,128]{1,0:T(8,128)(2,1)} %pad_select_fusion.settled), channel_id=1, source_target_pairs={{0,1},{3,2},{1,0},{2,3},{4,5},{7,6},{5,4},{6,7},{8,9},{11,10},{9,8... | collective-permute-start | bytes 3158024 | tf_op jit(solution)/shard_map/ppermute | solution.py:837
  415.8 22.7 %collective-permute-start.44 = (bf16[4096,128]{1,0:T(8,128)(2,1)S(1)}, bf16[4096,128]{1,0:T(8,128)(2,1)S(1)}, u32[]{:S(2)}, u32[]{:S(2)}) collective-permute-start(bf16[4096,128]{1,0:T(8,128)(2,1)S(1)} %add_convert_fusion.3), channel_id=1, source_target_pairs={{1,2},{2,1},{5,6},{6,5},{9,10},{10,9},{13,14},{14,13},{17,18},{18,... | collective-permute-start | bytes 3145736 | tf_op jit(solution)/shard_map/ppermute | solution.py:834
  437.8 26.1 %collective-permute-start.43 = (bf16[4112,128]{1,0:T(8,128)(2,1)S(1)}, bf16[4112,128]{1,0:T(8,128)(2,1)S(1)}, u32[]{:S(2)}, u32[]{:S(2)}) collective-permute-start(bf16[4112,128]{1,0:T(8,128)(2,1)S(1)} %add_convert_fusion.1), channel_id=1, source_target_pairs={{1,2},{2,1},{5,6},{6,5},{9,10},{10,9},{13,14},{14,13},{17,18},{18,... | collective-permute-start | bytes 3158024 | tf_op jit(solution)/shard_map/ppermute | solution.py:834
  438.8 25.0 %collective-permute-start.45 = (bf16[4096,128]{1,0:T(8,128)(2,1)S(1)}, bf16[4096,128]{1,0:T(8,128)(2,1)S(1)}, u32[]{:S(2)}, u32[]{:S(2)}) collective-permute-start(bf16[4096,128]{1,0:T(8,128)(2,1)S(1)} %add_convert_fusion.2.settled), channel_id=1, source_target_pairs={{1,0},{2,3},{5,4},{6,7},{9,8},{10,11},{13,12},{14,15},{17,16},{18,... | collective-permute-start | bytes 3145736 | tf_op jit(solution)/shard_map/ppermute | solution.py:837
  464.1 23.7 %collective-permute-start.46 = (bf16[4112,128]{1,0:T(8,128)(2,1)S(1)}, bf16[4112,128]{1,0:T(8,128)(2,1)S(1)}, u32[]{:S(2)}, u32[]{:S(2)}) collective-permute-start(bf16[4112,128]{1,0:T(8,128)(2,1)S(1)} %add_convert_fusion.settled), channel_id=1, source_target_pairs={{1,0},{2,3},{5,4},{6,7},{9,8},{10,11},{13,12},{14,15},{17,16},{18,... | collective-permute-start | bytes 3158024 | tf_op jit(solution)/shard_map/ppermute | solution.py:837
  (52 other events, 631.7 us)
Sparse Core Ops, SparseCore 0:
  253.7 83.3 reduce-scatter.2
  398.0 105.8 reduce-scatter.4

commit v4 on v3

--- a/solution.py
+++ b/solution.py
@@ -976,7 +976,7 @@
     active, slope = expand(after(two_a, sent), two_b, expand_mine + expand_theirs, full_expand_bias)
     grad_attended = dense_back(after(up_a, active), up_b, project_a, project_b, turned_width)
     blocks = [spread_down.pair(0, active)] if cube else []
-    spread_down.weight = after(spread_down.weight, (left, active))
+    spread_down.weight = after(spread_down.weight, (left, grad_attended))
     seen_down = spread_down.first()
     if not cube:
         blocks = [spread_down.pair(0)]
@@ -1013,21 +1013,23 @@
         grad_mixed, project_a, project_b, grad_second, tok, mean, inverse, gains, 0, 1
     )
     seen = line.slot(tails[0], sums)
+    second, more_sums = input_back(
+        after(grad_mixed, (sums, seen)), project_a, project_b, grad_second, tok, mean, inverse, gains, 1, 1
+    )
+    widths = grad_hidden.shape[1], grad_mixed.shape[1]
+    expanded = row_grad(places, two_a, two_b, after(grad_hidden, second), sum(widths))
+    seen = line.slot(second, expanded)
     *more, part = input_back(
-        after(grad_mixed, (sums, seen)), project_a, project_b, grad_second, tok, mean, inverse, gains, 1, 3
+        after(grad_mixed, (expanded, seen)), project_a, project_b, grad_second, tok, mean, inverse, gains, 2, 2
     )
-    tails += more
-    sums = sums + part
-    seen = line.slot(tails[1], part)
-    widths = grad_hidden.shape[1], grad_mixed.shape[1]
-    row_blocks = row_grad(places, two_a, two_b, after(grad_hidden, seen), sum(widths))
+    tails += [second, *more]
+    sums = sums + more_sums + part
+    row_blocks = row_grad(places, one_a, one_b, after(grad_mixed, part), sum(widths), widths[0], expanded)
+    seen = line.slot(tails[2], row_blocks)
     vector = part
     if cube:
         vector = after(vector_parts(sums, grad_bias, expand_bias_sums, project_bias_sums), seen)
-        vector = halved(halved(vector, CORE), ALONG_Y)
-        vector = halved(after(vector, row_blocks), ALONG_X)[0]
-    seen = line.slot(tails[2], row_blocks)
-    row_blocks = row_grad(places, one_a, one_b, after(grad_mixed, seen), sum(widths), widths[0], row_blocks)
+        vector = halved(halved(halved(vector, CORE), ALONG_Y), ALONG_X)[0]
     row_blocks, grad_down, vector = lax.optimization_barrier((row_blocks, grad_down, vector))
     if cube:
         grad_rows = scatter_blocks(row_blocks, True)

time: 525 us -> 521 us (level)
  starting transfers between devices: 78.9 us -> 67 us
  Pallas kernels: 235 us -> 242 us
    reduce_scatter x2, waiting for transfers between devices: 11.1 us -> 0.02 us  [scatter_blocks(): return lax.psum_scatter(blocks, 'dp', scatter_dimension=0, tiled=True)[0]]
    ppermute x25, starting transfers between devices: 34.4 us -> 24.3 us  [swap(): return lax.ppermute(value, 'dp', [(i, i ^ bit) for i in range(count)])]
    ppermute x25, waiting for transfers between devices: 29.9 us -> 36.5 us  [swap(): return lax.ppermute(value, 'dp', [(i, i ^ bit) for i in range(count)])]
    pallas_call x2 -> x3, Pallas kernels: 24.2 us -> 27.4 us  [input_back(): pl.pallas_call(input_kernel, grid=(count,), in_specs=[row(depth), weight,...]
    unnamed x122 -> x120, local copies, waits for them, and re-layouts: 14.2 us -> 13.9 us
  transfers between devices with their start and end apart: 49 -> 49, of which waited for: 15 -> 16; matrix products, arithmetic and copies ran while one was open for 10% -> 11% of each run, Pallas kernels for 46% -> 47%
where the time goes in v4:
time: 521 us; the launch traced here: 512 us
  Pallas kernels  242 us (46%)
  waiting for transfers between devices  92.4 us (18%)
  starting transfers between devices  67 us (13%)
  other arithmetic  44.9 us (9%)
  local copies, waits for them, and re-layouts  26 us (5%)
  blocking collectives  24.3 us (5%)
  between operations  15.5 us (3%)
    ppermute x10, waiting for transfers between devices, slot(): self.inward = lax.ppermute(operand, 'tensor', pairs)  55.8 us
    ppermute x25, waiting for transfers between devices, swap(): return lax.ppermute(value, 'dp', [(i, i ^ bit) for i in range(count)])  36.5 us
    pallas_call x3, Pallas kernels, input_back(): pl.pallas_call(input_kernel, grid=(count,), in_specs=[row(depth), weight,...  27.4 us
    pallas_call x4, Pallas kernels, branch_piece(): pl.pallas_call(branch_kernel, grid=(rows // tile,), in_specs=[row(attende...  26.5 us
    pallas_call x2, Pallas kernels, row_grad(): pl.pallas_call(row_grad_kernel, grid_spec=pltpu.PrefetchScalarGridSpec(nu...  26.2 us
    all_gather x1, blocking collectives, on_device(): gathered = lax.all_gather(own, 'dp', axis=0).reshape(count, -1)  24.3 us
    ppermute x25, starting transfers between devices, swap(): return lax.ppermute(value, 'dp', [(i, i ^ bit) for i in range(count)])  24.3 us
    pallas_call x2, Pallas kernels, column_grad(): pl.pallas_call(column_grad_kernel, grid_spec=pltpu.PrefetchScalarGridSpec...  21.6 us
  transfers between devices with their start and end apart: 49, of which 16 were waited for; matrix products, arithmetic and copies ran while one was open for 11% of the time, Pallas kernels for 47%

profile of v4, /device:TPU:0, one launch (start us, length us, event | category | flops | bytes accessed | tf_op | source)
XLA Modules:
  0.0 512.3 jit_solution(199623332075341960)
XLA Ops:
  9.1 3.0 collective-permute-start
  15.4 24.3 %all_gather.3 = bf16[8,16,128]{2,1,0:T(8,128)(2,1)S(1)} all-gather(bf16[1,16,128]{2,1,0:T(8,128)(2,1)S(1)} %pad_bitcast_fusion), channel_id=1, replica_groups=mesh['dp'=8,'tensor'=4] {'dp'}, dimensions={0}, use_global_device_ids=true | all-gather | bytes 36864 | tf_op jit(solution)/shard_map/all_gather | solution.py:909
  43.4 10.7 %collective-permute-done.2 = bf16[128,2048]{1,0:T(8,128)(2,1)S(1)} collective-permute-done((bf16[128,2048]{1,0:T(8,128)(2,1)S(1)}, bf16[128,2048]{1,0:T(8,128)(2,1)S(1)}, u32[]{:S(2)}, u32[]{:S(2)}) %collective-permute-start.2) | collective-permute-done | bytes 524320 | tf_op jit(solution)/shard_map/ppermute | solution.py:47
  66.2 3.1 fusion.7
  69.3 12.0 %norm.1 = (bf16[1024,2048]{1,0:T(8,128)(2,1)}, bf16[1024,1024]{1,0:T(8,128)(2,1)}, bf16[1024,1024]{1,0:T(8,128)(2,1)}, bf16[1024,1024]{1,0:T(8,128)(2,1)}, bf16[...) custom-call(s32[8]{0:T(128)} %fusion.17.places.where, ...), custom_call_target="tpu_custom_call" | custom-call | flops 41943040 | bytes 41943040 | tf_op jit(solution)/shard_map/norm/pallas_call | solution.py:151
  81.3 5.9 %collective-permute-done.4.refs_1_ = bf16[256,2048]{1,0:T(8,128)(2,1)S(1)} collective-permute-done((bf16[256,2048]{1,0:T(8,128)(2,1)S(1)}, bf16[256,2048]{1,0:T(8,128)(2,1)S(1)}, u32[]{:S(2)}, u32[]{:S(2)}) %collective-permute-start.4) | collective-permute-done | bytes 1048608 | tf_op jit(solution)/shard_map/ppermute | solution.py:47
  91.4 11.5 %project.1 = (bf16[1024,512]{1,0:T(8,128)(2,1)}, bf16[1024,1024]{1,0:T(8,128)(2,1)}) custom-call(bf16[1024,1024]{1,0:T(8,128)(2,1)} %get-tuple-element.131.one_a.left_a, bf16[1024,1024]{1,0:T(8,128)(2,1)} %get-tuple-element.130.one_b.left_b, bf16[1024,2048]{1,0:T(8,128)(2,1)} %constant_dynamic-update-slice_fusion.w_a.dense_a, ...), custom_call_target="tpu_custom_call" | custom-call | flops 8589934592 | bytes 14000000 | tf_op jit(solution)/shard_map/project/pallas_call | solution.py:192
  103.9 2.6 collective-permute-start.9
  118.2 17.0 %expand.1 = (bf16[1024,2048]{1,0:T(8,128)(2,1)}, bf16[1024,2048]{1,0:T(8,128)(2,1)}) custom-call(bf16[1024,1024]{1,0:T(8,128)(2,1)} %get-tuple-element.139.two_a.left_a, bf16[1024,1024]{1,0:T(8,128)(2,1)} %get-tuple-element.140.two_b.left_b, f32[1,2048]{1,0:T(1,128)} %bitcast.125, bf16[256,2048]{1,0:T(8,128)(2,1)} %copy-done.9, ...), custom_call_target="tpu_custom_call" | custom-call | tf_op jit(solution)/shard_map/expand/pallas_call | solution.py:239
  135.2 6.2 %dense_back.1.grad = bf16[1024,512]{1,0:T(8,128)(2,1)} custom-call(bf16[1024,1024]{1,0:T(8,128)(2,1)} %get-tuple-element.220.up_a.right_a.a.rest_0_, bf16[1024,1024]{1,0:T(8,128)(2,1)} %get-tuple-element.148.up_b.right_b.b, bf16[1024,2048]{1,0:T(8,128)(2,1)} %constant_dynamic-update-slice_fusion.w_a.dense_a, ...), custom_call_target="tpu_custom_call" | custom-call | tf_op jit(solution)/shard_map/dense_back/pallas_call | solution.py:295
  145.8 12.0 %attend.1 = (bf16[1024,512]{1,0:T(8,128)(2,1)}, f32[2,1,1024]{2,1,0:T(1,128)}) custom-call(s32[4]{0:T(128)} %get-tuple-element.251.first, s32[4]{0:T(128)} %get-tuple-element.250.last, bf16[1024,512]{1,0:T(8,128)(2,1)} %get-tuple-element.149.q, bf16[1024,1024]{1,0:T(8,128)(2,1)} %collective-permute-done.9.left, bf16[1024,1024]{1,0:T(8,128)(2,1)} %get-tuple-element.136.own, ...), custom_call_target="tpu_custom_call" | custom-call | flops 8000000000 | bytes 10000000 | tf_op jit(solution)/shard_map/attend/pallas_call | solution.py:522
  157.8 9.0 %collective-permute-done.16.mine.rest_1_ = bf16[2048,256]{1,0:T(8,128)(2,1)S(1)} collective-permute-done((bf16[2048,256]{1,0:T(8,128)(2,1)S(1)}, bf16[2048,256]{1,0:T(8,128)(2,1)S(1)}, u32[]{:S(2)}, u32[]{:S(2)}) %collective-permute-start.16) | collective-permute-done | bytes 1048608 | tf_op jit(solution)/shard_map/ppermute | solution.py:47
  170.3 18.2 %attend_back.1 = (bf16[1024,512]{1,0:T(8,128)(2,1)}, bf16[1024,1024]{1,0:T(8,128)(2,1)}, bf16[1024,1024]{1,0:T(8,128)(2,1)}, bf16[512,1024]{1,0:T(8,128)(2,1)}) custom-call(s32[4]{0:T(128)} %get-tuple-element.251.first, s32[4]{0:T(128)} %get-tuple-element.250.last, bf16[1024,512]{1,0:T(8,128)(2,1)} %get-tuple-element.149.q, ...), custom_call_target="tpu_custom_call" | custom-call | flops 16000000000 | bytes 20000000 | tf_op jit(solution)/shard_map/attend_back/pallas_call | solution.py:605
  189.6 6.4 %branch.4 = bf16[4,1024,128]{2,1,0:T(8,128)(2,1)} custom-call(bf16[1024,512]{1,0:T(8,128)(2,1)} %get-tuple-element.175.attended.left, bf16[1024,2048]{1,0:T(8,128)(2,1)} %get-tuple-element.165.active.left, bf16[1024,2048]{1,0:T(8,128)(2,1)} %constant_dynamic-update-slice_fusion.w_a.dense_a, bf16[1024,2048]{1,0:T(8,128)(2,1)} %collective-permute-done.6.w_b.dense_b, ...), custom_call_target="tpu_custom_call" | custom-call | tf_op jit(solution)/shard_map/branch/pallas_call | solution.py:268
  195.9 3.6 collective-permute-start.23
  200.8 6.1 %collective-permute-start.30 = (bf16[512,1024]{1,0:T(8,128)(2,1)}, bf16[512,1024]{1,0:T(8,128)(2,1)}, u32[]{:S(2)}, u32[]{:S(2)}) collective-permute-start(bf16[512,1024]{1,0:T(8,128)(2,1)} %get-tuple-element.183), channel_id=1, source_target_pairs={{0,4},{4,8},{8,12},{12,16},{16,20},{20,24},{24,28},{1,5},{5,9},{9,... | collective-permute-start | bytes 3145736 | tf_op jit(solution)/shard_map/ppermute | solution.py:857
  208.8 6.4 %branch.5 = bf16[4,1024,128]{2,1,0:T(8,128)(2,1)} custom-call(bf16[1024,512]{1,0:T(8,128)(2,1)} %get-tuple-element.175.attended.left, bf16[1024,2048]{1,0:T(8,128)(2,1)} %get-tuple-element.165.active.left, bf16[1024,2048]{1,0:T(8,128)(2,1)} %constant_dynamic-update-slice_fusion.w_a.dense_a, bf16[1024,2048]{1,0:T(8,128)(2,1)} %collective-permute-done.6.w_b.dense_b, ...), custom_call_target="tpu_custom_call" | custom-call | tf_op jit(solution)/shard_map/branch/pallas_call | solution.py:268
  215.3 7.1 %column_grad.2.rest_0_ = bf16[8,2560,256]{2,1,0:T(8,128)(2,1)} custom-call(s32[8]{0:T(128)} %fusion.17.places.where, bf16[1024,512]{1,0:T(8,128)(2,1)} %get-tuple-element.175.attended.left, bf16[1024,1024]{1,0:T(8,128)(2,1)} %get-tuple-element.220.up_a.right_a.a.rest_0_, bf16[1024,1024]{1,0:T(8,128)(2,1)} %get-tuple-element.148.up_b.right_b.b), custom_call_target="tpu_custom_call" | custom-call | tf_op jit(solution)/shard_map/column_grad/pallas_call | solution.py:443
  222.4 2.5 collective-permute-start.22
  230.7 14.5 %column_grad.3 = bf16[8,2560,256]{2,1,0:T(8,128)(2,1)} custom-call(s32[8]{0:T(128)} %fusion.17.places.where, bf16[1024,2048]{1,0:T(8,128)(2,1)} %get-tuple-element.165.active.left, bf16[1024,1024]{1,0:T(8,128)(2,1)} %get-tuple-element.220.up_a.right_a.a.rest_0_, ...), custom_call_target="tpu_custom_call", output_to_operand_aliasing={{}: (4, {})} | custom-call | tf_op jit(solution)/shard_map/column_grad/pallas_call | solution.py:443
  245.2 6.4 %branch.6 = bf16[4,1024,128]{2,1,0:T(8,128)(2,1)} custom-call(bf16[1024,512]{1,0:T(8,128)(2,1)} %get-tuple-element.175.attended.left, bf16[1024,2048]{1,0:T(8,128)(2,1)} %get-tuple-element.165.active.left, bf16[1024,2048]{1,0:T(8,128)(2,1)} %constant_dynamic-update-slice_fusion.w_a.dense_a, bf16[1024,2048]{1,0:T(8,128)(2,1)} %collective-permute-done.6.w_b.dense_b, ...), custom_call_target="tpu_custom_call" | custom-call | tf_op jit(solution)/shard_map/branch/pallas_call | solution.py:268
  252.9 2.6 fusion
  260.7 16.5 %back.1 = (bf16[1024,2048]{1,0:T(8,128)(2,1)}, f32[1,2048]{1,0:T(1,128)}) custom-call(bf16[1024,1024]{1,0:T(8,128)(2,1)} %get-tuple-element.220.up_a.right_a.a.rest_0_, bf16[1024,1024]{1,0:T(8,128)(2,1)} %get-tuple-element.148.up_b.right_b.b, bf16[2048,256]{1,0:T(8,128)(2,1)} %copy-done.2, bf16[2048,256]{1,0:T(8,128)(2,1)} %copy-done.10, ...), custom_call_target="tpu_custom_call" | custom-call | flops 8589934592 | bytes 20971520 | tf_op jit(solution)/shard_map/back/pallas_call | solution.py:341
  277.2 7.3 %branch.7 = bf16[4,1024,128]{2,1,0:T(8,128)(2,1)} custom-call(bf16[1024,512]{1,0:T(8,128)(2,1)} %get-tuple-element.175.attended.left, bf16[1024,2048]{1,0:T(8,128)(2,1)} %get-tuple-element.165.active.left, bf16[1024,2048]{1,0:T(8,128)(2,1)} %constant_dynamic-update-slice_fusion.w_a.dense_a, bf16[1024,2048]{1,0:T(8,128)(2,1)} %collective-permute-done.6.w_b.dense_b, ...), custom_call_target="tpu_custom_call" | custom-call | tf_op jit(solution)/shard_map/branch/pallas_call | solution.py:268
  284.5 2.6 fusion.1
  291.6 14.8 %second_back.1.second = bf16[1024,2048]{1,0:T(8,128)(2,1)} custom-call(bf16[1024,2048]{1,0:T(8,128)(2,1)} %get-tuple-element.196.grad.right, bf16[256,2048]{1,0:T(8,128)(2,1)} %copy-done.9, bf16[256,2048]{1,0:T(8,128)(2,1)} %copy-done.14, bf16[256,2048]{1,0:T(8,128)(2,1)} %collective-permute-done.5.refs_2_, ...), custom_call_target="tpu_custom_call" | custom-call | flops 8589934592 | bytes 16777216 | tf_op jit(solution)/shard_map/second_back/pallas_call | solution.py:389
  306.4 5.0 mix.1
  311.4 7.4 %input_back.3 = (bf16[16,256,128]{2,1,0:T(8,128)(2,1)}, f32[8,2048]{1,0:T(8,128)}) custom-call(bf16[1024,1536]{1,0:T(8,128)(2,1)} %get-tuple-element.202.mixed.right, bf16[1024,2048]{1,0:T(8,128)(2,1)} %constant_dynamic-update-slice_fusion.w_a.dense_a, bf16[1024,2048]{1,0:T(8,128)(2,1)} %collective-permute-done.6.w_b.dense_b, ...), custom_call_target="tpu_custom_call" | custom-call | flops 1610612736 | bytes 14000000 | tf_op jit(solution)/shard_map/input_back/pallas_call | solution.py:719
  319.6 2.4 fusion.2
  323.9 7.4 %input_back.4 = (bf16[16,256,128]{2,1,0:T(8,128)(2,1)}, f32[8,2048]{1,0:T(8,128)}) custom-call(bf16[1024,1536]{1,0:T(8,128)(2,1)} %get-tuple-element.202.mixed.right, bf16[1024,2048]{1,0:T(8,128)(2,1)} %constant_dynamic-update-slice_fusion.w_a.dense_a, bf16[1024,2048]{1,0:T(8,128)(2,1)} %collective-permute-done.6.w_b.dense_b, ...), custom_call_target="tpu_custom_call" | custom-call | flops 1610612736 | bytes 14000000 | tf_op jit(solution)/shard_map/input_back/pallas_call | solution.py:719
  331.3 14.4 %row_grad.2.rest_0_ = bf16[8,256,3584]{2,1,0:T(8,128)(2,1)} custom-call(s32[8]{0:T(128)} %fusion.17.places.where, bf16[1024,1024]{1,0:T(8,128)(2,1)} %get-tuple-element.139.two_a.left_a, bf16[1024,1024]{1,0:T(8,128)(2,1)} %get-tuple-element.140.two_b.left_b, bf16[1024,2048]{1,0:T(8,128)(2,1)} %get-tuple-element.196.grad.right), custom_call_target="tpu_custom_call" | custom-call | flops 8589934592 | bytes 16777216 | tf_op jit(solution)/shard_map/row_grad/pallas_call | solution.py:414
  348.3 4.0 collective-permute-start.35
  354.7 12.6 %input_back.5 = (bf16[16,256,128]{2,1,0:T(8,128)(2,1)}, bf16[16,256,128]{2,1,0:T(8,128)(2,1)}, f32[8,2048]{1,0:T(8,128)}) custom-call(bf16[1024,1536]{1,0:T(8,128)(2,1)} %get-tuple-element.202.mixed.right, bf16[1024,2048]{1,0:T(8,128)(2,1)} %constant_dynamic-update-slice_fusion.w_a.dense_a, bf16[1024,2048]{1,0:T(8,128)(2,1)} %collective-permute-done.6.w_b.dense_b, ...), custom_call_target="tpu_custom_call" | custom-call | flops 3221225472 | bytes 14000000 | tf_op jit(solution)/shard_map/input_back/pallas_call | solution.py:719
  368.2 11.8 %row_grad.3 = bf16[8,256,3584]{2,1,0:T(8,128)(2,1)} custom-call(s32[8]{0:T(128)} %fusion.17.places.where, bf16[1024,1024]{1,0:T(8,128)(2,1)} %get-tuple-element.131.one_a.left_a, bf16[1024,1024]{1,0:T(8,128)(2,1)} %get-tuple-element.130.one_b.left_b, bf16[1024,1536]{1,0:T(8,128)(2,1)} %get-tuple-element.202.mixed.right, ...), custom_call_target="tpu_custom_call", output_to_operand_aliasing={{}: (4, {})} | custom-call | flops 6442450944 | bytes 13631488 | tf_op jit(solution)/shard_map/row_grad/pallas_call | solution.py:414
  381.7 2.9 fusion.4.settled
  394.1 2.6 collective-permute-start.41
  396.8 9.2 %output_sum.1 = bf16[1024,2048]{1,0:T(8,128)(2,1)} custom-call(s32[8]{0:T(128)} %fusion.17.places.where, s32[1]{0:T(128)} %bitcast.middle, bf16[1024,2048]{1,0:T(8,128)(2,1)} %tokens.3, f32[1,2048]{1,0:T(1,128)} %bitcast.128, bf16[4,1024,128]{2,1,0:T(8,128)(2,1)} %bitcast.27.refs_0_, bf16[4,1024,128]{2,1,0:T(8,128)(2,1)} %bitcast.28.refs_1_, ...), custom_call_target="tpu_custom_call" | custom-call | flops 35999997952 | bytes 17000000 | tf_op jit(solution)/shard_map/output_sum/pallas_call | solution.py:751
  406.0 2.5 maximum_maximum_fusion
  408.6 10.2 %collective-permute-done.41.passed = bf16[4096,128]{1,0:T(8,128)(2,1)} collective-permute-done((bf16[4096,128]{1,0:T(8,128)(2,1)}, bf16[4096,128]{1,0:T(8,128)(2,1)}, u32[]{:S(2)}, u32[]{:S(2)}) %collective-permute-start.41) | collective-permute-done | bytes 1048608 | tf_op jit(solution)/shard_map/ppermute | solution.py:837
  425.6 4.9 tokens_sum.4.rest_0_
  433.5 2.7 slice_convert_fusion.1
  436.2 8.7 %collective-permute-done.42.passed = bf16[4112,128]{1,0:T(8,128)(2,1)} collective-permute-done((bf16[4112,128]{1,0:T(8,128)(2,1)}, bf16[4112,128]{1,0:T(8,128)(2,1)}, u32[]{:S(2)}, u32[]{:S(2)}) %collective-permute-start.42) | collective-permute-done | bytes 1052704 | tf_op jit(solution)/shard_map/ppermute | solution.py:837
  448.9 4.4 tokens_sum.5.rest_0_
  453.3 19.0 %collective-permute-done.45.passed = bf16[4096,128]{1,0:T(8,128)(2,1)S(1)} collective-permute-done((bf16[4096,128]{1,0:T(8,128)(2,1)S(1)}, bf16[4096,128]{1,0:T(8,128)(2,1)S(1)}, u32[]{:S(2)}, u32[]{:S(2)}) %collective-permute-start.45) | collective-permute-done | bytes 1048608 | tf_op jit(solution)/shard_map/ppermute | solution.py:837
  473.9 4.8 tokens_sum.6.rest_0_
  478.7 16.7 %collective-permute-done.46.passed = bf16[4112,128]{1,0:T(8,128)(2,1)S(1)} collective-permute-done((bf16[4112,128]{1,0:T(8,128)(2,1)S(1)}, bf16[4112,128]{1,0:T(8,128)(2,1)S(1)}, u32[]{:S(2)}, u32[]{:S(2)}) %collective-permute-start.46) | collective-permute-done | bytes 1052704 | tf_op jit(solution)/shard_map/ppermute | solution.py:837
  496.4 4.0 tokens_sum.7
  500.3 2.6 slice_convert_fusion.2
  (303 shorter events, 104.2 us)
Async XLA Ops:
  7.2 389.5 %reduce-scatter.3.cloned.1.call-start = ((), (), s32[]{:S(2)}) async-start(), calls=%async_computation.2 | async-start | bytes 11796480 | tf_op jit(solution)/shard_map/reduce_scatter | solution.py:846
  9.1 30.7 %collective-permute-start = (bf16[256,2048]{1,0:T(8,128)(2,1)S(1)}, bf16[256,2048]{1,0:T(8,128)(2,1)S(1)}, u32[]{:S(2)}, u32[]{:S(2)}) collective-permute-start(bf16[256,2048]{1,0:T(8,128)(2,1)S(1)} %pad_maximum_fusion), channel_id=1, source_target_pairs={{0,8},{4,12},{8,0},{12,4},{16,24},{20,28},{24,16},{28,20},{1,9},{5... | collective-permute-start | bytes 3145736 | tf_op jit(solution)/shard_map/ppermute | solution.py:47
  12.1 27.8 %collective-permute-start.1 = (bf16[256,2048]{1,0:T(8,128)(2,1)S(1)}, bf16[256,2048]{1,0:T(8,128)(2,1)S(1)}, u32[]{:S(2)}, u32[]{:S(2)}) collective-permute-start(bf16[256,2048]{1,0:T(8,128)(2,1)S(1)} %pad_maximum_fusion), channel_id=1, source_target_pairs={{0,16},{4,20},{8,24},{12,28},{16,0},{20,4},{24,8},{28,12},{1,17},{... | collective-permute-start | bytes 3145736 | tf_op jit(solution)/shard_map/ppermute | solution.py:47
  39.8 14.2 %collective-permute-start.2 = (bf16[128,2048]{1,0:T(8,128)(2,1)S(1)}, bf16[128,2048]{1,0:T(8,128)(2,1)S(1)}, u32[]{:S(2)}, u32[]{:S(2)}) collective-permute-start(bf16[128,2048]{1,0:T(8,128)(2,1)S(1)} %slice.171), channel_id=1, source_target_pairs={{0,16},{4,20},{8,24},{12,28},{16,0},{20,4},{24,8},{28,12},{1,17},{... | collective-permute-start | bytes 1572872 | tf_op jit(solution)/shard_map/ppermute | solution.py:47
  41.7 13.9 %collective-permute-start.3 = (bf16[128,2048]{1,0:T(8,128)(2,1)S(1)}, bf16[128,2048]{1,0:T(8,128)(2,1)S(1)}, u32[]{:S(2)}, u32[]{:S(2)}) collective-permute-start(bf16[128,2048]{1,0:T(8,128)(2,1)S(1)} %slice.172), channel_id=1, source_target_pairs={{0,8},{4,12},{8,0},{12,4},{16,24},{20,28},{24,16},{28,20},{1,9},{5... | collective-permute-start | bytes 1572872 | tf_op jit(solution)/shard_map/ppermute | solution.py:47
  60.4 31.0 %collective-permute-start.6 = (bf16[1024,2048]{1,0:T(8,128)(2,1)}, bf16[1024,2048]{1,0:T(8,128)(2,1)}, u32[]{:S(2)}, u32[]{:S(2)}) collective-permute-start(bf16[1024,2048]{1,0:T(8,128)(2,1)} %constant_dynamic-update-slice_fusion.w_a.dense_a), channel_id=1, source_target_pairs={{0,4},{4,0},{8,12},{12,8},{16,20},{20,16},{24,28},{28,24},{1,5},{5... | collective-permute-start | bytes 12582920 | tf_op jit(solution)/shard_map/ppermute | solution.py:47
  61.6 25.6 %collective-permute-start.4 = (bf16[256,2048]{1,0:T(8,128)(2,1)S(1)}, bf16[256,2048]{1,0:T(8,128)(2,1)S(1)}, u32[]{:S(2)}, u32[]{:S(2)}) collective-permute-start(bf16[256,2048]{1,0:T(8,128)(2,1)S(1)} %convert_element_type.247.refs_0_), channel_id=1, source_target_pairs={{0,8},{4,12},{8,0},{12,4},{16,24},{20,28},{24,16},{28,20},{1,9},{5... | collective-permute-start | bytes 3145736 | tf_op jit(solution)/shard_map/ppermute | solution.py:47
  63.2 25.4 %collective-permute-start.5 = (bf16[256,2048]{1,0:T(8,128)(2,1)S(1)}, bf16[256,2048]{1,0:T(8,128)(2,1)}, u32[]{:S(2)}, u32[]{:S(2)}) collective-permute-start(bf16[256,2048]{1,0:T(8,128)(2,1)S(1)} %convert_element_type.247.refs_0_), channel_id=1, source_target_pairs={{0,16},{4,20},{8,24},{12,28},{16,0},{20,4},{24,8},{28,12},{1,17},{... | collective-permute-start | bytes 3145736 | tf_op jit(solution)/shard_map/ppermute | solution.py:47
  88.6 14.3 %collective-permute-start.7 = (bf16[128,2048]{1,0:T(8,128)(2,1)S(1)}, bf16[128,2048]{1,0:T(8,128)(2,1)}, u32[]{:S(2)}, u32[]{:S(2)}) collective-permute-start(bf16[128,2048]{1,0:T(8,128)(2,1)S(1)} %slice.174), channel_id=1, source_target_pairs={{0,16},{4,20},{8,24},{12,28},{16,0},{20,4},{24,8},{28,12},{1,17},{... | collective-permute-start | bytes 1572872 | tf_op jit(solution)/shard_map/ppermute | solution.py:47
  90.8 13.1 %collective-permute-start.8 = (bf16[128,2048]{1,0:T(8,128)(2,1)S(1)}, bf16[128,2048]{1,0:T(8,128)(2,1)}, u32[]{:S(2)}, u32[]{:S(2)}) collective-permute-start(bf16[128,2048]{1,0:T(8,128)(2,1)S(1)} %slice.175), channel_id=1, source_target_pairs={{0,8},{4,12},{8,0},{12,4},{16,24},{20,28},{24,16},{28,20},{1,9},{5... | collective-permute-start | bytes 1572872 | tf_op jit(solution)/shard_map/ppermute | solution.py:47
  103.9 37.4 %collective-permute-start.9 = (bf16[1024,1024]{1,0:T(8,128)(2,1)}, bf16[1024,1024]{1,0:T(8,128)(2,1)}, u32[]{:S(2)}, u32[]{:S(2)}) collective-permute-start(bf16[1024,1024]{1,0:T(8,128)(2,1)} %get-tuple-element.136.own), channel_id=1, source_target_pairs={{0,4},{4,8},{8,12},{12,16},{16,20},{20,24},{24,28},{1,5},{5,9},{9,... | collective-permute-start | bytes 6291464 | tf_op jit(solution)/shard_map/ppermute | solution.py:857
  106.5 5.5 %collective-permute-start.11 = (bf16[256,2048]{1,0:T(8,128)(2,1)S(1)}, bf16[256,2048]{1,0:T(8,128)(2,1)S(1)}, u32[]{:S(2)}, u32[]{:S(2)}) collective-permute-start(bf16[256,2048]{1,0:T(8,128)(2,1)S(1)} %convert_element_type.247.refs_0_), channel_id=1, source_target_pairs={{0,4},{4,0},{8,12},{12,8},{16,20},{20,16},{24,28},{28,24},{1,5},{5... | collective-permute-start | bytes 3145736 | tf_op jit(solution)/shard_map/ppermute | solution.py:47
  106.6 6.9 %collective-permute-start.12 = (bf16[256,2048]{1,0:T(8,128)(2,1)S(1)}, bf16[256,2048]{1,0:T(8,128)(2,1)S(1)}, u32[]{:S(2)}, u32[]{:S(2)}) collective-permute-start(bf16[256,2048]{1,0:T(8,128)(2,1)S(1)} %collective-permute-done.4.refs_1_), channel_id=1, source_target_pairs={{0,4},{4,0},{8,12},{12,8},{16,20},{20,16},{24,28},{28,24},{1,5},{5... | collective-permute-start | bytes 3145736 | tf_op jit(solution)/shard_map/ppermute | solution.py:47
  107.0 10.0 %collective-permute-start.13 = (bf16[256,2048]{1,0:T(8,128)(2,1)}, bf16[256,2048]{1,0:T(8,128)(2,1)}, u32[]{:S(2)}, u32[]{:S(2)}) collective-permute-start(bf16[256,2048]{1,0:T(8,128)(2,1)} %collective-permute-done.5.refs_2_), channel_id=1, source_target_pairs={{0,4},{4,0},{8,12},{12,8},{16,20},{20,16},{24,28},{28,24},{1,5},{5... | collective-permute-start | bytes 3145736 | tf_op jit(solution)/shard_map/ppermute | solution.py:47
  108.4 37.4 %collective-permute-start.10 = (bf16[512,1024]{1,0:T(8,128)(2,1)S(1)}, bf16[512,1024]{1,0:T(8,128)(2,1)}, u32[]{:S(2)}, u32[]{:S(2)}) collective-permute-start(bf16[512,1024]{1,0:T(8,128)(2,1)S(1)} %slice.135), channel_id=1, source_target_pairs={{4,0},{8,4},{12,8},{16,12},{20,16},{24,20},{28,24},{5,1},{9,5},{13... | collective-permute-start | bytes 3145736 | tf_op jit(solution)/shard_map/ppermute | solution.py:857
  112.0 5.0 collective-permute-start.14
  113.5 3.6 collective-permute-start.15
  141.4 25.4 %collective-permute-start.16 = (bf16[2048,256]{1,0:T(8,128)(2,1)S(1)}, bf16[2048,256]{1,0:T(8,128)(2,1)S(1)}, u32[]{:S(2)}, u32[]{:S(2)}) collective-permute-start(bf16[2048,256]{1,0:T(8,128)(2,1)S(1)} %convert_element_type.251.mine.rest_0_), channel_id=1, source_target_pairs={{0,8},{4,12},{8,0},{12,4},{16,24},{20,28},{24,16},{28,20},{1,9},{5... | collective-permute-start | bytes 3145736 | tf_op jit(solution)/shard_map/ppermute | solution.py:47
  142.6 25.1 %collective-permute-start.17 = (bf16[2048,256]{1,0:T(8,128)(2,1)S(1)}, bf16[2048,256]{1,0:T(8,128)(2,1)S(1)}, u32[]{:S(2)}, u32[]{:S(2)}) collective-permute-start(bf16[2048,256]{1,0:T(8,128)(2,1)S(1)} %convert_element_type.251.mine.rest_0_), channel_id=1, source_target_pairs={{0,16},{4,20},{8,24},{12,28},{16,0},{20,4},{24,8},{28,12},{1,17},{... | collective-permute-start | bytes 3145736 | tf_op jit(solution)/shard_map/ppermute | solution.py:47
  145.8 42.7 %collective-permute-start.20 = (bf16[2048,256]{1,0:T(8,128)(2,1)S(1)}, bf16[2048,256]{1,0:T(8,128)(2,1)S(1)}, u32[]{:S(2)}, u32[]{:S(2)}) collective-permute-start(bf16[2048,256]{1,0:T(8,128)(2,1)S(1)} %convert_element_type.251.mine.rest_0_), channel_id=1, source_target_pairs={{0,4},{4,0},{8,12},{12,8},{16,20},{20,16},{24,28},{28,24},{1,5},{5... | collective-permute-start | bytes 3145736 | tf_op jit(solution)/shard_map/ppermute | solution.py:47
  167.8 20.7 %collective-permute-start.18 = (bf16[1024,256]{1,0:T(8,128)(2,1)S(1)}, bf16[1024,256]{1,0:T(8,128)(2,1)S(1)}, u32[]{:S(2)}, u32[]{:S(2)}) collective-permute-start(bf16[1024,256]{1,0:T(8,128)(2,1)S(1)} %slice.177), channel_id=1, source_target_pairs={{0,16},{4,20},{8,24},{12,28},{16,0},{20,4},{24,8},{28,12},{1,17},{... | collective-permute-start | bytes 1572872 | tf_op jit(solution)/shard_map/ppermute | solution.py:47
  168.6 19.9 %collective-permute-start.19 = (bf16[1024,256]{1,0:T(8,128)(2,1)S(1)}, bf16[1024,256]{1,0:T(8,128)(2,1)S(1)}, u32[]{:S(2)}, u32[]{:S(2)}) collective-permute-start(bf16[1024,256]{1,0:T(8,128)(2,1)S(1)} %slice.178), channel_id=1, source_target_pairs={{0,8},{4,12},{8,0},{12,4},{16,24},{20,28},{24,16},{28,20},{1,9},{5... | collective-permute-start | bytes 1572872 | tf_op jit(solution)/shard_map/ppermute | solution.py:47
  170.3 37.5 %collective-permute-start.21 = (bf16[2048,256]{1,0:T(8,128)(2,1)S(1)}, bf16[2048,256]{1,0:T(8,128)(2,1)S(1)}, u32[]{:S(2)}, u32[]{:S(2)}) collective-permute-start(bf16[2048,256]{1,0:T(8,128)(2,1)S(1)} %collective-permute-done.16.mine.rest_1_), channel_id=1, source_target_pairs={{0,4},{4,0},{8,12},{12,8},{16,20},{20,16},{24,28},{28,24},{1,5},{5... | collective-permute-start | bytes 3145736 | tf_op jit(solution)/shard_map/ppermute | solution.py:47
  195.9 29.0 %collective-permute-start.23 = (bf16[4096,128]{1,0:T(8,128)(2,1)}, bf16[4096,128]{1,0:T(8,128)(2,1)S(1)}, u32[]{:S(2)}, u32[]{:S(2)}) collective-permute-start(bf16[4096,128]{1,0:T(8,128)(2,1)} %bitcast.103), channel_id=1, source_target_pairs={{0,1},{3,2},{4,5},{7,6},{8,9},{11,10},{12,13},{15,14},{16,17},{19,... | collective-permute-start | bytes 3145736 | tf_op jit(solution)/shard_map/ppermute | solution.py:837
  199.5 52.1 %collective-permute-start.29 = (bf16[1024,1024]{1,0:T(8,128)(2,1)}, bf16[1024,1024]{1,0:T(8,128)(2,1)}, u32[]{:S(2)}, u32[]{:S(2)}) collective-permute-start(bf16[1024,1024]{1,0:T(8,128)(2,1)} %get-tuple-element.182), channel_id=1, source_target_pairs={{4,0},{8,4},{12,8},{16,12},{20,16},{24,20},{28,24},{5,1},{9,5},{13... | collective-permute-start | bytes 6291464 | tf_op jit(solution)/shard_map/ppermute | solution.py:857
  200.8 50.8 %collective-permute-start.30 = (bf16[512,1024]{1,0:T(8,128)(2,1)}, bf16[512,1024]{1,0:T(8,128)(2,1)}, u32[]{:S(2)}, u32[]{:S(2)}) collective-permute-start(bf16[512,1024]{1,0:T(8,128)(2,1)} %get-tuple-element.183), channel_id=1, source_target_pairs={{0,4},{4,8},{8,12},{12,16},{16,20},{20,24},{24,28},{1,5},{5,9},{9,... | collective-permute-start | bytes 3145736 | tf_op jit(solution)/shard_map/ppermute | solution.py:857
  207.0 38.2 %collective-permute-start.24 = (bf16[2048,256]{1,0:T(8,128)(2,1)S(1)}, bf16[2048,256]{1,0:T(8,128)(2,1)}, u32[]{:S(2)}, u32[]{:S(2)}) collective-permute-start(bf16[2048,256]{1,0:T(8,128)(2,1)S(1)} %collective-permute-done.17.mine.rest_2_), channel_id=1, source_target_pairs={{0,4},{4,0},{8,12},{12,8},{16,20},{20,16},{24,28},{28,24},{1,5},{5... | collective-permute-start | bytes 3145736 | tf_op jit(solution)/shard_map/ppermute | solution.py:47
  222.4 29.3 %collective-permute-start.22 = (bf16[4096,128]{1,0:T(8,128)(2,1)S(1)}, bf16[4096,128]{1,0:T(8,128)(2,1)}, u32[]{:S(2)}, u32[]{:S(2)}) collective-permute-start(bf16[4096,128]{1,0:T(8,128)(2,1)S(1)} %bitcast.100), channel_id=1, source_target_pairs={{0,1},{3,2},{4,5},{7,6},{8,9},{11,10},{12,13},{15,14},{16,17},{19,... | collective-permute-start | bytes 3145736 | tf_op jit(solution)/shard_map/ppermute | solution.py:837
  225.3 26.4 %collective-permute-start.25 = (bf16[4096,128]{1,0:T(8,128)(2,1)S(1)}, bf16[4096,128]{1,0:T(8,128)(2,1)}, u32[]{:S(2)}, u32[]{:S(2)}) collective-permute-start(bf16[4096,128]{1,0:T(8,128)(2,1)S(1)} %add_convert_fusion.15), channel_id=1, source_target_pairs={{1,2},{2,1},{5,6},{6,5},{9,10},{10,9},{13,14},{14,13},{17,18},{18,... | collective-permute-start | bytes 3145736 | tf_op jit(solution)/shard_map/ppermute | solution.py:834
  245.2 15.5 %collective-permute-start.26 = (bf16[2048,256]{1,0:T(8,128)(2,1)}, bf16[2048,256]{1,0:T(8,128)(2,1)}, u32[]{:S(2)}, u32[]{:S(2)}) collective-permute-start(bf16[2048,256]{1,0:T(8,128)(2,1)} %constant_dynamic-update-slice_fusion.5.rest_3_.mine), channel_id=1, source_target_pairs={{0,4},{4,0},{8,12},{12,8},{16,20},{20,16},{24,28},{28,24},{1,5},{5... | collective-permute-start | bytes 3145736 | tf_op jit(solution)/shard_map/ppermute | solution.py:47
  251.7 248.7 %reduce-scatter.5.cloned.1.call-start = ((), (), s32[]{:S(2)}) async-start(), calls=%async_computation.3 | async-start | bytes 16515072 | tf_op jit(solution)/shard_map/reduce_scatter | solution.py:846
  255.5 29.1 %collective-permute-start.27 = (bf16[4096,128]{1,0:T(8,128)(2,1)}, bf16[4096,128]{1,0:T(8,128)(2,1)}, u32[]{:S(2)}, u32[]{:S(2)}) collective-permute-start(bf16[4096,128]{1,0:T(8,128)(2,1)} %fusion), channel_id=1, source_target_pairs={{0,1},{3,2},{1,0},{2,3},{4,5},{7,6},{5,4},{6,7},{8,9},{11,10},{9,8... | collective-permute-start | bytes 3145736 | tf_op jit(solution)/shard_map/ppermute | solution.py:837
  259.1 25.4 %collective-permute-start.28 = (bf16[4096,128]{1,0:T(8,128)(2,1)S(1)}, bf16[4096,128]{1,0:T(8,128)(2,1)S(1)}, u32[]{:S(2)}, u32[]{:S(2)}) collective-permute-start(bf16[4096,128]{1,0:T(8,128)(2,1)S(1)} %add_convert_fusion.14), channel_id=1, source_target_pairs={{1,2},{2,1},{5,6},{6,5},{9,10},{10,9},{13,14},{14,13},{17,18},{18,... | collective-permute-start | bytes 3145736 | tf_op jit(solution)/shard_map/ppermute | solution.py:834
  287.1 32.4 %collective-permute-start.31 = (bf16[4096,128]{1,0:T(8,128)(2,1)}, bf16[4096,128]{1,0:T(8,128)(2,1)S(1)}, u32[]{:S(2)}, u32[]{:S(2)}) collective-permute-start(bf16[4096,128]{1,0:T(8,128)(2,1)} %fusion.1), channel_id=1, source_target_pairs={{0,1},{3,2},{1,0},{2,3},{4,5},{7,6},{5,4},{6,7},{8,9},{11,10},{9,8... | collective-permute-start | bytes 3145736 | tf_op jit(solution)/shard_map/ppermute | solution.py:837
  289.8 29.7 %collective-permute-start.32 = (bf16[4096,128]{1,0:T(8,128)(2,1)S(1)}, bf16[4096,128]{1,0:T(8,128)(2,1)}, u32[]{:S(2)}, u32[]{:S(2)}) collective-permute-start(bf16[4096,128]{1,0:T(8,128)(2,1)S(1)} %add_convert_fusion.12), channel_id=1, source_target_pairs={{1,2},{2,1},{5,6},{6,5},{9,10},{10,9},{13,14},{14,13},{17,18},{18,... | collective-permute-start | bytes 3145736 | tf_op jit(solution)/shard_map/ppermute | solution.py:834
  322.0 24.9 %collective-permute-start.33 = (bf16[4096,128]{1,0:T(8,128)(2,1)S(1)}, bf16[4096,128]{1,0:T(8,128)(2,1)S(1)}, u32[]{:S(2)}, u32[]{:S(2)}) collective-permute-start(bf16[4096,128]{1,0:T(8,128)(2,1)S(1)} %fusion.2), channel_id=1, source_target_pairs={{0,1},{3,2},{1,0},{2,3},{4,5},{7,6},{5,4},{6,7},{8,9},{11,10},{9,8... | collective-permute-start | bytes 3145736 | tf_op jit(solution)/shard_map/ppermute | solution.py:837
  323.1 23.8 %collective-permute-start.34 = (bf16[4096,128]{1,0:T(8,128)(2,1)S(1)}, bf16[4096,128]{1,0:T(8,128)(2,1)S(1)}, u32[]{:S(2)}, u32[]{:S(2)}) collective-permute-start(bf16[4096,128]{1,0:T(8,128)(2,1)S(1)} %add_convert_fusion.10), channel_id=1, source_target_pairs={{1,2},{2,1},{5,6},{6,5},{9,10},{10,9},{13,14},{14,13},{17,18},{18,... | collective-permute-start | bytes 3145736 | tf_op jit(solution)/shard_map/ppermute | solution.py:834
  348.3 31.7 %collective-permute-start.35 = (bf16[4096,128]{1,0:T(8,128)(2,1)}, bf16[4096,128]{1,0:T(8,128)(2,1)}, u32[]{:S(2)}, u32[]{:S(2)}) collective-permute-start(bf16[4096,128]{1,0:T(8,128)(2,1)} %fusion.3), channel_id=1, source_target_pairs={{0,1},{3,2},{1,0},{2,3},{4,5},{7,6},{5,4},{6,7},{8,9},{11,10},{9,8... | collective-permute-start | bytes 3145736 | tf_op jit(solution)/shard_map/ppermute | solution.py:837
  352.7 27.4 %collective-permute-start.36 = (bf16[4096,128]{1,0:T(8,128)(2,1)S(1)}, bf16[4096,128]{1,0:T(8,128)(2,1)}, u32[]{:S(2)}, u32[]{:S(2)}) collective-permute-start(bf16[4096,128]{1,0:T(8,128)(2,1)S(1)} %add_convert_fusion.8), channel_id=1, source_target_pairs={{1,2},{2,1},{5,6},{6,5},{9,10},{10,9},{13,14},{14,13},{17,18},{18,... | collective-permute-start | bytes 3145736 | tf_op jit(solution)/shard_map/ppermute | solution.py:834
  385.9 3.9 collective-permute-start.38
  389.8 6.9 %collective-permute-start.39 = (f32[1,1728]{1,0:T(1,128)S(1)}, f32[1,1728]{1,0:T(1,128)S(1)}, u32[]{:S(2)}, u32[]{:S(2)}) collective-permute-start(f32[1,1728]{1,0:T(1,128)S(1)} %slice.185), channel_id=1, source_target_pairs={{0,8},{4,12},{8,0},{12,4},{16,24},{20,28},{24,16},{28,20},{1,9},{5... | collective-permute-start | bytes 20744 | tf_op jit(solution)/shard_map/ppermute | solution.py:47
  392.4 16.1 %collective-permute-start.40 = (bf16[4096,128]{1,0:T(8,128)(2,1)S(1)}, bf16[4096,128]{1,0:T(8,128)(2,1)}, u32[]{:S(2)}, u32[]{:S(2)}) collective-permute-start(bf16[4096,128]{1,0:T(8,128)(2,1)S(1)} %add_convert_fusion.6), channel_id=1, source_target_pairs={{1,2},{2,1},{5,6},{6,5},{9,10},{10,9},{13,14},{14,13},{17,18},{18,... | collective-permute-start | bytes 3145736 | tf_op jit(solution)/shard_map/ppermute | solution.py:834
  394.1 24.7 %collective-permute-start.41 = (bf16[4096,128]{1,0:T(8,128)(2,1)}, bf16[4096,128]{1,0:T(8,128)(2,1)}, u32[]{:S(2)}, u32[]{:S(2)}) collective-permute-start(bf16[4096,128]{1,0:T(8,128)(2,1)} %fusion.4.settled), channel_id=1, source_target_pairs={{0,1},{3,2},{1,0},{2,3},{4,5},{7,6},{5,4},{6,7},{8,9},{11,10},{9,8... | collective-permute-start | bytes 3145736 | tf_op jit(solution)/shard_map/ppermute | solution.py:837
  421.6 23.3 %collective-permute-start.42 = (bf16[4112,128]{1,0:T(8,128)(2,1)}, bf16[4112,128]{1,0:T(8,128)(2,1)}, u32[]{:S(2)}, u32[]{:S(2)}) collective-permute-start(bf16[4112,128]{1,0:T(8,128)(2,1)} %pad_select_fusion.settled), channel_id=1, source_target_pairs={{0,1},{3,2},{1,0},{2,3},{4,5},{7,6},{5,4},{6,7},{8,9},{11,10},{9,8... | collective-permute-start | bytes 3158024 | tf_op jit(solution)/shard_map/ppermute | solution.py:837
  424.9 22.5 %collective-permute-start.44 = (bf16[4096,128]{1,0:T(8,128)(2,1)S(1)}, bf16[4096,128]{1,0:T(8,128)(2,1)S(1)}, u32[]{:S(2)}, u32[]{:S(2)}) collective-permute-start(bf16[4096,128]{1,0:T(8,128)(2,1)S(1)} %add_convert_fusion.3), channel_id=1, source_target_pairs={{1,2},{2,1},{5,6},{6,5},{9,10},{10,9},{13,14},{14,13},{17,18},{18,... | collective-permute-start | bytes 3145736 | tf_op jit(solution)/shard_map/ppermute | solution.py:834
  446.6 25.7 %collective-permute-start.43 = (bf16[4112,128]{1,0:T(8,128)(2,1)S(1)}, bf16[4112,128]{1,0:T(8,128)(2,1)S(1)}, u32[]{:S(2)}, u32[]{:S(2)}) collective-permute-start(bf16[4112,128]{1,0:T(8,128)(2,1)S(1)} %add_convert_fusion.1), channel_id=1, source_target_pairs={{1,2},{2,1},{5,6},{6,5},{9,10},{10,9},{13,14},{14,13},{17,18},{18,... | collective-permute-start | bytes 3158024 | tf_op jit(solution)/shard_map/ppermute | solution.py:834
  447.6 24.7 %collective-permute-start.45 = (bf16[4096,128]{1,0:T(8,128)(2,1)S(1)}, bf16[4096,128]{1,0:T(8,128)(2,1)S(1)}, u32[]{:S(2)}, u32[]{:S(2)}) collective-permute-start(bf16[4096,128]{1,0:T(8,128)(2,1)S(1)} %add_convert_fusion.2.settled), channel_id=1, source_target_pairs={{1,0},{2,3},{5,4},{6,7},{9,8},{10,11},{13,12},{14,15},{17,16},{18,... | collective-permute-start | bytes 3145736 | tf_op jit(solution)/shard_map/ppermute | solution.py:837
  472.6 22.8 %collective-permute-start.46 = (bf16[4112,128]{1,0:T(8,128)(2,1)S(1)}, bf16[4112,128]{1,0:T(8,128)(2,1)S(1)}, u32[]{:S(2)}, u32[]{:S(2)}) collective-permute-start(bf16[4112,128]{1,0:T(8,128)(2,1)S(1)} %add_convert_fusion.settled), channel_id=1, source_target_pairs={{1,0},{2,3},{5,4},{6,7},{9,8},{10,11},{13,12},{14,15},{17,16},{18,... | collective-permute-start | bytes 3158024 | tf_op jit(solution)/shard_map/ppermute | solution.py:837
  (51 other events, 582.2 us)
Sparse Core Ops, SparseCore 0:
  251.8 81.8 reduce-scatter.2
  396.9 102.5 reduce-scatter.4

commit v5 on v4

--- a/solution.py
+++ b/solution.py
@@ -423,7 +423,7 @@
         out_shape=jax.ShapeDtypeStruct((blocks, BLOCK, total), bf16),
         input_output_aliases={4: 0} if extra else {},
         compiler_params=params(),
-        cost_estimate=cost(2 * rows * blocks * BLOCK * width, 2 * blocks * BLOCK * (rows + width) + 2 * rows * width),
+        cost_estimate=cost(0 if extra else 2 * rows * blocks * BLOCK * width, 0),
         name="row_grad",
     )(where, left_a, left_b, right, *extra)
 
@@ -725,7 +725,7 @@
         out_specs=[out] * count + [pl.BlockSpec((8, width), lambda i: (0, 0))],
         out_shape=[jax.ShapeDtypeStruct(slabs, bf16)] * count + [jax.ShapeDtypeStruct((8, width), f32)],
         compiler_params=params(),
-        cost_estimate=cost(2 * count * tile * depth * width, 14_000_000),
+        cost_estimate=cost(0, 0) if count == 2 else cost(2 * count * tile * depth * width, 14_000_000),
         name="input_back",
     )(mixed, w_a, w_b, second, tok, mean, inverse, gains)
 
@@ -1025,11 +1025,13 @@
     tails += [second, *more]
     sums = sums + more_sums + part
     row_blocks = row_grad(places, one_a, one_b, after(grad_mixed, part), sum(widths), widths[0], expanded)
-    seen = line.slot(tails[2], row_blocks)
     vector = part
     if cube:
-        vector = after(vector_parts(sums, grad_bias, expand_bias_sums, project_bias_sums), seen)
-        vector = halved(halved(halved(vector, CORE), ALONG_Y), ALONG_X)[0]
+        vector = after(vector_parts(sums, grad_bias, expand_bias_sums, project_bias_sums), part)
+        vector = halved(halved(vector, CORE), ALONG_Y)
+    seen = line.slot(tails[2], row_blocks)
+    if cube:
+        vector = halved(after(vector, seen), ALONG_X)[0]
     row_blocks, grad_down, vector = lax.optimization_barrier((row_blocks, grad_down, vector))
     if cube:
         grad_rows = scatter_blocks(row_blocks, True)

time: 521 us -> 524 us (level)
    ppermute x10, waiting for transfers between devices: 55.8 us -> 61.6 us  [slot(): self.inward = lax.ppermute(operand, 'tensor', pairs)]
    unnamed x120 -> x124, local copies, waits for them, and re-layouts: 13.9 us -> 12.8 us
  transfers between devices with their start and end apart: 49 -> 49, of which waited for: 16 -> 14; matrix products, arithmetic and copies ran while one was open for 11% -> 11% of each run, Pallas kernels for 47% -> 47%
where the time goes in v5:
time: 524 us; the launch traced here: 515 us
  Pallas kernels  240 us (46%)
  waiting for transfers between devices  96.5 us (18%)
  starting transfers between devices  67.7 us (13%)
  other arithmetic  46.3 us (9%)
  local copies, waits for them, and re-layouts  24.9 us (5%)
  blocking collectives  24.3 us (5%)
  between operations  15.5 us (3%)
    ppermute x10, waiting for transfers between devices, slot(): self.inward = lax.ppermute(operand, 'tensor', pairs)  61.6 us
    ppermute x25, waiting for transfers between devices, swap(): return lax.ppermute(value, 'dp', [(i, i ^ bit) for i in range(count)])  34.9 us
    pallas_call x3, Pallas kernels, input_back(): pl.pallas_call(input_kernel, grid=(count,), in_specs=[row(depth), weight,...  28.4 us
    pallas_call x2, Pallas kernels, row_grad(): pl.pallas_call(row_grad_kernel, grid_spec=pltpu.PrefetchScalarGridSpec(nu...  26 us
    pallas_call x4, Pallas kernels, branch_piece(): pl.pallas_call(branch_kernel, grid=(rows // tile,), in_specs=[row(attende...  25.5 us
    all_gather x1, blocking collectives, on_device(): gathered = lax.all_gather(own, 'dp', axis=0).reshape(count, -1)  24.3 us
    ppermute x25, starting transfers between devices, swap(): return lax.ppermute(value, 'dp', [(i, i ^ bit) for i in range(count)])  23.9 us
    ppermute x10, starting transfers between devices, slot(): self.inward = lax.ppermute(operand, 'tensor', pairs)  22.2 us
  transfers between devices with their start and end apart: 49, of which 14 were waited for; matrix products, arithmetic and copies ran while one was open for 11% of the time, Pallas kernels for 47%

profile of v5, /device:TPU:0, one launch (start us, length us, event | category | flops | bytes accessed | tf_op | source)
XLA Modules:
  0.0 515.0 jit_solution(475541937814838584)
XLA Ops:
  9.1 3.0 collective-permute-start
  15.4 24.3 %all_gather.3 = bf16[8,16,128]{2,1,0:T(8,128)(2,1)S(1)} all-gather(bf16[1,16,128]{2,1,0:T(8,128)(2,1)S(1)} %pad_bitcast_fusion), channel_id=1, replica_groups=mesh['dp'=8,'tensor'=4] {'dp'}, dimensions={0}, use_global_device_ids=true | all-gather | bytes 36864 | tf_op jit(solution)/shard_map/all_gather | solution.py:909
  43.4 10.7 %collective-permute-done.2 = bf16[128,2048]{1,0:T(8,128)(2,1)S(1)} collective-permute-done((bf16[128,2048]{1,0:T(8,128)(2,1)S(1)}, bf16[128,2048]{1,0:T(8,128)(2,1)S(1)}, u32[]{:S(2)}, u32[]{:S(2)}) %collective-permute-start.2) | collective-permute-done | bytes 524320 | tf_op jit(solution)/shard_map/ppermute | solution.py:47
  66.5 3.1 fusion.7
  69.6 12.0 %norm.1 = (bf16[1024,2048]{1,0:T(8,128)(2,1)}, bf16[1024,1024]{1,0:T(8,128)(2,1)}, bf16[1024,1024]{1,0:T(8,128)(2,1)}, bf16[1024,1024]{1,0:T(8,128)(2,1)}, bf16[...) custom-call(s32[8]{0:T(128)} %fusion.16.places.where, ...), custom_call_target="tpu_custom_call" | custom-call | flops 41943040 | bytes 41943040 | tf_op jit(solution)/shard_map/norm/pallas_call | solution.py:151
  81.6 5.7 %collective-permute-done.4.refs_1_ = bf16[256,2048]{1,0:T(8,128)(2,1)S(1)} collective-permute-done((bf16[256,2048]{1,0:T(8,128)(2,1)S(1)}, bf16[256,2048]{1,0:T(8,128)(2,1)S(1)}, u32[]{:S(2)}, u32[]{:S(2)}) %collective-permute-start.4) | collective-permute-done | bytes 1048608 | tf_op jit(solution)/shard_map/ppermute | solution.py:47
  91.7 11.4 %project.1 = (bf16[1024,512]{1,0:T(8,128)(2,1)}, bf16[1024,1024]{1,0:T(8,128)(2,1)}) custom-call(bf16[1024,1024]{1,0:T(8,128)(2,1)} %get-tuple-element.132.one_a.left_a, bf16[1024,1024]{1,0:T(8,128)(2,1)} %get-tuple-element.131.one_b.left_b, bf16[1024,2048]{1,0:T(8,128)(2,1)} %constant_dynamic-update-slice_fusion.w_a.dense_a, ...), custom_call_target="tpu_custom_call" | custom-call | flops 8589934592 | bytes 14000000 | tf_op jit(solution)/shard_map/project/pallas_call | solution.py:192
  104.2 2.6 collective-permute-start.9
  118.4 17.0 %expand.1 = (bf16[1024,2048]{1,0:T(8,128)(2,1)}, bf16[1024,2048]{1,0:T(8,128)(2,1)}) custom-call(bf16[1024,1024]{1,0:T(8,128)(2,1)} %get-tuple-element.140.two_a.left_a, bf16[1024,1024]{1,0:T(8,128)(2,1)} %get-tuple-element.141.two_b.left_b, f32[1,2048]{1,0:T(1,128)} %bitcast.125, bf16[256,2048]{1,0:T(8,128)(2,1)} %copy-done.8, ...), custom_call_target="tpu_custom_call" | custom-call | tf_op jit(solution)/shard_map/expand/pallas_call | solution.py:239
  135.5 6.2 %dense_back.1.grad = bf16[1024,512]{1,0:T(8,128)(2,1)} custom-call(bf16[1024,1024]{1,0:T(8,128)(2,1)} %get-tuple-element.222.up_a.right_a.a.rest_0_, bf16[1024,1024]{1,0:T(8,128)(2,1)} %get-tuple-element.149.up_b.right_b.b, bf16[1024,2048]{1,0:T(8,128)(2,1)} %constant_dynamic-update-slice_fusion.w_a.dense_a, ...), custom_call_target="tpu_custom_call" | custom-call | tf_op jit(solution)/shard_map/dense_back/pallas_call | solution.py:295
  145.9 12.0 %attend.1 = (bf16[1024,512]{1,0:T(8,128)(2,1)}, f32[2,1,1024]{2,1,0:T(1,128)}) custom-call(s32[4]{0:T(128)} %get-tuple-element.253.first, s32[4]{0:T(128)} %get-tuple-element.252.last, bf16[1024,512]{1,0:T(8,128)(2,1)} %get-tuple-element.150.q, bf16[1024,1024]{1,0:T(8,128)(2,1)} %collective-permute-done.9.left, bf16[1024,1024]{1,0:T(8,128)(2,1)} %get-tuple-element.137.own, ...), custom_call_target="tpu_custom_call" | custom-call | flops 8000000000 | bytes 10000000 | tf_op jit(solution)/shard_map/attend/pallas_call | solution.py:522
  157.8 9.3 %collective-permute-done.16.mine.rest_1_ = bf16[2048,256]{1,0:T(8,128)(2,1)S(1)} collective-permute-done((bf16[2048,256]{1,0:T(8,128)(2,1)S(1)}, bf16[2048,256]{1,0:T(8,128)(2,1)S(1)}, u32[]{:S(2)}, u32[]{:S(2)}) %collective-permute-start.16) | collective-permute-done | bytes 1048608 | tf_op jit(solution)/shard_map/ppermute | solution.py:47
  170.3 18.2 %attend_back.1 = (bf16[1024,512]{1,0:T(8,128)(2,1)}, bf16[1024,1024]{1,0:T(8,128)(2,1)}, bf16[1024,1024]{1,0:T(8,128)(2,1)}, bf16[512,1024]{1,0:T(8,128)(2,1)}) custom-call(s32[4]{0:T(128)} %get-tuple-element.253.first, s32[4]{0:T(128)} %get-tuple-element.252.last, bf16[1024,512]{1,0:T(8,128)(2,1)} %get-tuple-element.150.q, ...), custom_call_target="tpu_custom_call" | custom-call | flops 16000000000 | bytes 20000000 | tf_op jit(solution)/shard_map/attend_back/pallas_call | solution.py:605
  189.6 6.4 %branch.4 = bf16[4,1024,128]{2,1,0:T(8,128)(2,1)} custom-call(bf16[1024,512]{1,0:T(8,128)(2,1)} %get-tuple-element.176.attended.left, bf16[1024,2048]{1,0:T(8,128)(2,1)} %get-tuple-element.166.active.left, bf16[1024,2048]{1,0:T(8,128)(2,1)} %constant_dynamic-update-slice_fusion.w_a.dense_a, bf16[1024,2048]{1,0:T(8,128)(2,1)} %collective-permute-done.6.w_b.dense_b, ...), custom_call_target="tpu_custom_call" | custom-call | tf_op jit(solution)/shard_map/branch/pallas_call | solution.py:268
  196.0 3.5 collective-permute-start.23
  200.8 6.2 %collective-permute-start.30 = (bf16[512,1024]{1,0:T(8,128)(2,1)}, bf16[512,1024]{1,0:T(8,128)(2,1)}, u32[]{:S(2)}, u32[]{:S(2)}) collective-permute-start(bf16[512,1024]{1,0:T(8,128)(2,1)} %get-tuple-element.184), channel_id=1, source_target_pairs={{0,4},{4,8},{8,12},{12,16},{16,20},{20,24},{24,28},{1,5},{5,9},{9,... | collective-permute-start | bytes 3145736 | tf_op jit(solution)/shard_map/ppermute | solution.py:857
  208.8 6.4 %branch.5 = bf16[4,1024,128]{2,1,0:T(8,128)(2,1)} custom-call(bf16[1024,512]{1,0:T(8,128)(2,1)} %get-tuple-element.176.attended.left, bf16[1024,2048]{1,0:T(8,128)(2,1)} %get-tuple-element.166.active.left, bf16[1024,2048]{1,0:T(8,128)(2,1)} %constant_dynamic-update-slice_fusion.w_a.dense_a, bf16[1024,2048]{1,0:T(8,128)(2,1)} %collective-permute-done.6.w_b.dense_b, ...), custom_call_target="tpu_custom_call" | custom-call | tf_op jit(solution)/shard_map/branch/pallas_call | solution.py:268
  215.2 7.2 %column_grad.2.rest_0_ = bf16[8,2560,256]{2,1,0:T(8,128)(2,1)} custom-call(s32[8]{0:T(128)} %fusion.16.places.where, bf16[1024,512]{1,0:T(8,128)(2,1)} %get-tuple-element.176.attended.left, bf16[1024,1024]{1,0:T(8,128)(2,1)} %get-tuple-element.222.up_a.right_a.a.rest_0_, bf16[1024,1024]{1,0:T(8,128)(2,1)} %get-tuple-element.149.up_b.right_b.b), custom_call_target="tpu_custom_call" | custom-call | tf_op jit(solution)/shard_map/column_grad/pallas_call | solution.py:443
  226.9 14.6 %column_grad.3 = bf16[8,2560,256]{2,1,0:T(8,128)(2,1)} custom-call(s32[8]{0:T(128)} %fusion.16.places.where, bf16[1024,2048]{1,0:T(8,128)(2,1)} %get-tuple-element.166.active.left, bf16[1024,1024]{1,0:T(8,128)(2,1)} %get-tuple-element.222.up_a.right_a.a.rest_0_, ...), custom_call_target="tpu_custom_call", output_to_operand_aliasing={{}: (4, {})} | custom-call | tf_op jit(solution)/shard_map/column_grad/pallas_call | solution.py:443
  241.4 6.4 %branch.6 = bf16[4,1024,128]{2,1,0:T(8,128)(2,1)} custom-call(bf16[1024,512]{1,0:T(8,128)(2,1)} %get-tuple-element.176.attended.left, bf16[1024,2048]{1,0:T(8,128)(2,1)} %get-tuple-element.166.active.left, bf16[1024,2048]{1,0:T(8,128)(2,1)} %constant_dynamic-update-slice_fusion.w_a.dense_a, bf16[1024,2048]{1,0:T(8,128)(2,1)} %collective-permute-done.6.w_b.dense_b, ...), custom_call_target="tpu_custom_call" | custom-call | tf_op jit(solution)/shard_map/branch/pallas_call | solution.py:268
  251.8 2.6 fusion
  259.9 16.4 %back.1 = (bf16[1024,2048]{1,0:T(8,128)(2,1)}, f32[1,2048]{1,0:T(1,128)}) custom-call(bf16[1024,1024]{1,0:T(8,128)(2,1)} %get-tuple-element.222.up_a.right_a.a.rest_0_, bf16[1024,1024]{1,0:T(8,128)(2,1)} %get-tuple-element.149.up_b.right_b.b, bf16[2048,256]{1,0:T(8,128)(2,1)} %copy-done.2, bf16[2048,256]{1,0:T(8,128)(2,1)} %copy-done.9, ...), custom_call_target="tpu_custom_call" | custom-call | flops 8589934592 | bytes 20971520 | tf_op jit(solution)/shard_map/back/pallas_call | solution.py:341
  276.3 6.4 %branch.7 = bf16[4,1024,128]{2,1,0:T(8,128)(2,1)} custom-call(bf16[1024,512]{1,0:T(8,128)(2,1)} %get-tuple-element.176.attended.left, bf16[1024,2048]{1,0:T(8,128)(2,1)} %get-tuple-element.166.active.left, bf16[1024,2048]{1,0:T(8,128)(2,1)} %constant_dynamic-update-slice_fusion.w_a.dense_a, bf16[1024,2048]{1,0:T(8,128)(2,1)} %collective-permute-done.6.w_b.dense_b, ...), custom_call_target="tpu_custom_call" | custom-call | tf_op jit(solution)/shard_map/branch/pallas_call | solution.py:268
  282.7 2.6 fusion.1
  289.9 14.7 %second_back.1.second = bf16[1024,2048]{1,0:T(8,128)(2,1)} custom-call(bf16[1024,2048]{1,0:T(8,128)(2,1)} %get-tuple-element.197.grad.right, bf16[256,2048]{1,0:T(8,128)(2,1)} %copy-done.8, bf16[256,2048]{1,0:T(8,128)(2,1)} %copy-done.15, bf16[256,2048]{1,0:T(8,128)(2,1)} %collective-permute-done.5.refs_2_, ...), custom_call_target="tpu_custom_call" | custom-call | flops 8589934592 | bytes 16777216 | tf_op jit(solution)/shard_map/second_back/pallas_call | solution.py:389
  304.6 5.0 mix.1
  309.6 8.2 %input_back.3 = (bf16[16,256,128]{2,1,0:T(8,128)(2,1)}, f32[8,2048]{1,0:T(8,128)}) custom-call(bf16[1024,1536]{1,0:T(8,128)(2,1)} %get-tuple-element.203.mixed.right, bf16[1024,2048]{1,0:T(8,128)(2,1)} %constant_dynamic-update-slice_fusion.w_a.dense_a, bf16[1024,2048]{1,0:T(8,128)(2,1)} %collective-permute-done.6.w_b.dense_b, ...), custom_call_target="tpu_custom_call" | custom-call | flops 1610612736 | bytes 14000000 | tf_op jit(solution)/shard_map/input_back/pallas_call | solution.py:719
  324.3 7.5 %input_back.4 = (bf16[16,256,128]{2,1,0:T(8,128)(2,1)}, f32[8,2048]{1,0:T(8,128)}) custom-call(bf16[1024,1536]{1,0:T(8,128)(2,1)} %get-tuple-element.203.mixed.right, bf16[1024,2048]{1,0:T(8,128)(2,1)} %constant_dynamic-update-slice_fusion.w_a.dense_a, bf16[1024,2048]{1,0:T(8,128)(2,1)} %collective-permute-done.6.w_b.dense_b, ...), custom_call_target="tpu_custom_call" | custom-call | flops 1610612736 | bytes 14000000 | tf_op jit(solution)/shard_map/input_back/pallas_call | solution.py:719
  331.7 14.3 %row_grad.2.rest_0_ = bf16[8,256,3584]{2,1,0:T(8,128)(2,1)} custom-call(s32[8]{0:T(128)} %fusion.16.places.where, bf16[1024,1024]{1,0:T(8,128)(2,1)} %get-tuple-element.140.two_a.left_a, bf16[1024,1024]{1,0:T(8,128)(2,1)} %get-tuple-element.141.two_b.left_b, bf16[1024,2048]{1,0:T(8,128)(2,1)} %get-tuple-element.197.grad.right), custom_call_target="tpu_custom_call" | custom-call | flops 8589934592 | tf_op jit(solution)/shard_map/row_grad/pallas_call | solution.py:414
  347.4 3.8 collective-permute-start.37
  353.6 12.7 %input_back.5 = (bf16[16,256,128]{2,1,0:T(8,128)(2,1)}, bf16[16,256,128]{2,1,0:T(8,128)(2,1)}, f32[8,2048]{1,0:T(8,128)}) custom-call(bf16[1024,1536]{1,0:T(8,128)(2,1)} %get-tuple-element.203.mixed.right, bf16[1024,2048]{1,0:T(8,128)(2,1)} %constant_dynamic-update-slice_fusion.w_a.dense_a, bf16[1024,2048]{1,0:T(8,128)(2,1)} %collective-permute-done.6.w_b.dense_b, ...), custom_call_target="tpu_custom_call" | custom-call | tf_op jit(solution)/shard_map/input_back/pallas_call | solution.py:719
  368.5 3.6 collective-permute-start.36
  372.1 11.8 %row_grad.3 = bf16[8,256,3584]{2,1,0:T(8,128)(2,1)} custom-call(s32[8]{0:T(128)} %fusion.16.places.where, bf16[1024,1024]{1,0:T(8,128)(2,1)} %get-tuple-element.132.one_a.left_a, bf16[1024,1024]{1,0:T(8,128)(2,1)} %get-tuple-element.131.one_b.left_b, bf16[1024,1536]{1,0:T(8,128)(2,1)} %get-tuple-element.203.mixed.right, ...), custom_call_target="tpu_custom_call", output_to_operand_aliasing={{}: (4, {})} | custom-call | tf_op jit(solution)/shard_map/row_grad/pallas_call | solution.py:414
  383.9 2.5 add_convert_fusion.6
  386.4 2.6 fusion.4.settled
  391.5 2.6 collective-permute-start.41
  394.2 9.2 %output_sum.1 = bf16[1024,2048]{1,0:T(8,128)(2,1)} custom-call(s32[8]{0:T(128)} %fusion.16.places.where, s32[1]{0:T(128)} %bitcast.middle, bf16[1024,2048]{1,0:T(8,128)(2,1)} %tokens.3, f32[1,2048]{1,0:T(1,128)} %bitcast.128, bf16[4,1024,128]{2,1,0:T(8,128)(2,1)} %bitcast.27.refs_0_, bf16[4,1024,128]{2,1,0:T(8,128)(2,1)} %bitcast.28.refs_1_, ...), custom_call_target="tpu_custom_call" | custom-call | flops 35999997952 | bytes 17000000 | tf_op jit(solution)/shard_map/output_sum/pallas_call | solution.py:751
  403.4 2.5 maximum_maximum_fusion
  406.0 11.3 %collective-permute-done.41.passed = bf16[4096,128]{1,0:T(8,128)(2,1)S(1)} collective-permute-done((bf16[4096,128]{1,0:T(8,128)(2,1)}, bf16[4096,128]{1,0:T(8,128)(2,1)S(1)}, u32[]{:S(2)}, u32[]{:S(2)}) %collective-permute-start.41) | collective-permute-done | bytes 1048608 | tf_op jit(solution)/shard_map/ppermute | solution.py:837
  424.7 4.0 tokens_sum.4.rest_0_
  431.7 2.7 slice_convert_fusion.1
  434.4 10.8 %collective-permute-done.42.passed = bf16[4112,128]{1,0:T(8,128)(2,1)} collective-permute-done((bf16[4112,128]{1,0:T(8,128)(2,1)}, bf16[4112,128]{1,0:T(8,128)(2,1)}, u32[]{:S(2)}, u32[]{:S(2)}) %collective-permute-start.42) | collective-permute-done | bytes 1052704 | tf_op jit(solution)/shard_map/ppermute | solution.py:837
  449.0 4.0 tokens_sum.5.rest_0_
  453.0 20.5 %collective-permute-done.45.passed = bf16[4096,128]{1,0:T(8,128)(2,1)S(1)} collective-permute-done((bf16[4096,128]{1,0:T(8,128)(2,1)S(1)}, bf16[4096,128]{1,0:T(8,128)(2,1)S(1)}, u32[]{:S(2)}, u32[]{:S(2)}) %collective-permute-start.45) | collective-permute-done | bytes 1048608 | tf_op jit(solution)/shard_map/ppermute | solution.py:837
  475.1 4.0 tokens_sum.6.rest_0_
  479.1 19.0 %collective-permute-done.46.passed = bf16[4112,128]{1,0:T(8,128)(2,1)S(1)} collective-permute-done((bf16[4112,128]{1,0:T(8,128)(2,1)S(1)}, bf16[4112,128]{1,0:T(8,128)(2,1)S(1)}, u32[]{:S(2)}, u32[]{:S(2)}) %collective-permute-start.46) | collective-permute-done | bytes 1052704 | tf_op jit(solution)/shard_map/ppermute | solution.py:837
  499.1 4.0 tokens_sum.7
  503.0 2.6 slice_convert_fusion.2
  (307 shorter events, 101.7 us)
Async XLA Ops:
  7.2 386.9 %reduce-scatter.3.cloned.1.call-start = ((), (), s32[]{:S(2)}) async-start(), calls=%async_computation.2 | async-start | bytes 11796480 | tf_op jit(solution)/shard_map/reduce_scatter | solution.py:846
  9.1 30.7 %collective-permute-start = (bf16[256,2048]{1,0:T(8,128)(2,1)S(1)}, bf16[256,2048]{1,0:T(8,128)(2,1)S(1)}, u32[]{:S(2)}, u32[]{:S(2)}) collective-permute-start(bf16[256,2048]{1,0:T(8,128)(2,1)S(1)} %pad_maximum_fusion), channel_id=1, source_target_pairs={{0,8},{4,12},{8,0},{12,4},{16,24},{20,28},{24,16},{28,20},{1,9},{5... | collective-permute-start | bytes 3145736 | tf_op jit(solution)/shard_map/ppermute | solution.py:47
  12.1 27.8 %collective-permute-start.1 = (bf16[256,2048]{1,0:T(8,128)(2,1)S(1)}, bf16[256,2048]{1,0:T(8,128)(2,1)S(1)}, u32[]{:S(2)}, u32[]{:S(2)}) collective-permute-start(bf16[256,2048]{1,0:T(8,128)(2,1)S(1)} %pad_maximum_fusion), channel_id=1, source_target_pairs={{0,16},{4,20},{8,24},{12,28},{16,0},{20,4},{24,8},{28,12},{1,17},{... | collective-permute-start | bytes 3145736 | tf_op jit(solution)/shard_map/ppermute | solution.py:47
  39.9 14.2 %collective-permute-start.2 = (bf16[128,2048]{1,0:T(8,128)(2,1)S(1)}, bf16[128,2048]{1,0:T(8,128)(2,1)S(1)}, u32[]{:S(2)}, u32[]{:S(2)}) collective-permute-start(bf16[128,2048]{1,0:T(8,128)(2,1)S(1)} %slice.171), channel_id=1, source_target_pairs={{0,16},{4,20},{8,24},{12,28},{16,0},{20,4},{24,8},{28,12},{1,17},{... | collective-permute-start | bytes 1572872 | tf_op jit(solution)/shard_map/ppermute | solution.py:47
  41.7 13.9 %collective-permute-start.3 = (bf16[128,2048]{1,0:T(8,128)(2,1)S(1)}, bf16[128,2048]{1,0:T(8,128)(2,1)S(1)}, u32[]{:S(2)}, u32[]{:S(2)}) collective-permute-start(bf16[128,2048]{1,0:T(8,128)(2,1)S(1)} %slice.172), channel_id=1, source_target_pairs={{0,8},{4,12},{8,0},{12,4},{16,24},{20,28},{24,16},{28,20},{1,9},{5... | collective-permute-start | bytes 1572872 | tf_op jit(solution)/shard_map/ppermute | solution.py:47
  60.4 31.3 %collective-permute-start.6 = (bf16[1024,2048]{1,0:T(8,128)(2,1)}, bf16[1024,2048]{1,0:T(8,128)(2,1)}, u32[]{:S(2)}, u32[]{:S(2)}) collective-permute-start(bf16[1024,2048]{1,0:T(8,128)(2,1)} %constant_dynamic-update-slice_fusion.w_a.dense_a), channel_id=1, source_target_pairs={{0,4},{4,0},{8,12},{12,8},{16,20},{20,16},{24,28},{28,24},{1,5},{5... | collective-permute-start | bytes 12582920 | tf_op jit(solution)/shard_map/ppermute | solution.py:47
  61.6 25.6 %collective-permute-start.4 = (bf16[256,2048]{1,0:T(8,128)(2,1)S(1)}, bf16[256,2048]{1,0:T(8,128)(2,1)S(1)}, u32[]{:S(2)}, u32[]{:S(2)}) collective-permute-start(bf16[256,2048]{1,0:T(8,128)(2,1)S(1)} %convert_element_type.247.refs_0_), channel_id=1, source_target_pairs={{0,8},{4,12},{8,0},{12,4},{16,24},{20,28},{24,16},{28,20},{1,9},{5... | collective-permute-start | bytes 3145736 | tf_op jit(solution)/shard_map/ppermute | solution.py:47
  63.2 25.4 %collective-permute-start.5 = (bf16[256,2048]{1,0:T(8,128)(2,1)S(1)}, bf16[256,2048]{1,0:T(8,128)(2,1)}, u32[]{:S(2)}, u32[]{:S(2)}) collective-permute-start(bf16[256,2048]{1,0:T(8,128)(2,1)S(1)} %convert_element_type.247.refs_0_), channel_id=1, source_target_pairs={{0,16},{4,20},{8,24},{12,28},{16,0},{20,4},{24,8},{28,12},{1,17},{... | collective-permute-start | bytes 3145736 | tf_op jit(solution)/shard_map/ppermute | solution.py:47
  88.6 14.5 %collective-permute-start.7 = (bf16[128,2048]{1,0:T(8,128)(2,1)S(1)}, bf16[128,2048]{1,0:T(8,128)(2,1)}, u32[]{:S(2)}, u32[]{:S(2)}) collective-permute-start(bf16[128,2048]{1,0:T(8,128)(2,1)S(1)} %slice.174), channel_id=1, source_target_pairs={{0,16},{4,20},{8,24},{12,28},{16,0},{20,4},{24,8},{28,12},{1,17},{... | collective-permute-start | bytes 1572872 | tf_op jit(solution)/shard_map/ppermute | solution.py:47
  91.1 13.1 %collective-permute-start.8 = (bf16[128,2048]{1,0:T(8,128)(2,1)S(1)}, bf16[128,2048]{1,0:T(8,128)(2,1)}, u32[]{:S(2)}, u32[]{:S(2)}) collective-permute-start(bf16[128,2048]{1,0:T(8,128)(2,1)S(1)} %slice.175), channel_id=1, source_target_pairs={{0,8},{4,12},{8,0},{12,4},{16,24},{20,28},{24,16},{28,20},{1,9},{5... | collective-permute-start | bytes 1572872 | tf_op jit(solution)/shard_map/ppermute | solution.py:47
  104.2 37.4 %collective-permute-start.9 = (bf16[1024,1024]{1,0:T(8,128)(2,1)}, bf16[1024,1024]{1,0:T(8,128)(2,1)}, u32[]{:S(2)}, u32[]{:S(2)}) collective-permute-start(bf16[1024,1024]{1,0:T(8,128)(2,1)} %get-tuple-element.137.own), channel_id=1, source_target_pairs={{0,4},{4,8},{8,12},{12,16},{16,20},{20,24},{24,28},{1,5},{5,9},{9,... | collective-permute-start | bytes 6291464 | tf_op jit(solution)/shard_map/ppermute | solution.py:857
  106.8 5.5 %collective-permute-start.11 = (bf16[256,2048]{1,0:T(8,128)(2,1)S(1)}, bf16[256,2048]{1,0:T(8,128)(2,1)S(1)}, u32[]{:S(2)}, u32[]{:S(2)}) collective-permute-start(bf16[256,2048]{1,0:T(8,128)(2,1)S(1)} %convert_element_type.247.refs_0_), channel_id=1, source_target_pairs={{0,4},{4,0},{8,12},{12,8},{16,20},{20,16},{24,28},{28,24},{1,5},{5... | collective-permute-start | bytes 3145736 | tf_op jit(solution)/shard_map/ppermute | solution.py:47
  106.9 6.9 %collective-permute-start.12 = (bf16[256,2048]{1,0:T(8,128)(2,1)S(1)}, bf16[256,2048]{1,0:T(8,128)(2,1)S(1)}, u32[]{:S(2)}, u32[]{:S(2)}) collective-permute-start(bf16[256,2048]{1,0:T(8,128)(2,1)S(1)} %collective-permute-done.4.refs_1_), channel_id=1, source_target_pairs={{0,4},{4,0},{8,12},{12,8},{16,20},{20,16},{24,28},{28,24},{1,5},{5... | collective-permute-start | bytes 3145736 | tf_op jit(solution)/shard_map/ppermute | solution.py:47
  107.3 10.0 %collective-permute-start.13 = (bf16[256,2048]{1,0:T(8,128)(2,1)}, bf16[256,2048]{1,0:T(8,128)(2,1)}, u32[]{:S(2)}, u32[]{:S(2)}) collective-permute-start(bf16[256,2048]{1,0:T(8,128)(2,1)} %collective-permute-done.5.refs_2_), channel_id=1, source_target_pairs={{0,4},{4,0},{8,12},{12,8},{16,20},{20,16},{24,28},{28,24},{1,5},{5... | collective-permute-start | bytes 3145736 | tf_op jit(solution)/shard_map/ppermute | solution.py:47
  108.7 37.1 %collective-permute-start.10 = (bf16[512,1024]{1,0:T(8,128)(2,1)S(1)}, bf16[512,1024]{1,0:T(8,128)(2,1)}, u32[]{:S(2)}, u32[]{:S(2)}) collective-permute-start(bf16[512,1024]{1,0:T(8,128)(2,1)S(1)} %slice.135), channel_id=1, source_target_pairs={{4,0},{8,4},{12,8},{16,12},{20,16},{24,20},{28,24},{5,1},{9,5},{13... | collective-permute-start | bytes 3145736 | tf_op jit(solution)/shard_map/ppermute | solution.py:857
  112.3 5.1 collective-permute-start.14
  113.8 3.6 collective-permute-start.15
  141.7 25.4 %collective-permute-start.16 = (bf16[2048,256]{1,0:T(8,128)(2,1)S(1)}, bf16[2048,256]{1,0:T(8,128)(2,1)S(1)}, u32[]{:S(2)}, u32[]{:S(2)}) collective-permute-start(bf16[2048,256]{1,0:T(8,128)(2,1)S(1)} %convert_element_type.251.mine.rest_0_), channel_id=1, source_target_pairs={{0,8},{4,12},{8,0},{12,4},{16,24},{20,28},{24,16},{28,20},{1,9},{5... | collective-permute-start | bytes 3145736 | tf_op jit(solution)/shard_map/ppermute | solution.py:47
  142.9 25.1 %collective-permute-start.17 = (bf16[2048,256]{1,0:T(8,128)(2,1)S(1)}, bf16[2048,256]{1,0:T(8,128)(2,1)S(1)}, u32[]{:S(2)}, u32[]{:S(2)}) collective-permute-start(bf16[2048,256]{1,0:T(8,128)(2,1)S(1)} %convert_element_type.251.mine.rest_0_), channel_id=1, source_target_pairs={{0,16},{4,20},{8,24},{12,28},{16,0},{20,4},{24,8},{28,12},{1,17},{... | collective-permute-start | bytes 3145736 | tf_op jit(solution)/shard_map/ppermute | solution.py:47
  145.9 42.7 %collective-permute-start.20 = (bf16[2048,256]{1,0:T(8,128)(2,1)S(1)}, bf16[2048,256]{1,0:T(8,128)(2,1)S(1)}, u32[]{:S(2)}, u32[]{:S(2)}) collective-permute-start(bf16[2048,256]{1,0:T(8,128)(2,1)S(1)} %convert_element_type.251.mine.rest_0_), channel_id=1, source_target_pairs={{0,4},{4,0},{8,12},{12,8},{16,20},{20,16},{24,28},{28,24},{1,5},{5... | collective-permute-start | bytes 3145736 | tf_op jit(solution)/shard_map/ppermute | solution.py:47
  168.0 20.5 %collective-permute-start.18 = (bf16[1024,256]{1,0:T(8,128)(2,1)S(1)}, bf16[1024,256]{1,0:T(8,128)(2,1)S(1)}, u32[]{:S(2)}, u32[]{:S(2)}) collective-permute-start(bf16[1024,256]{1,0:T(8,128)(2,1)S(1)} %slice.177), channel_id=1, source_target_pairs={{0,16},{4,20},{8,24},{12,28},{16,0},{20,4},{24,8},{28,12},{1,17},{... | collective-permute-start | bytes 1572872 | tf_op jit(solution)/shard_map/ppermute | solution.py:47
  168.6 20.0 %collective-permute-start.19 = (bf16[1024,256]{1,0:T(8,128)(2,1)S(1)}, bf16[1024,256]{1,0:T(8,128)(2,1)S(1)}, u32[]{:S(2)}, u32[]{:S(2)}) collective-permute-start(bf16[1024,256]{1,0:T(8,128)(2,1)S(1)} %slice.178), channel_id=1, source_target_pairs={{0,8},{4,12},{8,0},{12,4},{16,24},{20,28},{24,16},{28,20},{1,9},{5... | collective-permute-start | bytes 1572872 | tf_op jit(solution)/shard_map/ppermute | solution.py:47
  170.3 37.5 %collective-permute-start.21 = (bf16[2048,256]{1,0:T(8,128)(2,1)S(1)}, bf16[2048,256]{1,0:T(8,128)(2,1)S(1)}, u32[]{:S(2)}, u32[]{:S(2)}) collective-permute-start(bf16[2048,256]{1,0:T(8,128)(2,1)S(1)} %collective-permute-done.16.mine.rest_1_), channel_id=1, source_target_pairs={{0,4},{4,0},{8,12},{12,8},{16,20},{20,16},{24,28},{28,24},{1,5},{5... | collective-permute-start | bytes 3145736 | tf_op jit(solution)/shard_map/ppermute | solution.py:47
  196.0 28.9 %collective-permute-start.23 = (bf16[4096,128]{1,0:T(8,128)(2,1)}, bf16[4096,128]{1,0:T(8,128)(2,1)S(1)}, u32[]{:S(2)}, u32[]{:S(2)}) collective-permute-start(bf16[4096,128]{1,0:T(8,128)(2,1)} %bitcast.103), channel_id=1, source_target_pairs={{0,1},{3,2},{4,5},{7,6},{8,9},{11,10},{12,13},{15,14},{16,17},{19,... | collective-permute-start | bytes 3145736 | tf_op jit(solution)/shard_map/ppermute | solution.py:837
  199.5 48.3 %collective-permute-start.29 = (bf16[1024,1024]{1,0:T(8,128)(2,1)}, bf16[1024,1024]{1,0:T(8,128)(2,1)}, u32[]{:S(2)}, u32[]{:S(2)}) collective-permute-start(bf16[1024,1024]{1,0:T(8,128)(2,1)} %get-tuple-element.183), channel_id=1, source_target_pairs={{4,0},{8,4},{12,8},{16,12},{20,16},{24,20},{28,24},{5,1},{9,5},{13... | collective-permute-start | bytes 6291464 | tf_op jit(solution)/shard_map/ppermute | solution.py:857
  200.8 47.0 %collective-permute-start.30 = (bf16[512,1024]{1,0:T(8,128)(2,1)}, bf16[512,1024]{1,0:T(8,128)(2,1)}, u32[]{:S(2)}, u32[]{:S(2)}) collective-permute-start(bf16[512,1024]{1,0:T(8,128)(2,1)} %get-tuple-element.184), channel_id=1, source_target_pairs={{0,4},{4,8},{8,12},{12,16},{16,20},{20,24},{24,28},{1,5},{5,9},{9,... | collective-permute-start | bytes 3145736 | tf_op jit(solution)/shard_map/ppermute | solution.py:857
  207.0 34.4 %collective-permute-start.24 = (bf16[2048,256]{1,0:T(8,128)(2,1)S(1)}, bf16[2048,256]{1,0:T(8,128)(2,1)}, u32[]{:S(2)}, u32[]{:S(2)}) collective-permute-start(bf16[2048,256]{1,0:T(8,128)(2,1)S(1)} %collective-permute-done.17.mine.rest_2_), channel_id=1, source_target_pairs={{0,4},{4,0},{8,12},{12,8},{16,20},{20,16},{24,28},{28,24},{1,5},{5... | collective-permute-start | bytes 3145736 | tf_op jit(solution)/shard_map/ppermute | solution.py:47
  222.4 29.4 %collective-permute-start.22 = (bf16[4096,128]{1,0:T(8,128)(2,1)S(1)}, bf16[4096,128]{1,0:T(8,128)(2,1)}, u32[]{:S(2)}, u32[]{:S(2)}) collective-permute-start(bf16[4096,128]{1,0:T(8,128)(2,1)S(1)} %bitcast.101), channel_id=1, source_target_pairs={{0,1},{3,2},{4,5},{7,6},{8,9},{11,10},{12,13},{15,14},{16,17},{19,... | collective-permute-start | bytes 3145736 | tf_op jit(solution)/shard_map/ppermute | solution.py:837
  225.2 26.6 %collective-permute-start.25 = (bf16[4096,128]{1,0:T(8,128)(2,1)S(1)}, bf16[4096,128]{1,0:T(8,128)(2,1)}, u32[]{:S(2)}, u32[]{:S(2)}) collective-permute-start(bf16[4096,128]{1,0:T(8,128)(2,1)S(1)} %add_convert_fusion.15), channel_id=1, source_target_pairs={{1,2},{2,1},{5,6},{6,5},{9,10},{10,9},{13,14},{14,13},{17,18},{18,... | collective-permute-start | bytes 3145736 | tf_op jit(solution)/shard_map/ppermute | solution.py:834
  247.8 255.2 %reduce-scatter.5.cloned.1.call-start = ((), (), s32[]{:S(2)}) async-start(), calls=%async_computation.3 | async-start | bytes 16515072 | tf_op jit(solution)/shard_map/reduce_scatter | solution.py:846
  251.8 8.2 %collective-permute-start.26 = (bf16[2048,256]{1,0:T(8,128)(2,1)}, bf16[2048,256]{1,0:T(8,128)(2,1)}, u32[]{:S(2)}, u32[]{:S(2)}) collective-permute-start(bf16[2048,256]{1,0:T(8,128)(2,1)} %constant_dynamic-update-slice_fusion.5.rest_3_.mine), channel_id=1, source_target_pairs={{0,4},{4,0},{8,12},{12,8},{16,20},{20,16},{24,28},{28,24},{1,5},{5... | collective-permute-start | bytes 3145736 | tf_op jit(solution)/shard_map/ppermute | solution.py:47
  254.4 28.3 %collective-permute-start.27 = (bf16[4096,128]{1,0:T(8,128)(2,1)}, bf16[4096,128]{1,0:T(8,128)(2,1)}, u32[]{:S(2)}, u32[]{:S(2)}) collective-permute-start(bf16[4096,128]{1,0:T(8,128)(2,1)} %fusion), channel_id=1, source_target_pairs={{0,1},{3,2},{1,0},{2,3},{4,5},{7,6},{5,4},{6,7},{8,9},{11,10},{9,8... | collective-permute-start | bytes 3145736 | tf_op jit(solution)/shard_map/ppermute | solution.py:837
  258.3 24.4 %collective-permute-start.28 = (bf16[4096,128]{1,0:T(8,128)(2,1)S(1)}, bf16[4096,128]{1,0:T(8,128)(2,1)S(1)}, u32[]{:S(2)}, u32[]{:S(2)}) collective-permute-start(bf16[4096,128]{1,0:T(8,128)(2,1)S(1)} %add_convert_fusion.14), channel_id=1, source_target_pairs={{1,2},{2,1},{5,6},{6,5},{9,10},{10,9},{13,14},{14,13},{17,18},{18,... | collective-permute-start | bytes 3145736 | tf_op jit(solution)/shard_map/ppermute | solution.py:834
  285.3 33.3 %collective-permute-start.31 = (bf16[4096,128]{1,0:T(8,128)(2,1)}, bf16[4096,128]{1,0:T(8,128)(2,1)S(1)}, u32[]{:S(2)}, u32[]{:S(2)}) collective-permute-start(bf16[4096,128]{1,0:T(8,128)(2,1)} %fusion.1), channel_id=1, source_target_pairs={{0,1},{3,2},{1,0},{2,3},{4,5},{7,6},{5,4},{6,7},{8,9},{11,10},{9,8... | collective-permute-start | bytes 3145736 | tf_op jit(solution)/shard_map/ppermute | solution.py:837
  288.1 30.6 %collective-permute-start.32 = (bf16[4096,128]{1,0:T(8,128)(2,1)S(1)}, bf16[4096,128]{1,0:T(8,128)(2,1)}, u32[]{:S(2)}, u32[]{:S(2)}) collective-permute-start(bf16[4096,128]{1,0:T(8,128)(2,1)S(1)} %add_convert_fusion.12), channel_id=1, source_target_pairs={{1,2},{2,1},{5,6},{6,5},{9,10},{10,9},{13,14},{14,13},{17,18},{18,... | collective-permute-start | bytes 3145736 | tf_op jit(solution)/shard_map/ppermute | solution.py:834
  321.1 24.9 %collective-permute-start.33 = (bf16[4096,128]{1,0:T(8,128)(2,1)S(1)}, bf16[4096,128]{1,0:T(8,128)(2,1)S(1)}, u32[]{:S(2)}, u32[]{:S(2)}) collective-permute-start(bf16[4096,128]{1,0:T(8,128)(2,1)S(1)} %fusion.2), channel_id=1, source_target_pairs={{0,1},{3,2},{1,0},{2,3},{4,5},{7,6},{5,4},{6,7},{8,9},{11,10},{9,8... | collective-permute-start | bytes 3145736 | tf_op jit(solution)/shard_map/ppermute | solution.py:837
  323.5 22.5 %collective-permute-start.34 = (bf16[4096,128]{1,0:T(8,128)(2,1)S(1)}, bf16[4096,128]{1,0:T(8,128)(2,1)S(1)}, u32[]{:S(2)}, u32[]{:S(2)}) collective-permute-start(bf16[4096,128]{1,0:T(8,128)(2,1)S(1)} %add_convert_fusion.10), channel_id=1, source_target_pairs={{1,2},{2,1},{5,6},{6,5},{9,10},{10,9},{13,14},{14,13},{17,18},{18,... | collective-permute-start | bytes 3145736 | tf_op jit(solution)/shard_map/ppermute | solution.py:834
  347.4 36.5 %collective-permute-start.37 = (bf16[4096,128]{1,0:T(8,128)(2,1)}, bf16[4096,128]{1,0:T(8,128)(2,1)}, u32[]{:S(2)}, u32[]{:S(2)}) collective-permute-start(bf16[4096,128]{1,0:T(8,128)(2,1)} %fusion.3), channel_id=1, source_target_pairs={{0,1},{3,2},{1,0},{2,3},{4,5},{7,6},{5,4},{6,7},{8,9},{11,10},{9,8... | collective-permute-start | bytes 3145736 | tf_op jit(solution)/shard_map/ppermute | solution.py:837
  351.6 32.3 %collective-permute-start.38 = (bf16[4096,128]{1,0:T(8,128)(2,1)S(1)}, bf16[4096,128]{1,0:T(8,128)(2,1)}, u32[]{:S(2)}, u32[]{:S(2)}) collective-permute-start(bf16[4096,128]{1,0:T(8,128)(2,1)S(1)} %add_convert_fusion.8), channel_id=1, source_target_pairs={{1,2},{2,1},{5,6},{6,5},{9,10},{10,9},{13,14},{14,13},{17,18},{18,... | collective-permute-start | bytes 3145736 | tf_op jit(solution)/shard_map/ppermute | solution.py:834
  368.5 15.3 %collective-permute-start.36 = (f32[2,1728]{1,0:T(2,128)S(1)}, f32[2,1728]{1,0:T(2,128)S(1)}, u32[]{:S(2)}, u32[]{:S(2)}) collective-permute-start(f32[2,1728]{1,0:T(2,128)S(1)} %slice.183), channel_id=1, source_target_pairs={{0,16},{4,20},{8,24},{12,28},{16,0},{20,4},{24,8},{28,12},{1,17},{... | collective-permute-start | bytes 41480 | tf_op jit(solution)/shard_map/ppermute | solution.py:47
  389.1 5.0 collective-permute-start.39
  389.8 16.1 %collective-permute-start.40 = (bf16[4096,128]{1,0:T(8,128)(2,1)}, bf16[4096,128]{1,0:T(8,128)(2,1)}, u32[]{:S(2)}, u32[]{:S(2)}) collective-permute-start(bf16[4096,128]{1,0:T(8,128)(2,1)} %add_convert_fusion.6), channel_id=1, source_target_pairs={{1,2},{2,1},{5,6},{6,5},{9,10},{10,9},{13,14},{14,13},{17,18},{18,... | collective-permute-start | bytes 3145736 | tf_op jit(solution)/shard_map/ppermute | solution.py:834
  391.5 25.7 %collective-permute-start.41 = (bf16[4096,128]{1,0:T(8,128)(2,1)}, bf16[4096,128]{1,0:T(8,128)(2,1)S(1)}, u32[]{:S(2)}, u32[]{:S(2)}) collective-permute-start(bf16[4096,128]{1,0:T(8,128)(2,1)} %fusion.4.settled), channel_id=1, source_target_pairs={{0,1},{3,2},{1,0},{2,3},{4,5},{7,6},{5,4},{6,7},{8,9},{11,10},{9,8... | collective-permute-start | bytes 3145736 | tf_op jit(solution)/shard_map/ppermute | solution.py:837
  420.7 24.5 %collective-permute-start.42 = (bf16[4112,128]{1,0:T(8,128)(2,1)}, bf16[4112,128]{1,0:T(8,128)(2,1)}, u32[]{:S(2)}, u32[]{:S(2)}) collective-permute-start(bf16[4112,128]{1,0:T(8,128)(2,1)} %pad_select_fusion.settled), channel_id=1, source_target_pairs={{0,1},{3,2},{1,0},{2,3},{4,5},{7,6},{5,4},{6,7},{8,9},{11,10},{9,8... | collective-permute-start | bytes 3158024 | tf_op jit(solution)/shard_map/ppermute | solution.py:837
  423.9 23.5 %collective-permute-start.44 = (bf16[4096,128]{1,0:T(8,128)(2,1)S(1)}, bf16[4096,128]{1,0:T(8,128)(2,1)S(1)}, u32[]{:S(2)}, u32[]{:S(2)}) collective-permute-start(bf16[4096,128]{1,0:T(8,128)(2,1)S(1)} %add_convert_fusion.3), channel_id=1, source_target_pairs={{1,2},{2,1},{5,6},{6,5},{9,10},{10,9},{13,14},{14,13},{17,18},{18,... | collective-permute-start | bytes 3145736 | tf_op jit(solution)/shard_map/ppermute | solution.py:834
  446.7 26.8 %collective-permute-start.43 = (bf16[4112,128]{1,0:T(8,128)(2,1)S(1)}, bf16[4112,128]{1,0:T(8,128)(2,1)S(1)}, u32[]{:S(2)}, u32[]{:S(2)}) collective-permute-start(bf16[4112,128]{1,0:T(8,128)(2,1)S(1)} %add_convert_fusion.1), channel_id=1, source_target_pairs={{1,2},{2,1},{5,6},{6,5},{9,10},{10,9},{13,14},{14,13},{17,18},{18,... | collective-permute-start | bytes 3158024 | tf_op jit(solution)/shard_map/ppermute | solution.py:834
  447.7 25.8 %collective-permute-start.45 = (bf16[4096,128]{1,0:T(8,128)(2,1)S(1)}, bf16[4096,128]{1,0:T(8,128)(2,1)S(1)}, u32[]{:S(2)}, u32[]{:S(2)}) collective-permute-start(bf16[4096,128]{1,0:T(8,128)(2,1)S(1)} %add_convert_fusion.2.settled), channel_id=1, source_target_pairs={{1,0},{2,3},{5,4},{6,7},{9,8},{10,11},{13,12},{14,15},{17,16},{18,... | collective-permute-start | bytes 3145736 | tf_op jit(solution)/shard_map/ppermute | solution.py:837
  473.8 24.2 %collective-permute-start.46 = (bf16[4112,128]{1,0:T(8,128)(2,1)S(1)}, bf16[4112,128]{1,0:T(8,128)(2,1)S(1)}, u32[]{:S(2)}, u32[]{:S(2)}) collective-permute-start(bf16[4112,128]{1,0:T(8,128)(2,1)S(1)} %add_convert_fusion.settled), channel_id=1, source_target_pairs={{1,0},{2,3},{5,4},{6,7},{9,8},{10,11},{13,12},{14,15},{17,16},{18,... | collective-permute-start | bytes 3158024 | tf_op jit(solution)/shard_map/ppermute | solution.py:837
  (53 other events, 598.8 us)
Sparse Core Ops, SparseCore 0:
  248.0 82.0 reduce-scatter.2
  394.3 102.1 reduce-scatter.4
